TPU v7x, 32 devices: a whole 2x2x4 slice. The times are simulated.
32 devices in a mesh: dp: 8 (over y, x, core), mp: 4 (over z).
Axes of the slice: x: 2, y: 2, z: 4, core: 2. Of those that a mesh axis runs over, the one named last changes fastest.
Arguments:
- byte_in: float32 [32, 2048, 768], P('dp', 'mp'), may hold values from -6 to 6
- latents: float32 [32, 256, 1280], P('dp', 'mp'), may hold values from -6 to 6
- cotangent: float32 [32, 256, 1280], P('dp', 'mp'), may hold values from -6 to 6
- byte_gain: float32 [768], replicated, may hold values from 0.5 to 1.5
- latent_gain: float32 [1280], replicated, may hold values from 0.5 to 1.5
- mlp_gain: float32 [1280], replicated, may hold values from 0.5 to 1.5
- w_query: bfloat16 [1280, 1280], P(None, 'mp'), may hold values from -0.15625 to 0.15625
- w_key: bfloat16 [768, 1280], P(None, 'mp'), may hold values from -0.21875 to 0.21875
- w_value: bfloat16 [768, 1280], P(None, 'mp'), may hold values from -0.21875 to 0.21875
- w_out: bfloat16 [1280, 1280], P('mp'), may hold values from -4 to 4
- b_out: float32 [1280], replicated, may hold values from -3 to 3
- w_up: bfloat16 [1280, 1280], P(None, 'mp'), may hold values from -0.15625 to 0.15625
- b_up: float32 [1280], P('mp'), may hold values from -3 to 3
- w_down: bfloat16 [1280, 1280], P('mp'), may hold values from -0.15625 to 0.15625
- b_down: float32 [1280], replicated, may hold values from -3 to 3
- byte_seg: int32 [32, 2048], P('dp'), may hold values from 0 to 2, as said below
- byte_pad: int32 [32, 2048], P('dp'), may hold values from 0 to 1, as said below
- latent_seg: int32 [32, 256], P('dp'), may hold values from 0 to 2, as said below
Outputs:
- latents_out: float32 [32, 256, 1280], P('dp', 'mp')
- grad_bytes: float32 [32, 2048, 768], P('dp', 'mp')
- grad_latents: float32 [32, 256, 1280], P('dp', 'mp')
- grad_byte_gain: float32 [768], replicated
- grad_latent_gain: float32 [1280], replicated
- grad_mlp_gain: float32 [1280], replicated
- grad_w_query: float32 [1280, 1280], P(None, 'mp')
- grad_w_key: float32 [768, 1280], P(None, 'mp')
- grad_w_value: float32 [768, 1280], P(None, 'mp')
- grad_w_out: float32 [1280, 1280], P('mp')
- grad_b_out: float32 [1280], replicated
- grad_w_up: float32 [1280, 1280], P(None, 'mp')
- grad_b_up: float32 [1280], P('mp')
- grad_w_down: float32 [1280, 1280], P('mp')
- grad_b_down: float32 [1280], replicated
Inputs may be any that keep to these rules, and one draw needn't show every extreme that they name: `byte_seg`: each packed row holds three documents in order, each with bytes and latents; one of them, drawn from the seed, covers all but fewer than 256 of the row's bytes. `byte_pad`: padding is a tail of each row, at least one byte long and shorter than the row's last document. `latent_seg`: latents follow the documents of their row in order, every document has one or more latents.
All inputs are finite; a program needn't handle non-finite values.
Results may differ from a plain program's by a relative error of at most 0.015.
Values may be sent and summed in bfloat16 or wider, within the bound.
No kernel may reach another device: no remote copies, remote signals or barrier semaphores. Data moves between devices by JAX's collectives and lax.ppermute only.
A program may use at most 192 MiB of HBM per device.

v0:
```python
import jax
import jax.numpy as jnp
from jax import lax
from jax.sharding import PartitionSpec as P

HEAD_DIM = 160


EPS = 1e-05


def normalize(field):
    average = jnp.mean(field, -1, keepdims=True)
    centred = field - average
    inv_scale = lax.rsqrt(jnp.mean(centred * centred, -1, keepdims=True) + EPS)
    return (centred * inv_scale, inv_scale)


def norm_back(grad_out, normed, inv_scale, scale_vec):
    weighted = grad_out * scale_vec
    centred_grad = (
        weighted
        - jnp.mean(weighted, -1, keepdims=True)
        - normed * jnp.mean(weighted * normed, -1, keepdims=True)
    )
    return (inv_scale * centred_grad, jnp.sum(grad_out * normed, axis=(0, 1)))


def gelu_exact(field):
    return jax.nn.gelu(field, approximate=False)


def shards(
    byte_in,
    latents,
    cotangent,
    byte_gain,
    latent_gain,
    mlp_gain,
    w_query,
    w_key,
    w_value,
    w_out,
    b_out,
    w_up,
    b_up,
    w_down,
    b_down,
    byte_seg,
    byte_pad,
    latent_seg,
):
    score_scale = HEAD_DIM ** (-0.5)
    row_count = byte_in.shape[0]
    head_cols = w_query.shape[1]
    local_heads = head_cols // HEAD_DIM
    byte_hat, byte_inv = normalize(byte_in)
    byte_norm = (byte_hat * byte_gain).astype(jnp.bfloat16)
    lat_hat, lat_inv = normalize(latents)
    lat_norm = (lat_hat * latent_gain).astype(jnp.bfloat16)
    lat_all, byte_all = (
        lax.all_gather(lat_norm, "mp", axis=1, tiled=True),
        lax.all_gather(byte_norm, "mp", axis=1, tiled=True),
    )
    key_proj = jnp.einsum(
        "rsc,cd->rsd", byte_all, w_key, preferred_element_type=jnp.float32
    ).astype(jnp.bfloat16)
    value_proj = jnp.einsum(
        "rsc,cd->rsd", byte_all, w_value, preferred_element_type=jnp.float32
    ).astype(jnp.bfloat16)
    seq_len = key_proj.shape[1]
    lat_len = lat_all.shape[1]
    queries = (
        jnp.einsum("rlc,cd->rld", lat_all, w_query, preferred_element_type=jnp.float32)
        * score_scale
    ).astype(jnp.bfloat16)
    query_heads = queries.reshape(row_count, lat_len, local_heads, HEAD_DIM)
    key_heads = key_proj.reshape(row_count, seq_len, local_heads, HEAD_DIM)
    value_heads = value_proj.reshape(row_count, seq_len, local_heads, HEAD_DIM)
    allowed = (latent_seg[:, None, :, None] == byte_seg[:, None, None, :]) & (
        byte_pad[:, None, None, :] == 1
    )

    def scores_of():
        raw_scores = jnp.einsum(
            "rlhd,rshd->rhls", query_heads, key_heads, preferred_element_type=jnp.float32
        )
        return jnp.where(allowed, raw_scores, -1e30)

    scores = scores_of()
    row_peak = jnp.max(scores, -1, keepdims=True)
    exp_scores = jnp.exp(scores - row_peak)
    row_total = jnp.sum(exp_scores, -1, keepdims=True)
    attn_probs = exp_scores / row_total
    log_total = row_peak + jnp.log(row_total)
    attended = jnp.einsum(
        "rhls,rshd->rlhd",
        attn_probs.astype(jnp.bfloat16),
        value_heads,
        preferred_element_type=jnp.float32,
    )
    attended = attended.astype(jnp.bfloat16).reshape(row_count, lat_len, head_cols)
    attn_part = jnp.einsum("rlc,cd->rld", attended, w_out, preferred_element_type=jnp.float32)
    attn_sum = lax.psum_scatter(attn_part, "mp", scatter_dimension=1, tiled=True)
    hidden = latents + attn_sum + b_out
    mid_hat, mid_inv = normalize(hidden)
    mid_norm = (mid_hat * mlp_gain).astype(jnp.bfloat16)
    mid_all = lax.all_gather(mid_norm, "mp", axis=1, tiled=True)
    pre_act = jnp.einsum("rlc,cd->rld", mid_all, w_up, preferred_element_type=jnp.float32) + b_up
    activated = gelu_exact(pre_act).astype(jnp.bfloat16)
    down_part = jnp.einsum("rlc,cd->rld", activated, w_down, preferred_element_type=jnp.float32)
    down_sum = lax.psum_scatter(
        down_part.astype(jnp.bfloat16), "mp", scatter_dimension=1, tiled=True
    ).astype(jnp.float32)
    result = hidden + down_sum + b_down
    grad_down_all = lax.all_gather(cotangent.astype(jnp.bfloat16), "mp", axis=1, tiled=True)
    grad_w_down = jnp.einsum(
        "rlc,rld->cd", activated, grad_down_all, preferred_element_type=jnp.float32
    )
    grad_act = jnp.einsum("rld,cd->rlc", grad_down_all, w_down, preferred_element_type=jnp.float32)
    _, gelu_pull = jax.vjp(gelu_exact, pre_act)
    grad_pre = gelu_pull(grad_act)[0].astype(jnp.bfloat16)
    grad_b_up = jnp.sum(grad_pre.astype(jnp.float32), axis=(0, 1))
    grad_w_up = jnp.einsum("rlc,rld->cd", mid_all, grad_pre, preferred_element_type=jnp.float32)
    grad_mid_part = jnp.einsum("rld,cd->rlc", grad_pre, w_up, preferred_element_type=jnp.float32)
    grad_mid = lax.psum_scatter(grad_mid_part, "mp", scatter_dimension=1, tiled=True)
    grad_mid_back, grad_mlp_gain = norm_back(grad_mid, mid_hat, mid_inv, mlp_gain)
    grad_hidden = cotangent + grad_mid_back
    grad_attn_all = lax.all_gather(grad_hidden.astype(jnp.bfloat16), "mp", axis=1, tiled=True)
    grad_w_out = jnp.einsum(
        "rlc,rld->cd", attended, grad_attn_all, preferred_element_type=jnp.float32
    )
    grad_att = jnp.einsum(
        "rld,cd->rlc", grad_attn_all, w_out, preferred_element_type=jnp.float32
    ).astype(jnp.bfloat16)
    grad_att = grad_att.reshape(row_count, lat_len, local_heads, HEAD_DIM)
    probs_again = jnp.exp(scores_of() - log_total)
    grad_values = jnp.einsum(
        "rhls,rlhd->rshd",
        probs_again.astype(jnp.bfloat16),
        grad_att,
        preferred_element_type=jnp.float32,
    )
    grad_values = grad_values.astype(jnp.bfloat16).reshape(row_count, seq_len, head_cols)
    grad_probs = jnp.einsum(
        "rlhd,rshd->rhls", grad_att, value_heads, preferred_element_type=jnp.float32
    )
    grad_scores = probs_again * (grad_probs - jnp.sum(probs_again * grad_probs, -1, keepdims=True))
    grad_scores = grad_scores.astype(jnp.bfloat16)
    grad_queries = jnp.einsum(
        "rhls,rshd->rlhd", grad_scores, key_heads, preferred_element_type=jnp.float32
    )
    grad_queries = grad_queries.astype(jnp.bfloat16).reshape(row_count, lat_len, head_cols)
    grad_keys = jnp.einsum(
        "rhls,rlhd->rshd", grad_scores, query_heads, preferred_element_type=jnp.float32
    )
    grad_keys = grad_keys.astype(jnp.bfloat16).reshape(row_count, seq_len, head_cols)
    grad_w_query = (
        jnp.einsum("rlc,rld->cd", lat_all, grad_queries, preferred_element_type=jnp.float32)
        * score_scale
    )
    grad_lat_part = (
        jnp.einsum("rld,cd->rlc", grad_queries, w_query, preferred_element_type=jnp.float32)
        * score_scale
    )
    grad_w_key = jnp.einsum("rsc,rsd->cd", byte_all, grad_keys, preferred_element_type=jnp.float32)
    grad_w_value = jnp.einsum(
        "rsc,rsd->cd", byte_all, grad_values, preferred_element_type=jnp.float32
    )
    grad_byte_part = jnp.einsum("rsd,cd->rsc", grad_keys, w_key, preferred_element_type=jnp.float32)
    grad_byte_part = grad_byte_part + jnp.einsum(
        "rsd,cd->rsc", grad_values, w_value, preferred_element_type=jnp.float32
    )
    grad_lat_norm, grad_byte_norm = (
        lax.psum_scatter(
            grad_lat_part.astype(jnp.bfloat16), "mp", scatter_dimension=1, tiled=True
        ).astype(jnp.float32),
        lax.psum_scatter(
            grad_byte_part.astype(jnp.bfloat16), "mp", scatter_dimension=1, tiled=True
        ).astype(jnp.float32),
    )
    grad_lat_back, grad_latent_gain = norm_back(grad_lat_norm, lat_hat, lat_inv, latent_gain)
    grad_latents = grad_hidden + grad_lat_back
    grad_bytes, grad_byte_gain = norm_back(grad_byte_norm, byte_hat, byte_inv, byte_gain)
    grad_b_out = jnp.sum(grad_hidden, axis=(0, 1))
    grad_b_down = jnp.sum(cotangent, axis=(0, 1))
    summed = (
        lax.psum(grad_w_query.astype(jnp.bfloat16), "dp").astype(jnp.float32),
        lax.psum(grad_w_key.astype(jnp.bfloat16), "dp").astype(jnp.float32),
        lax.psum(grad_w_value.astype(jnp.bfloat16), "dp").astype(jnp.float32),
        lax.psum(grad_w_out.astype(jnp.bfloat16), "dp").astype(jnp.float32),
        lax.psum(grad_w_up.astype(jnp.bfloat16), "dp").astype(jnp.float32),
        lax.psum(grad_b_up.astype(jnp.bfloat16), "dp").astype(jnp.float32),
        lax.psum(grad_w_down.astype(jnp.bfloat16), "dp").astype(jnp.float32),
    )
    small_sums = lax.psum(
        (grad_byte_gain, grad_latent_gain, grad_mlp_gain, grad_b_out, grad_b_down), ("dp", "mp")
    )
    return (
        result,
        grad_bytes,
        grad_latents,
        small_sums[0],
        small_sums[1],
        small_sums[2],
        summed[0],
        summed[1],
        summed[2],
        summed[3],
        small_sums[3],
        summed[4],
        summed[5],
        summed[6],
        small_sums[4],
    )


def solution(mesh):
    placed = (
        P("dp", "mp", None),
        P("dp", "mp", None),
        P("dp", "mp", None),
        P(),
        P(),
        P(),
        P(None, "mp"),
        P(None, "mp"),
        P(None, "mp"),
        P("mp", None),
        P(),
        P(None, "mp"),
        P("mp"),
        P("mp", None),
        P(),
        P("dp", None),
        P("dp", None),
        P("dp", None),
    )
    return jax.shard_map(
        shards,
        mesh=mesh,
        in_specs=placed,
        out_specs=(
            P("dp", "mp", None),
            P("dp", "mp", None),
            P("dp", "mp", None),
            P(),
            P(),
            P(),
            P(None, "mp"),
            P(None, "mp"),
            P(None, "mp"),
            P("mp", None),
            P(),
            P(None, "mp"),
            P("mp"),
            P("mp", None),
            P(),
        ),
        check_vma=False,
    )
```

profile of v0, /device:TPU:9, one launch (start us, length us, event | category | flops | bytes accessed | tf_op | source)
XLA Modules:
  0.0 1240.8 jit_solution(14470321355546768429)
XLA Ops:
  17.9 4.9 multiply_convert_fusion.1
  26.1 38.4 %all-gather.8.cloned.1.call-done = bf16[4,256,1280]{2,1,0:T(8,128)(2,1)} async-done(((bf16[4,64,1280]{2,1,0:T(8,128)(2,1)}), bf16[4,256,1280]{2,1,0:T(8,128)(2,1)}) %all-gather.8.cloned.1.call-update) | async-done | bytes 2621456 | tf_op jit(solution)/shard_map/all_gather | solution.py:62
  64.5 3.8 fusion.26
  68.3 214.6 %all-gather.6.cloned.1.call-done = bf16[4,2048,768]{2,1,0:T(8,128)(2,1)} async-done(((bf16[4,512,768]{2,1,0:T(8,128)(2,1)}), bf16[4,2048,768]{2,1,0:T(8,128)(2,1)}) %all-gather.6.cloned.1.call-update) | async-done | bytes 12582928 | tf_op jit(solution)/shard_map/all_gather | solution.py:63
  282.9 14.6 %convolution_convert_fusion.1 = bf16[4,2048,320]{1,2,0:T(8,128)(2,1)} fusion(bf16[4,2048,768]{2,1,0:T(8,128)(2,1)} %all-gather.6.cloned.1.call-done, bf16[768,320]{0,1:T(8,128)(2,1)S(1)} %copy-done.25), kind=kOutput, calls=%fused_computation.30 | convolution fusion | flops 4029153280 | bytes 18317312 | tf_op jit(solution)/shard_map/rsc,cd->rsd/dot_general | solution.py:65
  297.4 6.0 select_reduce_fusion
  303.4 6.5 fusion
  310.0 14.6 %convolution_convert_fusion.2 = bf16[4,2048,320]{1,2,0:T(8,128)(2,1)} fusion(bf16[4,2048,768]{2,1,0:T(8,128)(2,1)} %all-gather.6.cloned.1.call-done, bf16[768,320]{0,1:T(8,128)(2,1)S(1)} %copy-done.27), kind=kOutput, calls=%fused_computation.31 | convolution fusion | flops 4029153280 | bytes 18317312 | tf_op jit(solution)/shard_map/rsc,cd->rsd/dot_general | solution.py:68
  324.6 10.4 fusion.27
  335.8 3.9 fusion.47
  339.8 94.9 %reduce-scatter.6.cloned.1.call-done = f32[4,64,1280]{2,1,0:T(8,128)} async-done(((f32[4,256,1280]{2,1,0:T(8,128)}), f32[4,64,1280]{2,1,0:T(8,128)}) %reduce-scatter.6.cloned.1.call-update) | async-done | bytes 1310736 | tf_op jit(solution)/shard_map/reduce_scatter | solution.py:104
  439.9 52.0 %all-gather.10.cloned.1.call-done = bf16[4,256,1280]{2,1,0:T(8,128)(2,1)} async-done(((bf16[4,64,1280]{2,1,0:T(8,128)(2,1)}), bf16[4,256,1280]{2,1,0:T(8,128)(2,1)}) %all-gather.10.cloned.1.call-update) | async-done | bytes 2621456 | tf_op jit(solution)/shard_map/all_gather | solution.py:108
  498.6 48.9 %all-gather.12.cloned.1.call-done = bf16[4,256,1280]{2,1,0:T(8,128)(2,1)} async-done(((bf16[4,64,1280]{2,1,0:T(8,128)(2,1)}), bf16[4,256,1280]{2,1,0:T(8,128)(2,1)}) %all-gather.12.cloned.1.call-update) | async-done | bytes 2621456 | tf_op jit(solution)/shard_map/all_gather | solution.py:116
  551.7 3.9 fusion.43
  560.1 90.4 %reduce-scatter.10.cloned.1.call-done = f32[4,64,1280]{2,1,0:T(8,128)} async-done(((f32[4,256,1280]{2,1,0:T(8,128)}), f32[4,64,1280]{2,1,0:T(8,128)}) %reduce-scatter.10.cloned.1.call-update) | async-done | bytes 1310736 | tf_op jit(solution)/shard_map/reduce_scatter | solution.py:126
  652.4 52.0 %reduce-scatter.8.cloned.1.call-done = bf16[4,64,1280]{2,1,0:T(8,128)(2,1)} async-done(((bf16[4,256,1280]{2,1,0:T(8,128)(2,1)}), bf16[4,64,1280]{2,1,0:T(8,128)(2,1)}) %reduce-scatter.8.cloned.1.call-update) | async-done | bytes 655376 | tf_op jit(solution)/shard_map/reduce_scatter | solution.py:112
  715.6 47.5 %all-gather.14.cloned.1.call-done = bf16[4,256,1280]{2,1,0:T(8,128)(2,1)} async-done(((bf16[4,64,1280]{2,1,0:T(8,128)(2,1)}), bf16[4,256,1280]{2,1,0:T(8,128)(2,1)}) %all-gather.14.cloned.1.call-update) | async-done | bytes 2621456 | tf_op jit(solution)/shard_map/all_gather | solution.py:129
  766.0 10.2 fusion.15
  776.2 14.6 %multiply_reduce_fusion = (f32[4,2,256]{2,1,0:T(2,128)S(1)}, f32[4,2,256,2048]{3,2,1,0:T(8,128)}) fusion(f32[4,2,256,2048]{3,2,1,0:T(8,128)} %copy-done.2, f32[4,2,256]{2,1,0:T(2,128)S(1)} %bitcast.130, pred[4,256,2048]{2,1,0:T(8,128)(4,1)S(1)} %copy-done.3, bf16[4,256,2,160]{1,3,2,0:T(8,128)(2,1)S(1)} %bitcast.124, bf16[4,2048,2,160]{1,3,2,0:T(8,128)(2,1)} %bitcast.120), kind=kOutput, calls=%fused_computation.2 | convolution fusion | flops 1358952448 | bytes 41566208 | tf_op jit(solution)/shard_map/rlhd,rshd->rhls/dot_general | solution.py:145
  790.8 12.0 multiply_convert_fusion
  802.8 5.6 convolution_convert_fusion.4
  812.3 9.7 fusion.40
  822.1 5.0 fusion.39
  834.3 15.0 %fusion.51 = f32[4,2048,768]{2,1,0:T(8,128)} fusion(bf16[4,2048,320]{1,2,0:T(8,128)(2,1)} %bitcast.114, bf16[768,320]{0,1:T(8,128)(2,1)S(1)} %copy-done.26), kind=kOutput, calls=%fused_computation.105 | convolution fusion | flops 4026531840 | bytes 30900224 | tf_op jit(solution)/shard_map/rsd,cd->rsc/dot_general | solution.py:170
  849.2 18.9 %add_convert_fusion = bf16[4,2048,768]{2,1,0:T(8,128)(2,1)} fusion(f32[4,2048,768]{2,1,0:T(8,128)} %fusion.51, bf16[4,2048,320]{1,2,0:T(8,128)(2,1)} %bitcast.115, bf16[768,320]{0,1:T(8,128)(2,1)S(1)} %copy-done.28), kind=kOutput, calls=%fused_computation | convolution fusion | flops 4039114752 | bytes 43483136 | tf_op jit(solution)/shard_map/rsd,cd->rsc/dot_general | solution.py:171
  868.1 11.9 psum.93
  880.6 32.2 %all-reduce.4.cloned.1.call-done = (bf16[1280,320]{0,1:T(8,128)(2,1)}, bf16[768,320]{0,1:T(8,128)(2,1)}, bf16[768,320]{0,1:T(8,128)(2,1)}, bf16[320,1280]{1,0:T(...) async-done(((bf16[1280,320]{0,1:T(8,128)(2,1)}, bf16[768,320]{0,1:T(8,128)(2,1)}, bf16[768,320]{0,1:T(8,128)(2,1)}, bf16[320,1280]{1,0:T(8,128)(2,1)}, ...) | async-done | bytes 4259856 | tf_op jit(solution)/shard_map/psum | solution.py:188
  921.5 45.2 %reduce-scatter.14.cloned.1.call-done = bf16[4,64,1280]{2,1,0:T(8,128)(2,1)} async-done(((bf16[4,256,1280]{2,1,0:T(8,128)(2,1)}), bf16[4,64,1280]{2,1,0:T(8,128)(2,1)}) %reduce-scatter.14.cloned.1.call-update) | async-done | bytes 655376 | tf_op jit(solution)/shard_map/reduce_scatter | solution.py:175
  970.1 211.6 %reduce-scatter.12.cloned.1.call-done = bf16[4,512,768]{2,1,0:T(8,128)(2,1)} async-done(((bf16[4,2048,768]{2,1,0:T(8,128)(2,1)}), bf16[4,512,768]{2,1,0:T(8,128)(2,1)}) %reduce-scatter.12.cloned.1.call-update) | async-done | bytes 3145744 | tf_op jit(solution)/shard_map/reduce_scatter | solution.py:178
  1181.7 5.3 fusion.14
  1187.1 40.6 %all-reduce = (f32[768]{0:T(1024)}, f32[1280]{0:T(1024)}, f32[1280]{0:T(1024)}, f32[1280]{0:T(1024)}, f32[1280]{0:T(1024)}) all-reduce(f32[768]{0:T(1024)S(1)} %get-tuple-element.15, f32[1280]{0:T(1024)S(1)} %get-tuple-element.20, f32[1280]{0:T(1024)S(1)} %get-tuple-element.18, ...), channel_id=1, replica_groups=mesh['dp'=8,'mp'=4] {'dp','mp'}, use_global_device_ids=true, to_apply=%region_21.22 | all-reduce | flops 5888 | bytes 47104 | tf_op jit(solution)/shard_map/psum | solution.py:196
  1227.7 6.4 fusion.12
  (190 shorter events, 75.0 us)
Async XLA Ops:
  7.2 484.7 %copy-start = (bf16[1280,320]{0,1:T(8,128)(2,1)S(1)}, bf16[1280,320]{0,1:T(8,128)(2,1)}, u32[]{:S(2)}) copy-start(bf16[1280,320]{0,1:T(8,128)(2,1)} %param.29) | copy-start | bytes 2457604
  7.2 57.3 %all-gather.8.cloned.1.call-start = ((), (), s32[]{:S(2)}) async-start(), calls=%async_computation.6 | async-start | bytes 3276800 | tf_op jit(solution)/shard_map/all_gather | solution.py:62
  10.4 272.4 %all-gather.6.cloned.1.call-start = ((), (), s32[]{:S(2)}) async-start(), calls=%async_computation.5 | async-start | bytes 15728640 | tf_op jit(solution)/shard_map/all_gather | solution.py:63
  22.8 411.9 %reduce-scatter.6.cloned.1.call-start = ((), (), s32[]{:S(2)}) async-start(), calls=%async_computation.7 | async-start | bytes 6553600 | tf_op jit(solution)/shard_map/reduce_scatter | solution.py:104
  26.1 256.7 %copy-start.25 = (bf16[768,320]{0,1:T(8,128)(2,1)S(1)}, bf16[768,320]{0,1:T(8,128)(2,1)}, u32[]{:S(2)}) copy-start(bf16[768,320]{0,1:T(8,128)(2,1)} %param.25) | copy-start | bytes 1474564
  324.6 11.3 copy-start.15
  339.7 95.0 %copy-start.46 = (f32[1280]{0:T(1024)S(1)}, f32[1280]{0:T(1024)}, u32[]{:S(2)}) copy-start(f32[1280]{0:T(1024)} %param.28) | copy-start | bytes 15364
  339.7 152.2 %all-gather.10.cloned.1.call-start = ((), (), s32[]{:S(2)}) async-start(), calls=%async_computation.8 | async-start | bytes 3276800 | tf_op jit(solution)/shard_map/all_gather | solution.py:108
  438.5 53.4 %copy-start.54 = (f32[320]{0:T(512)S(1)}, f32[320]{0:T(512)}, u32[]{:S(2)}) copy-start(f32[320]{0:T(512)} %param.30) | copy-start | bytes 3844
  438.5 109.0 %all-gather.12.cloned.1.call-start = ((), (), s32[]{:S(2)}) async-start(), calls=%async_computation.10 | async-start | bytes 3276800 | tf_op jit(solution)/shard_map/all_gather | solution.py:116
  439.9 210.5 %reduce-scatter.10.cloned.1.call-start = ((), (), s32[]{:S(2)}) async-start(), calls=%async_computation.11 | async-start | bytes 6553600 | tf_op jit(solution)/shard_map/reduce_scatter | solution.py:126
  555.6 148.7 %reduce-scatter.8.cloned.1.call-start = ((), (), s32[]{:S(2)}) async-start(), calls=%async_computation.9 | async-start | bytes 3276800 | tf_op jit(solution)/shard_map/reduce_scatter | solution.py:112
  560.0 90.4 %copy-start.8 = (f32[4,64,1280]{2,1,0:T(8,128)S(1)}, f32[4,64,1280]{2,1,0:T(8,128)}, u32[]{:S(2)}) copy-start(f32[4,64,1280]{2,1,0:T(8,128)} %copy-done.7) | copy-start | bytes 3932164
  560.0 144.4 %copy-start.47 = (f32[1280]{0:T(1024)S(1)}, f32[1280]{0:T(1024)}, u32[]{:S(2)}) copy-start(f32[1280]{0:T(1024)} %param.32) | copy-start | bytes 15364
  560.0 203.0 %all-gather.14.cloned.1.call-start = ((), (), s32[]{:S(2)}) async-start(), calls=%async_computation.12 | async-start | bytes 3276800 | tf_op jit(solution)/shard_map/all_gather | solution.py:129
  650.4 54.0 %copy-start.11 = (f32[4,64,1280]{2,1,0:T(8,128)S(1)}, f32[4,64,1280]{2,1,0:T(8,128)}, u32[]{:S(2)}) copy-start(f32[4,64,1280]{2,1,0:T(8,128)} %reduce-scatter.10.cloned.1.call-done) | copy-start | bytes 3932164
  709.5 203.3 %all-reduce.4.cloned.1.call-start = ((), (), s32[]{:S(2)}) async-start(), calls=%async_computation.15 | async-start | bytes 8519680 | tf_op jit(solution)/shard_map/psum | solution.py:188
  715.6 50.4 %copy-start.3 = (pred[4,256,2048]{2,1,0:T(8,128)(4,1)S(1)}, pred[4,256,2048]{2,1,0:T(8,128)(4,1)}, u32[]{:S(2)}) copy-start(pred[4,256,2048]{2,1,0:T(8,128)(4,1)} %compare_and_fusion) | copy-start | bytes 6291460
  810.4 11.7 copy-start.4
  810.4 11.7 slice-start.2
  812.3 9.8 slice-start.4
  829.1 137.6 %reduce-scatter.14.cloned.1.call-start = ((), (), s32[]{:S(2)}) async-start(), calls=%async_computation.14 | async-start | bytes 3276800 | tf_op jit(solution)/shard_map/reduce_scatter | solution.py:175
  833.3 16.0 %copy-start.28 = (bf16[768,320]{0,1:T(8,128)(2,1)S(1)}, bf16[768,320]{0,1:T(8,128)(2,1)}, u32[]{:S(2)}) copy-start(bf16[768,320]{0,1:T(8,128)(2,1)} %param.26) | copy-start | bytes 1474564
  833.3 348.4 %reduce-scatter.12.cloned.1.call-start = ((), (), s32[]{:S(2)}) async-start(), calls=%async_computation.13 | async-start | bytes 15728640 | tf_op jit(solution)/shard_map/reduce_scatter | solution.py:178
  920.2 46.5 %copy-start.6 = (f32[4,64,1280]{2,1,0:T(8,128)S(1)}, f32[4,64,1280]{2,1,0:T(8,128)}, u32[]{:S(2)}) copy-start(f32[4,64,1280]{2,1,0:T(8,128)} %param.19) | copy-start | bytes 3932164
  920.2 46.5 %copy-start.37 = (f32[1280]{0:T(1024)S(1)}, f32[1280]{0:T(1024)}, u32[]{:S(2)}) copy-start(f32[1280]{0:T(1024)} %param.22) | copy-start | bytes 15364
  920.2 46.5 %copy-start.39 = (f32[4,64]{1,0:T(4,128)S(1)}, f32[4,64]{1,0:T(4,128)}, u32[]{:S(2)}) copy-start(f32[4,64]{1,0:T(4,128)} %copy-done.38) | copy-start | bytes 3076
  920.2 46.5 %copy-start.45 = (f32[4,64]{1,0:T(4,128)S(1)}, f32[4,64]{1,0:T(4,128)}, u32[]{:S(2)}) copy-start(f32[4,64]{1,0:T(4,128)} %copy-done.44) | copy-start | bytes 3076
  921.5 47.0 %copy-start.10 = (f32[4,64,1280]{2,1,0:T(8,128)S(1)}, f32[4,64,1280]{2,1,0:T(8,128)}, u32[]{:S(2)}) copy-start(f32[4,64,1280]{2,1,0:T(8,128)} %copy-done.9) | copy-start | bytes 3932164
  968.5 213.2 %copy-start.32 = (f32[4,512]{1,0:T(4,128)S(1)}, f32[4,512]{1,0:T(4,128)}, u32[]{:S(2)}) copy-start(f32[4,512]{1,0:T(4,128)} %copy-done.31) | copy-start | bytes 24580
  968.5 213.2 %copy-start.34 = (f32[4,512]{1,0:T(4,128)S(1)}, f32[4,512]{1,0:T(4,128)}, u32[]{:S(2)}) copy-start(f32[4,512]{1,0:T(4,128)} %copy-done.33) | copy-start | bytes 24580
  968.5 213.2 %copy-start.41 = (f32[768]{0:T(1024)S(1)}, f32[768]{0:T(1024)}, u32[]{:S(2)}) copy-start(f32[768]{0:T(1024)} %param.21) | copy-start | bytes 9220
  (39 other events, 104.4 us)
Sparse Core Ops, SparseCore 0:
  10.5 53.9 all-gather.7
  66.6 216.1 all-gather.5
  339.8 94.8 reduce-scatter.5
  438.6 53.2 all-gather.9
  493.9 53.5 all-gather.11
  555.7 94.6 reduce-scatter.9
  652.7 51.6 reduce-scatter.7
  709.6 53.4 all-gather.13
  829.2 83.5 all-reduce.3
  915.1 51.5 reduce-scatter.13
  969.1 212.4 reduce-scatter.11
where the time goes:
time: 1250 us; the launch traced here: 1240 us
  waiting for transfers between devices  928 us (74%)
  matrix products  163 us (13%)
  other arithmetic  73.3 us (6%)
  blocking collectives  52.4 us (4%)
  between operations  14.6 us (1%)
    all_gather x1, waiting for transfers between devices, shards(): lax.all_gather(byte_norm, 'mp', axis=1, tiled=True)  215 us
    reduce_scatter x1, waiting for transfers between devices, shards(): lax.psum_scatter(grad_byte_part.astype(jnp.bfloat16), 'mp', scatter_dimen...  212 us
    reduce_scatter x1, waiting for transfers between devices, shards(): lax.psum_scatter(attn_part, 'mp', scatter_dimension=1, tiled=True)  94.9 us
    reduce_scatter x1, waiting for transfers between devices, shards(): lax.psum_scatter(grad_mid_part, 'mp', scatter_dimension=1, tiled=True)  90.4 us
    reduce_scatter x1, waiting for transfers between devices, shards(): lax.psum_scatter(down_part.astype(jnp.bfloat16), 'mp', scatter_dimension=...  52 us
    all_gather x1, waiting for transfers between devices, shards(): mid_all = lax.all_gather(mid_norm, 'mp', axis=1, tiled=True)  52 us
    all_gather x1, waiting for transfers between devices, shards(): lax.all_gather(cotangent.astype(jnp.bfloat16), 'mp', axis=1, tiled=True)  48.9 us
    all_gather x1, waiting for transfers between devices, shards(): lax.all_gather(grad_hidden.astype(jnp.bfloat16), 'mp', axis=1, tiled=True)  47.5 us
  transfers between devices with their start and end apart: 11, of which 11 were waited for; matrix products, arithmetic and copies ran while one was open for 7% of the time, Pallas kernels for 0%

commit v1 on v0

v1 whole, which is shorter than its diff:
```python
import functools

import jax
import jax.numpy as jnp
from jax import lax
from jax.experimental import pallas as pl
from jax.experimental.pallas import tpu as pltpu
from jax.sharding import PartitionSpec as P

HEAD_DIM = 160
EPS = 1e-05
NEG = -1e30
LANES = 128
F32 = jnp.float32
BF16 = jnp.bfloat16
NN = (((1,), (0,)), ((), ()))
NT = (((1,), (1,)), ((), ()))
TN = (((0,), (0,)), ((), ()))


def dot(a, b, dims=NN):
    return lax.dot_general(a, b, dims, preferred_element_type=F32)


def normalize(field):
    average = jnp.mean(field, -1, keepdims=True)
    centred = field - average
    inv_scale = lax.rsqrt(jnp.mean(centred * centred, -1, keepdims=True) + EPS)
    return (centred * inv_scale, inv_scale)


def norm_back(grad_out, normed, inv_scale, scale_vec):
    weighted = grad_out * scale_vec
    centred_grad = (
        weighted
        - jnp.mean(weighted, -1, keepdims=True)
        - normed * jnp.mean(weighted * normed, -1, keepdims=True)
    )
    return (inv_scale * centred_grad, jnp.sum(grad_out * normed, axis=0))


def gelu_exact(field):
    return jax.nn.gelu(field, approximate=False)


def windows(columns):
    out = []
    for head in range(columns // HEAD_DIM):
        start = head * HEAD_DIM
        base = start // LANES * LANES
        assert start + HEAD_DIM <= base + 2 * LANES
        out.append((base, start - base, start - base + HEAD_DIM))
    return out


def own_columns(shape, low, high):
    lane = lax.broadcasted_iota(jnp.int32, shape, 1)
    return (lane >= low) & (lane < high)


def lse_kernel(query_ref, key_ref, lat_seg_ref, byte_seg_ref, lse_ref):
    allowed = byte_seg_ref[0] == lat_seg_ref[0]
    for head, (base, low, high) in enumerate(windows(query_ref.shape[2])):
        query = query_ref[0, :, base : base + 2 * LANES]
        query = jnp.where(own_columns(query.shape, low, high), query, 0)
        key = key_ref[0, :, base : base + 2 * LANES]
        scores = jnp.where(allowed, dot(key, query, NT), NEG)
        peak = jnp.max(scores, 0, keepdims=True)
        total = jnp.sum(jnp.exp(scores - peak), 0, keepdims=True)
        lse_ref[0, head : head + 1, :] = peak + jnp.log(total)


class Tiles:
    def __init__(self, ref):
        self.ref = ref
        self.held = {}

    def add(self, base, window):
        for part in range(2):
            tile = base + part * LANES
            piece = window[:, part * LANES : (part + 1) * LANES]
            self.held[tile] = self.held[tile] + piece if tile in self.held else piece
        for tile in [t for t in self.held if t < base]:
            self.store(tile)

    def store(self, tile):
        self.ref[0, :, tile : tile + LANES] = self.held.pop(tile).astype(self.ref.dtype)

    def finish(self):
        for tile in list(self.held):
            self.store(tile)


def attend_kernel(query_ref, key_ref, value_ref, lat_seg_ref, byte_seg_ref, lse_ref, out_ref):
    allowed = lat_seg_ref[0] == byte_seg_ref[0]
    tiles = Tiles(out_ref)
    for head, (base, low, high) in enumerate(windows(query_ref.shape[2])):
        query = query_ref[0, :, base : base + 2 * LANES]
        mine = own_columns(query.shape, low, high)
        query = jnp.where(mine, query, 0)
        key = key_ref[0, :, base : base + 2 * LANES]
        value = value_ref[0, :, base : base + 2 * LANES]
        scores = jnp.where(allowed, dot(query, key, NT), NEG)
        probs = jnp.exp(scores - lse_ref[0, :, head : head + 1]).astype(BF16)
        tiles.add(base, jnp.where(mine, dot(probs, value), 0.0))
    tiles.finish()


def attend_back_kernel(
    query_ref,
    key_ref,
    value_ref,
    grad_ref,
    lat_seg_ref,
    byte_seg_ref,
    lse_ref,
    delta_ref,
    grad_query_ref,
    grad_key_ref,
    grad_value_ref,
):
    allowed = byte_seg_ref[0] == lat_seg_ref[0]
    query_tiles, key_tiles, value_tiles = (
        Tiles(grad_query_ref),
        Tiles(grad_key_ref),
        Tiles(grad_value_ref),
    )
    for head, (base, low, high) in enumerate(windows(query_ref.shape[2])):
        query = query_ref[0, :, base : base + 2 * LANES]
        mine = own_columns(query.shape, low, high)
        query = jnp.where(mine, query, 0)
        grad = jnp.where(mine, grad_ref[0, :, base : base + 2 * LANES], 0)
        key = key_ref[0, :, base : base + 2 * LANES]
        value = value_ref[0, :, base : base + 2 * LANES]
        scores = jnp.where(allowed, dot(key, query, NT), NEG)
        probs = jnp.exp(scores - lse_ref[0, head : head + 1, :])
        grad_probs = dot(value, grad, NT)
        grad_scores = (probs * (grad_probs - delta_ref[0, head : head + 1, :])).astype(BF16)
        value_tiles.add(base, dot(probs.astype(BF16), grad))
        key_tiles.add(base, dot(grad_scores, query))
        query_tiles.add(base, jnp.where(mine, dot(grad_scores, key, TN), 0.0))
    query_tiles.finish()
    key_tiles.finish()
    value_tiles.finish()


def row_call(kernel, name, args, outs, flops):
    def spec(shape):
        rest = len(shape) - 1
        return pl.BlockSpec((1,) + tuple(shape[1:]), lambda row: (row,) + (0,) * rest)

    moved = sum(a.size * a.dtype.itemsize for a in list(args) + list(outs))
    return pl.pallas_call(
        kernel,
        grid=(args[0].shape[0],),
        in_specs=[spec(a.shape) for a in args],
        out_specs=[spec(o.shape) for o in outs],
        out_shape=outs,
        name=name,
        cost_estimate=pl.CostEstimate(flops=flops, bytes_accessed=moved, transcendentals=0),
        compiler_params=pltpu.CompilerParams(vmem_limit_bytes=48 * 1024 * 1024),
    )(*args)


def shards(
    dp,
    mp,
    byte_in,
    latents,
    cotangent,
    byte_gain,
    latent_gain,
    mlp_gain,
    w_query,
    w_key,
    w_value,
    w_out,
    b_out,
    w_up,
    b_up,
    w_down,
    b_down,
    byte_seg,
    byte_pad,
    latent_seg,
):
    score_scale = HEAD_DIM ** (-0.5)
    rows, byte_len, byte_width = byte_in.shape
    own_lat, lat_width = latents.shape[1:]
    lat_len = own_lat * mp
    dp_index = lax.axis_index("dp")
    mp_index = lax.axis_index("mp")
    heads = w_query.shape[1] * mp // HEAD_DIM

    def whole(shard):
        part = shard.shape[0] // dp
        mine = lax.dynamic_slice_in_dim(shard, dp_index * part, part, 0)
        return lax.all_gather(mine, ("mp", "dp"), axis=0, tiled=True)

    key_t, value_t = whole(w_key.T), whole(w_value.T)
    query_t = whole(w_query.T)
    out_w = whole(w_out)
    up_t, down_w = whole(w_up.T), whole(w_down)
    b_up_all = lax.all_gather(b_up, "mp", axis=0, tiled=True)

    latents = latents.reshape(rows * own_lat, lat_width)
    cotangent = cotangent.reshape(rows * own_lat, lat_width)
    byte_in = byte_in.reshape(rows * byte_len, byte_width)
    lat_hat, lat_inv = normalize(latents)
    lat_norm = (lat_hat * latent_gain).astype(BF16)
    lat_all = lax.all_gather(
        lat_norm.reshape(rows, own_lat, lat_width), "mp", axis=1, tiled=True
    ).reshape(rows * lat_len, lat_width)
    byte_hat, byte_inv = normalize(byte_in)
    byte_norm = (byte_hat * byte_gain).astype(BF16)

    keys = dot(byte_norm, key_t, NT).astype(BF16).reshape(rows, byte_len, -1)
    values = dot(byte_norm, value_t, NT).astype(BF16).reshape(rows, byte_len, -1)
    queries = (dot(lat_all, query_t, NT) * score_scale).astype(BF16).reshape(rows, lat_len, -1)

    real_seg = jnp.where(byte_pad == 1, byte_seg, -1)
    real_seg = lax.dynamic_slice_in_dim(real_seg, mp_index * byte_len, byte_len, 1)
    byte_col, byte_row = real_seg[:, :, None], real_seg[:, None, :]
    lat_col, lat_row = latent_seg[:, :, None], latent_seg[:, None, :]
    unit = 2 * rows * lat_len * byte_len * heads * 2 * LANES

    (lse_part,) = row_call(
        lse_kernel,
        "lse",
        (queries, keys, lat_row, byte_col),
        [jax.ShapeDtypeStruct((rows, heads, lat_len), F32)],
        unit,
    )
    lse_parts = lax.all_gather(lse_part, "mp", axis=0)
    lse_peak = jnp.max(lse_parts, 0)
    lse = lse_peak + jnp.log(jnp.sum(jnp.exp(lse_parts - lse_peak), 0))
    (attended_part,) = row_call(
        attend_kernel,
        "attend",
        (queries, keys, values, lat_col, byte_row, lse.transpose(0, 2, 1)),
        [jax.ShapeDtypeStruct((rows, lat_len, lat_width), BF16)],
        2 * unit,
    )
    attended = lax.psum_scatter(attended_part, "mp", scatter_dimension=1, tiled=True)
    attended = attended.reshape(rows * own_lat, lat_width)

    hidden = latents + dot(attended, out_w) + b_out
    mid_hat, mid_inv = normalize(hidden)
    mid_norm = (mid_hat * mlp_gain).astype(BF16)
    pre_act = dot(mid_norm, up_t, NT) + b_up_all
    activated = gelu_exact(pre_act).astype(BF16)
    result = hidden + dot(activated, down_w) + b_down

    grad_down = cotangent.astype(BF16)
    grad_act = dot(grad_down, down_w, NT)
    _, gelu_pull = jax.vjp(gelu_exact, pre_act)
    grad_pre = gelu_pull(grad_act)[0].astype(BF16)
    grad_b_up = jnp.sum(grad_pre.astype(F32), axis=0)
    grad_mid = dot(grad_pre, up_t)
    grad_mid_back, grad_mlp_gain = norm_back(grad_mid, mid_hat, mid_inv, mlp_gain)
    grad_hidden = cotangent + grad_mid_back
    grad_attn = grad_hidden.astype(BF16)
    grad_att = dot(grad_attn, out_w, NT).astype(BF16)
    delta = jnp.sum(
        (attended.astype(F32) * grad_att.astype(F32)).reshape(rows, own_lat, heads, HEAD_DIM), -1
    )
    grad_att_all = lax.all_gather(
        grad_att.reshape(rows, own_lat, lat_width), "mp", axis=1, tiled=True
    )
    delta_all = lax.all_gather(delta.transpose(0, 2, 1), "mp", axis=2, tiled=True)

    def summed(partial):
        piece = lax.psum_scatter(
            partial.astype(BF16), ("mp", "dp"), scatter_dimension=0, tiled=True
        )
        return lax.all_gather(piece, "dp", axis=0, tiled=True).astype(F32)

    grad_w_down = summed(dot(activated, grad_down, TN))
    grad_w_up = summed(dot(grad_pre, mid_norm, TN)).T
    grad_w_out = summed(dot(attended, grad_attn, TN))

    grad_queries, grad_keys, grad_values = row_call(
        attend_back_kernel,
        "attend_back",
        (queries, keys, values, grad_att_all, lat_row, byte_col, lse, delta_all),
        [
            jax.ShapeDtypeStruct((rows, lat_len, lat_width), BF16),
            jax.ShapeDtypeStruct((rows, byte_len, lat_width), BF16),
            jax.ShapeDtypeStruct((rows, byte_len, lat_width), BF16),
        ],
        5 * unit,
    )
    grad_queries_own = lax.psum_scatter(grad_queries, "mp", scatter_dimension=1, tiled=True)
    grad_queries_own = grad_queries_own.reshape(rows * own_lat, lat_width)
    grad_queries = grad_queries.reshape(rows * lat_len, lat_width)
    grad_keys = grad_keys.reshape(rows * byte_len, lat_width)
    grad_values = grad_values.reshape(rows * byte_len, lat_width)
    grad_w_value = summed(dot(grad_values, byte_norm, TN)).T
    grad_w_key = summed(dot(grad_keys, byte_norm, TN)).T
    grad_w_query = summed(dot(grad_queries, lat_all, TN) * score_scale).T
    grad_byte_norm = dot(grad_keys, key_t) + dot(grad_values, value_t)
    grad_bytes, grad_byte_gain = norm_back(grad_byte_norm, byte_hat, byte_inv, byte_gain)
    grad_lat_norm = dot(grad_queries_own, query_t) * score_scale
    grad_lat_back, grad_latent_gain = norm_back(grad_lat_norm, lat_hat, lat_inv, latent_gain)
    grad_latents = grad_hidden + grad_lat_back
    grad_b_out = jnp.sum(grad_hidden, axis=0)
    grad_b_down = jnp.sum(cotangent, axis=0)
    small = lax.psum(
        (grad_byte_gain, grad_latent_gain, grad_mlp_gain, grad_b_out, grad_b_down, grad_b_up),
        ("dp", "mp"),
    )
    own_units = b_up.shape[0]
    return (
        result.reshape(rows, own_lat, lat_width),
        grad_bytes.reshape(rows, byte_len, byte_width),
        grad_latents.reshape(rows, own_lat, lat_width),
        small[0],
        small[1],
        small[2],
        grad_w_query,
        grad_w_key,
        grad_w_value,
        grad_w_out,
        small[3],
        grad_w_up,
        lax.dynamic_slice_in_dim(small[5], mp_index * own_units, own_units, 0),
        grad_w_down,
        small[4],
    )


def solution(mesh):
    by_row = P("dp", "mp", None)
    columns, lines = P(None, "mp"), P("mp", None)
    return jax.shard_map(
        functools.partial(shards, mesh.shape["dp"], mesh.shape["mp"]),
        mesh=mesh,
        in_specs=(
            by_row,
            by_row,
            by_row,
            P(),
            P(),
            P(),
            columns,
            columns,
            columns,
            lines,
            P(),
            columns,
            P("mp"),
            lines,
            P(),
            P("dp", None),
            P("dp", None),
            P("dp", None),
        ),
        out_specs=(
            by_row,
            by_row,
            by_row,
            P(),
            P(),
            P(),
            columns,
            columns,
            columns,
            lines,
            P(),
            columns,
            P("mp"),
            lines,
            P(),
        ),
        check_vma=False,
    )
```

time: 1250 us -> 1390 us (1.11); the launches traced: 1240 us -> 1370 us
  blocking collectives: 52.4 us -> 171 us
  matrix products: 163 us -> 102 us
  waiting for transfers between devices: 928 us -> 989 us
  other arithmetic: 73.3 us -> 32.2 us
  Pallas kernels: 0 us -> 34.5 us
    reduce_scatter x5 -> x8, waiting for transfers between devices: 494 us -> 638 us  [the longest x6 532 us: summed(): lax.psum_scatter(partial.astype(BF16), ('mp', 'dp'), scatter_dimension=0,...]
    all_gather x0 -> x8, blocking collectives: none -> 121 us  [the longest x6 89.9 us: summed(): return lax.all_gather(piece, 'dp', axis=0, tiled=True).astype(F32)]
    dot_general x24 -> x18, matrix products: 163 us -> 102 us  [dot(): return lax.dot_general(a, b, dims, preferred_element_type=F32)]
    all_gather x5 -> x8, waiting for transfers between devices: 401 us -> 350 us  [the longest x6 278 us: whole(): return lax.all_gather(mine, ('mp', 'dp'), axis=0, tiled=True)]
    pallas_call x0 -> x3, Pallas kernels: none -> 34.5 us  [row_call(): pl.pallas_call(kernel, grid=(args[0].shape[0],), in_specs=[spec(a.shape)...]
    psum x1 -> x0, waiting for transfers between devices: 32.2 us -> none  [shards(): lax.psum(grad_w_query.astype(jnp.bfloat16), 'dp').astype(jnp.float32)]
    convert_element_type x13 -> x4, other arithmetic: 32.5 us -> 8.62 us  [the longest x1 4.98 us: shards(): byte_norm = (byte_hat * byte_gain).astype(BF16)]
    reduce_sum x6 -> x4, other arithmetic: 19.6 us -> 2.67 us  [the longest x1 2.03 us: shards(): jnp.sum((attended.astype(F32) * grad_att.astype(F32)).reshape(rows, own_l...]
  transfers between devices with their start and end apart: 11 -> 16, of which waited for: 11 -> 16; matrix products, arithmetic and copies ran while one was open for 7% -> 10% of each run, Pallas kernels for 0% -> 3%
where the time goes in v1:
time: 1390 us; the launch traced here: 1370 us
  waiting for transfers between devices  989 us (71%)
  blocking collectives  171 us (12%)
  matrix products  102 us (7%)
  Pallas kernels  34.5 us (2%)
  other arithmetic  32.2 us (2%)
  local copies, waits for them, and re-layouts  20.6 us (1%)
  between operations  15.4 us (1%)
    reduce_scatter x6, waiting for transfers between devices, summed(): lax.psum_scatter(partial.astype(BF16), ('mp', 'dp'), scatter_dimension=0,...  532 us
    all_gather x6, waiting for transfers between devices, whole(): return lax.all_gather(mine, ('mp', 'dp'), axis=0, tiled=True)  278 us
    dot_general x18, matrix products, dot(): return lax.dot_general(a, b, dims, preferred_element_type=F32)  102 us
    all_gather x6, blocking collectives, summed(): return lax.all_gather(piece, 'dp', axis=0, tiled=True).astype(F32)  89.9 us
    reduce_scatter x1, waiting for transfers between devices, shards(): lax.psum_scatter(grad_queries, 'mp', scatter_dimension=1, tiled=True)  53.8 us
    reduce_scatter x1, waiting for transfers between devices, shards(): lax.psum_scatter(attended_part, 'mp', scatter_dimension=1, tiled=True)  52.5 us
    all_gather x1, waiting for transfers between devices, shards(): lax.all_gather(lat_norm.reshape(rows, own_lat, lat_width), 'mp', axis=1,...  45.1 us
    psum x1, blocking collectives, shards(): lax.psum((grad_byte_gain, grad_latent_gain, grad_mlp_gain, grad_b_out, gr...  41.6 us
  transfers between devices with their start and end apart: 16, of which 16 were waited for; matrix products, arithmetic and copies ran while one was open for 10% of the time, Pallas kernels for 3%

profile of v1, /device:TPU:9, one launch (start us, length us, event | category | flops | bytes accessed | tf_op | source)
XLA Modules:
  0.0 1366.3 jit_solution(14207441085503545961)
XLA Ops:
  29.9 38.4 %all-gather.14.cloned.1.call-done = bf16[1280,768]{1,0:T(8,128)(2,1)} async-done(((bf16[40,768]{1,0:T(8,128)(2,1)}), bf16[1280,768]{1,0:T(8,128)(2,1)}) %all-gather.14.cloned.1.call-update) | async-done | bytes 1966096 | tf_op jit(solution)/shard_map/all_gather | solution.py:198
  68.3 9.1 convolution_convert_fusion.4
  77.5 49.3 %all-gather.16.cloned.1.call-done = bf16[1280,768]{1,0:T(8,128)(2,1)} async-done(((bf16[40,768]{1,0:T(8,128)(2,1)}), bf16[1280,768]{1,0:T(8,128)(2,1)}) %all-gather.16.cloned.1.call-update) | async-done | bytes 1966096 | tf_op jit(solution)/shard_map/all_gather | solution.py:198
  126.8 9.2 convolution_convert_fusion.3
  136.0 45.1 %all-gather.10.cloned.1.call-done = bf16[4,256,1280]{2,1,0:T(8,128)(2,1)} async-done(((bf16[4,64,1280]{2,1,0:T(8,128)(2,1)}), bf16[4,256,1280]{2,1,0:T(8,128)(2,1)}) %all-gather.10.cloned.1.call-update) | async-done | bytes 2621456 | tf_op jit(solution)/shard_map/all_gather | solution.py:211
  181.1 63.1 %all-gather.12.cloned.1.call-done = bf16[1280,1280]{1,0:T(8,128)(2,1)} async-done(((bf16[40,1280]{1,0:T(8,128)(2,1)}), bf16[1280,1280]{1,0:T(8,128)(2,1)}) %all-gather.12.cloned.1.call-update) | async-done | bytes 3276816 | tf_op jit(solution)/shard_map/all_gather | solution.py:198
  258.7 10.3 all-gather
  269.3 9.7 attend.1
  283.9 8.5 all-reduce
  292.5 13.2 all-gather.18.cloned.1.call-done
  305.8 52.5 %reduce-scatter.9.cloned.1.call-done = bf16[4,64,1280]{2,1,0:T(8,128)(2,1)} async-done(((bf16[4,256,1280]{2,1,0:T(8,128)(2,1)}), bf16[4,64,1280]{2,1,0:T(8,128)(2,1)}) %reduce-scatter.9.cloned.1.call-update) | async-done | bytes 655376 | tf_op jit(solution)/shard_map/reduce_scatter | solution.py:244
  361.9 59.5 %all-gather.20.cloned.1.call-done = bf16[1280,1280]{1,0:T(8,128)(2,1)} async-done(((bf16[40,1280]{1,0:T(8,128)(2,1)}), bf16[1280,1280]{1,0:T(8,128)(2,1)}) %all-gather.20.cloned.1.call-update) | async-done | bytes 3276816 | tf_op jit(solution)/shard_map/all_gather | solution.py:198
  428.1 54.8 %all-gather.22.cloned.1.call-done = bf16[1280,1280]{1,0:T(8,128)(2,1)} async-done(((bf16[40,1280]{1,0:T(8,128)(2,1)}), bf16[1280,1280]{1,0:T(8,128)(2,1)}) %all-gather.22.cloned.1.call-update) | async-done | bytes 3276816 | tf_op jit(solution)/shard_map/all_gather | solution.py:198
  506.2 20.8 %all_gather.65 = f32[4,8,256]{1,0,2:T(4,128)S(1)} all-gather(f32[4,8,64]{1,0,2:T(4,128)S(1)} %copy.47), channel_id=1, replica_groups=mesh['dp'=8,'mp'=4] {'mp'}, dimensions={2}, use_global_device_ids=true | all-gather | bytes 40960 | tf_op jit(solution)/shard_map/all_gather | solution.py:270
  527.1 26.5 %all-gather.24.cloned.1.call-done.grad_ref = bf16[4,256,1280]{2,1,0:T(8,128)(2,1)} async-done(((bf16[4,64,1280]{2,1,0:T(8,128)(2,1)}), bf16[4,256,1280]{2,1,0:T(8,128)(2,1)}) %all-gather.24.cloned.1.call-update) | async-done | bytes 2621456 | tf_op jit(solution)/shard_map/all_gather | solution.py:267
  553.6 16.8 %attend_back.1 = (bf16[4,256,1280]{2,1,0:T(8,128)(2,1)}, bf16[4,512,1280]{2,1,0:T(8,128)(2,1)}, bf16[4,512,1280]{2,1,0:T(8,128)(2,1)}) custom-call(bf16[4,256,1280]{2,1,0:T(8,128)(2,1)} %bitcast.113, bf16[4,512,1280]{2,1,0:T(8,128)(2,1)} %bitcast.120, bf16[4,512,1280]{2,1,0:T(8,128)(2,1)} %bitcast.123, ...), custom_call_target="tpu_custom_call" | custom-call | flops 10737418240 | bytes 28913664 | tf_op jit(solution)/shard_map/attend_back/pallas_call | solution.py:153
  570.4 10.4 bitcast_convert_fusion.1
  581.1 10.6 bitcast_convert_fusion
  627.3 43.9 %reduce-scatter.19.cloned.1.call-done = bf16[40,1280]{1,0:T(8,128)(2,1)} async-done(((bf16[1280,1280]{1,0:T(8,128)(2,1)}), bf16[40,1280]{1,0:T(8,128)(2,1)}) %reduce-scatter.19.cloned.1.call-update) | async-done | bytes 102416 | tf_op jit(solution)/shard_map/reduce_scatter | solution.py:273
  671.3 16.4 %all_gather.69 = bf16[320,1280]{1,0:T(8,128)(2,1)S(1)} all-gather(bf16[40,1280]{1,0:T(8,128)(2,1)} %reduce-scatter.19.cloned.1.call-done), channel_id=1, replica_groups=mesh['dp'=8,'mp'=4] {'dp'}, dimensions={0}, use_global_device_ids=true | all-gather | bytes 921600 | tf_op jit(solution)/shard_map/all_gather | solution.py:276
  688.9 119.7 %reduce-scatter.23.cloned.1.call-done = bf16[40,1280]{1,0:T(8,128)(2,1)} async-done(((bf16[1280,1280]{1,0:T(8,128)(2,1)}), bf16[40,1280]{1,0:T(8,128)(2,1)}) %reduce-scatter.23.cloned.1.call-update) | async-done | bytes 102416 | tf_op jit(solution)/shard_map/reduce_scatter | solution.py:273
  808.6 16.2 %all_gather.71 = bf16[320,1280]{1,0:T(8,128)(2,1)S(1)} all-gather(bf16[40,1280]{1,0:T(8,128)(2,1)} %reduce-scatter.23.cloned.1.call-done), channel_id=1, replica_groups=mesh['dp'=8,'mp'=4] {'dp'}, dimensions={0}, use_global_device_ids=true | all-gather | bytes 921600 | tf_op jit(solution)/shard_map/all_gather | solution.py:276
  826.1 103.9 %reduce-scatter.15.cloned.1.call-done = bf16[40,768]{1,0:T(8,128)(2,1)} async-done(((bf16[1280,768]{1,0:T(8,128)(2,1)}), bf16[40,768]{1,0:T(8,128)(2,1)}) %reduce-scatter.15.cloned.1.call-update) | async-done | bytes 61456 | tf_op jit(solution)/shard_map/reduce_scatter | solution.py:273
  930.0 12.1 all_gather.67
  942.1 90.0 %reduce-scatter.17.cloned.1.call-done = bf16[40,768]{1,0:T(8,128)(2,1)} async-done(((bf16[1280,768]{1,0:T(8,128)(2,1)}), bf16[40,768]{1,0:T(8,128)(2,1)}) %reduce-scatter.17.cloned.1.call-update) | async-done | bytes 61456 | tf_op jit(solution)/shard_map/reduce_scatter | solution.py:273
  1032.2 12.1 all_gather.68
  1044.3 105.5 %reduce-scatter.21.cloned.1.call-done = bf16[40,1280]{1,0:T(8,128)(2,1)} async-done(((bf16[1280,1280]{1,0:T(8,128)(2,1)}), bf16[40,1280]{1,0:T(8,128)(2,1)}) %reduce-scatter.21.cloned.1.call-update) | async-done | bytes 102416 | tf_op jit(solution)/shard_map/reduce_scatter | solution.py:273
  1149.8 16.6 %all_gather.70 = bf16[320,1280]{1,0:T(8,128)(2,1)S(1)} all-gather(bf16[40,1280]{1,0:T(8,128)(2,1)} %reduce-scatter.21.cloned.1.call-done), channel_id=1, replica_groups=mesh['dp'=8,'mp'=4] {'dp'}, dimensions={0}, use_global_device_ids=true | all-gather | bytes 921600 | tf_op jit(solution)/shard_map/all_gather | solution.py:276
  1169.7 53.8 %reduce-scatter.11.cloned.1.call-done = bf16[4,64,1280]{2,1,0:T(8,128)(2,1)} async-done(((bf16[4,256,1280]{2,1,0:T(8,128)(2,1)}), bf16[4,64,1280]{2,1,0:T(8,128)(2,1)}) %reduce-scatter.11.cloned.1.call-update) | async-done | bytes 655376 | tf_op jit(solution)/shard_map/reduce_scatter | solution.py:293
  1228.0 41.6 %all-reduce.1 = (f32[768]{0:T(1024)}, f32[1280]{0:T(1024)}, f32[1280]{0:T(1024)}, f32[1280]{0:T(1024)}, f32[1280]{0:T(1024)S(1)}, /*index=5*/f32[1280]{0:T(1024)}) all-reduce(f32[768]{0:T(1024)S(1)} %get-tuple-element.21, f32[1280]{0:T(1024)S(1)} %get-tuple-element.26, ...), channel_id=1, replica_groups=mesh['dp'=8,'mp'=4] {'dp','mp'}, use_global_device_ids=true, to_apply=%region_18.19 | all-reduce | flops 7168 | bytes 57344 | tf_op jit(solution)/shard_map/psum | solution.py:308
  1273.1 68.7 %reduce-scatter.13.cloned.1.call-done = bf16[40,1280]{1,0:T(8,128)(2,1)} async-done(((bf16[1280,1280]{1,0:T(8,128)(2,1)}), bf16[40,1280]{1,0:T(8,128)(2,1)}) %reduce-scatter.13.cloned.1.call-update) | async-done | bytes 102416 | tf_op jit(solution)/shard_map/reduce_scatter | solution.py:273
  1341.7 16.5 %all_gather.66 = bf16[320,1280]{1,0:T(8,128)(2,1)S(1)} all-gather(bf16[40,1280]{1,0:T(8,128)(2,1)} %reduce-scatter.13.cloned.1.call-done), channel_id=1, replica_groups=mesh['dp'=8,'mp'=4] {'dp'}, dimensions={0}, use_global_device_ids=true | all-gather | bytes 921600 | tf_op jit(solution)/shard_map/all_gather | solution.py:276
  (170 shorter events, 125.9 us)
Async XLA Ops:
  7.2 6.2 copy-start
  7.2 4.8 copy-start.5
  7.2 61.1 %all-gather.14.cloned.1.call-start = ((), (), s32[]{:S(2)}) async-start(), calls=%async_computation.10 | async-start | bytes 2027520 | tf_op jit(solution)/shard_map/all_gather | solution.py:198
  8.9 117.9 %all-gather.16.cloned.1.call-start = ((), (), s32[]{:S(2)}) async-start(), calls=%async_computation.11 | async-start | bytes 2027520 | tf_op jit(solution)/shard_map/all_gather | solution.py:198
  10.4 170.6 %all-gather.10.cloned.1.call-start = ((), (), s32[]{:S(2)}) async-start(), calls=%async_computation.8 | async-start | bytes 3276800 | tf_op jit(solution)/shard_map/all_gather | solution.py:211
  13.4 230.8 %all-gather.12.cloned.1.call-start = ((), (), s32[]{:S(2)}) async-start(), calls=%async_computation.9 | async-start | bytes 3379200 | tf_op jit(solution)/shard_map/all_gather | solution.py:198
  14.1 291.7 %all-gather.18.cloned.1.call-start = ((), (), s32[]{:S(2)}) async-start(), calls=%async_computation.13 | async-start | bytes 3379200 | tf_op jit(solution)/shard_map/all_gather | solution.py:198
  15.7 342.6 %reduce-scatter.9.cloned.1.call-start = ((), (), s32[]{:S(2)}) async-start(), calls=%async_computation.12 | async-start | bytes 3276800 | tf_op jit(solution)/shard_map/reduce_scatter | solution.py:244
  244.2 6.4 copy-start.3
  250.6 8.1 copy-start.2
  278.9 4.7 copy-start.24
  278.9 13.5 copy-start.10
  279.0 79.3 %copy-start.28 = (f32[1280]{0:T(1024)S(1)}, f32[1280]{0:T(1024)}, u32[]{:S(2)}) copy-start(f32[1280]{0:T(1024)} %param.28) | copy-start | bytes 15364
  279.0 142.4 %all-gather.20.cloned.1.call-start = ((), (), s32[]{:S(2)}) async-start(), calls=%async_computation.14 | async-start | bytes 3379200 | tf_op jit(solution)/shard_map/all_gather | solution.py:198
  280.7 202.3 %all-gather.22.cloned.1.call-start = ((), (), s32[]{:S(2)}) async-start(), calls=%async_computation.15 | async-start | bytes 3379200 | tf_op jit(solution)/shard_map/all_gather | solution.py:198
  282.3 271.3 %all-gather.24.cloned.1.call-start = ((), (), s32[]{:S(2)}) async-start(), calls=%async_computation.16 | async-start | bytes 3276800 | tf_op jit(solution)/shard_map/all_gather | solution.py:267
  292.5 190.4 %copy-start.14 = (bf16[256,1280]{1,0:T(8,128)(2,1)}, bf16[256,1280]{1,0:T(8,128)(2,1)S(1)}, u32[]{:S(2)}) copy-start(bf16[256,1280]{1,0:T(8,128)(2,1)S(1)} %get-tuple-element.41) | copy-start | bytes 1966084
  361.6 59.8 %copy-start.20 = (f32[1280]{0:T(1024)S(1)}, f32[1280]{0:T(1024)}, u32[]{:S(2)}) copy-start(f32[1280]{0:T(1024)} %param.23) | copy-start | bytes 15364
  493.3 178.0 %reduce-scatter.19.cloned.1.call-start = ((), (), s32[]{:S(2)}) async-start(), calls=%async_computation.21 | async-start | bytes 3379200 | tf_op jit(solution)/shard_map/reduce_scatter | solution.py:273
  496.1 312.5 %reduce-scatter.23.cloned.1.call-start = ((), (), s32[]{:S(2)}) async-start(), calls=%async_computation.23 | async-start | bytes 3379200 | tf_op jit(solution)/shard_map/reduce_scatter | solution.py:273
  500.2 429.8 %reduce-scatter.15.cloned.1.call-start = ((), (), s32[]{:S(2)}) async-start(), calls=%async_computation.19 | async-start | bytes 2027520 | tf_op jit(solution)/shard_map/reduce_scatter | solution.py:273
  504.0 49.6 %copy-start.4 = (s32[4,512,1]{2,1,0:T(8,128)S(1)}, s32[4,512,1]{2,1,0:T(8,128)}, u32[]{:S(2)}) copy-start(s32[4,512,1]{2,1,0:T(8,128)} %copy.44.byte_seg_ref) | copy-start | bytes 24580
  580.9 451.3 %reduce-scatter.17.cloned.1.call-start = ((), (), s32[]{:S(2)}) async-start(), calls=%async_computation.20 | async-start | bytes 2027520 | tf_op jit(solution)/shard_map/reduce_scatter | solution.py:273
  591.7 558.2 %reduce-scatter.21.cloned.1.call-start = ((), (), s32[]{:S(2)}) async-start(), calls=%async_computation.22 | async-start | bytes 3379200 | tf_op jit(solution)/shard_map/reduce_scatter | solution.py:273
  595.7 627.9 %reduce-scatter.11.cloned.1.call-start = ((), (), s32[]{:S(2)}) async-start(), calls=%async_computation.17 | async-start | bytes 3276800 | tf_op jit(solution)/shard_map/reduce_scatter | solution.py:293
  596.3 745.5 %reduce-scatter.13.cloned.1.call-start = ((), (), s32[]{:S(2)}) async-start(), calls=%async_computation.18 | async-start | bytes 3379200 | tf_op jit(solution)/shard_map/reduce_scatter | solution.py:273
  601.0 14.7 %slice-start = ((s8[6291456]{0:T(1024)(128)(4,1)}), s8[2097152]{0:T(1024)(128)(4,1)S(1)}, s32[]{:S(2)}) async-start(s8[6291456]{0:T(1024)(128)(4,1)} %bitcast.115), calls=%async_computation.24 | async-start | bytes 4194304
  608.7 7.0 slice-start.1
  608.7 7.0 copy-start.27
  1168.4 55.1 %copy-start.6 = (f32[4,64,1280]{2,1,0:T(8,128)S(1)}, f32[4,64,1280]{2,1,0:T(8,128)}, u32[]{:S(2)}) copy-start(f32[4,64,1280]{2,1,0:T(8,128)} %param.19) | copy-start | bytes 3932164
  1223.6 46.7 %copy-start.8 = (f32[256,1280]{1,0:T(8,128)S(1)}, f32[256,1280]{1,0:T(8,128)}, u32[]{:S(2)}) copy-start(f32[256,1280]{1,0:T(8,128)} %copy-done.7) | copy-start | bytes 3932164
  1341.7 17.8 %copy-start.1 = (bf16[1280,320]{0,1:T(8,128)(2,1)S(1)}, bf16[1280,320]{0,1:T(8,128)(2,1)}, u32[]{:S(2)}) copy-start(bf16[1280,320]{0,1:T(8,128)(2,1)} %param.24) | copy-start | bytes 2457604
  (17 other events, 37.4 us)
Sparse Core Ops, SparseCore 0:
  11.5 56.7 all-gather.13
  71.8 54.9 all-gather.15
  129.0 52.0 all-gather.9
  184.4 59.7 all-gather.11
  247.5 58.2 all-gather.17
  307.9 50.3 reduce-scatter.8
  361.8 59.5 all-gather.19
  424.8 58.1 all-gather.21
  493.4 60.2 all-gather.23
  555.8 115.4 reduce-scatter.18
  673.7 134.8 reduce-scatter.22
  813.7 116.2 reduce-scatter.14
  935.2 96.9 reduce-scatter.16
  1034.3 115.4 reduce-scatter.20
  1152.1 71.4 reduce-scatter.10
  1225.8 115.8 reduce-scatter.12

commit v2 on v1

--- a/solution.py
+++ b/solution.py
@@ -160,6 +160,97 @@
         cost_estimate=pl.CostEstimate(flops=flops, bytes_accessed=moved, transcendentals=0),
         compiler_params=pltpu.CompilerParams(vmem_limit_bytes=48 * 1024 * 1024),
     )(*args)
+
+
+def ring(size, step=1):
+    return [(i, (i + step) % size) for i in range(size)]
+
+
+def add(a, b):
+    return (a.astype(F32) + b.astype(F32)).astype(a.dtype)
+
+
+class Mesh:
+    def __init__(self, dp, mp):
+        self.dp, self.mp = dp, mp
+        self.dp_index = lax.axis_index("dp")
+        self.mp_index = lax.axis_index("mp")
+        self.links = [1 << k for k in range(1, dp.bit_length() - 1)]
+
+    def order(self, turn):
+        turn %= len(self.links)
+        return [1] + self.links[turn:] + self.links[:turn]
+
+    def swap(self, x, bit):
+        return lax.ppermute(x, "dp", [(i, i ^ bit) for i in range(self.dp)])
+
+    def bit(self, bit):
+        return (self.dp_index // bit) % 2
+
+    def ring_gather(self, x):
+        blocks = [x]
+        for _ in range(self.mp - 1):
+            blocks.append(lax.ppermute(blocks[-1], "mp", ring(self.mp)))
+        return blocks
+
+    def ring_scatter(self, parts):
+        total = parts[1] if self.mp > 1 else parts[0]
+        for step in range(2, self.mp + 1):
+            total = add(lax.ppermute(total, "mp", ring(self.mp)), parts[step % self.mp])
+        return total
+
+    def keep_half(self, x, bit):
+        half = x.shape[1] // 2
+        mine = self.bit(bit)
+        sent = lax.dynamic_slice_in_dim(x, (1 - mine) * half, half, 1)
+        kept = lax.dynamic_slice_in_dim(x, mine * half, half, 1)
+        return add(self.swap(sent, bit), kept)
+
+    def double(self, x, bit):
+        other = self.swap(x, bit)
+        low = self.bit(bit) == 0
+        return jnp.concatenate([jnp.where(low, x, other), jnp.where(low, other, x)], 1)
+
+    def whole(self, shard, turn):
+        order = self.order(turn)
+        lines = shard.shape[0]
+        place, part = 0, lines
+        for bit in order:
+            part //= 2
+            place = place + self.bit(bit) * part
+        mine = lax.dynamic_slice_in_dim(shard, place, part, 0)
+        others = jnp.stack(self.ring_gather(mine)[1:])
+        for bit in reversed(order):
+            others = self.double(others, bit)
+        blocks = jnp.concatenate([shard[None], others])
+        back = (self.mp_index - jnp.arange(self.mp)) % self.mp
+        return jnp.take(blocks, back, axis=0).reshape(self.mp * lines, -1)
+
+    def summed(self, partial, turn):
+        order = self.order(turn)
+        blocks = partial.astype(BF16).reshape(self.mp, -1, partial.shape[1])
+        for bit in order:
+            blocks = self.keep_half(blocks, bit)
+        parts = [
+            lax.dynamic_index_in_dim(blocks, (self.mp_index - r) % self.mp, 0, False)
+            for r in range(self.mp)
+        ]
+        total = self.ring_scatter(parts)[None]
+        for bit in reversed(order):
+            total = self.double(total, bit)
+        return total[0].astype(F32)
+
+    def total(self, x):
+        for bit in self.order(0):
+            x = x + self.swap(x, bit)
+        return sum(
+            (lax.ppermute(x, "mp", ring(self.mp, step)) for step in range(1, self.mp)), x
+        )
+
+    def turned(self, x, axis, back):
+        blocks = x.reshape(x.shape[:axis] + (self.mp, -1) + x.shape[axis + 1 :])
+        index = (self.mp_index - jnp.arange(self.mp)) % self.mp
+        return jnp.take(blocks, index, axis=axis).reshape(x.shape)
 
 
 def shards(
@@ -188,38 +279,40 @@
     rows, byte_len, byte_width = byte_in.shape
     own_lat, lat_width = latents.shape[1:]
     lat_len = own_lat * mp
-    dp_index = lax.axis_index("dp")
-    mp_index = lax.axis_index("mp")
     heads = w_query.shape[1] * mp // HEAD_DIM
-
-    def whole(shard):
-        part = shard.shape[0] // dp
-        mine = lax.dynamic_slice_in_dim(shard, dp_index * part, part, 0)
-        return lax.all_gather(mine, ("mp", "dp"), axis=0, tiled=True)
-
-    key_t, value_t = whole(w_key.T), whole(w_value.T)
-    query_t = whole(w_query.T)
-    out_w = whole(w_out)
-    up_t, down_w = whole(w_up.T), whole(w_down)
-    b_up_all = lax.all_gather(b_up, "mp", axis=0, tiled=True)
+    net = Mesh(dp, mp)
+    mp_index = net.mp_index
 
     latents = latents.reshape(rows * own_lat, lat_width)
     cotangent = cotangent.reshape(rows * own_lat, lat_width)
     byte_in = byte_in.reshape(rows * byte_len, byte_width)
     lat_hat, lat_inv = normalize(latents)
     lat_norm = (lat_hat * latent_gain).astype(BF16)
-    lat_all = lax.all_gather(
-        lat_norm.reshape(rows, own_lat, lat_width), "mp", axis=1, tiled=True
-    ).reshape(rows * lat_len, lat_width)
+
+    def gather_latents(x):
+        blocks = net.ring_gather(x.reshape(rows, own_lat, lat_width))
+        return jnp.concatenate(blocks, 1)
+
+    def scatter_latents(x):
+        blocks = x.reshape(rows, mp, own_lat, lat_width)
+        return net.ring_scatter([blocks[:, r] for r in range(mp)]).reshape(-1, lat_width)
+
+    key_t, value_t = net.whole(w_key.T, 0), net.whole(w_value.T, 1)
+    query_t = net.whole(w_query.T, 0)
+    lat_all = gather_latents(lat_norm).reshape(rows * lat_len, lat_width)
+    out_w = net.whole(w_out, 1)
+    up_t, down_w = net.whole(w_up.T, 0), net.whole(w_down, 1)
+    b_up_all = net.turned(jnp.concatenate(net.ring_gather(b_up)), 0, True)
+
     byte_hat, byte_inv = normalize(byte_in)
     byte_norm = (byte_hat * byte_gain).astype(BF16)
-
     keys = dot(byte_norm, key_t, NT).astype(BF16).reshape(rows, byte_len, -1)
     values = dot(byte_norm, value_t, NT).astype(BF16).reshape(rows, byte_len, -1)
     queries = (dot(lat_all, query_t, NT) * score_scale).astype(BF16).reshape(rows, lat_len, -1)
 
     real_seg = jnp.where(byte_pad == 1, byte_seg, -1)
     real_seg = lax.dynamic_slice_in_dim(real_seg, mp_index * byte_len, byte_len, 1)
+    latent_seg = net.turned(latent_seg, 1, False)
     byte_col, byte_row = real_seg[:, :, None], real_seg[:, None, :]
     lat_col, lat_row = latent_seg[:, :, None], latent_seg[:, None, :]
     unit = 2 * rows * lat_len * byte_len * heads * 2 * LANES
@@ -231,9 +324,13 @@
         [jax.ShapeDtypeStruct((rows, heads, lat_len), F32)],
         unit,
     )
-    lse_parts = lax.all_gather(lse_part, "mp", axis=0)
+    lse_part = net.turned(lse_part, 2, True)
+    lse_parts = jnp.stack(
+        [lse_part] + [lax.ppermute(lse_part, "mp", ring(mp, step)) for step in range(1, mp)]
+    )
     lse_peak = jnp.max(lse_parts, 0)
     lse = lse_peak + jnp.log(jnp.sum(jnp.exp(lse_parts - lse_peak), 0))
+    lse = net.turned(lse, 2, False)
     (attended_part,) = row_call(
         attend_kernel,
         "attend",
@@ -241,8 +338,7 @@
         [jax.ShapeDtypeStruct((rows, lat_len, lat_width), BF16)],
         2 * unit,
     )
-    attended = lax.psum_scatter(attended_part, "mp", scatter_dimension=1, tiled=True)
-    attended = attended.reshape(rows * own_lat, lat_width)
+    attended = scatter_latents(attended_part)
 
     hidden = latents + dot(attended, out_w) + b_out
     mid_hat, mid_inv = normalize(hidden)
@@ -264,20 +360,12 @@
     delta = jnp.sum(
         (attended.astype(F32) * grad_att.astype(F32)).reshape(rows, own_lat, heads, HEAD_DIM), -1
     )
-    grad_att_all = lax.all_gather(
-        grad_att.reshape(rows, own_lat, lat_width), "mp", axis=1, tiled=True
-    )
-    delta_all = lax.all_gather(delta.transpose(0, 2, 1), "mp", axis=2, tiled=True)
-
-    def summed(partial):
-        piece = lax.psum_scatter(
-            partial.astype(BF16), ("mp", "dp"), scatter_dimension=0, tiled=True
-        )
-        return lax.all_gather(piece, "dp", axis=0, tiled=True).astype(F32)
-
-    grad_w_down = summed(dot(activated, grad_down, TN))
-    grad_w_up = summed(dot(grad_pre, mid_norm, TN)).T
-    grad_w_out = summed(dot(attended, grad_attn, TN))
+    grad_att_all = gather_latents(grad_att)
+    delta_all = jnp.concatenate(net.ring_gather(delta.transpose(0, 2, 1)), 2)
+
+    grad_w_down = net.summed(dot(activated, grad_down, TN), 0)
+    grad_w_up = net.summed(dot(grad_pre, mid_norm, TN), 1).T
+    grad_w_out = net.summed(dot(attended, grad_attn, TN), 0)
 
     grad_queries, grad_keys, grad_values = row_call(
         attend_back_kernel,
@@ -290,14 +378,13 @@
         ],
         5 * unit,
     )
-    grad_queries_own = lax.psum_scatter(grad_queries, "mp", scatter_dimension=1, tiled=True)
-    grad_queries_own = grad_queries_own.reshape(rows * own_lat, lat_width)
+    grad_queries_own = scatter_latents(grad_queries)
     grad_queries = grad_queries.reshape(rows * lat_len, lat_width)
     grad_keys = grad_keys.reshape(rows * byte_len, lat_width)
     grad_values = grad_values.reshape(rows * byte_len, lat_width)
-    grad_w_value = summed(dot(grad_values, byte_norm, TN)).T
-    grad_w_key = summed(dot(grad_keys, byte_norm, TN)).T
-    grad_w_query = summed(dot(grad_queries, lat_all, TN) * score_scale).T
+    grad_w_query = net.summed(dot(grad_queries, lat_all, TN) * score_scale, 0).T
+    grad_w_value = net.summed(dot(grad_values, byte_norm, TN), 1).T
+    grad_w_key = net.summed(dot(grad_keys, byte_norm, TN), 1).T
     grad_byte_norm = dot(grad_keys, key_t) + dot(grad_values, value_t)
     grad_bytes, grad_byte_gain = norm_back(grad_byte_norm, byte_hat, byte_inv, byte_gain)
     grad_lat_norm = dot(grad_queries_own, query_t) * score_scale
@@ -305,27 +392,32 @@
     grad_latents = grad_hidden + grad_lat_back
     grad_b_out = jnp.sum(grad_hidden, axis=0)
     grad_b_down = jnp.sum(cotangent, axis=0)
-    small = lax.psum(
-        (grad_byte_gain, grad_latent_gain, grad_mlp_gain, grad_b_out, grad_b_down, grad_b_up),
-        ("dp", "mp"),
-    )
+
+    def small_sums(*vectors):
+        sums = net.total(jnp.concatenate(vectors))
+        return jnp.split(sums, [sum(v.size for v in vectors[:k]) for k in range(1, len(vectors))])
+
+    sum_mlp_gain, sum_b_out, sum_b_down, sum_b_up = small_sums(
+        grad_mlp_gain, grad_b_out, grad_b_down, grad_b_up
+    )
+    sum_byte_gain, sum_latent_gain = small_sums(grad_byte_gain, grad_latent_gain)
     own_units = b_up.shape[0]
     return (
         result.reshape(rows, own_lat, lat_width),
         grad_bytes.reshape(rows, byte_len, byte_width),
         grad_latents.reshape(rows, own_lat, lat_width),
-        small[0],
-        small[1],
-        small[2],
+        sum_byte_gain,
+        sum_latent_gain,
+        sum_mlp_gain,
         grad_w_query,
         grad_w_key,
         grad_w_value,
         grad_w_out,
-        small[3],
+        sum_b_out,
         grad_w_up,
-        lax.dynamic_slice_in_dim(small[5], mp_index * own_units, own_units, 0),
+        lax.dynamic_slice_in_dim(sum_b_up, mp_index * own_units, own_units, 0),
         grad_w_down,
-        small[4],
+        sum_b_down,
     )
 
 

time: 1390 us -> 643 us (0.46)
  waiting for transfers between devices: 989 us -> 227 us
  blocking collectives: 171 us -> 0 us
  starting transfers between devices: 1.24 us -> 165 us
  other arithmetic: 32.2 us -> 84.2 us
  matrix products: 102 us -> 75.5 us
  local copies, waits for them, and re-layouts: 20.6 us -> 43 us
    reduce_scatter x8 -> x0, waiting for transfers between devices: 638 us -> none  [the longest x6 532 us: summed(): lax.psum_scatter(partial.astype(BF16), ('mp', 'dp'), scatter_dimension=0,...]
    all_gather x8 -> x0, waiting for transfers between devices: 350 us -> none  [the longest x6 278 us: whole(): return lax.all_gather(mine, ('mp', 'dp'), axis=0, tiled=True)]
    ppermute x0 -> x123, waiting for transfers between devices: none -> 227 us  [the longest x24 104 us: ring_scatter(): total = add(lax.ppermute(total, 'mp', ring(self.mp)), parts[step % self.mp])]
    ppermute x0 -> x123, starting transfers between devices: none -> 165 us  [the longest x60 104 us: swap(): return lax.ppermute(x, 'dp', [(i, i ^ bit) for i in range(self.dp)])]
    all_gather x8 -> x0, blocking collectives: 121 us -> none  [the longest x6 89.9 us: summed(): return lax.all_gather(piece, 'dp', axis=0, tiled=True).astype(F32)]
    psum x1 -> x0, blocking collectives: 41.6 us -> none  [shards(): lax.psum((grad_byte_gain, grad_latent_gain, grad_mlp_gain, grad_b_out, gr...]
    select_n x0 -> x42, other arithmetic: none -> 26.8 us  [the longest x3 13 us: whole(): return jnp.take(blocks, back, axis=0).reshape(self.mp * lines, -1)]
    dot_general x18, matrix products: 102 us -> 75.5 us  [dot(): return lax.dot_general(a, b, dims, preferred_element_type=F32)]
  transfers between devices with their start and end apart: 16 -> 123, of which waited for: 16 -> 50; matrix products, arithmetic and copies ran while one was open for 10% -> 24% of each run, Pallas kernels for 3% -> 3%
where the time goes in v2:
time: 643 us; the launch traced here: 630 us
  waiting for transfers between devices  227 us (35%)
  starting transfers between devices  165 us (26%)
  other arithmetic  84.2 us (13%)
  matrix products  75.5 us (12%)
  local copies, waits for them, and re-layouts  43 us (7%)
  Pallas kernels  33.2 us (5%)
    ppermute x60, starting transfers between devices, swap(): return lax.ppermute(x, 'dp', [(i, i ^ bit) for i in range(self.dp)])  104 us
    ppermute x24, waiting for transfers between devices, ring_scatter(): total = add(lax.ppermute(total, 'mp', ring(self.mp)), parts[step % self.mp])  104 us
    dot_general x18, matrix products, dot(): return lax.dot_general(a, b, dims, preferred_element_type=F32)  75.5 us
    ppermute x30, waiting for transfers between devices, ring_gather(): blocks.append(lax.ppermute(blocks[-1], 'mp', ring(self.mp)))  54.9 us
    ppermute x60, waiting for transfers between devices, swap(): return lax.ppermute(x, 'dp', [(i, i ^ bit) for i in range(self.dp)])  54.3 us
    pallas_call x3, Pallas kernels, row_call(): pl.pallas_call(kernel, grid=(args[0].shape[0],), in_specs=[spec(a.shape)...  33.2 us
    ppermute x30, starting transfers between devices, ring_gather(): blocks.append(lax.ppermute(blocks[-1], 'mp', ring(self.mp)))  29.6 us
    ppermute x24, starting transfers between devices, ring_scatter(): total = add(lax.ppermute(total, 'mp', ring(self.mp)), parts[step % self.mp])  15.6 us
  transfers between devices with their start and end apart: 123, of which 50 were waited for; matrix products, arithmetic and copies ran while one was open for 24% of the time, Pallas kernels for 3%

profile of v2, /device:TPU:9, one launch (start us, length us, event | category | flops | bytes accessed | tf_op | source)
XLA Modules:
  0.0 630.5 jit_solution(8471628152964983148)
XLA Ops:
  42.7 14.3 %collective-permute-done.28 = bf16[40,1280]{1,0:T(8,128)(2,1)S(1)} collective-permute-done((bf16[40,1280]{1,0:T(8,128)(2,1)S(1)}, bf16[40,1280]{1,0:T(8,128)(2,1)S(1)}, u32[]{:S(2)}, u32[]{:S(2)}) %collective-permute-start.28) | collective-permute-done | bytes 102432 | tf_op jit(solution)/shard_map/ppermute | solution.py:193
  58.2 5.4 collective-permute-done.44
  86.4 7.5 %collective-permute-done.19 = bf16[3,80,768]{2,1,0:T(8,128)(2,1)S(1)} collective-permute-done((bf16[3,80,768]{2,1,0:T(8,128)(2,1)S(1)}, bf16[3,80,768]{2,1,0:T(8,128)(2,1)S(1)}, u32[]{:S(2)}, u32[]{:S(2)}) %collective-permute-start.19) | collective-permute-done | bytes 368672 | tf_op jit(solution)/shard_map/ppermute | solution.py:185
  95.8 11.2 %collective-permute-done.46 = bf16[3,80,1280]{2,1,0:T(8,128)(2,1)S(1)} collective-permute-done((bf16[3,80,1280]{2,1,0:T(8,128)(2,1)S(1)}, bf16[3,80,1280]{2,1,0:T(8,128)(2,1)S(1)}, u32[]{:S(2)}, u32[]{:S(2)}) %collective-permute-start.46) | collective-permute-done | bytes 614432 | tf_op jit(solution)/shard_map/ppermute | solution.py:185
  107.0 11.0 %collective-permute-start.20 = (bf16[3,160,768]{2,1,0:T(8,128)(2,1)S(1)}, bf16[3,160,768]{2,1,0:T(8,128)(2,1)S(1)}, u32[]{:S(2)}, u32[]{:S(2)}) collective-permute-start(bf16[3,160,768]{2,1,0:T(8,128)(2,1)S(1)} %pad_maximum_fusion.7), channel_id=1, source_target_pairs={{0,4},{4,0},{8,12},{12,8},{16,20},{20,16},{24,28},{28,24},{1,5},{5... | collective-permute-start | bytes 2211848 | tf_op jit(solution)/shard_map/ppermute | solution.py:185
  120.2 5.7 collective-permute-start.14
  144.1 6.0 convolution_convert_fusion.4
  174.2 9.0 %broadcast_select_fusion = (bf16[4,320,1280]{2,1,0:T(8,128)(2,1)}, bf16[4,320,1280]{2,1,0:T(8,128)(2,1)}, bf16[4,320,1280]{2,1,0:T(8,128)(2,1)}, bf16[4,320,1280]{2,1,0:T(8,128)(2,1)S(1)}) fusion(bf16[4,320,1280]{2,1,0:T(8,128)(2,1)} %gather_fusion.9, pred[4]{0:T(512)(128)(4,1)S(1)} %compare_and_fusion, bf16[4,320,1280]{2,1,0:T(8,128)(2,1)} %gather_fusion.7, ...), kind=kLoop, calls=%fused_computation.38 | loop fusion | flops 6553600 | bytes 26214404 | tf_op jit(solution)/shard_map/jit(_take)/select_n | solution.py:227
  187.1 8.2 %lse.1 = f32[4,8,256]{2,1,0:T(8,128)S(1)} custom-call(bf16[4,256,1280]{2,1,0:T(8,128)(2,1)S(1)} %bitcast.321, bf16[4,512,1280]{2,1,0:T(8,128)(2,1)} %bitcast.340, s32[4,1,256]{2,1,0:T(1,128)S(1)} %broadcast_select_fusion.79.lat_seg_ref, s32[4,512,1]{2,1,0:T(8,128)S(1)} %copy-done.1), custom_call_target="tpu_custom_call" | custom-call | flops 2147483648 | bytes 7909376 | tf_op jit(solution)/shard_map/lse/pallas_call | solution.py:153
  203.1 9.1 %convolution_convert_fusion.3 = bf16[2048,1280]{1,0:T(8,128)(2,1)} fusion(bf16[2048,768]{1,0:T(8,128)(2,1)} %bitcast.360, bf16[1280,768]{1,0:T(8,128)(2,1)} %bitcast.367), kind=kOutput, calls=%fused_computation.16 | convolution fusion | flops 4029153280 | bytes 10354688 | tf_op jit(solution)/shard_map/dot_general | solution.py:22
  214.9 8.4 %attend.1 = bf16[4,256,1280]{2,1,0:T(8,128)(2,1)S(1)} custom-call(bf16[4,256,1280]{2,1,0:T(8,128)(2,1)} %bitcast.322, bf16[4,512,1280]{2,1,0:T(8,128)(2,1)} %bitcast.341, bf16[4,512,1280]{2,1,0:T(8,128)(2,1)} %bitcast.350, s32[4,256,1]{2,1,0:T(8,128)S(1)} %copy-done.3, s32[4,1,512]{2,1,0:T(1,128)S(1)} %broadcast_in_dim.130.byte_seg_ref, ...), custom_call_target="tpu_custom_call" | custom-call | flops 4294967296 | bytes 15773696 | tf_op jit(solution)/shard_map/attend/pallas_call | solution.py:153
  223.4 15.0 %collective-permute-done.24 = bf16[4,64,1280]{2,1,0:T(8,128)(2,1)S(1)} collective-permute-done((bf16[4,64,1280]{2,1,0:T(8,128)(2,1)S(1)}, bf16[4,64,1280]{2,1,0:T(8,128)(2,1)S(1)}, u32[]{:S(2)}, u32[]{:S(2)}) %collective-permute-start.24) | collective-permute-done | bytes 655392 | tf_op jit(solution)/shard_map/ppermute | solution.py:199
  240.3 12.6 %collective-permute-done.25 = bf16[4,64,1280]{2,1,0:T(8,128)(2,1)} collective-permute-done((bf16[4,64,1280]{2,1,0:T(8,128)(2,1)S(1)}, bf16[4,64,1280]{2,1,0:T(8,128)(2,1)}, u32[]{:S(2)}, u32[]{:S(2)}) %collective-permute-start.25) | collective-permute-done | bytes 655392 | tf_op jit(solution)/shard_map/ppermute | solution.py:199
  257.6 13.3 %collective-permute-done.40 = f32[320]{0:T(512)S(1)} collective-permute-done((f32[320]{0:T(512)S(1)}, f32[320]{0:T(512)S(1)}, u32[]{:S(2)}, u32[]{:S(2)}) %collective-permute-start.40) | collective-permute-done | bytes 1312 | tf_op jit(solution)/shard_map/ppermute | solution.py:193
  304.6 5.1 collective-permute-start.63
  328.5 11.8 %collective-permute-done.67 = f32[5120]{0:T(1024)S(1)} collective-permute-done((f32[5120]{0:T(1024)S(1)}, f32[5120]{0:T(1024)S(1)}, u32[]{:S(2)}, u32[]{:S(2)}) %collective-permute-start.67) | collective-permute-done | bytes 20512 | tf_op jit(solution)/shard_map/ppermute | solution.py:247
  353.2 9.8 %collective-permute-done.50 = bf16[4,64,1280]{2,1,0:T(8,128)(2,1)S(1)} collective-permute-done((bf16[4,64,1280]{2,1,0:T(8,128)(2,1)S(1)}, bf16[4,64,1280]{2,1,0:T(8,128)(2,1)S(1)}, u32[]{:S(2)}, u32[]{:S(2)}) %collective-permute-start.50) | collective-permute-done | bytes 655392 | tf_op jit(solution)/shard_map/ppermute | solution.py:193
  366.1 16.7 %attend_back.1 = (bf16[4,256,1280]{2,1,0:T(8,128)(2,1)S(1)}, bf16[4,512,1280]{2,1,0:T(8,128)(2,1)}, bf16[4,512,1280]{2,1,0:T(8,128)(2,1)}) custom-call(bf16[4,256,1280]{2,1,0:T(8,128)(2,1)} %bitcast.323, bf16[4,512,1280]{2,1,0:T(8,128)(2,1)} %bitcast.342, bf16[4,512,1280]{2,1,0:T(8,128)(2,1)} %bitcast.351, bf16[4,256,1280]{2,1,0:T(8,128)(2,1)} %pad_maximum_fusion.1.grad_ref, ...), custom_call_target="tpu_custom_call" | custom-call | flops 10737418240 | bytes 28913664 | tf_op jit(solution)/shard_map/attend_back/pallas_call | solution.py:153
  382.9 8.3 %bitcast_convert_fusion.1 = bf16[1280,768]{1,0:T(8,128)(2,1)} fusion(bf16[4,512,1280]{2,1,0:T(8,128)(2,1)} %get-tuple-element.21, bf16[4,512,768]{2,1,0:T(8,128)(2,1)S(1)} %copy-done.26), kind=kOutput, calls=%fused_computation.28 | convolution fusion | flops 4027514880 | bytes 10354688 | tf_op jit(solution)/shard_map/dot_general | solution.py:22
  391.2 6.1 fusion.59
  397.3 5.6 bitcast_convert_fusion
  403.0 8.6 %multiply_reduce_fusion = (f32[768]{0:T(1024)S(1)}, f32[2048]{0:T(1024)S(1)}, f32[2048]{0:T(1024)S(1)}, f32[2048,768]{1,0:T(8,128)S(1)}) fusion(f32[4,512,768]{2,1,0:T(8,128)S(1)} %bitcast.334, f32[2048]{0:T(1024)S(1)} %bitcast.422, f32[2048]{0:T(1024)S(1)} %bitcast.424, f32[768]{0:T(1024)S(1)} %copy-done.49, f32[2048,768]{1,0:T(8,128)} %fusion.59, ...), kind=kOutput, calls=%fused_computation.20 | convolution fusion | flops 4040682752 | bytes 26122240 | tf_op jit(solution)/shard_map/dot_general | solution.py:22
  430.6 5.9 collective-permute-done.98
  467.9 5.3 collective-permute-done.109
  473.2 5.3 collective-permute-done.118
  478.5 5.7 collective-permute-done.101
  484.3 6.6 %collective-permute-done.110 = bf16[40,1280]{1,0:T(8,128)(2,1)S(1)} collective-permute-done((bf16[40,1280]{1,0:T(8,128)(2,1)S(1)}, bf16[40,1280]{1,0:T(8,128)(2,1)S(1)}, u32[]{:S(2)}, u32[]{:S(2)}) %collective-permute-start.110) | collective-permute-done | bytes 102432 | tf_op jit(solution)/shard_map/ppermute | solution.py:199
  511.1 11.7 %collective-permute-start.104 = (bf16[1,160,1280]{2,1,0:T(8,128)(2,1)S(1)}, bf16[1,160,1280]{2,1,0:T(8,128)(2,1)S(1)}, u32[]{:S(2)}, u32[]{:S(2)}) collective-permute-start(bf16[1,160,1280]{2,1,0:T(8,128)(2,1)S(1)} %pad_maximum_fusion.13), channel_id=1, source_target_pairs={{0,4},{4,0},{8,12},{12,8},{16,20},{20,16},{24,28},{28,24},{1,5},{5... | collective-permute-start | bytes 1228808 | tf_op jit(solution)/shard_map/ppermute | solution.py:185
  541.0 5.7 collective-permute-done.91
  565.4 9.6 %collective-permute-start.57 = (f32[2048]{0:T(1024)S(1)}, f32[2048]{0:T(1024)S(1)}, u32[]{:S(2)}, u32[]{:S(2)}) collective-permute-start(f32[2048]{0:T(1024)S(1)} %pad_maximum_fusion.34), channel_id=1, source_target_pairs={{0,4},{4,0},{8,12},{12,8},{16,20},{20,16},{24,28},{28,24},{1,5},{5... | collective-permute-start | bytes 24584 | tf_op jit(solution)/shard_map/ppermute | solution.py:185
  595.9 6.1 collective-permute-start.86
  610.1 7.3 %collective-permute-start.95 = (bf16[1,160,768]{2,1,0:T(8,128)(2,1)S(1)}, bf16[1,160,768]{2,1,0:T(8,128)(2,1)S(1)}, u32[]{:S(2)}, u32[]{:S(2)}) collective-permute-start(bf16[1,160,768]{2,1,0:T(8,128)(2,1)S(1)} %pad_maximum_fusion.23), channel_id=1, source_target_pairs={{0,4},{4,0},{8,12},{12,8},{16,20},{20,16},{24,28},{28,24},{1,5},{5... | collective-permute-start | bytes 737288 | tf_op jit(solution)/shard_map/ppermute | solution.py:185
  (602 shorter events, 350.0 us)
Async XLA Ops:
  1.7 31.2 %collective-permute-start.42 = (bf16[40,1280]{1,0:T(8,128)(2,1)S(1)}, bf16[40,1280]{1,0:T(8,128)(2,1)S(1)}, u32[]{:S(2)}, u32[]{:S(2)}) collective-permute-start(bf16[40,1280]{1,0:T(8,128)(2,1)S(1)} %constant_dynamic-slice_fusion.19), channel_id=1, source_target_pairs={{0,1},{1,2},{2,3},{3,0},{4,5},{5,6},{6,7},{7,4},{8,9},{9,10},{10,1... | collective-permute-start | bytes 307208 | tf_op jit(solution)/shard_map/ppermute | solution.py:193
  3.9 33.0 %collective-permute-start.27 = (bf16[40,1280]{1,0:T(8,128)(2,1)S(1)}, bf16[40,1280]{1,0:T(8,128)(2,1)S(1)}, u32[]{:S(2)}, u32[]{:S(2)}) collective-permute-start(bf16[40,1280]{1,0:T(8,128)(2,1)S(1)} %constant_dynamic-slice_fusion.20), channel_id=1, source_target_pairs={{0,1},{1,2},{2,3},{3,0},{4,5},{5,6},{6,7},{7,4},{8,9},{9,10},{10,1... | collective-permute-start | bytes 307208 | tf_op jit(solution)/shard_map/ppermute | solution.py:193
  6.1 31.3 %collective-permute-start.33 = (bf16[40,1280]{1,0:T(8,128)(2,1)S(1)}, bf16[40,1280]{1,0:T(8,128)(2,1)S(1)}, u32[]{:S(2)}, u32[]{:S(2)}) collective-permute-start(bf16[40,1280]{1,0:T(8,128)(2,1)S(1)} %dynamic-slice_bitcast_fusion.4), channel_id=1, source_target_pairs={{0,1},{1,2},{2,3},{3,0},{4,5},{5,6},{6,7},{7,4},{8,9},{9,10},{10,1... | collective-permute-start | bytes 307208 | tf_op jit(solution)/shard_map/ppermute | solution.py:193
  36.9 57.4 %collective-permute-start = (bf16[4,64,1280]{2,1,0:T(8,128)(2,1)S(1)}, bf16[4,64,1280]{2,1,0:T(8,128)(2,1)S(1)}, u32[]{:S(2)}, u32[]{:S(2)}) collective-permute-start(bf16[4,64,1280]{2,1,0:T(8,128)(2,1)S(1)} %multiply_convert_fusion.4), channel_id=1, source_target_pairs={{0,1},{1,2},{2,3},{3,0},{4,5},{5,6},{6,7},{7,4},{8,9},{9,10},{10,1... | collective-permute-start | bytes 1966088 | tf_op jit(solution)/shard_map/ppermute | solution.py:193
  41.0 24.6 %collective-permute-start.4 = (bf16[40,1280]{1,0:T(8,128)(2,1)S(1)}, bf16[40,1280]{1,0:T(8,128)(2,1)S(1)}, u32[]{:S(2)}, u32[]{:S(2)}) collective-permute-start(bf16[40,1280]{1,0:T(8,128)(2,1)S(1)} %collective-permute-done.3), channel_id=1, source_target_pairs={{0,1},{1,2},{2,3},{3,0},{4,5},{5,6},{6,7},{7,4},{8,9},{9,10},{10,1... | collective-permute-start | bytes 307208 | tf_op jit(solution)/shard_map/ppermute | solution.py:193
  83.7 23.4 %collective-permute-start.46 = (bf16[3,80,1280]{2,1,0:T(8,128)(2,1)S(1)}, bf16[3,80,1280]{2,1,0:T(8,128)(2,1)S(1)}, u32[]{:S(2)}, u32[]{:S(2)}) collective-permute-start(bf16[3,80,1280]{2,1,0:T(8,128)(2,1)S(1)} %pad_maximum_fusion.11), channel_id=1, source_target_pairs={{0,16},{4,20},{8,24},{12,28},{16,0},{20,4},{24,8},{28,12},{1,17},{... | collective-permute-start | bytes 1843208 | tf_op jit(solution)/shard_map/ppermute | solution.py:185
  86.0 34.2 %collective-permute-start.31 = (bf16[3,80,1280]{2,1,0:T(8,128)(2,1)S(1)}, bf16[3,80,1280]{2,1,0:T(8,128)(2,1)S(1)}, u32[]{:S(2)}, u32[]{:S(2)}) collective-permute-start(bf16[3,80,1280]{2,1,0:T(8,128)(2,1)S(1)} %pad_maximum_fusion.9), channel_id=1, source_target_pairs={{0,16},{4,20},{8,24},{12,28},{16,0},{20,4},{24,8},{28,12},{1,17},{... | collective-permute-start | bytes 1843208 | tf_op jit(solution)/shard_map/ppermute | solution.py:185
  93.9 34.6 %collective-permute-start.37 = (bf16[3,80,1280]{2,1,0:T(8,128)(2,1)S(1)}, bf16[3,80,1280]{2,1,0:T(8,128)(2,1)S(1)}, u32[]{:S(2)}, u32[]{:S(2)}) collective-permute-start(bf16[3,80,1280]{2,1,0:T(8,128)(2,1)S(1)} %pad_maximum_fusion.10), channel_id=1, source_target_pairs={{0,8},{4,12},{8,0},{12,4},{16,24},{20,28},{24,16},{28,20},{1,9},{5... | collective-permute-start | bytes 1843208 | tf_op jit(solution)/shard_map/ppermute | solution.py:185
  94.4 34.2 %collective-permute-start.7 = (bf16[3,80,1280]{2,1,0:T(8,128)(2,1)S(1)}, bf16[3,80,1280]{2,1,0:T(8,128)(2,1)S(1)}, u32[]{:S(2)}, u32[]{:S(2)}) collective-permute-start(bf16[3,80,1280]{2,1,0:T(8,128)(2,1)S(1)} %pad_maximum_fusion.8), channel_id=1, source_target_pairs={{0,8},{4,12},{8,0},{12,4},{16,24},{20,28},{24,16},{28,20},{1,9},{5... | collective-permute-start | bytes 1843208 | tf_op jit(solution)/shard_map/ppermute | solution.py:185
  95.6 36.3 %collective-permute-start.1 = (bf16[4,64,1280]{2,1,0:T(8,128)(2,1)S(1)}, bf16[4,64,1280]{2,1,0:T(8,128)(2,1)}, u32[]{:S(2)}, u32[]{:S(2)}) collective-permute-start(bf16[4,64,1280]{2,1,0:T(8,128)(2,1)S(1)} %collective-permute-done), channel_id=1, source_target_pairs={{0,1},{1,2},{2,3},{3,0},{4,5},{5,6},{6,7},{7,4},{8,9},{9,10},{10,1... | collective-permute-start | bytes 1966088 | tf_op jit(solution)/shard_map/ppermute | solution.py:193
  107.0 25.1 %collective-permute-start.20 = (bf16[3,160,768]{2,1,0:T(8,128)(2,1)S(1)}, bf16[3,160,768]{2,1,0:T(8,128)(2,1)S(1)}, u32[]{:S(2)}, u32[]{:S(2)}) collective-permute-start(bf16[3,160,768]{2,1,0:T(8,128)(2,1)S(1)} %pad_maximum_fusion.7), channel_id=1, source_target_pairs={{0,4},{4,0},{8,12},{12,8},{16,20},{20,16},{24,28},{28,24},{1,5},{5... | collective-permute-start | bytes 2211848 | tf_op jit(solution)/shard_map/ppermute | solution.py:185
  128.5 26.0 %collective-permute-start.47 = (bf16[3,160,1280]{2,1,0:T(8,128)(2,1)}, bf16[3,160,1280]{2,1,0:T(8,128)(2,1)}, u32[]{:S(2)}, u32[]{:S(2)}) collective-permute-start(bf16[3,160,1280]{2,1,0:T(8,128)(2,1)} %pad_maximum_fusion.5), channel_id=1, source_target_pairs={{0,4},{4,0},{8,12},{12,8},{16,20},{20,16},{24,28},{28,24},{1,5},{5... | collective-permute-start | bytes 3686408 | tf_op jit(solution)/shard_map/ppermute | solution.py:185
  128.6 30.6 %collective-permute-start.32 = (bf16[3,160,1280]{2,1,0:T(8,128)(2,1)}, bf16[3,160,1280]{2,1,0:T(8,128)(2,1)}, u32[]{:S(2)}, u32[]{:S(2)}) collective-permute-start(bf16[3,160,1280]{2,1,0:T(8,128)(2,1)} %pad_maximum_fusion.3), channel_id=1, source_target_pairs={{0,4},{4,0},{8,12},{12,8},{16,20},{20,16},{24,28},{28,24},{1,5},{5... | collective-permute-start | bytes 3686408 | tf_op jit(solution)/shard_map/ppermute | solution.py:185
  132.0 32.3 %collective-permute-start.38 = (bf16[3,160,1280]{2,1,0:T(8,128)(2,1)}, bf16[3,160,1280]{2,1,0:T(8,128)(2,1)}, u32[]{:S(2)}, u32[]{:S(2)}) collective-permute-start(bf16[3,160,1280]{2,1,0:T(8,128)(2,1)} %pad_maximum_fusion.4), channel_id=1, source_target_pairs={{0,4},{4,0},{8,12},{12,8},{16,20},{20,16},{24,28},{28,24},{1,5},{5... | collective-permute-start | bytes 3686408 | tf_op jit(solution)/shard_map/ppermute | solution.py:185
  132.1 37.1 %collective-permute-start.8 = (bf16[3,160,1280]{2,1,0:T(8,128)(2,1)}, bf16[3,160,1280]{2,1,0:T(8,128)(2,1)}, u32[]{:S(2)}, u32[]{:S(2)}) collective-permute-start(bf16[3,160,1280]{2,1,0:T(8,128)(2,1)} %pad_maximum_fusion.2), channel_id=1, source_target_pairs={{0,4},{4,0},{8,12},{12,8},{16,20},{20,16},{24,28},{28,24},{1,5},{5... | collective-permute-start | bytes 3686408 | tf_op jit(solution)/shard_map/ppermute | solution.py:185
  296.9 28.2 %collective-permute-start.48 = (bf16[4,64,1280]{2,1,0:T(8,128)(2,1)}, bf16[4,64,1280]{2,1,0:T(8,128)(2,1)}, u32[]{:S(2)}, u32[]{:S(2)}) collective-permute-start(bf16[4,64,1280]{2,1,0:T(8,128)(2,1)} %bitcast.63), channel_id=1, source_target_pairs={{0,1},{1,2},{2,3},{3,0},{4,5},{5,6},{6,7},{7,4},{8,9},{9,10},{10,1... | collective-permute-start | bytes 1966088 | tf_op jit(solution)/shard_map/ppermute | solution.py:193
  309.8 36.3 %collective-permute-start.96 = (bf16[4,160,1280]{2,1,0:T(8,128)(2,1)S(1)}, bf16[4,160,1280]{2,1,0:T(8,128)(2,1)S(1)}, u32[]{:S(2)}, u32[]{:S(2)}) collective-permute-start(bf16[4,160,1280]{2,1,0:T(8,128)(2,1)S(1)} %constant_dynamic-slice_fusion.9), channel_id=1, source_target_pairs={{0,4},{4,0},{8,12},{12,8},{16,20},{20,16},{24,28},{28,24},{1,5},{5... | collective-permute-start | bytes 4915208 | tf_op jit(solution)/shard_map/ppermute | solution.py:185
  311.8 35.9 %collective-permute-start.105 = (bf16[4,160,1280]{2,1,0:T(8,128)(2,1)S(1)}, bf16[4,160,1280]{2,1,0:T(8,128)(2,1)S(1)}, u32[]{:S(2)}, u32[]{:S(2)}) collective-permute-start(bf16[4,160,1280]{2,1,0:T(8,128)(2,1)S(1)} %constant_dynamic-slice_fusion.6), channel_id=1, source_target_pairs={{0,4},{4,0},{8,12},{12,8},{16,20},{20,16},{24,28},{28,24},{1,5},{5... | collective-permute-start | bytes 4915208 | tf_op jit(solution)/shard_map/ppermute | solution.py:185
  347.5 74.8 %collective-permute-start.97 = (bf16[4,80,1280]{2,1,0:T(8,128)(2,1)}, bf16[4,80,1280]{2,1,0:T(8,128)(2,1)}, u32[]{:S(2)}, u32[]{:S(2)}) collective-permute-start(bf16[4,80,1280]{2,1,0:T(8,128)(2,1)} %constant_dynamic-slice_fusion.8), channel_id=1, source_target_pairs={{0,8},{4,12},{8,0},{12,4},{16,24},{20,28},{24,16},{28,20},{1,9},{5... | collective-permute-start | bytes 2457608 | tf_op jit(solution)/shard_map/ppermute | solution.py:185
  349.1 76.7 %collective-permute-start.106 = (bf16[4,80,1280]{2,1,0:T(8,128)(2,1)}, bf16[4,80,1280]{2,1,0:T(8,128)(2,1)}, u32[]{:S(2)}, u32[]{:S(2)}) collective-permute-start(bf16[4,80,1280]{2,1,0:T(8,128)(2,1)} %constant_dynamic-slice_fusion.5), channel_id=1, source_target_pairs={{0,16},{4,20},{8,24},{12,28},{16,0},{20,4},{24,8},{28,12},{1,17},{... | collective-permute-start | bytes 2457608 | tf_op jit(solution)/shard_map/ppermute | solution.py:185
  351.9 72.5 %collective-permute-start.115 = (bf16[4,80,1280]{2,1,0:T(8,128)(2,1)}, bf16[4,80,1280]{2,1,0:T(8,128)(2,1)}, u32[]{:S(2)}, u32[]{:S(2)}) collective-permute-start(bf16[4,80,1280]{2,1,0:T(8,128)(2,1)} %constant_dynamic-slice_fusion.2), channel_id=1, source_target_pairs={{0,8},{4,12},{8,0},{12,4},{16,24},{20,28},{24,16},{28,20},{1,9},{5... | collective-permute-start | bytes 2457608 | tf_op jit(solution)/shard_map/ppermute | solution.py:185
  416.8 106.0 %collective-permute-start.69 = (bf16[4,160,1280]{2,1,0:T(8,128)(2,1)S(1)}, bf16[4,160,1280]{2,1,0:T(8,128)(2,1)S(1)}, u32[]{:S(2)}, u32[]{:S(2)}) collective-permute-start(bf16[4,160,1280]{2,1,0:T(8,128)(2,1)S(1)} %constant_dynamic-slice_fusion.18), channel_id=1, source_target_pairs={{0,4},{4,0},{8,12},{12,8},{16,20},{20,16},{24,28},{28,24},{1,5},{5... | collective-permute-start | bytes 4915208 | tf_op jit(solution)/shard_map/ppermute | solution.py:185
  422.3 25.7 %collective-permute-start.78 = (bf16[4,160,768]{2,1,0:T(8,128)(2,1)S(1)}, bf16[4,160,768]{2,1,0:T(8,128)(2,1)S(1)}, u32[]{:S(2)}, u32[]{:S(2)}) collective-permute-start(bf16[4,160,768]{2,1,0:T(8,128)(2,1)S(1)} %constant_dynamic-slice_fusion.15), channel_id=1, source_target_pairs={{0,4},{4,0},{8,12},{12,8},{16,20},{20,16},{24,28},{28,24},{1,5},{5... | collective-permute-start | bytes 2949128 | tf_op jit(solution)/shard_map/ppermute | solution.py:185
  424.3 28.1 %collective-permute-start.87 = (bf16[4,160,768]{2,1,0:T(8,128)(2,1)S(1)}, bf16[4,160,768]{2,1,0:T(8,128)(2,1)S(1)}, u32[]{:S(2)}, u32[]{:S(2)}) collective-permute-start(bf16[4,160,768]{2,1,0:T(8,128)(2,1)S(1)} %constant_dynamic-slice_fusion.12), channel_id=1, source_target_pairs={{0,4},{4,0},{8,12},{12,8},{16,20},{20,16},{24,28},{28,24},{1,5},{5... | collective-permute-start | bytes 2949128 | tf_op jit(solution)/shard_map/ppermute | solution.py:185
  438.7 57.2 %collective-permute-start.55 = (bf16[4,64,1280]{2,1,0:T(8,128)(2,1)S(1)}, bf16[4,64,1280]{2,1,0:T(8,128)(2,1)S(1)}, u32[]{:S(2)}, u32[]{:S(2)}) collective-permute-start(bf16[4,64,1280]{2,1,0:T(8,128)(2,1)S(1)} %fusion.8), channel_id=1, source_target_pairs={{0,1},{1,2},{2,3},{3,0},{4,5},{5,6},{6,7},{7,4},{8,9},{9,10},{10,1... | collective-permute-start | bytes 1966088 | tf_op jit(solution)/shard_map/ppermute | solution.py:199
  456.0 47.4 %collective-permute-start.79 = (bf16[4,80,768]{2,1,0:T(8,128)(2,1)S(1)}, bf16[4,80,768]{2,1,0:T(8,128)(2,1)S(1)}, u32[]{:S(2)}, u32[]{:S(2)}) collective-permute-start(bf16[4,80,768]{2,1,0:T(8,128)(2,1)S(1)} %constant_dynamic-slice_fusion.14), channel_id=1, source_target_pairs={{0,16},{4,20},{8,24},{12,28},{16,0},{20,4},{24,8},{28,12},{1,17},{... | collective-permute-start | bytes 1474568 | tf_op jit(solution)/shard_map/ppermute | solution.py:185
  458.2 45.5 %collective-permute-start.88 = (bf16[4,80,768]{2,1,0:T(8,128)(2,1)S(1)}, bf16[4,80,768]{2,1,0:T(8,128)(2,1)S(1)}, u32[]{:S(2)}, u32[]{:S(2)}) collective-permute-start(bf16[4,80,768]{2,1,0:T(8,128)(2,1)S(1)} %constant_dynamic-slice_fusion.11), channel_id=1, source_target_pairs={{0,16},{4,20},{8,24},{12,28},{16,0},{20,4},{24,8},{28,12},{1,17},{... | collective-permute-start | bytes 1474568 | tf_op jit(solution)/shard_map/ppermute | solution.py:185
  499.5 63.9 %collective-permute-start.56 = (bf16[4,64,1280]{2,1,0:T(8,128)(2,1)S(1)}, bf16[4,64,1280]{2,1,0:T(8,128)(2,1)S(1)}, u32[]{:S(2)}, u32[]{:S(2)}) collective-permute-start(bf16[4,64,1280]{2,1,0:T(8,128)(2,1)S(1)} %fusion.7), channel_id=1, source_target_pairs={{0,1},{1,2},{2,3},{3,0},{4,5},{5,6},{6,7},{7,4},{8,9},{9,10},{10,1... | collective-permute-start | bytes 1966088 | tf_op jit(solution)/shard_map/ppermute | solution.py:199
  511.1 46.4 %collective-permute-start.104 = (bf16[1,160,1280]{2,1,0:T(8,128)(2,1)S(1)}, bf16[1,160,1280]{2,1,0:T(8,128)(2,1)S(1)}, u32[]{:S(2)}, u32[]{:S(2)}) collective-permute-start(bf16[1,160,1280]{2,1,0:T(8,128)(2,1)S(1)} %pad_maximum_fusion.13), channel_id=1, source_target_pairs={{0,4},{4,0},{8,12},{12,8},{16,20},{20,16},{24,28},{28,24},{1,5},{5... | collective-permute-start | bytes 1228808 | tf_op jit(solution)/shard_map/ppermute | solution.py:185
  522.9 35.1 %collective-permute-start.113 = (bf16[1,160,1280]{2,1,0:T(8,128)(2,1)S(1)}, bf16[1,160,1280]{2,1,0:T(8,128)(2,1)S(1)}, u32[]{:S(2)}, u32[]{:S(2)}) collective-permute-start(bf16[1,160,1280]{2,1,0:T(8,128)(2,1)S(1)} %pad_maximum_fusion.14), channel_id=1, source_target_pairs={{0,4},{4,0},{8,12},{12,8},{16,20},{20,16},{24,28},{28,24},{1,5},{5... | collective-permute-start | bytes 1228808 | tf_op jit(solution)/shard_map/ppermute | solution.py:185
  523.5 35.9 %collective-permute-start.122 = (bf16[1,160,1280]{2,1,0:T(8,128)(2,1)S(1)}, bf16[1,160,1280]{2,1,0:T(8,128)(2,1)S(1)}, u32[]{:S(2)}, u32[]{:S(2)}) collective-permute-start(bf16[1,160,1280]{2,1,0:T(8,128)(2,1)S(1)} %pad_maximum_fusion.15), channel_id=1, source_target_pairs={{0,4},{4,0},{8,12},{12,8},{16,20},{20,16},{24,28},{28,24},{1,5},{5... | collective-permute-start | bytes 1228808 | tf_op jit(solution)/shard_map/ppermute | solution.py:185
  556.3 23.4 %collective-permute-start.70 = (bf16[4,80,1280]{2,1,0:T(8,128)(2,1)S(1)}, bf16[4,80,1280]{2,1,0:T(8,128)(2,1)S(1)}, u32[]{:S(2)}, u32[]{:S(2)}) collective-permute-start(bf16[4,80,1280]{2,1,0:T(8,128)(2,1)S(1)} %constant_dynamic-slice_fusion.17), channel_id=1, source_target_pairs={{0,8},{4,12},{8,0},{12,4},{16,24},{20,28},{24,16},{28,20},{1,9},{5... | collective-permute-start | bytes 2457608 | tf_op jit(solution)/shard_map/ppermute | solution.py:185
  (149 other events, 1309.6 us)

commit v3 on v1

v3 whole, which is shorter than its diff:
```python
import functools

import jax
import jax.numpy as jnp
from jax import lax
from jax.experimental import pallas as pl
from jax.experimental.pallas import tpu as pltpu
from jax.sharding import PartitionSpec as P

HEAD_DIM = 160
EPS = 1e-05
NEG = -1e30
LANES = 128
F32 = jnp.float32
BF16 = jnp.bfloat16
NN = (((1,), (0,)), ((), ()))
NT = (((1,), (1,)), ((), ()))
TN = (((0,), (0,)), ((), ()))


def dot(a, b, dims=NN):
    return lax.dot_general(a, b, dims, preferred_element_type=F32)


def normalize(field):
    average = jnp.mean(field, -1, keepdims=True)
    centred = field - average
    inv_scale = lax.rsqrt(jnp.mean(centred * centred, -1, keepdims=True) + EPS)
    return (centred * inv_scale, inv_scale)


def norm_back(grad_out, normed, inv_scale, scale_vec):
    weighted = grad_out * scale_vec
    centred_grad = (
        weighted
        - jnp.mean(weighted, -1, keepdims=True)
        - normed * jnp.mean(weighted * normed, -1, keepdims=True)
    )
    return (inv_scale * centred_grad, jnp.sum(grad_out * normed, axis=0))


def gelu_exact(field):
    return jax.nn.gelu(field, approximate=False)


def windows(columns):
    out = []
    for head in range(columns // HEAD_DIM):
        start = head * HEAD_DIM
        base = start // LANES * LANES
        assert start + HEAD_DIM <= base + 2 * LANES
        out.append((base, start - base, start - base + HEAD_DIM))
    return out


def lines_of(ref, base):
    return ref[:, 0, :, base : base + 2 * LANES].reshape(-1, 2 * LANES)


def own_columns(shape, low, high):
    lane = lax.broadcasted_iota(jnp.int32, shape, 1)
    return (lane >= low) & (lane < high)


def byte_norm_kernel(byte_ref, gain_ref, out_ref):
    out_ref[...] = (normalize(byte_ref[...])[0] * gain_ref[...]).astype(BF16)


def byte_back_kernel(
    halves, byte_ref, gain_ref, key_ref, value_ref, *refs
):
    grad_keys, grad_values = refs[:halves], refs[halves : 2 * halves]
    grad_ref, gain_grad_ref = refs[2 * halves :]
    grad = 0.0
    for part in range(halves):
        size = grad_keys[part].shape[1]
        grad = grad + dot(grad_keys[part][...], key_ref[part * size : (part + 1) * size, :])
        grad = grad + dot(grad_values[part][...], value_ref[part * size : (part + 1) * size, :])
    normed, inv_scale = normalize(byte_ref[...])
    grad_ref[...], gain_grad = norm_back(grad, normed, inv_scale, gain_ref[...])

    @pl.when(pl.program_id(0) == 0)
    def _():
        gain_grad_ref[...] = jnp.zeros_like(gain_grad_ref)

    gain_grad_ref[...] += gain_grad


def feed_kernel(
    latents_ref,
    cotangent_ref,
    grad_act_ref,
    gain_ref,
    b_out_ref,
    b_up_ref,
    out_ref,
    up_ref,
    attended_a_ref,
    attended_b_ref,
    hidden_ref,
    mid_norm_ref,
    activated_ref,
    grad_pre_ref,
    grad_hidden_ref,
    grad_attn_ref,
    attended_ref,
    grad_a_ref,
    grad_b_ref,
    delta_ref,
    sums_ref,
):
    half = attended_a_ref.shape[1]
    attended_ref[:, :half] = attended_a_ref[...]
    attended_ref[:, half:] = attended_b_ref[...]
    hidden_ref[...] = latents_ref[...] + dot(attended_ref[...], out_ref[...]) + b_out_ref[...]
    mid_hat, mid_inv = normalize(hidden_ref[...])
    mid_norm_ref[...] = (mid_hat * gain_ref[...]).astype(BF16)
    pre_act = dot(mid_norm_ref[...], up_ref[...], NT) + b_up_ref[...]
    below = 0.5 * (1.0 + lax.erf(pre_act * 0.5**0.5))
    activated_ref[...] = (pre_act * below).astype(BF16)
    slope = below + pre_act * (jnp.exp(-0.5 * pre_act * pre_act) * (2.0 * jnp.pi) ** -0.5)
    grad_pre_ref[...] = (grad_act_ref[...] * slope).astype(BF16)
    sums_ref[1:2, :] = jnp.sum(grad_pre_ref[...].astype(F32), axis=0, keepdims=True)
    grad_mid = dot(grad_pre_ref[...], up_ref[...])
    mid_hat, mid_inv = normalize(hidden_ref[...])
    back, gain_grad = norm_back(grad_mid, mid_hat, mid_inv, gain_ref[...])
    sums_ref[0:1, :] = gain_grad[None]
    grad_hidden_ref[...] = cotangent_ref[...] + back
    sums_ref[2:3, :] = jnp.sum(grad_hidden_ref[...], axis=0, keepdims=True)
    sums_ref[3:4, :] = jnp.sum(cotangent_ref[...], axis=0, keepdims=True)
    grad_attn_ref[...] = grad_hidden_ref[...].astype(BF16)
    grad_a_ref[...] = dot(grad_attn_ref[...], out_ref[:half, :], NT).astype(BF16)
    grad_b_ref[...] = dot(grad_attn_ref[...], out_ref[half:, :], NT).astype(BF16)
    for head, (base, low, high) in enumerate(windows(2 * half)):
        grad_ref, start = (grad_a_ref, base) if base < half else (grad_b_ref, base - half)
        product = attended_ref[:, base : base + 2 * LANES].astype(F32) * grad_ref[
            :, start : start + 2 * LANES
        ].astype(F32)
        product = jnp.where(own_columns(product.shape, low, high), product, 0.0)
        delta_ref[:, head : head + 1] = jnp.sum(product, 1, keepdims=True)


def lse_kernel(query_ref, key_ref, lat_seg_ref, byte_seg_ref, lse_ref):
    allowed = byte_seg_ref[0] == lat_seg_ref[0]
    for head, (base, low, high) in enumerate(windows(query_ref.shape[3])):
        query = lines_of(query_ref, base)
        query = jnp.where(own_columns(query.shape, low, high), query, 0)
        key = key_ref[0, :, base : base + 2 * LANES]
        scores = jnp.where(allowed, dot(key, query, NT), NEG)
        peak = jnp.max(scores, 0, keepdims=True)
        total = jnp.sum(jnp.exp(scores - peak), 0, keepdims=True)
        lse_ref[0, head : head + 1, :] = peak + jnp.log(total)


class Tiles:
    def __init__(self, ref):
        self.ref = ref
        self.held = {}

    def add(self, base, window):
        for part in range(2):
            tile = base + part * LANES
            piece = window[:, part * LANES : (part + 1) * LANES]
            self.held[tile] = self.held[tile] + piece if tile in self.held else piece
        for tile in [t for t in self.held if t < base]:
            self.store(tile)

    def store(self, tile):
        done = self.held.pop(tile).astype(self.ref.dtype)
        if len(self.ref.shape) == 4:
            self.ref[:, 0, :, tile : tile + LANES] = done.reshape(
                self.ref.shape[0], self.ref.shape[2], LANES
            )
        else:
            self.ref[0, :, tile : tile + LANES] = done

    def finish(self):
        for tile in list(self.held):
            self.store(tile)


def attend_kernel(own_lat, first_head, query_ref, key_ref, value_ref, lat_seg_ref, byte_seg_ref, *refs):
    part_refs, (out_ref, lse_ref) = refs[:-2], refs[-2:]
    parts = [part_refs[0][0]]
    for step, ref in enumerate(part_refs[1:], 1):
        parts.append(pltpu.roll(ref[0], step * own_lat, 1))
    peak = functools.reduce(jnp.maximum, parts)
    lse_ref[0] = peak + jnp.log(sum(jnp.exp(part - peak) for part in parts))
    allowed = byte_seg_ref[0] == lat_seg_ref[0]
    tiles = Tiles(out_ref)
    for head, (base, low, high) in enumerate(windows(query_ref.shape[3])):
        query = lines_of(query_ref, base)
        mine = own_columns(query.shape, low, high)
        query = jnp.where(mine, query, 0)
        key = key_ref[0, :, base : base + 2 * LANES]
        value = value_ref[0, :, base : base + 2 * LANES]
        scores = jnp.where(allowed, dot(key, query, NT), NEG)
        own = first_head + head
        probs = jnp.exp(scores - lse_ref[0, own : own + 1, :]).astype(BF16)
        tiles.add(base, jnp.where(mine, dot(probs, value, TN), 0.0))
    tiles.finish()


def attend_back_kernel(
    first_head,
    place_ref,
    query_ref,
    key_ref,
    value_ref,
    lat_seg_ref,
    byte_seg_ref,
    lse_ref,
    delta_ref,
    grad_ref,
    grad_query_ref,
    grad_key_ref,
    grad_value_ref,
):
    blocks = grad_ref.shape[0]
    ring_order = [lax.rem(place_ref[0] + (blocks - r), blocks) for r in range(blocks)]
    allowed = byte_seg_ref[0] == lat_seg_ref[0]
    query_tiles, key_tiles, value_tiles = (
        Tiles(grad_query_ref),
        Tiles(grad_key_ref),
        Tiles(grad_value_ref),
    )
    for head, (base, low, high) in enumerate(windows(query_ref.shape[3])):
        query = lines_of(query_ref, base)
        mine = own_columns(query.shape, low, high)
        query = jnp.where(mine, query, 0)
        grad = jnp.concatenate([grad_ref[at, 0, :, base : base + 2 * LANES] for at in ring_order])
        grad = jnp.where(mine, grad, 0)
        key = key_ref[0, :, base : base + 2 * LANES]
        value = value_ref[0, :, base : base + 2 * LANES]
        scores = jnp.where(allowed, dot(key, query, NT), NEG)
        own = first_head + head
        probs = jnp.exp(scores - lse_ref[0, own : own + 1, :])
        grad_probs = dot(value, grad, NT)
        grad_scores = (probs * (grad_probs - delta_ref[0, own : own + 1, :])).astype(BF16)
        value_tiles.add(base, dot(probs.astype(BF16), grad))
        key_tiles.add(base, dot(grad_scores, query))
        query_tiles.add(base, jnp.where(mine, dot(grad_scores, key, TN), 0.0))
    query_tiles.finish()
    key_tiles.finish()
    value_tiles.finish()


def row_call(kernel, name, args, outs, flops, half=None):
    def spec(shape, halved=False):
        if len(shape) == 1:
            return pl.BlockSpec(memory_space=pltpu.SMEM)
        block = list(shape)
        block[1 if len(shape) == 4 else 0] = 1
        if halved:
            block[-1] //= 2
        at = half if halved else 0
        if len(shape) == 4:
            return pl.BlockSpec(tuple(block), lambda row: (0, row, 0, at))
        return pl.BlockSpec(tuple(block), lambda row: (row, 0, at))

    moved = sum(a.size * a.dtype.itemsize for a, _ in args)
    return pl.pallas_call(
        kernel,
        grid=(outs[-1].shape[0],),
        in_specs=[spec(a.shape, halved) for a, halved in args],
        out_specs=[spec(o.shape) for o in outs],
        out_shape=outs,
        name=name,
        cost_estimate=pl.CostEstimate(flops=flops, bytes_accessed=moved, transcendentals=0),
        compiler_params=pltpu.CompilerParams(vmem_limit_bytes=48 * 1024 * 1024),
    )(*[a for a, _ in args])


def block_call(kernel, name, lines, args, outs, flops):
    def spec(shape, cut):
        block = (lines if cut else shape[0], shape[1])
        return pl.BlockSpec(block, (lambda i: (i, 0)) if cut else (lambda i: (0, 0)))

    moved = sum(a.size * a.dtype.itemsize for a, _ in args)
    return pl.pallas_call(
        kernel,
        grid=(args[0][0].shape[0] // lines,),
        in_specs=[spec(a.shape, cut) for a, cut in args],
        out_specs=[spec(o.shape, cut) for o, cut in outs],
        out_shape=[o for o, _ in outs],
        name=name,
        cost_estimate=pl.CostEstimate(flops=flops, bytes_accessed=moved, transcendentals=0),
        compiler_params=pltpu.CompilerParams(vmem_limit_bytes=56 * 1024 * 1024),
    )(*[a for a, _ in args])


def ring(size, step=1):
    return [(i, (i + step) % size) for i in range(size)]


def add(first, *others):
    total = first.astype(F32)
    for other in others:
        total = total + other.astype(F32)
    return total.astype(first.dtype)


def panels(widths):
    return [(m, p) for m, width in enumerate(widths) for p in range(width // (2 * LANES))]


def join_kernel(widths, core_ref, mine_ref, other_ref, *out_refs):
    chips, part = mine_ref.shape[0], mine_ref.shape[3]

    def copy(sides):
        for number, (m, p) in enumerate(panels(widths)):
            for side, ref in enumerate(sides):
                at = side * widths[m] // 2 + p * LANES
                for chip in range(chips):
                    out_refs[m][chip * part : (chip + 1) * part, at : at + LANES] = ref[
                        chip, 0, number
                    ]

    @pl.when(core_ref[0] == 0)
    def _():
        copy((mine_ref, other_ref))

    @pl.when(core_ref[0] == 1)
    def _():
        copy((other_ref, mine_ref))


def split_kernel(widths, core_ref, *refs):
    in_refs, (kept_ref, sent_ref) = refs[:-2], refs[-2:]
    chips, part = kept_ref.shape[0], kept_ref.shape[3]

    def copy(sides):
        for number, (m, p) in enumerate(panels(widths)):
            for side, ref in enumerate(sides):
                at = side * widths[m] // 2 + p * LANES
                for chip in range(chips):
                    ref[chip, 0, number] = in_refs[m][
                        chip * part : (chip + 1) * part, at : at + LANES
                    ]

    @pl.when(core_ref[0] == 0)
    def _():
        copy((kept_ref, sent_ref))

    @pl.when(core_ref[0] == 1)
    def _():
        copy((sent_ref, kept_ref))


def packed_spec(shape):
    chips, _, count, part, lanes = shape
    return pl.BlockSpec((chips, 1, count, part, lanes), lambda z: (0, z, 0, 0, 0))


def matrix_spec(lines, width):
    return pl.BlockSpec((lines, width), lambda z: (z, 0))


def join(core, mine, other, widths):
    chips, blocks, _, part, _ = mine.shape
    lines = chips * part
    return pl.pallas_call(
        functools.partial(join_kernel, widths),
        grid=(blocks,),
        in_specs=[
            pl.BlockSpec(memory_space=pltpu.SMEM),
            packed_spec(mine.shape),
            packed_spec(mine.shape),
        ],
        out_specs=[matrix_spec(lines, width) for width in widths],
        out_shape=[jax.ShapeDtypeStruct((blocks * lines, width), mine.dtype) for width in widths],
        name="join",
        cost_estimate=pl.CostEstimate(
            flops=0, bytes_accessed=4 * mine.size * 2, transcendentals=0
        ),
        compiler_params=pltpu.CompilerParams(vmem_limit_bytes=48 * 1024 * 1024),
    )(core, mine, other)


def split(core, matrices, chips, blocks):
    widths = [m.shape[1] for m in matrices]
    lines = matrices[0].shape[0] // blocks
    shape = (chips, blocks, len(panels(widths)), lines // chips, LANES)
    packed = jax.ShapeDtypeStruct(shape, matrices[0].dtype)
    return pl.pallas_call(
        functools.partial(split_kernel, widths),
        grid=(blocks,),
        in_specs=[pl.BlockSpec(memory_space=pltpu.SMEM)]
        + [matrix_spec(lines, width) for width in widths],
        out_specs=[packed_spec(shape)] * 2,
        out_shape=[packed] * 2,
        name="split",
        cost_estimate=pl.CostEstimate(
            flops=0, bytes_accessed=8 * sum(m.size for m in matrices) // 2, transcendentals=0
        ),
        compiler_params=pltpu.CompilerParams(vmem_limit_bytes=48 * 1024 * 1024),
    )(core, *matrices)


def after(x, *earlier):
    return lax.optimization_barrier((x, *earlier))[0]


def three_parts(x, shape):
    parts = []
    for _ in range(3):
        part = lax.reduce_precision(x, 8, 7)
        parts.append(part.astype(BF16))
        x = x - part
    parts = jnp.concatenate(parts)
    size = shape[0] * shape[1]
    return jnp.pad(parts, (0, size - parts.size)).reshape(shape)


def from_three_parts(x, size):
    parts = x.reshape(x.shape[0], -1)[:, : 3 * size].astype(F32).reshape(-1, 3, size)
    return (parts[:, 0] + (parts[:, 1] + parts[:, 2])).reshape(-1)


class Mesh:
    def __init__(self, dp, mp):
        self.dp, self.mp = dp, mp
        self.dp_index = lax.axis_index("dp")
        self.mp_index = lax.axis_index("mp")
        self.core = self.dp_index % 2

    def cut(self, lines):
        chips = 1
        while 2 * chips <= self.dp // 2 and lines % (32 * chips) == 0:
            chips *= 2
        return chips, [2 * k for k in (1 << b for b in range(8)) if chips <= k < self.dp // 2]

    def swap(self, x, bit):
        return lax.ppermute(x, "dp", [(i, i ^ bit) for i in range(self.dp)])

    def shift(self, x, step):
        return lax.ppermute(x, "mp", ring(self.mp, step))

    def ring_gather(self, x):
        blocks = [x]
        for _ in range(self.mp - 1):
            blocks.append(self.shift(blocks[-1], 1))
        return blocks

    def ring_scatter(self, parts):
        total = parts[1] if self.mp > 1 else parts[0]
        for step in range(2, self.mp + 1):
            total = add(self.shift(total, 1), parts[step % self.mp])
        return total

    def chip_groups(self, chips):
        return [
            [2 * (chip + chips * rest) + core for chip in range(chips)]
            for rest in range(self.dp // 2 // chips)
            for core in range(2)
        ]

    def slice_of(self, shards):
        chips, _ = self.cut(shards[0].shape[0])
        part = shards[0].shape[0] // chips
        chip = self.dp_index // 2 % chips
        return jnp.concatenate(
            [
                lax.dynamic_slice(
                    shard,
                    (chip * part, self.core * (shard.shape[1] // 2)),
                    (part, shard.shape[1] // 2),
                )
                .reshape(part, -1, LANES)
                .transpose(1, 0, 2)
                for shard in shards
            ]
        )

    def in_order(self, parts):
        blocks = jnp.stack(parts)
        back = (self.mp_index - jnp.arange(self.mp)) % self.mp
        return jnp.take(blocks, back, axis=0)

    def gather_chips(self, x, lines):
        chips, _ = self.cut(lines)
        return lax.all_gather(x, "dp", axis=0, axis_index_groups=self.chip_groups(chips))

    def both_cores(self, mine, widths):
        return join(self.core[None], mine, self.swap(mine, 1), widths)

    def split_core(self, partials, lines):
        chips, _ = self.cut(lines)
        blocks = partials[0].shape[0] // lines
        return split(self.core[None], partials, chips, blocks)

    def scatter_chips(self, total, lines):
        chips, _ = self.cut(lines)
        return lax.psum_scatter(
            total, "dp", scatter_dimension=0, axis_index_groups=self.chip_groups(chips)
        )

    def link_pieces(self, total, lines):
        chips, _ = self.cut(lines)
        bits = [1 << b for b in range(chips.bit_length() - 1)]
        middle = (total.shape[2] + 1) // 2
        return [
            (piece.reshape((2,) * len(bits) + piece.shape[1:]), order, sorted(bits, reverse=True))
            for order, piece in ((bits, total[:, :, :middle]), (bits[::-1], total[:, :, middle:]))
        ]

    def link_step(self, pieces, *earlier):
        out = []
        for piece, order, left in pieces:
            mine = self.dp_index // (2 * order[0]) % 2
            axis = left.index(order[0])
            if earlier:
                piece = after(piece, *earlier)
            sent = lax.dynamic_index_in_dim(piece, 1 - mine, axis, False)
            kept = lax.dynamic_index_in_dim(piece, mine, axis, False)
            piece = add(kept, self.swap(sent, 2 * order[0]))
            out.append((piece, order[1:], [bit for bit in left if bit != order[0]]))
        return out

    def finish_sum(self, total, lines, widths, small=None):
        chips, rest = self.cut(lines)
        for bit in rest:
            total = add(total, self.swap(total, bit))
        blocks = [
            lax.dynamic_index_in_dim(total, (self.mp_index + step) % self.mp, 0, False)
            for step in range(self.mp)
        ]
        if small is not None:
            panel = small.astype(BF16)
            panel = jnp.pad(panel, (0, total[0, 0].size - panel.size)).reshape(1, -1, LANES)
            blocks = [jnp.concatenate([block, panel]) for block in blocks]
        total = add(blocks[0], *[self.shift(blocks[step], step) for step in range(1, self.mp)])
        slices = [total] + [self.swap(total, 2 * k) for k in range(1, chips)]
        if small is not None:
            panel = add(*[piece[-1] for piece in slices])
            for bit in rest:
                panel = add(panel, self.swap(panel, bit))
            slices = [jnp.concatenate([piece[:-1], panel[None]]) for piece in slices]
        chip = self.dp_index // 2 % chips
        mine = jnp.take(jnp.stack(slices), chip ^ jnp.arange(chips), axis=0)[:, None]
        other = self.swap(mine, 1)
        out = join(self.core[None], mine, other, widths)
        if small is None:
            return out
        panel = mine[0, 0, -1].astype(F32) + other[0, 0, -1].astype(F32)
        return out, panel.reshape(-1)[: small.size]

    def turned(self, x, axis):
        blocks = x.reshape(x.shape[:axis] + (self.mp, -1) + x.shape[axis + 1 :])
        index = (self.mp_index - jnp.arange(self.mp)) % self.mp
        return jnp.take(blocks, index, axis=axis).reshape(x.shape)


def shards(
    dp,
    mp,
    byte_in,
    latents,
    cotangent,
    byte_gain,
    latent_gain,
    mlp_gain,
    w_query,
    w_key,
    w_value,
    w_out,
    b_out,
    w_up,
    b_up,
    w_down,
    b_down,
    byte_seg,
    byte_pad,
    latent_seg,
):
    score_scale = HEAD_DIM ** (-0.5)
    rows, byte_len, byte_width = byte_in.shape
    own_lat, lat_width = latents.shape[1:]
    lat_len = own_lat * mp
    own_lines, half_width = rows * own_lat, lat_width // 2
    heads = w_query.shape[1] * mp // HEAD_DIM
    half_heads = heads // 2
    net = Mesh(dp, mp)
    mp_index = net.mp_index
    shape = jax.ShapeDtypeStruct

    lines = w_query.shape[1]
    head_widths = [lat_width, byte_width, byte_width]
    feed_widths = [lat_width] * 3
    feed_slice = net.slice_of([w_out, w_up.T, w_down])
    feed_slice = jnp.concatenate([feed_slice, three_parts(b_up, feed_slice.shape[1:])[None]])
    head_slice = net.slice_of([w_query.T, w_key.T, w_value.T])
    head_parts = [head_slice] + [net.shift(head_slice, step) for step in range(1, mp)]

    latents = latents.reshape(own_lines, lat_width)
    cotangent = cotangent.reshape(own_lines, lat_width)
    byte_in = byte_in.reshape(rows * byte_len, byte_width)
    lat_hat, lat_inv = normalize(latents)
    lat_norm = (lat_hat * latent_gain).astype(BF16).reshape(rows, own_lat, lat_width)
    (byte_norm,) = block_call(
        byte_norm_kernel,
        "byte_norm",
        byte_len,
        [(byte_in, True), (byte_gain[None], False)],
        [(shape(byte_in.shape, BF16), True)],
        10 * byte_in.size,
    )
    lat_blocks = [lat_norm, net.shift(lat_norm, 1)]
    head_parts, lat_blocks, byte_norm = lax.optimization_barrier(
        (head_parts, lat_blocks, byte_norm)
    )
    head_slices = net.in_order(head_parts)
    for step in range(2, mp):
        block = lat_blocks[-1]
        if step == 3:
            block = after(block, head_slices)
        lat_blocks.append(net.shift(block, 1))
    feed_slices = lax.all_gather(after(feed_slice, lat_blocks[mp - 2]), "mp", axis=0)
    lat_all = jnp.stack(lat_blocks)
    lat_flat = lat_all.reshape(rows * lat_len, lat_width)
    head_slices = after(net.gather_chips(head_slices, lines), lat_blocks[-1])
    query_t, key_t, value_t = net.both_cores(head_slices, head_widths)

    real_seg = jnp.where(byte_pad == 1, byte_seg, -1)
    real_seg = lax.dynamic_slice_in_dim(real_seg, mp_index * byte_len, byte_len, 1)
    byte_col = real_seg[:, :, None]
    lat_row = net.turned(latent_seg, 1)[:, None, :]
    unit = 2 * rows * lat_len * byte_len * half_heads * 2 * LANES

    keys = dot(byte_norm, key_t, NT).astype(BF16).reshape(rows, byte_len, lat_width)
    queries = (dot(lat_flat, query_t, NT) * score_scale).astype(BF16)
    queries = queries.reshape(lat_all.shape)
    (lse_part,) = row_call(
        lse_kernel,
        "lse",
        [(queries, False), (keys, False), (lat_row, False), (byte_col, False)],
        [shape((rows, heads, lat_len), F32)],
        2 * unit,
    )
    lse_parts = [lse_part] + [net.shift(lse_part, step) for step in range(1, mp)]
    feed_slices = after(feed_slices, lse_part)
    b_up_all = from_three_parts(feed_slices[:, -1], b_up.shape[0])
    feed_slices = net.gather_chips(feed_slices[:, :-1], lines)
    values = dot(after(byte_norm, lse_part), value_t, NT).astype(BF16)
    values = values.reshape(rows, byte_len, lat_width)

    lat_half = shape((mp, rows, own_lat, half_width), BF16)
    parts = []
    for half in range(2):
        attended_part, lse = row_call(
            functools.partial(attend_kernel, own_lat, half * half_heads),
            "attend",
            [(queries, True), (keys, True), (values, True), (lat_row, False), (byte_col, False)]
            + [(part, False) for part in lse_parts],
            [lat_half, shape((rows, heads, lat_len), F32)],
            2 * unit,
            half,
        )
        parts.append(attended_part)
    attended = [parts[0][1], parts[1][1]]
    for step in range(2, mp + 1):
        moved = net.shift(attended[0], 1)
        if step == 2:
            moved, attended[1] = lax.optimization_barrier((moved, attended[1]))
            feed_slices = after(feed_slices, moved)
        attended[0] = add(moved, parts[0][step % mp])
        attended[1] = add(net.shift(after(attended[1], moved), 1), parts[1][step % mp])
    attended = [x.reshape(own_lines, half_width) for x in attended]

    out_w, up_t, down_w = net.both_cores(feed_slices, feed_widths)
    grad_down = cotangent.astype(BF16)
    grad_act = dot(grad_down, down_w, NT)
    whole = shape((own_lines, lat_width), BF16)
    wide = shape((own_lines, lat_width), F32)
    part = shape((own_lines, half_width), BF16)
    (
        hidden,
        mid_norm,
        activated,
        grad_pre,
        grad_hidden,
        grad_attn,
        attended,
        grad_att_a,
        grad_att_b,
        delta,
        feed_vectors,
    ) = block_call(
        feed_kernel,
        "feed",
        own_lines,
        [(latents, True), (cotangent, True), (grad_act, True)]
        + [(v[None], False) for v in (mlp_gain, b_out, b_up_all)]
        + [(out_w, False), (up_t, False), (attended[0], True), (attended[1], True)],
        [(wide, True), (whole, True), (whole, True), (whole, True), (wide, True), (whole, True)]
        + [(whole, True), (part, True), (part, True), (shape((own_lines, heads), F32), True)]
        + [(shape((4, lat_width), F32), False)],
        8 * own_lines * lat_width * lat_width,
    )

    result = hidden + dot(activated, down_w) + b_down
    delta = delta.reshape(rows, own_lat, heads).transpose(0, 2, 1)
    delta = jnp.concatenate([delta] + [net.shift(delta, step) for step in range(1, mp)], 2)
    feed_partials = [
        dot(activated, grad_down, TN).astype(BF16),
        dot(grad_pre, mid_norm, TN).astype(BF16),
        dot(attended, grad_attn, TN).astype(BF16),
    ]
    def gathered(grad, *earlier):
        grad = grad.reshape(rows, own_lat, half_width)
        return lax.all_gather(after(grad, *earlier) if earlier else grad, "mp", axis=0)

    grads_a = gathered(grad_att_a)
    grads_b = gathered(grad_att_b)
    feed_kept, feed_sent = net.split_core(feed_partials, lines)
    feed_sums = add(feed_kept, net.swap(feed_sent, 1))
    grads_a, feed_sums, result, delta = lax.optimization_barrier(
        (grads_a, feed_sums, result, delta)
    )
    feed_sums = net.scatter_chips(feed_sums, lines)

    def attend_back(half, grads):
        return row_call(
            functools.partial(attend_back_kernel, half * half_heads),
            "attend_back",
            [(mp_index[None], False), (queries, True), (keys, True), (values, True)]
            + [(lat_row, False), (byte_col, False), (lse, False), (delta, False), (grads, False)],
            [lat_half] + [shape((rows, byte_len, half_width), BF16)] * 2,
            5 * unit,
            half,
        )

    def head_partials(grads):
        grad_query, grad_key, grad_value = grads
        return [
            (dot(grad_query.reshape(-1, half_width), lat_flat, TN) * score_scale).astype(BF16),
            dot(grad_key.reshape(-1, half_width), byte_norm, TN).astype(BF16),
            dot(grad_value.reshape(-1, half_width), byte_norm, TN).astype(BF16),
        ]

    back_a, *rest_a = attend_back(0, grads_a)
    total_a = back_a[1]
    moved_a = net.shift(total_a, 1)
    partials_a = head_partials((back_a, *rest_a))
    kept_a, sent_a = net.split_core(partials_a, lines)
    sums_a = net.link_pieces(add(kept_a, net.swap(sent_a, 1)), lines)

    grads_b = after(grads_b, moved_a, sums_a[0][0])
    back_b, *rest_b = attend_back(1, grads_b)
    sums_a = net.link_step(sums_a) if sums_a[0][1] else sums_a
    total_a = add(moved_a, back_a[2 % mp])
    moved_a = net.shift(total_a, 1) if mp > 2 else total_a
    total_b = back_b[1]
    tied = lax.optimization_barrier((back_b, *rest_b, moved_a, sums_a[0][0], sums_a[1][0]))
    partials_b = head_partials(tied[:3])
    moved_a = tied[3]
    sums_a = [(piece, *state[1:]) for piece, state in zip(tied[4:], sums_a)]
    while sums_a[0][1]:
        sums_a = net.link_step(sums_a)
    if mp > 2:
        total_a = add(moved_a, back_a[3 % mp])
    for step in range(4, mp + 1):
        total_a = add(net.shift(total_a, 1), back_a[step % mp])
    moved_b = net.shift(after(total_b, moved_a), 1)
    tied = lax.optimization_barrier(
        (total_a, moved_b, sums_a[0][0], sums_a[1][0], *partials_b)
    )
    total_a, moved_b, partials_b = tied[0], tied[1], tied[4:]
    sums_a = [(piece, *state[1:]) for piece, state in zip(tied[2:4], sums_a)]
    kept_b, sent_b = net.split_core(partials_b, lines)
    total_b = add(moved_b, back_b[2 % mp])
    moved_b = net.shift(total_b, 1) if mp > 2 else total_b
    sums_b = net.link_pieces(add(kept_b, net.swap(sent_b, 1)), lines)
    if sums_b[0][1]:
        sums_b = net.link_step(sums_b)
    halves = [x.reshape(-1, half_width) for x in (rest_a[0], rest_b[0], rest_a[1], rest_b[1])]
    halves[0] = after(halves[0], sent_b)
    grad_bytes, grad_byte_gain = block_call(
        functools.partial(byte_back_kernel, 2),
        "byte_back",
        byte_len,
        [(byte_in, True), (byte_gain[None], False), (key_t, False), (value_t, False)]
        + [(half, True) for half in halves],
        [(shape(byte_in.shape, F32), True), (shape((1, byte_width), F32), False)],
        4 * rows * byte_len * lat_width * byte_width,
    )
    tied = lax.optimization_barrier((grad_bytes, moved_b, sums_b[0][0], sums_b[1][0]))
    grad_bytes, moved_b = tied[:2]
    sums_b = [(piece, *state[1:]) for piece, state in zip(tied[2:], sums_b)]
    while sums_b[0][1]:
        sums_b = net.link_step(sums_b)
    total_b = add(moved_b, back_b[3 % mp]) if mp > 2 else total_b
    for step in range(4, mp + 1):
        total_b = add(net.shift(total_b, 1), back_b[step % mp])
    grad_queries_own = [t.reshape(own_lines, half_width) for t in (total_a, total_b)]

    head_sums = jnp.concatenate(
        [jnp.concatenate([piece for piece, _, _ in sums], 1) for sums in (sums_a, sums_b)]
    )
    head_grads = net.finish_sum(head_sums, lines, head_widths)
    grad_lat_norm = score_scale * (
        dot(grad_queries_own[0], query_t[:half_width])
        + dot(grad_queries_own[1], query_t[half_width:])
    )
    grad_lat_back, grad_latent_gain = norm_back(grad_lat_norm, lat_hat, lat_inv, latent_gain)
    grad_latents = grad_hidden + grad_lat_back

    small = jnp.concatenate([grad_byte_gain[0], grad_latent_gain, feed_vectors.reshape(-1)])
    feed_grads, sums = net.finish_sum(
        after(feed_sums, sums_b[0][0]), lines, feed_widths, small
    )
    sums = [sums[:byte_width]] + list(sums[byte_width:].reshape(5, lat_width))
    own_units = b_up.shape[0]
    return (
        result.reshape(rows, own_lat, lat_width),
        grad_bytes.reshape(rows, byte_len, byte_width),
        grad_latents.reshape(rows, own_lat, lat_width),
        sums[0],
        sums[1],
        sums[2],
        head_grads[0].astype(F32).T,
        head_grads[1].astype(F32).T,
        head_grads[2].astype(F32).T,
        feed_grads[2].astype(F32),
        sums[4],
        feed_grads[1].astype(F32).T,
        lax.dynamic_slice_in_dim(sums[3], mp_index * own_units, own_units, 0),
        feed_grads[0].astype(F32),
        sums[5],
    )


def solution(mesh):
    by_row = P("dp", "mp", None)
    columns, lines = P(None, "mp"), P("mp", None)
    return jax.shard_map(
        functools.partial(shards, mesh.shape["dp"], mesh.shape["mp"]),
        mesh=mesh,
        in_specs=(
            by_row,
            by_row,
            by_row,
            P(),
            P(),
            P(),
            columns,
            columns,
            columns,
            lines,
            P(),
            columns,
            P("mp"),
            lines,
            P(),
            P("dp", None),
            P("dp", None),
            P("dp", None),
        ),
        out_specs=(
            by_row,
            by_row,
            by_row,
            P(),
            P(),
            P(),
            columns,
            columns,
            columns,
            lines,
            P(),
            columns,
            P("mp"),
            lines,
            P(),
        ),
        check_vma=False,
    )
```

time: 1390 us -> 559 us (0.40); the launches traced: 1370 us -> 550 us
  waiting for transfers between devices: 989 us -> 237 us
  blocking collectives: 171 us -> 0 us
  Pallas kernels: 34.5 us -> 98.7 us
  starting transfers between devices: 1.24 us -> 59.4 us
  matrix products: 102 us -> 58.4 us
  other arithmetic: 32.2 us -> 46.2 us
    reduce_scatter x8 -> x0, waiting for transfers between devices: 638 us -> none  [the longest x6 532 us: summed(): lax.psum_scatter(partial.astype(BF16), ('mp', 'dp'), scatter_dimension=0,...]
    all_gather x8 -> x5, waiting for transfers between devices: 350 us -> 63.5 us  [the longest x2 46.4 us: gather_chips(): lax.all_gather(x, 'dp', axis=0, axis_index_groups=self.chip_groups(chips))]
    ppermute x0 -> x51, waiting for transfers between devices: none -> 174 us  [the longest x30 149 us: shift(): return lax.ppermute(x, 'mp', ring(self.mp, step))]
    all_gather x8 -> x0, blocking collectives: 121 us -> none  [the longest x6 89.9 us: summed(): return lax.all_gather(piece, 'dp', axis=0, tiled=True).astype(F32)]
    pallas_call x3 -> x15, Pallas kernels: 34.5 us -> 98.7 us  [the longest x5 40.5 us: row_call(): pl.pallas_call(kernel, grid=(outs[-1].shape[0],), in_specs=[spec(a.shape,...]
    ppermute x0 -> x51, starting transfers between devices: none -> 58.9 us  [the longest x30 35.7 us: shift(): return lax.ppermute(x, 'mp', ring(self.mp, step))]
    dot_general x18 -> x16, matrix products: 102 us -> 58.4 us  [dot(): return lax.dot_general(a, b, dims, preferred_element_type=F32)]
    psum x1 -> x0, blocking collectives: 41.6 us -> none  [shards(): lax.psum((grad_byte_gain, grad_latent_gain, grad_mlp_gain, grad_b_out, gr...]
  transfers between devices with their start and end apart: 16 -> 57, of which waited for: 16 -> 26; matrix products, arithmetic and copies ran while one was open for 10% -> 19% of each run, Pallas kernels for 3% -> 13%
where the time goes in v3:
time: 559 us; the launch traced here: 550 us
  waiting for transfers between devices  237 us (42%)
  Pallas kernels  98.7 us (18%)
  starting transfers between devices  59.4 us (11%)
  matrix products  58.4 us (10%)
  other arithmetic  46.2 us (8%)
  local copies, waits for them, and re-layouts  32.9 us (6%)
  between operations  17.2 us (3%)
    ppermute x30, waiting for transfers between devices, shift(): return lax.ppermute(x, 'mp', ring(self.mp, step))  149 us
    dot_general x16, matrix products, dot(): return lax.dot_general(a, b, dims, preferred_element_type=F32)  58.4 us
    all_gather x2, waiting for transfers between devices, gather_chips(): lax.all_gather(x, 'dp', axis=0, axis_index_groups=self.chip_groups(chips))  46.4 us
    pallas_call x5, Pallas kernels, row_call(): pl.pallas_call(kernel, grid=(outs[-1].shape[0],), in_specs=[spec(a.shape,...  40.5 us
    ppermute x30, starting transfers between devices, shift(): return lax.ppermute(x, 'mp', ring(self.mp, step))  35.7 us
    pallas_call x3, Pallas kernels, block_call(): pl.pallas_call(kernel, grid=(args[0][0].shape[0] // lines,), in_specs=[sp...  33.3 us
    convert_element_type x26, other arithmetic, add(): return total.astype(first.dtype)  25.8 us
    ppermute x21, waiting for transfers between devices, swap(): return lax.ppermute(x, 'dp', [(i, i ^ bit) for i in range(self.dp)])  24.2 us
  transfers between devices with their start and end apart: 57, of which 26 were waited for; matrix products, arithmetic and copies ran while one was open for 19% of the time, Pallas kernels for 13%

profile of v3, /device:TPU:9, one launch (start us, length us, event | category | flops | bytes accessed | tf_op | source)
XLA Modules:
  0.0 550.0 jit_solution(81291250417573844)
XLA Ops:
  16.6 5.7 %byte_norm.1 = bf16[2048,768]{1,0:T(8,128)(2,1)} custom-call(f32[2048,768]{1,0:T(8,128)} %bitcast.294, f32[1,768]{1,0:T(1,128)} %broadcast_in_dim.79.gain_ref), custom_call_target="tpu_custom_call" | custom-call | flops 15728640 | bytes 6294528 | tf_op jit(solution)/shard_map/byte_norm/pallas_call | solution.py:280
  22.4 9.1 %collective-permute-done = bf16[11,80,128]{2,1,0:T(8,128)(2,1)S(1)} collective-permute-done((bf16[11,80,128]{2,1,0:T(8,128)(2,1)S(1)}, bf16[11,80,128]{2,1,0:T(8,128)(2,1)S(1)}, u32[]{:S(2)}, u32[]{:S(2)}) %collective-permute-start) | collective-permute-done | bytes 225312 | tf_op jit(solution)/shard_map/ppermute | solution.py:437
  31.4 13.6 %collective-permute-done.1 = bf16[11,80,128]{2,1,0:T(8,128)(2,1)S(1)} collective-permute-done((bf16[11,80,128]{2,1,0:T(8,128)(2,1)S(1)}, bf16[11,80,128]{2,1,0:T(8,128)(2,1)S(1)}, u32[]{:S(2)}, u32[]{:S(2)}) %collective-permute-start.1) | collective-permute-done | bytes 225312 | tf_op jit(solution)/shard_map/ppermute | solution.py:437
  50.0 15.9 %collective-permute-done.4 = bf16[4,64,1280]{2,1,0:T(8,128)(2,1)S(1)} collective-permute-done((bf16[4,64,1280]{2,1,0:T(8,128)(2,1)S(1)}, bf16[4,64,1280]{2,1,0:T(8,128)(2,1)S(1)}, u32[]{:S(2)}, u32[]{:S(2)}) %collective-permute-start.4) | collective-permute-done | bytes 655392 | tf_op jit(solution)/shard_map/ppermute | solution.py:437
  66.2 14.8 %collective-permute-done.5 = bf16[4,64,1280]{2,1,0:T(8,128)(2,1)S(1)} collective-permute-done((bf16[4,64,1280]{2,1,0:T(8,128)(2,1)S(1)}, bf16[4,64,1280]{2,1,0:T(8,128)(2,1)S(1)}, u32[]{:S(2)}, u32[]{:S(2)}) %collective-permute-start.5) | collective-permute-done | bytes 655392 | tf_op jit(solution)/shard_map/ppermute | solution.py:437
  81.0 16.8 %all-gather.15.cloned.1.call-done = bf16[16,11,80,128]{3,2,1,0:T(8,128)(2,1)} async-done(((bf16[4,11,80,128]{3,2,1,0:T(8,128)(2,1)}), bf16[16,11,80,128]{3,2,1,0:T(8,128)(2,1)}) %all-gather.15.cloned.1.call-update) | async-done | bytes 3604496 | tf_op jit(solution)/shard_map/all_gather | solution.py:482
  106.0 5.7 %join.4 = (bf16[1280,1280]{1,0:T(8,128)(2,1)}, bf16[1280,768]{1,0:T(8,128)(2,1)S(1)}, bf16[1280,768]{1,0:T(8,128)(2,1)S(1)}) custom-call(s32[1]{0:T(128)} %bitcast.2.core_ref, bf16[4,4,11,80,128]{4,3,2,1,0:T(8,128)(2,1)} %bitcast.303, bf16[4,4,11,80,128]{4,3,2,1,0:T(8,128)(2,1)} %collective-permute-done.6.other_ref), custom_call_target="tpu_custom_call" | custom-call | bytes 14417920 | tf_op jit(solution)/shard_map/join/pallas_call | solution.py:362
  111.7 7.3 %multiply_convert_fusion = bf16[1024,1280]{1,0:T(8,128)(2,1)S(1)} fusion(bf16[1024,1280]{1,0:T(8,128)(2,1)S(1)} %bitcast.308, bf16[1280,1280]{1,0:T(8,128)(2,1)} %get-tuple-element.108), kind=kOutput, calls=%fused_computation.10 | convolution fusion | flops 3358064640 | bytes 8519680 | tf_op jit(solution)/shard_map/dot_general | solution.py:22
  119.0 6.0 %convolution_convert_fusion.4 = bf16[2048,1280]{1,0:T(8,128)(2,1)} fusion(bf16[2048,768]{1,0:T(8,128)(2,1)S(1)} %copy-done.21, bf16[1280,768]{1,0:T(8,128)(2,1)S(1)} %get-tuple-element.110.key_ref), kind=kOutput, calls=%fused_computation.9 | convolution fusion | flops 4029153280 | bytes 10354688 | tf_op jit(solution)/shard_map/dot_general | solution.py:22
  125.0 7.3 %lse.1.refs_0_ = f32[4,8,256]{2,1,0:T(8,128)S(1)} custom-call(bf16[4,4,64,1280]{3,2,1,0:T(8,128)(2,1)S(1)} %bitcast.279, bf16[4,512,1280]{2,1,0:T(8,128)(2,1)} %bitcast.284, s32[4,1,256]{2,1,0:T(1,128)S(1)} %broadcast_select_fusion.1.lat_seg_ref, s32[4,512,1]{2,1,0:T(8,128)S(1)} %copy-done.3), custom_call_target="tpu_custom_call" | custom-call | flops 2147483648 | bytes 7876608 | tf_op jit(solution)/shard_map/lse/pallas_call | solution.py:262
  142.9 9.2 %convolution_convert_fusion.3 = bf16[2048,1280]{1,0:T(8,128)(2,1)} fusion(bf16[2048,768]{1,0:T(8,128)(2,1)} %byte_norm.1, bf16[1280,768]{1,0:T(8,128)(2,1)} %copy-done.12), kind=kOutput, calls=%fused_computation.8 | convolution fusion | flops 4029153280 | bytes 10354688 | tf_op jit(solution)/shard_map/dot_general | solution.py:22
  152.1 7.2 %attend.2 = (bf16[4,4,64,640]{3,2,1,0:T(8,128)(2,1)}, f32[4,8,256]{2,1,0:T(8,128)}) custom-call(bf16[4,4,64,1280]{3,2,1,0:T(8,128)(2,1)S(1)} %bitcast.280, bf16[4,512,1280]{2,1,0:T(8,128)(2,1)} %bitcast.285, bf16[4,512,1280]{2,1,0:T(8,128)(2,1)} %bitcast.289, s32[4,1,256]{2,1,0:T(1,128)S(1)} %broadcast_select_fusion.1.lat_seg_ref, ...), custom_call_target="tpu_custom_call" | custom-call | flops 2147483648 | bytes 13250560 | tf_op jit(solution)/shard_map/attend/pallas_call | solution.py:262
  161.9 6.4 %attend.3 = (bf16[4,4,64,640]{3,2,1,0:T(8,128)(2,1)S(1)}, f32[4,8,256]{2,1,0:T(8,128)S(1)}) custom-call(bf16[4,4,64,1280]{3,2,1,0:T(8,128)(2,1)S(1)} %bitcast.281, bf16[4,512,1280]{2,1,0:T(8,128)(2,1)} %bitcast.286, bf16[4,512,1280]{2,1,0:T(8,128)(2,1)} %bitcast.290, s32[4,1,256]{2,1,0:T(1,128)S(1)} %broadcast_select_fusion.1.lat_seg_ref, ...), custom_call_target="tpu_custom_call" | custom-call | flops 2147483648 | bytes 13250560 | tf_op jit(solution)/shard_map/attend/pallas_call | solution.py:262
  169.4 29.6 %all-gather.17.cloned.1.call-done = bf16[16,15,80,128]{3,2,1,0:T(8,128)(2,1)} async-done(((bf16[4,15,80,128]{3,2,1,0:T(8,128)(2,1)}), bf16[16,15,80,128]{3,2,1,0:T(8,128)(2,1)}) %all-gather.17.cloned.1.call-update) | async-done | bytes 4915216 | tf_op jit(solution)/shard_map/all_gather | solution.py:482
  209.1 6.9 %collective-permute-done.12 = bf16[4,64,640]{2,1,0:T(8,128)(2,1)S(1)} collective-permute-done((bf16[4,64,640]{2,1,0:T(8,128)(2,1)S(1)}, bf16[4,64,640]{2,1,0:T(8,128)(2,1)S(1)}, u32[]{:S(2)}, u32[]{:S(2)}) %collective-permute-start.12) | collective-permute-done | bytes 327712 | tf_op jit(solution)/shard_map/ppermute | solution.py:437
  219.6 5.7 %collective-permute-done.15 = bf16[4,64,640]{2,1,0:T(8,128)(2,1)S(1)} collective-permute-done((bf16[4,64,640]{2,1,0:T(8,128)(2,1)S(1)}, bf16[4,64,640]{2,1,0:T(8,128)(2,1)S(1)}, u32[]{:S(2)}, u32[]{:S(2)}) %collective-permute-start.15) | collective-permute-done | bytes 327712 | tf_op jit(solution)/shard_map/ppermute | solution.py:437
  225.5 6.9 %collective-permute-done.13 = bf16[4,64,640]{2,1,0:T(8,128)(2,1)S(1)} collective-permute-done((bf16[4,64,640]{2,1,0:T(8,128)(2,1)S(1)}, bf16[4,64,640]{2,1,0:T(8,128)(2,1)S(1)}, u32[]{:S(2)}, u32[]{:S(2)}) %collective-permute-start.13) | collective-permute-done | bytes 327712 | tf_op jit(solution)/shard_map/ppermute | solution.py:437
  235.6 6.5 %collective-permute-done.16 = bf16[4,64,640]{2,1,0:T(8,128)(2,1)S(1)} collective-permute-done((bf16[4,64,640]{2,1,0:T(8,128)(2,1)S(1)}, bf16[4,64,640]{2,1,0:T(8,128)(2,1)S(1)}, u32[]{:S(2)}, u32[]{:S(2)}) %collective-permute-start.16) | collective-permute-done | bytes 327712 | tf_op jit(solution)/shard_map/ppermute | solution.py:437
  242.9 7.4 %join.5 = (bf16[1280,1280]{1,0:T(8,128)(2,1)S(1)}, bf16[1280,1280]{1,0:T(8,128)(2,1)}, bf16[1280,1280]{1,0:T(8,128)(2,1)}) custom-call(s32[1]{0:T(128)} %bitcast.2.core_ref, bf16[4,4,15,80,128]{4,3,2,1,0:T(8,128)(2,1)} %bitcast.297, bf16[4,4,15,80,128]{4,3,2,1,0:T(8,128)(2,1)} %collective-permute-done.11.other_ref), custom_call_target="tpu_custom_call" | custom-call | bytes 19660800 | tf_op jit(solution)/shard_map/join/pallas_call | solution.py:362
  255.5 10.6 %feed.1 = (f32[256,1280]{1,0:T(8,128)}, bf16[256,1280]{1,0:T(8,128)(2,1)}, bf16[256,1280]{1,0:T(8,128)(2,1)}, bf16[256,1280]{1,0:T(8,128)(2,1)}, f32[256,1280]{1...) custom-call(f32[256,1280]{1,0:T(8,128)} %bitcast.293, ...), custom_call_target="tpu_custom_call" | custom-call | flops 3355443200 | bytes 11156480 | tf_op jit(solution)/shard_map/feed/pallas_call | solution.py:280
  274.0 7.5 %split.3 = (bf16[4,4,15,80,128]{4,3,2,1,0:T(8,128)(2,1)}, bf16[4,4,15,80,128]{4,3,2,1,0:T(8,128)(2,1)}) custom-call(s32[1]{0:T(128)} %bitcast.2.core_ref, bf16[1280,1280]{1,0:T(8,128)(2,1)S(1)} %convolution_convert_fusion.2.refs_0_, bf16[1280,1280]{1,0:T(8,128)(2,1)} %convolution_convert_fusion.1.refs_1_, bf16[1280,1280]{1,0:T(8,128)(2,1)} %convolution_convert_fusion.refs_2_), custom_call_target="tpu_custom_call" | custom-call | bytes 19660800 | tf_op jit(solution)/shard_map/split/pallas_call | solution.py:385
  294.3 7.5 %add_convert_fusion = bf16[4,4,15,80,128]{4,3,2,1,0:T(8,128)(2,1)} fusion(bf16[4,4,15,80,128]{4,3,2,1,0:T(8,128)(2,1)} %collective-permute-done.17, bf16[4,4,15,80,128]{4,3,2,1,0:T(8,128)(2,1)} %get-tuple-element.131), kind=kLoop, calls=%fused_computation.4 | loop fusion | flops 9830400 | bytes 14745600 | tf_op jit(solution)/shard_map/convert_element_type | solution.py:300
  301.7 13.5 %all-gather.9.cloned.1.call-done.grad_ref = bf16[4,4,64,640]{3,2,1,0:T(8,128)(2,1)} async-done(((bf16[1,4,64,640]{3,2,1,0:T(8,128)(2,1)}), bf16[4,4,64,640]{3,2,1,0:T(8,128)(2,1)}) %all-gather.9.cloned.1.call-update) | async-done | bytes 1310736 | tf_op jit(solution)/shard_map/all_gather | solution.py:711
  316.5 9.8 %attend_back.2 = (bf16[4,4,64,640]{3,2,1,0:T(8,128)(2,1)S(1)}, bf16[4,512,640]{2,1,0:T(8,128)(2,1)}, bf16[4,512,640]{2,1,0:T(8,128)(2,1)}) custom-call(s32[1]{0:T(128)} %bitcast.48.place_ref, bf16[4,4,64,1280]{3,2,1,0:T(8,128)(2,1)} %bitcast.282, bf16[4,512,1280]{2,1,0:T(8,128)(2,1)} %bitcast.287, bf16[4,512,1280]{2,1,0:T(8,128)(2,1)} %bitcast.291, ...), custom_call_target="tpu_custom_call" | custom-call | flops 5368709120 | bytes 14495748 | tf_op jit(solution)/shard_map/attend_back/pallas_call | solution.py:262
  339.0 14.9 %collective-permute-done.21 = bf16[4,64,640]{2,1,0:T(8,128)(2,1)} collective-permute-done((bf16[4,64,640]{2,1,0:T(8,128)(2,1)S(1)}, bf16[4,64,640]{2,1,0:T(8,128)(2,1)}, u32[]{:S(2)}, u32[]{:S(2)}) %collective-permute-start.21) | collective-permute-done | bytes 327712 | tf_op jit(solution)/shard_map/ppermute | solution.py:437
  365.2 9.7 %attend_back.3 = (bf16[4,4,64,640]{3,2,1,0:T(8,128)(2,1)S(1)}, bf16[4,512,640]{2,1,0:T(8,128)(2,1)}, bf16[4,512,640]{2,1,0:T(8,128)(2,1)}) custom-call(s32[1]{0:T(128)} %bitcast.48.place_ref, bf16[4,4,64,1280]{3,2,1,0:T(8,128)(2,1)} %bitcast.283, bf16[4,512,1280]{2,1,0:T(8,128)(2,1)} %bitcast.288, bf16[4,512,1280]{2,1,0:T(8,128)(2,1)} %bitcast.292, ...), custom_call_target="tpu_custom_call" | custom-call | flops 5368709120 | bytes 14495748 | tf_op jit(solution)/shard_map/attend_back/pallas_call | solution.py:262
  375.0 5.6 %collective-permute-done.25 = bf16[2,2,5,80,128]{4,3,2,1,0:T(8,128)(2,1)} collective-permute-done((bf16[2,2,5,80,128]{4,3,2,1,0:T(8,128)(2,1)}, bf16[2,2,5,80,128]{4,3,2,1,0:T(8,128)(2,1)}, u32[]{:S(2)}, u32[]{:S(2)}) %collective-permute-start.25) | collective-permute-done | bytes 409632 | tf_op jit(solution)/shard_map/ppermute | solution.py:434
  399.6 11.6 %collective-permute-done.26 = bf16[4,64,640]{2,1,0:T(8,128)(2,1)S(1)} collective-permute-done((bf16[4,64,640]{2,1,0:T(8,128)(2,1)S(1)}, bf16[4,64,640]{2,1,0:T(8,128)(2,1)S(1)}, u32[]{:S(2)}, u32[]{:S(2)}) %collective-permute-start.26) | collective-permute-done | bytes 327712 | tf_op jit(solution)/shard_map/ppermute | solution.py:437
  423.6 17.0 %byte_back.1 = (f32[2048,768]{1,0:T(8,128)}, f32[1,768]{1,0:T(1,128)}) custom-call(f32[2048,768]{1,0:T(8,128)} %bitcast.295, f32[1,768]{1,0:T(1,128)} %broadcast_in_dim.79.gain_ref, bf16[1280,768]{1,0:T(8,128)(2,1)} %copy-done.11, bf16[1280,768]{1,0:T(8,128)(2,1)} %copy-done.12, bf16[2048,640]{1,0:T(8,128)(2,1)} %bitcast.357, bf16[2048,640]{1,0:T(8,128)(2,1)} %bitcast.361, ...), custom_call_target="tpu_custom_call" | custom-call | flops 8053063680 | bytes 20712448 | tf_op jit(solution)/shard_map/byte_back/pallas_call | solution.py:280
  462.1 7.5 %collective-permute-done.45 = bf16[11,80,128]{2,1,0:T(8,128)(2,1)} collective-permute-done((bf16[11,80,128]{2,1,0:T(8,128)(2,1)}, bf16[11,80,128]{2,1,0:T(8,128)(2,1)}, u32[]{:S(2)}, u32[]{:S(2)}) %collective-permute-start.45) | collective-permute-done | bytes 225312 | tf_op jit(solution)/shard_map/ppermute | solution.py:437
  469.5 19.8 %collective-permute-done.46 = bf16[11,80,128]{2,1,0:T(8,128)(2,1)} collective-permute-done((bf16[11,80,128]{2,1,0:T(8,128)(2,1)}, bf16[11,80,128]{2,1,0:T(8,128)(2,1)}, u32[]{:S(2)}, u32[]{:S(2)}) %collective-permute-start.46) | collective-permute-done | bytes 225312 | tf_op jit(solution)/shard_map/ppermute | solution.py:437
  513.4 6.9 %collective-permute-done.40 = bf16[16,80,128]{2,1,0:T(8,128)(2,1)} collective-permute-done((bf16[16,80,128]{2,1,0:T(8,128)(2,1)S(1)}, bf16[16,80,128]{2,1,0:T(8,128)(2,1)}, u32[]{:S(2)}, u32[]{:S(2)}) %collective-permute-start.40) | collective-permute-done | bytes 327712 | tf_op jit(solution)/shard_map/ppermute | solution.py:434
  (382 shorter events, 202.8 us)
Async XLA Ops:
  8.1 89.7 %all-gather.15.cloned.1.call-start = ((), (), s32[]{:S(2)}) async-start(), calls=%async_computation.4 | async-start | bytes 4505600 | tf_op jit(solution)/shard_map/all_gather | solution.py:482
  11.0 36.9 %collective-permute-start.3 = (bf16[4,64,1280]{2,1,0:T(8,128)(2,1)S(1)}, bf16[4,64,1280]{2,1,0:T(8,128)(2,1)S(1)}, u32[]{:S(2)}, u32[]{:S(2)}) collective-permute-start(bf16[4,64,1280]{2,1,0:T(8,128)(2,1)S(1)} %multiply_convert_fusion.1), channel_id=1, source_target_pairs={{0,1},{1,2},{2,3},{3,0},{4,5},{5,6},{6,7},{7,4},{8,9},{9,10},{10,1... | collective-permute-start | bytes 1966088 | tf_op jit(solution)/shard_map/ppermute | solution.py:437
  13.3 18.1 %collective-permute-start = (bf16[11,80,128]{2,1,0:T(8,128)(2,1)S(1)}, bf16[11,80,128]{2,1,0:T(8,128)(2,1)S(1)}, u32[]{:S(2)}, u32[]{:S(2)}) collective-permute-start(bf16[11,80,128]{2,1,0:T(8,128)(2,1)S(1)} %pad_maximum_fusion.13), channel_id=1, source_target_pairs={{0,1},{1,2},{2,3},{3,0},{4,5},{5,6},{6,7},{7,4},{8,9},{9,10},{10,1... | collective-permute-start | bytes 675848 | tf_op jit(solution)/shard_map/ppermute | solution.py:437
  14.7 30.4 %collective-permute-start.1 = (bf16[11,80,128]{2,1,0:T(8,128)(2,1)S(1)}, bf16[11,80,128]{2,1,0:T(8,128)(2,1)S(1)}, u32[]{:S(2)}, u32[]{:S(2)}) collective-permute-start(bf16[11,80,128]{2,1,0:T(8,128)(2,1)S(1)} %pad_maximum_fusion.13), channel_id=1, source_target_pairs={{0,2},{1,3},{2,0},{3,1},{4,6},{5,7},{6,4},{7,5},{8,10},{9,11},{10,... | collective-permute-start | bytes 675848 | tf_op jit(solution)/shard_map/ppermute | solution.py:437
  15.6 32.2 %collective-permute-start.2 = (bf16[11,80,128]{2,1,0:T(8,128)(2,1)S(1)}, bf16[11,80,128]{2,1,0:T(8,128)(2,1)S(1)}, u32[]{:S(2)}, u32[]{:S(2)}) collective-permute-start(bf16[11,80,128]{2,1,0:T(8,128)(2,1)S(1)} %pad_maximum_fusion.13), channel_id=1, source_target_pairs={{0,3},{1,0},{2,1},{3,2},{4,7},{5,4},{6,5},{7,6},{8,11},{9,8},{10,9... | collective-permute-start | bytes 675848 | tf_op jit(solution)/shard_map/ppermute | solution.py:437
  49.8 86.1 %all-gather.13.cloned.1.call-start = ((), (), s32[]{:S(2)}) async-start(), calls=%async_computation.3 | async-start | bytes 1638400 | tf_op jit(solution)/shard_map/all_gather | solution.py:618
  49.9 16.0 %collective-permute-start.4 = (bf16[4,64,1280]{2,1,0:T(8,128)(2,1)S(1)}, bf16[4,64,1280]{2,1,0:T(8,128)(2,1)S(1)}, u32[]{:S(2)}, u32[]{:S(2)}) collective-permute-start(bf16[4,64,1280]{2,1,0:T(8,128)(2,1)S(1)} %collective-permute-done.3), channel_id=1, source_target_pairs={{0,1},{1,2},{2,3},{3,0},{4,5},{5,6},{6,7},{7,4},{8,9},{9,10},{10,1... | collective-permute-start | bytes 1966088 | tf_op jit(solution)/shard_map/ppermute | solution.py:437
  65.9 15.1 %collective-permute-start.5 = (bf16[4,64,1280]{2,1,0:T(8,128)(2,1)S(1)}, bf16[4,64,1280]{2,1,0:T(8,128)(2,1)S(1)}, u32[]{:S(2)}, u32[]{:S(2)}) collective-permute-start(bf16[4,64,1280]{2,1,0:T(8,128)(2,1)S(1)} %collective-permute-done.4), channel_id=1, source_target_pairs={{0,1},{1,2},{2,3},{3,0},{4,5},{5,6},{6,7},{7,4},{8,9},{9,10},{10,1... | collective-permute-start | bytes 1966088 | tf_op jit(solution)/shard_map/ppermute | solution.py:437
  105.5 93.5 %all-gather.17.cloned.1.call-start = ((), (), s32[]{:S(2)}) async-start(), calls=%async_computation.5 | async-start | bytes 6144000 | tf_op jit(solution)/shard_map/all_gather | solution.py:482
  139.2 175.9 %all-gather.9.cloned.1.call-start = ((), (), s32[]{:S(2)}) async-start(), calls=%async_computation.1 | async-start | bytes 1638400 | tf_op jit(solution)/shard_map/all_gather | solution.py:711
  199.0 43.9 %collective-permute-start.11 = (bf16[4,4,15,80,128]{4,3,2,1,0:T(8,128)(2,1)}, bf16[4,4,15,80,128]{4,3,2,1,0:T(8,128)(2,1)}, u32[]{:S(2)}, u32[]{:S(2)}) collective-permute-start(bf16[4,4,15,80,128]{4,3,2,1,0:T(8,128)(2,1)} %bitcast.296), channel_id=1, source_target_pairs={{0,4},{4,0},{8,12},{12,8},{16,20},{20,16},{24,28},{28,24},{1,5},{5... | collective-permute-start | bytes 14745608 | tf_op jit(solution)/shard_map/ppermute | solution.py:434
  283.9 80.0 %all-gather.11.cloned.1.call-start = ((), (), s32[]{:S(2)}) async-start(), calls=%async_computation.2 | async-start | bytes 1638400 | tf_op jit(solution)/shard_map/all_gather | solution.py:711
  289.4 167.7 %reduce-scatter.4.cloned.1.call-start = ((), (), s32[]{:S(2)}) async-start(), calls=%async_computation.6 | async-start | bytes 6144000
  337.0 20.4 %collective-permute-start.22 = (bf16[4,2,11,80,128]{4,3,2,1,0:T(8,128)(2,1)}, bf16[4,2,11,80,128]{4,3,2,1,0:T(8,128)(2,1)}, u32[]{:S(2)}, u32[]{:S(2)}) collective-permute-start(bf16[4,2,11,80,128]{4,3,2,1,0:T(8,128)(2,1)} %get-tuple-element.144), channel_id=1, source_target_pairs={{0,4},{4,0},{8,12},{12,8},{16,20},{20,16},{24,28},{28,24},{1,5},{5... | collective-permute-start | bytes 5406728 | tf_op jit(solution)/shard_map/ppermute | solution.py:434
  338.1 15.8 %collective-permute-start.21 = (bf16[4,64,640]{2,1,0:T(8,128)(2,1)S(1)}, bf16[4,64,640]{2,1,0:T(8,128)(2,1)}, u32[]{:S(2)}, u32[]{:S(2)}) collective-permute-start(bf16[4,64,640]{2,1,0:T(8,128)(2,1)S(1)} %slice_bitcast_fusion.1), channel_id=1, source_target_pairs={{0,1},{1,2},{2,3},{3,0},{4,5},{5,6},{6,7},{7,4},{8,9},{9,10},{10,1... | collective-permute-start | bytes 983048 | tf_op jit(solution)/shard_map/ppermute | solution.py:437
  355.8 30.3 %collective-permute-start.23 = (bf16[4,64,640]{2,1,0:T(8,128)(2,1)}, bf16[4,64,640]{2,1,0:T(8,128)(2,1)S(1)}, u32[]{:S(2)}, u32[]{:S(2)}) collective-permute-start(bf16[4,64,640]{2,1,0:T(8,128)(2,1)} %fusion.16), channel_id=1, source_target_pairs={{0,1},{1,2},{2,3},{3,0},{4,5},{5,6},{6,7},{7,4},{8,9},{9,10},{10,1... | collective-permute-start | bytes 983048 | tf_op jit(solution)/shard_map/ppermute | solution.py:437
  360.4 20.2 %collective-permute-start.25 = (bf16[2,2,5,80,128]{4,3,2,1,0:T(8,128)(2,1)}, bf16[2,2,5,80,128]{4,3,2,1,0:T(8,128)(2,1)}, u32[]{:S(2)}, u32[]{:S(2)}) collective-permute-start(bf16[2,2,5,80,128]{4,3,2,1,0:T(8,128)(2,1)} %dynamic-slice_bitcast_fusion.3), channel_id=1, source_target_pairs={{0,16},{4,20},{8,24},{12,28},{16,0},{20,4},{24,8},{28,12},{1,17},{... | collective-permute-start | bytes 1228808 | tf_op jit(solution)/shard_map/ppermute | solution.py:434
  362.6 22.3 %collective-permute-start.24 = (bf16[2,2,6,80,128]{4,3,2,1,0:T(8,128)(2,1)}, bf16[2,2,6,80,128]{4,3,2,1,0:T(8,128)(2,1)}, u32[]{:S(2)}, u32[]{:S(2)}) collective-permute-start(bf16[2,2,6,80,128]{4,3,2,1,0:T(8,128)(2,1)} %dynamic-slice_bitcast_fusion.1), channel_id=1, source_target_pairs={{0,8},{4,12},{8,0},{12,4},{16,24},{20,28},{24,16},{28,20},{1,9},{5... | collective-permute-start | bytes 1474568 | tf_op jit(solution)/shard_map/ppermute | solution.py:434
  396.4 15.6 %collective-permute-start.27 = (bf16[4,64,640]{2,1,0:T(8,128)(2,1)S(1)}, bf16[4,64,640]{2,1,0:T(8,128)(2,1)S(1)}, u32[]{:S(2)}, u32[]{:S(2)}) collective-permute-start(bf16[4,64,640]{2,1,0:T(8,128)(2,1)S(1)} %slice_bitcast_fusion), channel_id=1, source_target_pairs={{0,1},{1,2},{2,3},{3,0},{4,5},{5,6},{6,7},{7,4},{8,9},{9,10},{10,1... | collective-permute-start | bytes 983048 | tf_op jit(solution)/shard_map/ppermute | solution.py:437
  417.5 24.2 %collective-permute-start.30 = (bf16[4,64,640]{2,1,0:T(8,128)(2,1)S(1)}, bf16[4,64,640]{2,1,0:T(8,128)(2,1)S(1)}, u32[]{:S(2)}, u32[]{:S(2)}) collective-permute-start(bf16[4,64,640]{2,1,0:T(8,128)(2,1)S(1)} %fusion.13), channel_id=1, source_target_pairs={{0,1},{1,2},{2,3},{3,0},{4,5},{5,6},{6,7},{7,4},{8,9},{9,10},{10,1... | collective-permute-start | bytes 983048 | tf_op jit(solution)/shard_map/ppermute | solution.py:437
  422.0 19.4 %collective-permute-start.33 = (bf16[2,2,5,80,128]{4,3,2,1,0:T(8,128)(2,1)S(1)}, bf16[2,2,5,80,128]{4,3,2,1,0:T(8,128)(2,1)S(1)}, u32[]{:S(2)}, u32[]{:S(2)}) collective-permute-start(bf16[2,2,5,80,128]{4,3,2,1,0:T(8,128)(2,1)S(1)} %dynamic-slice_bitcast_fusion.2), channel_id=1, source_target_pairs={{0,16},{4,20},{8,24},{12,28},{16,0},{20,4},{24,8},{28,12},{1,17},{... | collective-permute-start | bytes 1228808 | tf_op jit(solution)/shard_map/ppermute | solution.py:434
  422.4 19.1 %collective-permute-start.32 = (bf16[2,2,6,80,128]{4,3,2,1,0:T(8,128)(2,1)S(1)}, bf16[2,2,6,80,128]{4,3,2,1,0:T(8,128)(2,1)S(1)}, u32[]{:S(2)}, u32[]{:S(2)}) collective-permute-start(bf16[2,2,6,80,128]{4,3,2,1,0:T(8,128)(2,1)S(1)} %dynamic-slice_bitcast_fusion), channel_id=1, source_target_pairs={{0,8},{4,12},{8,0},{12,4},{16,24},{20,28},{24,16},{28,20},{1,9},{5... | collective-permute-start | bytes 1474568 | tf_op jit(solution)/shard_map/ppermute | solution.py:434
  450.8 18.8 %collective-permute-start.45 = (bf16[11,80,128]{2,1,0:T(8,128)(2,1)}, bf16[11,80,128]{2,1,0:T(8,128)(2,1)}, u32[]{:S(2)}, u32[]{:S(2)}) collective-permute-start(bf16[11,80,128]{2,1,0:T(8,128)(2,1)} %get-tuple-element.191), channel_id=1, source_target_pairs={{0,2},{1,3},{2,0},{3,1},{4,6},{5,7},{6,4},{7,5},{8,10},{9,11},{10,... | collective-permute-start | bytes 675848 | tf_op jit(solution)/shard_map/ppermute | solution.py:437
  453.7 35.6 %collective-permute-start.46 = (bf16[11,80,128]{2,1,0:T(8,128)(2,1)}, bf16[11,80,128]{2,1,0:T(8,128)(2,1)}, u32[]{:S(2)}, u32[]{:S(2)}) collective-permute-start(bf16[11,80,128]{2,1,0:T(8,128)(2,1)} %get-tuple-element.190), channel_id=1, source_target_pairs={{0,3},{1,0},{2,1},{3,2},{4,7},{5,4},{6,5},{7,6},{8,11},{9,8},{10,9... | collective-permute-start | bytes 675848 | tf_op jit(solution)/shard_map/ppermute | solution.py:437
  458.6 33.5 %collective-permute-start.36 = (bf16[16,80,128]{2,1,0:T(8,128)(2,1)S(1)}, bf16[16,80,128]{2,1,0:T(8,128)(2,1)S(1)}, u32[]{:S(2)}, u32[]{:S(2)}) collective-permute-start(bf16[16,80,128]{2,1,0:T(8,128)(2,1)S(1)} %get-tuple-element.201), channel_id=1, source_target_pairs={{0,1},{1,2},{2,3},{3,0},{4,5},{5,6},{6,7},{7,4},{8,9},{9,10},{10,1... | collective-permute-start | bytes 983048 | tf_op jit(solution)/shard_map/ppermute | solution.py:437
  460.1 37.6 %collective-permute-start.37 = (bf16[16,80,128]{2,1,0:T(8,128)(2,1)S(1)}, bf16[16,80,128]{2,1,0:T(8,128)(2,1)S(1)}, u32[]{:S(2)}, u32[]{:S(2)}) collective-permute-start(bf16[16,80,128]{2,1,0:T(8,128)(2,1)S(1)} %get-tuple-element.202), channel_id=1, source_target_pairs={{0,2},{1,3},{2,0},{3,1},{4,6},{5,7},{6,4},{7,5},{8,10},{9,11},{10,... | collective-permute-start | bytes 983048 | tf_op jit(solution)/shard_map/ppermute | solution.py:437
  462.0 41.2 %collective-permute-start.38 = (bf16[16,80,128]{2,1,0:T(8,128)(2,1)S(1)}, bf16[16,80,128]{2,1,0:T(8,128)(2,1)S(1)}, u32[]{:S(2)}, u32[]{:S(2)}) collective-permute-start(bf16[16,80,128]{2,1,0:T(8,128)(2,1)S(1)} %get-tuple-element.203), channel_id=1, source_target_pairs={{0,3},{1,0},{2,1},{3,2},{4,7},{5,4},{6,5},{7,6},{8,11},{9,8},{10,9... | collective-permute-start | bytes 983048 | tf_op jit(solution)/shard_map/ppermute | solution.py:437
  490.5 14.5 %collective-permute-start.47 = (bf16[11,80,128]{2,1,0:T(8,128)(2,1)S(1)}, bf16[11,80,128]{2,1,0:T(8,128)(2,1)S(1)}, u32[]{:S(2)}, u32[]{:S(2)}) collective-permute-start(bf16[11,80,128]{2,1,0:T(8,128)(2,1)S(1)} %fusion.27), channel_id=1, source_target_pairs={{0,8},{4,12},{8,0},{12,4},{16,24},{20,28},{24,16},{28,20},{1,9},{5... | collective-permute-start | bytes 675848 | tf_op jit(solution)/shard_map/ppermute | solution.py:434
  491.8 14.4 %collective-permute-start.48 = (bf16[11,80,128]{2,1,0:T(8,128)(2,1)S(1)}, bf16[11,80,128]{2,1,0:T(8,128)(2,1)S(1)}, u32[]{:S(2)}, u32[]{:S(2)}) collective-permute-start(bf16[11,80,128]{2,1,0:T(8,128)(2,1)S(1)} %fusion.27), channel_id=1, source_target_pairs={{0,16},{4,20},{8,24},{12,28},{16,0},{20,4},{24,8},{28,12},{1,17},{... | collective-permute-start | bytes 675848 | tf_op jit(solution)/shard_map/ppermute | solution.py:434
  504.7 15.6 %collective-permute-start.40 = (bf16[16,80,128]{2,1,0:T(8,128)(2,1)S(1)}, bf16[16,80,128]{2,1,0:T(8,128)(2,1)}, u32[]{:S(2)}, u32[]{:S(2)}) collective-permute-start(bf16[16,80,128]{2,1,0:T(8,128)(2,1)S(1)} %add_convert_fusion.3), channel_id=1, source_target_pairs={{0,16},{4,20},{8,24},{12,28},{16,0},{20,4},{24,8},{28,12},{1,17},{... | collective-permute-start | bytes 983048 | tf_op jit(solution)/shard_map/ppermute | solution.py:434
  505.0 16.3 %collective-permute-start.41 = (bf16[16,80,128]{2,1,0:T(8,128)(2,1)S(1)}, bf16[16,80,128]{2,1,0:T(8,128)(2,1)}, u32[]{:S(2)}, u32[]{:S(2)}) collective-permute-start(bf16[16,80,128]{2,1,0:T(8,128)(2,1)S(1)} %add_convert_fusion.3), channel_id=1, source_target_pairs={{0,24},{4,28},{8,16},{12,20},{16,8},{20,12},{24,0},{28,4},{1,25},{... | collective-permute-start | bytes 983048 | tf_op jit(solution)/shard_map/ppermute | solution.py:434
  507.2 25.3 %collective-permute-start.50 = (bf16[4,1,11,80,128]{4,3,2,1,0:T(8,128)(2,1)S(1)}, bf16[4,1,11,80,128]{4,3,2,1,0:T(8,128)(2,1)S(1)}, u32[]{:S(2)}, u32[]{:S(2)}) collective-permute-start(bf16[4,1,11,80,128]{4,3,2,1,0:T(8,128)(2,1)S(1)} %select_bitcast_fusion.mine_ref), channel_id=1, source_target_pairs={{0,4},{4,0},{8,12},{12,8},{16,20},{20,16},{24,28},{28,24},{1,5},{5... | collective-permute-start | bytes 2703368 | tf_op jit(solution)/shard_map/ppermute | solution.py:434
  (89 other events, 980.9 us)
Sparse Core Ops, SparseCore 0:
  49.9 47.7 all-gather.14
  139.4 59.5 all-gather.16
  339.1 70.0 reduce-scatter.3
Sparse Core Ops, SparseCore 1:
  105.6 30.3 all-gather.12
  283.9 31.2 all-gather.8
  316.6 36.9 all-gather.10

commit v4 on v3

v4 whole, which is shorter than its diff:
```python
import functools

import jax
import jax.numpy as jnp
from jax import lax
from jax.experimental import pallas as pl
from jax.experimental.pallas import tpu as pltpu
from jax.sharding import PartitionSpec as P

HEAD_DIM = 160
EPS = 1e-05
NEG = -1e30
LANES = 128
F32 = jnp.float32
BF16 = jnp.bfloat16
NN = (((1,), (0,)), ((), ()))
NT = (((1,), (1,)), ((), ()))
TN = (((0,), (0,)), ((), ()))


def dot(a, b, dims=NN):
    return lax.dot_general(a, b, dims, preferred_element_type=F32)


def normalize(field):
    average = jnp.mean(field, -1, keepdims=True)
    centred = field - average
    inv_scale = lax.rsqrt(jnp.mean(centred * centred, -1, keepdims=True) + EPS)
    return (centred * inv_scale, inv_scale)


def norm_back(grad_out, normed, inv_scale, scale_vec):
    weighted = grad_out * scale_vec
    centred_grad = (
        weighted
        - jnp.mean(weighted, -1, keepdims=True)
        - normed * jnp.mean(weighted * normed, -1, keepdims=True)
    )
    return (inv_scale * centred_grad, jnp.sum(grad_out * normed, axis=0))


def gelu_exact(field):
    return jax.nn.gelu(field, approximate=False)


def windows(columns):
    out = []
    for head in range(columns // HEAD_DIM):
        start = head * HEAD_DIM
        base = start // LANES * LANES
        assert start + HEAD_DIM <= base + 2 * LANES
        out.append((base, start - base, start - base + HEAD_DIM))
    return out


def lines_of(ref, base):
    return ref[:, 0, :, base : base + 2 * LANES].reshape(-1, 2 * LANES)


def own_columns(shape, low, high):
    lane = lax.broadcasted_iota(jnp.int32, shape, 1)
    return (lane >= low) & (lane < high)


def byte_norm_kernel(byte_ref, gain_ref, out_ref):
    out_ref[...] = (normalize(byte_ref[...])[0] * gain_ref[...]).astype(BF16)


def byte_back_kernel(
    byte_ref,
    gain_ref,
    key_ref,
    value_ref,
    grad_key_ref,
    grad_value_ref,
    grad_ref,
    gain_grad_ref,
):
    grad = dot(grad_key_ref[...], key_ref[...]) + dot(grad_value_ref[...], value_ref[...])
    normed, inv_scale = normalize(byte_ref[...])
    grad_ref[...], gain_grad = norm_back(grad, normed, inv_scale, gain_ref[...])

    @pl.when(pl.program_id(0) == 0)
    def _():
        gain_grad_ref[...] = jnp.zeros_like(gain_grad_ref)

    gain_grad_ref[...] += gain_grad


def feed_kernel(
    latents_ref,
    cotangent_ref,
    gain_ref,
    b_out_ref,
    b_up_ref,
    b_down_ref,
    out_ref,
    up_ref,
    down_ref,
    attended_ref,
    result_ref,
    mid_norm_ref,
    activated_ref,
    grad_pre_ref,
    grad_hidden_ref,
    grad_attn_ref,
    grad_att_ref,
    delta_ref,
    sums_ref,
    hidden_ref,
):
    hidden_ref[...] = latents_ref[...] + dot(attended_ref[...], out_ref[...]) + b_out_ref[...]
    mid_hat, mid_inv = normalize(hidden_ref[...])
    mid_norm_ref[...] = (mid_hat * gain_ref[...]).astype(BF16)
    pre_act = dot(mid_norm_ref[...], up_ref[...], NT) + b_up_ref[...]
    below = 0.5 * (1.0 + lax.erf(pre_act * 0.5**0.5))
    activated_ref[...] = (pre_act * below).astype(BF16)
    slope = below + pre_act * (jnp.exp(-0.5 * pre_act * pre_act) * (2.0 * jnp.pi) ** -0.5)
    grad_act = dot(cotangent_ref[...].astype(BF16), down_ref[...], NT)
    grad_pre_ref[...] = (grad_act * slope).astype(BF16)
    sums_ref[1:2, :] = jnp.sum(grad_pre_ref[...].astype(F32), axis=0, keepdims=True)
    grad_mid = dot(grad_pre_ref[...], up_ref[...])
    mid_hat, mid_inv = normalize(hidden_ref[...])
    back, gain_grad = norm_back(grad_mid, mid_hat, mid_inv, gain_ref[...])
    sums_ref[0:1, :] = gain_grad[None]
    grad_hidden_ref[...] = cotangent_ref[...] + back
    sums_ref[2:3, :] = jnp.sum(grad_hidden_ref[...], axis=0, keepdims=True)
    sums_ref[3:4, :] = jnp.sum(cotangent_ref[...], axis=0, keepdims=True)
    grad_attn_ref[...] = grad_hidden_ref[...].astype(BF16)
    grad_att_ref[...] = dot(grad_attn_ref[...], out_ref[...], NT).astype(BF16)
    for head, (base, low, high) in enumerate(windows(attended_ref.shape[1])):
        product = attended_ref[:, base : base + 2 * LANES].astype(F32) * grad_att_ref[
            :, base : base + 2 * LANES
        ].astype(F32)
        product = jnp.where(own_columns(product.shape, low, high), product, 0.0)
        delta_ref[:, head : head + 1] = jnp.sum(product, 1, keepdims=True)
    result_ref[...] = hidden_ref[...] + dot(activated_ref[...], down_ref[...]) + b_down_ref[...]


def lse_kernel(query_ref, key_ref, lat_seg_ref, byte_seg_ref, lse_ref):
    allowed = byte_seg_ref[0] == lat_seg_ref[0]
    for head, (base, low, high) in enumerate(windows(query_ref.shape[3])):
        query = lines_of(query_ref, base)
        query = jnp.where(own_columns(query.shape, low, high), query, 0)
        key = key_ref[0, :, base : base + 2 * LANES]
        scores = jnp.where(allowed, dot(key, query, NT), NEG)
        peak = jnp.max(scores, 0, keepdims=True)
        total = jnp.sum(jnp.exp(scores - peak), 0, keepdims=True)
        lse_ref[0, head : head + 1, :] = peak + jnp.log(total)


class Tiles:
    def __init__(self, ref):
        self.ref = ref
        self.held = {}

    def add(self, base, window):
        for part in range(2):
            tile = base + part * LANES
            piece = window[:, part * LANES : (part + 1) * LANES]
            self.held[tile] = self.held[tile] + piece if tile in self.held else piece
        for tile in [t for t in self.held if t < base]:
            self.store(tile)

    def store(self, tile):
        done = self.held.pop(tile).astype(self.ref.dtype)
        if len(self.ref.shape) == 4:
            self.ref[:, 0, :, tile : tile + LANES] = done.reshape(
                self.ref.shape[0], self.ref.shape[2], LANES
            )
        else:
            self.ref[0, :, tile : tile + LANES] = done

    def finish(self):
        for tile in list(self.held):
            self.store(tile)


def attend_kernel(own_lat, query_ref, key_ref, value_ref, lat_seg_ref, byte_seg_ref, *refs):
    part_refs, (out_ref, lse_ref) = refs[:-2], refs[-2:]
    parts = [part_refs[0][0]]
    for step, ref in enumerate(part_refs[1:], 1):
        parts.append(pltpu.roll(ref[0], step * own_lat, 1))
    peak = functools.reduce(jnp.maximum, parts)
    lse_ref[0] = peak + jnp.log(sum(jnp.exp(part - peak) for part in parts))
    allowed = byte_seg_ref[0] == lat_seg_ref[0]
    tiles = Tiles(out_ref)
    for head, (base, low, high) in enumerate(windows(query_ref.shape[3])):
        query = lines_of(query_ref, base)
        mine = own_columns(query.shape, low, high)
        query = jnp.where(mine, query, 0)
        key = key_ref[0, :, base : base + 2 * LANES]
        value = value_ref[0, :, base : base + 2 * LANES]
        scores = jnp.where(allowed, dot(key, query, NT), NEG)
        probs = jnp.exp(scores - lse_ref[0, head : head + 1, :]).astype(BF16)
        tiles.add(base, jnp.where(mine, dot(probs, value, TN), 0.0))
    tiles.finish()


def attend_back_kernel(
    query_ref,
    key_ref,
    value_ref,
    lat_seg_ref,
    byte_seg_ref,
    lse_ref,
    delta_ref,
    *refs,
):
    grad_refs, (grad_query_ref, grad_key_ref, grad_value_ref) = refs[:-3], refs[-3:]
    allowed = byte_seg_ref[0] == lat_seg_ref[0]
    query_tiles, key_tiles, value_tiles = (
        Tiles(grad_query_ref),
        Tiles(grad_key_ref),
        Tiles(grad_value_ref),
    )
    for head, (base, low, high) in enumerate(windows(query_ref.shape[3])):
        query = lines_of(query_ref, base)
        mine = own_columns(query.shape, low, high)
        query = jnp.where(mine, query, 0)
        grad = jnp.concatenate([ref[0, :, base : base + 2 * LANES] for ref in grad_refs])
        grad = jnp.where(mine, grad, 0)
        key = key_ref[0, :, base : base + 2 * LANES]
        value = value_ref[0, :, base : base + 2 * LANES]
        scores = jnp.where(allowed, dot(key, query, NT), NEG)
        probs = jnp.exp(scores - lse_ref[0, head : head + 1, :])
        grad_probs = dot(value, grad, NT)
        grad_scores = (probs * (grad_probs - delta_ref[0, head : head + 1, :])).astype(BF16)
        value_tiles.add(base, dot(probs.astype(BF16), grad))
        key_tiles.add(base, dot(grad_scores, query))
        query_tiles.add(base, jnp.where(mine, dot(grad_scores, key, TN), 0.0))
    query_tiles.finish()
    key_tiles.finish()
    value_tiles.finish()


def row_call(kernel, name, args, outs, flops):
    def spec(shape):
        if len(shape) == 1:
            return pl.BlockSpec(memory_space=pltpu.SMEM)
        if len(shape) == 4:
            return pl.BlockSpec((shape[0], 1, *shape[2:]), lambda row: (0, row, 0, 0))
        return pl.BlockSpec((1, *shape[1:]), lambda row: (row, 0, 0))

    moved = sum(a.size * a.dtype.itemsize for a in args)
    return pl.pallas_call(
        kernel,
        grid=(outs[-1].shape[0],),
        in_specs=[spec(a.shape) for a in args],
        out_specs=[spec(o.shape) for o in outs],
        out_shape=outs,
        name=name,
        cost_estimate=pl.CostEstimate(flops=flops // 8, bytes_accessed=moved // 8, transcendentals=0),
        compiler_params=pltpu.CompilerParams(vmem_limit_bytes=48 * 1024 * 1024),
    )(*args)


def block_call(kernel, name, lines, args, outs, flops, scratch=()):
    def spec(shape, cut):
        block = (lines if cut else shape[0], shape[1])
        return pl.BlockSpec(block, (lambda i: (i, 0)) if cut else (lambda i: (0, 0)))

    moved = sum(a.size * a.dtype.itemsize for a, _ in args)
    return pl.pallas_call(
        kernel,
        grid=(args[0][0].shape[0] // lines,),
        in_specs=[spec(a.shape, cut) for a, cut in args],
        out_specs=[spec(o.shape, cut) for o, cut in outs],
        out_shape=[o for o, _ in outs],
        scratch_shapes=list(scratch),
        name=name,
        cost_estimate=pl.CostEstimate(flops=flops // 8, bytes_accessed=moved // 8, transcendentals=0),
        compiler_params=pltpu.CompilerParams(vmem_limit_bytes=56 * 1024 * 1024),
    )(*[a for a, _ in args])


def ring(size, step=1):
    return [(i, (i + step) % size) for i in range(size)]


def add(first, *others):
    total = first.astype(F32)
    for other in others:
        total = total + other.astype(F32)
    return total.astype(first.dtype)


def panels(widths):
    return [(m, p) for m, width in enumerate(widths) for p in range(width // (2 * LANES))]


def join_kernel(widths, core_ref, mine_ref, other_ref, *out_refs):
    chips, part = mine_ref.shape[0], mine_ref.shape[3]

    def copy(sides):
        for number, (m, p) in enumerate(panels(widths)):
            for side, ref in enumerate(sides):
                at = side * widths[m] // 2 + p * LANES
                for chip in range(chips):
                    out_refs[m][chip * part : (chip + 1) * part, at : at + LANES] = ref[
                        chip, 0, number
                    ]

    @pl.when(core_ref[0] == 0)
    def _():
        copy((mine_ref, other_ref))

    @pl.when(core_ref[0] == 1)
    def _():
        copy((other_ref, mine_ref))


def join_own_kernel(widths, where_ref, *refs):
    count = len(widths)
    own_refs, (mine_ref, other_ref), out_refs = refs[:count], refs[count : count + 2], refs[count + 2 :]
    first = pl.program_id(0) == 0

    @pl.when(first)
    def _():
        for own_ref, out_ref in zip(own_refs, out_refs):
            out_ref[...] = own_ref[...]

    @pl.when(jnp.logical_not(first))
    def _():
        join_kernel(widths, where_ref, mine_ref, other_ref, *out_refs)


def grads_kernel(widths, core_ref, *refs):
    count = len(widths)
    (kept_ref, sent_ref), work_refs = refs[2 * count : 2 * count + 2], refs[2 * count + 2 :]
    chips, blocks, _, part, _ = kept_ref.shape
    for m in range(count):
        work_refs[m][...] = dot(refs[m][...], refs[count + m][...], TN).astype(BF16)

    def copy(sides):
        for number, (m, p) in enumerate(panels(widths)):
            for side, ref in enumerate(sides):
                at = side * widths[m] // 2 + p * LANES
                for block in range(blocks):
                    for chip in range(chips):
                        start = (block * chips + chip) * part
                        ref[chip, block, number] = work_refs[m][
                            start : start + part, at : at + LANES
                        ]

    @pl.when(core_ref[0] == 0)
    def _():
        copy((kept_ref, sent_ref))

    @pl.when(core_ref[0] == 1)
    def _():
        copy((sent_ref, kept_ref))


def add_kernel(a_ref, b_ref, out_ref):
    out_ref[...] = (a_ref[...].astype(F32) + b_ref[...].astype(F32)).astype(out_ref.dtype)


def split_kernel(widths, core_ref, *refs):
    in_refs, (kept_ref, sent_ref) = refs[:-2], refs[-2:]
    chips, _, _, part, _ = kept_ref.shape

    def copy(sides):
        for number, (m, p) in enumerate(panels(widths)):
            for side, ref in enumerate(sides):
                at = side * widths[m] // 2 + p * LANES
                for chip in range(chips):
                    ref[chip, 0, number] = in_refs[m][
                        chip * part : (chip + 1) * part, at : at + LANES
                    ]

    @pl.when(core_ref[0] == 0)
    def _():
        copy((kept_ref, sent_ref))

    @pl.when(core_ref[0] == 1)
    def _():
        copy((sent_ref, kept_ref))


def packed_spec(shape):
    chips, _, count, part, lanes = shape
    return pl.BlockSpec((chips, 1, count, part, lanes), lambda z: (0, z, 0, 0, 0))


def matrix_spec(lines, width):
    return pl.BlockSpec((lines, width), lambda z: (z, 0))


def join(core, mine, other, widths):
    chips, blocks, _, part, _ = mine.shape
    lines = chips * part
    return pl.pallas_call(
        functools.partial(join_kernel, widths),
        grid=(blocks,),
        in_specs=[
            pl.BlockSpec(memory_space=pltpu.SMEM),
            packed_spec(mine.shape),
            packed_spec(mine.shape),
        ],
        out_specs=[matrix_spec(lines, width) for width in widths],
        out_shape=[jax.ShapeDtypeStruct((blocks * lines, width), mine.dtype) for width in widths],
        name="join",
        cost_estimate=pl.CostEstimate(
            flops=0, bytes_accessed=mine.size, transcendentals=0
        ),
        compiler_params=pltpu.CompilerParams(vmem_limit_bytes=48 * 1024 * 1024),
    )(core, mine, other)


def join_own(where, own, mine, other, widths, total):
    chips, blocks, count, part, _ = mine.shape
    lines = chips * part

    def packed(r, where_ref):
        return (0, jnp.maximum(r, 1) - 1, 0, 0, 0)

    return pl.pallas_call(
        functools.partial(join_own_kernel, widths),
        grid_spec=pltpu.PrefetchScalarGridSpec(
            num_scalar_prefetch=1,
            grid=(blocks + 1,),
            in_specs=[pl.BlockSpec((lines, width), lambda r, where_ref: (0, 0)) for width in widths]
            + [pl.BlockSpec((chips, 1, count, part, LANES), packed)] * 2,
            out_specs=[
                pl.BlockSpec(
                    (lines, width),
                    lambda r, where_ref: (lax.rem(where_ref[1] + (total - r), total), 0),
                )
                for width in widths
            ],
        ),
        out_shape=[jax.ShapeDtypeStruct((total * lines, width), mine.dtype) for width in widths],
        name="join_own",
        cost_estimate=pl.CostEstimate(flops=0, bytes_accessed=mine.size, transcendentals=0),
        compiler_params=pltpu.CompilerParams(vmem_limit_bytes=48 * 1024 * 1024),
    )(where, *own, mine, other)


def split(core, matrices, chips, lines):
    widths = [m.shape[1] for m in matrices]
    blocks = matrices[0].shape[0] // lines
    shape = (chips, blocks, len(panels(widths)), lines // chips, LANES)
    packed = jax.ShapeDtypeStruct(shape, BF16)
    return pl.pallas_call(
        functools.partial(split_kernel, widths),
        grid=(blocks,),
        in_specs=[pl.BlockSpec(memory_space=pltpu.SMEM)]
        + [matrix_spec(lines, width) for width in widths],
        out_specs=[packed_spec(shape)] * 2,
        out_shape=[packed] * 2,
        name="split",
        cost_estimate=pl.CostEstimate(
            flops=0, bytes_accessed=sum(m.size for m in matrices) // 2, transcendentals=0
        ),
        compiler_params=pltpu.CompilerParams(vmem_limit_bytes=48 * 1024 * 1024),
    )(core, *matrices)


def add_packed(a, b):
    return pl.pallas_call(
        add_kernel,
        grid=(a.shape[1],),
        in_specs=[packed_spec(a.shape)] * 2,
        out_specs=packed_spec(a.shape),
        out_shape=jax.ShapeDtypeStruct(a.shape, a.dtype),
        name="add_packed",
        cost_estimate=pl.CostEstimate(flops=0, bytes_accessed=a.size // 2, transcendentals=0),
    )(a, b)


def grads(core, pairs, chips, lines, columns):
    widths = [rhs.shape[1] for _, rhs in pairs]
    steps = pairs[0][0].shape[1] // columns
    blocks = columns // lines
    shape = (chips, blocks * steps, len(panels(widths)), lines // chips, LANES)
    packed = jax.ShapeDtypeStruct(shape, BF16)
    block = (chips, blocks) + shape[2:]
    return pl.pallas_call(
        functools.partial(grads_kernel, widths),
        grid=(steps,),
        in_specs=[pl.BlockSpec(memory_space=pltpu.SMEM)]
        + [pl.BlockSpec((lhs.shape[0], columns), lambda i: (0, i)) for lhs, _ in pairs]
        + [pl.BlockSpec(rhs.shape, lambda i: (0, 0)) for _, rhs in pairs],
        out_specs=[pl.BlockSpec(block, lambda i: (0, i, 0, 0, 0))] * 2,
        out_shape=[packed] * 2,
        scratch_shapes=[pltpu.VMEM((columns, width), BF16) for width in widths],
        name="grads",
        cost_estimate=pl.CostEstimate(
            flops=sum(lhs.size * rhs.shape[1] for lhs, rhs in pairs) // 4,
            bytes_accessed=sum(lhs.size + rhs.size for lhs, rhs in pairs) // 4,
            transcendentals=0,
        ),
        compiler_params=pltpu.CompilerParams(vmem_limit_bytes=56 * 1024 * 1024),
    )(core, *[lhs for lhs, _ in pairs], *[rhs for _, rhs in pairs])


def after(x, *earlier):
    return lax.optimization_barrier((x, *earlier))[0]


def three_parts(x, shape):
    parts = []
    for _ in range(3):
        part = lax.reduce_precision(x, 8, 7)
        parts.append(part.astype(BF16))
        x = x - part
    parts = jnp.concatenate(parts)
    size = shape[0] * shape[1]
    return jnp.pad(parts, (0, size - parts.size)).reshape(shape)


def from_three_parts(x, size):
    parts = x.reshape(x.shape[0], -1)[:, : 3 * size].astype(F32).reshape(-1, 3, size)
    return (parts[:, 0] + (parts[:, 1] + parts[:, 2])).reshape(-1)


def pick(x, index, axis):
    return jnp.take(x, index, axis=axis, mode="clip")


class Mesh:
    def __init__(self, dp, mp):
        self.dp, self.mp = dp, mp
        self.dp_index = lax.axis_index("dp")
        self.mp_index = lax.axis_index("mp")
        self.core = self.dp_index % 2

    def cut(self, lines):
        chips = 1
        while 2 * chips <= self.dp // 2 and lines % (32 * chips) == 0:
            chips *= 2
        return chips, [2 * k for k in (1 << b for b in range(8)) if chips <= k < self.dp // 2]

    def swap(self, x, bit):
        return lax.ppermute(x, "dp", [(i, i ^ bit) for i in range(self.dp)])

    def shift(self, x, step):
        return lax.ppermute(x, "mp", ring(self.mp, step))

    def ring_gather(self, x):
        blocks = [x]
        for _ in range(self.mp - 1):
            blocks.append(self.shift(blocks[-1], 1))
        return blocks

    def ring_scatter(self, parts):
        total = parts[1] if self.mp > 1 else parts[0]
        for step in range(2, self.mp + 1):
            total = add(self.shift(total, 1), parts[step % self.mp])
        return total

    def chip_groups(self, chips):
        return [
            [2 * (chip + chips * rest) + core for chip in range(chips)]
            for rest in range(self.dp // 2 // chips)
            for core in range(2)
        ]

    def slice_of(self, shards):
        chips, _ = self.cut(shards[0].shape[0])
        part = shards[0].shape[0] // chips
        chip = self.dp_index // 2 % chips
        return jnp.concatenate(
            [
                lax.dynamic_slice(
                    shard,
                    (chip * part, self.core * (shard.shape[1] // 2)),
                    (part, shard.shape[1] // 2),
                )
                .reshape(part, -1, LANES)
                .transpose(1, 0, 2)
                for shard in shards
            ]
        )

    def gather_chips(self, x, lines):
        chips, _ = self.cut(lines)
        return lax.all_gather(x, "dp", axis=0, axis_index_groups=self.chip_groups(chips))

    def both_cores(self, own, mine):
        where = jnp.stack([self.core, self.mp_index])
        widths = [shard.shape[1] for shard in own]
        return join_own(where, own, mine, self.swap(mine, 1), widths, self.mp)

    def split_core(self, pairs, lines):
        chips, _ = self.cut(lines)
        columns = self.mp * lines // 2
        return grads(self.core[None], pairs, chips, lines, columns)

    def scatter_chips(self, total, lines):
        chips, _ = self.cut(lines)
        return lax.psum_scatter(
            total, "dp", scatter_dimension=0, axis_index_groups=self.chip_groups(chips)
        )

    def link_pieces(self, total, lines):
        chips, _ = self.cut(lines)
        bits = [1 << b for b in range(chips.bit_length() - 1)]
        middle = (total.shape[2] + 1) // 2
        return [
            (piece.reshape((2,) * len(bits) + piece.shape[1:]), order, sorted(bits, reverse=True))
            for order, piece in ((bits, total[:, :, :middle]), (bits[::-1], total[:, :, middle:]))
        ]

    def link_step(self, pieces, *earlier):
        out = []
        for piece, order, left in pieces:
            mine = self.dp_index // (2 * order[0]) % 2
            axis = left.index(order[0])
            if earlier:
                piece = after(piece, *earlier)
            sent = lax.dynamic_index_in_dim(piece, 1 - mine, axis, False)
            kept = lax.dynamic_index_in_dim(piece, mine, axis, False)
            piece = add(kept, self.swap(sent, 2 * order[0]))
            out.append((piece, order[1:], [bit for bit in left if bit != order[0]]))
        return out

    def arrays(self, pieces):
        return [piece for piece, _, _ in pieces]

    def with_arrays(self, pieces, arrays):
        return [(array, *piece[1:]) for array, piece in zip(arrays, pieces)]

    def blocks_back(self, total, lines):
        _, rest = self.cut(lines)
        for bit in rest:
            total = add(total, self.swap(total, bit))
        return [
            lax.dynamic_index_in_dim(total, (self.mp_index + self.mp - r) % self.mp, 0, False)
            for r in range(self.mp)
        ]

    def sum_blocks(self, total, lines, small=None):
        _, rest = self.cut(lines)
        for bit in rest:
            total = add(total, self.swap(total, bit))
        blocks = [
            lax.dynamic_index_in_dim(total, (self.mp_index + step) % self.mp, 0, False)
            for step in range(self.mp)
        ]
        if small is not None:
            panel = small.astype(BF16)
            panel = jnp.pad(panel, (0, total[0, 0].size - panel.size)).reshape(1, -1, LANES)
            blocks = [jnp.concatenate([block, panel]) for block in blocks]
        return add(blocks[0], *[self.shift(blocks[step], step) for step in range(1, self.mp)])

    def finish_sum(self, total, lines, widths, small=0):
        chips, rest = self.cut(lines)
        slices = [total] + [self.swap(total, 2 * k) for k in range(1, chips)]
        if small:
            panel = add(*[piece[-1] for piece in slices])
            for bit in rest:
                panel = add(panel, self.swap(panel, bit))
            slices = [jnp.concatenate([piece[:-1], panel[None]]) for piece in slices]
        chip = self.dp_index // 2 % chips
        mine = pick(jnp.stack(slices), chip ^ jnp.arange(chips), 0)[:, None]
        other = self.swap(mine, 1)
        out = join(self.core[None], mine, other, widths)
        if not small:
            return out
        panel = mine[0, 0, -1].astype(F32) + other[0, 0, -1].astype(F32)
        return out, panel.reshape(-1)[:small]

    def turned(self, x, axis):
        blocks = x.reshape(x.shape[:axis] + (self.mp, -1) + x.shape[axis + 1 :])
        index = (self.mp_index - jnp.arange(self.mp)) % self.mp
        return pick(blocks, index, axis).reshape(x.shape)


def shards(
    dp,
    mp,
    byte_in,
    latents,
    cotangent,
    byte_gain,
    latent_gain,
    mlp_gain,
    w_query,
    w_key,
    w_value,
    w_out,
    b_out,
    w_up,
    b_up,
    w_down,
    b_down,
    byte_seg,
    byte_pad,
    latent_seg,
):
    score_scale = HEAD_DIM ** (-0.5)
    rows, byte_len, byte_width = byte_in.shape
    own_lat, lat_width = latents.shape[1:]
    lat_len = own_lat * mp
    own_lines = rows * own_lat
    heads = w_query.shape[1] * mp // HEAD_DIM
    net = Mesh(dp, mp)
    mp_index = net.mp_index
    shape = jax.ShapeDtypeStruct
    lines = w_query.shape[1]
    head_widths = [lat_width, byte_width, byte_width]
    feed_widths = [lat_width] * 3

    head_own = [w_query.T, w_key.T, w_value.T]
    feed_own = [w_out, w_up.T, w_down]
    head_slice = net.slice_of(head_own)
    head_blocks = [net.shift(head_slice, step) for step in range(1, mp)]
    latents = latents.reshape(own_lines, lat_width)
    cotangent = cotangent.reshape(own_lines, lat_width)
    byte_in = byte_in.reshape(rows * byte_len, byte_width)
    lat_hat, lat_inv = normalize(latents)
    lat_norm = (lat_hat * latent_gain).astype(BF16).reshape(rows, own_lat, lat_width)
    (byte_norm,) = block_call(
        byte_norm_kernel,
        "byte_norm",
        byte_len,
        [(byte_in, True), (byte_gain[None], False)],
        [(shape(byte_in.shape, BF16), True)],
        10 * byte_in.size,
    )
    feed_slice = net.slice_of(feed_own)
    feed_slice = jnp.concatenate([feed_slice, three_parts(b_up, feed_slice.shape[1:])[None]])
    head_blocks, byte_norm, lat_norm, feed_slice = lax.optimization_barrier(
        (head_blocks, byte_norm, lat_norm, feed_slice)
    )
    head_slices = net.gather_chips(jnp.stack(head_blocks), lines)
    lat_blocks = net.ring_gather(lat_norm)
    feed_blocks = [feed_slice, net.shift(after(feed_slice, lat_blocks[-1]), 1)]
    head_slices = after(head_slices, lat_blocks[-1])
    query_t, key_t, value_t = net.both_cores(head_own, head_slices)

    real_seg = jnp.where(byte_pad == 1, byte_seg, -1)
    real_seg = lax.dynamic_slice_in_dim(real_seg, mp_index * byte_len, byte_len, 1)
    byte_col = real_seg[:, :, None]
    lat_row = net.turned(latent_seg, 1)[:, None, :]
    unit = 2 * rows * lat_len * byte_len * heads * 2 * LANES

    key_t, feed_blocks[1] = lax.optimization_barrier((key_t, feed_blocks[1]))
    feed_blocks.append(net.shift(feed_blocks[1], 1))
    keys = dot(byte_norm, key_t, NT).astype(BF16).reshape(rows, byte_len, lat_width)
    lat_all = jnp.stack(lat_blocks)
    lat_flat = after(lat_all.reshape(rows * lat_len, lat_width), keys)
    queries = (dot(lat_flat, query_t, NT) * score_scale).astype(BF16).reshape(lat_all.shape)
    queries, feed_blocks[2] = lax.optimization_barrier((queries, feed_blocks[2]))
    for _ in range(3, mp):
        feed_blocks.append(net.shift(feed_blocks[-1], 1))
    (lse_part,) = row_call(
        lse_kernel,
        "lse",
        [queries, keys, lat_row, byte_col],
        [shape((rows, heads, lat_len), F32)],
        unit,
    )
    lse_part, feed_blocks[-1] = lax.optimization_barrier((lse_part, feed_blocks[-1]))
    lse_parts = [lse_part] + [net.shift(lse_part, step) for step in range(1, mp)]
    feed_slices = net.gather_chips(jnp.stack([block[:-1] for block in feed_blocks[1:]]), lines)
    b_up_all = from_three_parts(jnp.stack([block[-1] for block in feed_blocks]), b_up.shape[0])
    b_up_all = net.turned(b_up_all, 0)
    values = dot(after(byte_norm, lse_part), value_t, NT).astype(BF16)
    values = values.reshape(rows, byte_len, lat_width)
    lat_shape = shape(lat_all.shape, BF16)
    parts, lse = row_call(
        functools.partial(attend_kernel, own_lat),
        "attend",
        [queries, keys, values, lat_row, byte_col] + lse_parts,
        [lat_shape, shape((rows, heads, lat_len), F32)],
        2 * unit,
    )
    attended = parts[1]
    for step in range(2, mp + 1):
        moved = net.shift(attended, 1)
        if step == 2:
            feed_slices = after(feed_slices, moved)
            out_w, up_t, down_w = net.both_cores(feed_own, feed_slices)
        if step == mp - 1:
            moved, out_w = lax.optimization_barrier((moved, out_w))
        attended = add(moved, parts[step % mp])
    attended = attended.reshape(own_lines, lat_width)

    whole = shape((own_lines, lat_width), BF16)
    wide = shape((own_lines, lat_width), F32)
    (
        result,
        mid_norm,
        activated,
        grad_pre,
        grad_hidden,
        grad_attn,
        grad_att,
        delta,
        feed_vectors,
    ) = block_call(
        feed_kernel,
        "feed",
        own_lines,
        [(latents, True), (cotangent, True)]
        + [(v[None], False) for v in (mlp_gain, b_out, b_up_all, b_down)]
        + [(w, False) for w in (out_w, up_t, down_w)]
        + [(attended, True)],
        [(wide, True), (whole, True), (whole, True), (whole, True), (wide, True), (whole, True)]
        + [(whole, True), (shape((own_lines, heads), F32), True)]
        + [(shape((4, lat_width), F32), False)],
        8 * own_lines * lat_width * lat_width,
        [pltpu.VMEM((own_lines, lat_width), F32)],
    )

    grads = [grad_att.reshape(rows, own_lat, lat_width)]
    block = net.shift(grads[0], 1)
    feed_kept, feed_sent = net.split_core(
        [(activated, cotangent.astype(BF16)), (grad_pre, mid_norm), (attended, grad_attn)], lines
    )
    delta = delta.reshape(rows, own_lat, heads).transpose(0, 2, 1)
    delta = jnp.concatenate([delta] + [net.shift(delta, step) for step in range(1, mp)], 2)
    block, feed_kept, feed_sent, delta = lax.optimization_barrier(
        (block, feed_kept, feed_sent, delta)
    )
    grads.append(block)
    feed_sums = add_packed(feed_kept, net.swap(feed_sent, 1))
    if mp > 2:
        block = net.shift(grads[-1], 1)
        block, feed_sums = lax.optimization_barrier((block, feed_sums))
        grads.append(block)
    for _ in range(3, mp):
        grads.append(net.shift(grads[-1], 1))
    feed_sums = net.link_pieces(feed_sums, lines)
    if feed_sums[0][1]:
        feed_sums = net.link_step(feed_sums)

    back, grad_keys, grad_values = row_call(
        attend_back_kernel,
        "attend_back",
        [queries, keys, values, lat_row, byte_col, lse, delta] + grads,
        [lat_shape] + [shape((rows, byte_len, lat_width), BF16)] * 2,
        5 * unit,
    )
    grad_keys = grad_keys.reshape(-1, lat_width)
    grad_values = grad_values.reshape(-1, lat_width)
    total = back[1]
    moved = net.shift(total, 1)
    products = [dot(grad_values, byte_norm, TN).astype(BF16)]
    while feed_sums[0][1]:
        feed_sums = net.link_step(feed_sums)
    moved, products[0], feed_half = lax.optimization_barrier(
        (moved, products[0], net.arrays(feed_sums))
    )
    feed_parts = net.blocks_back(jnp.concatenate(feed_half, 1), lines)
    feed_total = feed_parts[1]
    total = add(moved, back[2 % mp])
    grad_keys, back_flat = lax.optimization_barrier(
        (grad_keys, back.reshape(-1, lat_width), moved)
    )[:2]
    products.insert(0, dot(grad_keys, byte_norm, TN).astype(BF16))
    products.insert(0, dot(back_flat, lat_flat, TN).astype(BF16))
    kept, sent = split(net.core[None], products, net.cut(lines)[0], lines)
    if mp > 2:
        moved, feed_moved = net.shift(total, 1), net.shift(feed_total, 1)
        moved, feed_moved, sent = lax.optimization_barrier((moved, feed_moved, sent))
        total = add(moved, back[3 % mp])
        feed_total = add(feed_moved, feed_parts[2])
    head_sums = net.link_pieces(add_packed(kept, net.swap(sent, 1)), lines)
    if head_sums[0][1]:
        head_sums = net.link_step(head_sums)
    grad_bytes, grad_byte_gain = block_call(
        byte_back_kernel,
        "byte_back",
        byte_len,
        [(byte_in, True), (byte_gain[None], False), (key_t, False), (value_t, False)]
        + [(after(grad_keys, sent), True), (grad_values, True)],
        [(shape(byte_in.shape, F32), True), (shape((1, byte_width), F32), False)],
        4 * rows * byte_len * lat_width * byte_width,
    )
    if mp > 3:
        moved, feed_moved = net.shift(total, 1), net.shift(feed_total, 1)
        grad_bytes, moved, feed_moved, done = lax.optimization_barrier(
            (grad_bytes, moved, feed_moved, net.arrays(head_sums))
        )
        head_sums = net.with_arrays(head_sums, done)
        total = add(moved, back[4 % mp])
        feed_total = add(feed_moved, feed_parts[3])
    for step in range(5, mp + 1):
        total = add(net.shift(total, 1), back[step % mp])
        feed_total = add(net.shift(feed_total, 1), feed_parts[step - 1])
    while head_sums[0][1]:
        head_sums = net.link_step(head_sums)
    feed_total = add(net.shift(feed_total, 1), feed_parts[0])
    feed_total, done = lax.optimization_barrier((feed_total, net.arrays(head_sums)))
    head_sums = net.with_arrays(head_sums, done)
    feed_grads = net.finish_sum(feed_total, lines, feed_widths)
    grad_lat_norm = score_scale * dot(total.reshape(own_lines, lat_width), query_t)
    grad_lat_back, grad_latent_gain = norm_back(grad_lat_norm, lat_hat, lat_inv, latent_gain)
    grad_latents = grad_hidden + grad_lat_back
    small = jnp.concatenate([grad_byte_gain[0], grad_latent_gain, feed_vectors.reshape(-1)])
    head_sums = jnp.concatenate(net.arrays(head_sums), 1)
    head_total = net.sum_blocks(head_sums, lines, small)
    head_grads, sums = net.finish_sum(head_total, lines, head_widths, small.size)
    sums = [sums[:byte_width]] + list(sums[byte_width:].reshape(5, lat_width))
    own_units = b_up.shape[0]
    return (
        result.reshape(rows, own_lat, lat_width),
        grad_bytes.reshape(rows, byte_len, byte_width),
        grad_latents.reshape(rows, own_lat, lat_width),
        sums[0],
        sums[1],
        sums[2],
        head_grads[0].astype(F32).T * score_scale,
        head_grads[1].astype(F32).T,
        head_grads[2].astype(F32).T,
        feed_grads[2].astype(F32),
        sums[4],
        feed_grads[1].astype(F32).T,
        lax.dynamic_slice_in_dim(sums[3], mp_index * own_units, own_units, 0),
        feed_grads[0].astype(F32),
        sums[5],
    )


def solution(mesh):
    by_row = P("dp", "mp", None)
    columns, lines = P(None, "mp"), P("mp", None)
    return jax.shard_map(
        functools.partial(shards, mesh.shape["dp"], mesh.shape["mp"]),
        mesh=mesh,
        in_specs=(
            by_row,
            by_row,
            by_row,
            P(),
            P(),
            P(),
            columns,
            columns,
            columns,
            lines,
            P(),
            columns,
            P("mp"),
            lines,
            P(),
            P("dp", None),
            P("dp", None),
            P("dp", None),
        ),
        out_specs=(
            by_row,
            by_row,
            by_row,
            P(),
            P(),
            P(),
            columns,
            columns,
            columns,
            lines,
            P(),
            columns,
            P("mp"),
            lines,
            P(),
        ),
        check_vma=False,
    )
```

time: 559 us -> 511 us (0.914)
  waiting for transfers between devices: 237 us -> 202 us
  matrix products: 58.4 us -> 34.5 us
  local copies, waits for them, and re-layouts: 32.9 us -> 44.4 us
  Pallas kernels: 98.7 us -> 109 us
  other arithmetic: 46.2 us -> 36 us
    all_gather x2, waiting for transfers between devices: 46.4 us -> 13.5 us  [gather_chips(): lax.all_gather(x, 'dp', axis=0, axis_index_groups=self.chip_groups(chips))]
    pallas_call x5 -> x8, Pallas kernels: 40.5 us -> 68.7 us  [the longest x3 33.5 us: row_call(): pl.pallas_call(kernel, grid=(outs[-1].shape[0],), in_specs=[spec(a.shape)...]
    dot_general x16 -> x7, matrix products: 58.4 us -> 34.5 us  [dot(): return lax.dot_general(a, b, dims, preferred_element_type=F32)]
    ppermute x21 -> x20, waiting for transfers between devices: 24.2 us -> 42.9 us  [swap(): return lax.ppermute(x, 'dp', [(i, i ^ bit) for i in range(self.dp)])]
    all_gather x3 -> x0, waiting for transfers between devices: 17.1 us -> none  [the longest x2 13.5 us: gathered(): lax.all_gather(after(grad, *earlier) if earlier else grad, 'mp', axis=0)]
    pallas_call x4 -> x2, Pallas kernels: 13.9 us -> 0.73 us  [join(): pl.pallas_call(functools.partial(join_kernel, widths), grid=(blocks,), in...]
    convert_element_type x26 -> x19, other arithmetic: 25.8 us -> 15.6 us  [add(): return total.astype(first.dtype)]
    unnamed x128 -> x102, local copies, waits for them, and re-layouts: 6.19 us -> 11.6 us
  transfers between devices with their start and end apart: 57 -> 52, of which waited for: 26 -> 33; matrix products, arithmetic and copies ran while one was open for 19% -> 15% of each run, Pallas kernels for 13% -> 19%
where the time goes in v4:
time: 511 us; the launch traced here: 502 us
  waiting for transfers between devices  202 us (40%)
  Pallas kernels  109 us (21%)
  starting transfers between devices  59.8 us (12%)
  local copies, waits for them, and re-layouts  44.4 us (9%)
  other arithmetic  36 us (7%)
  matrix products  34.5 us (7%)
  between operations  15.5 us (3%)
    ppermute x30, waiting for transfers between devices, shift(): return lax.ppermute(x, 'mp', ring(self.mp, step))  146 us
    ppermute x20, waiting for transfers between devices, swap(): return lax.ppermute(x, 'dp', [(i, i ^ bit) for i in range(self.dp)])  42.9 us
    ppermute x30, starting transfers between devices, shift(): return lax.ppermute(x, 'mp', ring(self.mp, step))  36.9 us
    dot_general x7, matrix products, dot(): return lax.dot_general(a, b, dims, preferred_element_type=F32)  34.5 us
    pallas_call x3, Pallas kernels, block_call(): pl.pallas_call(kernel, grid=(args[0][0].shape[0] // lines,), in_specs=[sp...  33.9 us
    pallas_call x3, Pallas kernels, row_call(): pl.pallas_call(kernel, grid=(outs[-1].shape[0],), in_specs=[spec(a.shape)...  33.5 us
    ppermute x20, starting transfers between devices, swap(): return lax.ppermute(x, 'dp', [(i, i ^ bit) for i in range(self.dp)])  22.9 us
    convert_element_type x19, other arithmetic, add(): return total.astype(first.dtype)  15.6 us
  transfers between devices with their start and end apart: 52, of which 33 were waited for; matrix products, arithmetic and copies ran while one was open for 15% of the time, Pallas kernels for 19%

profile of v4, /device:TPU:9, one launch (start us, length us, event | category | flops | bytes accessed | tf_op | source)
XLA Modules:
  0.0 501.7 jit_solution(16408276899263986355)
XLA Ops:
  15.4 5.7 %byte_norm.1 = bf16[2048,768]{1,0:T(8,128)(2,1)} custom-call(f32[2048,768]{1,0:T(8,128)} %bitcast.223, f32[1,768]{1,0:T(1,128)} %broadcast_in_dim.27.gain_ref), custom_call_target="tpu_custom_call" | custom-call | flops 1966080 | bytes 786816 | tf_op jit(solution)/shard_map/byte_norm/pallas_call | solution.py:264
  22.1 16.3 %collective-permute-done.1 = bf16[11,80,128]{2,0,1:T(8,128)(2,1)} collective-permute-done((bf16[11,80,128]{2,0,1:T(8,128)(2,1)S(1)}, bf16[11,80,128]{2,0,1:T(8,128)(2,1)}, u32[]{:S(2)}, u32[]{:S(2)}) %collective-permute-start.1) | collective-permute-done | bytes 225312 | tf_op jit(solution)/shard_map/ppermute | solution.py:539
  43.9 15.9 %collective-permute-done.3 = bf16[4,64,1280]{2,1,0:T(8,128)(2,1)S(1)} collective-permute-done((bf16[4,64,1280]{2,1,0:T(8,128)(2,1)S(1)}, bf16[4,64,1280]{2,1,0:T(8,128)(2,1)S(1)}, u32[]{:S(2)}, u32[]{:S(2)}) %collective-permute-start.3) | collective-permute-done | bytes 655392 | tf_op jit(solution)/shard_map/ppermute | solution.py:539
  60.9 14.8 %collective-permute-done.4 = bf16[4,64,1280]{2,1,0:T(8,128)(2,1)S(1)} collective-permute-done((bf16[4,64,1280]{2,1,0:T(8,128)(2,1)S(1)}, bf16[4,64,1280]{2,1,0:T(8,128)(2,1)S(1)}, u32[]{:S(2)}, u32[]{:S(2)}) %collective-permute-start.4) | collective-permute-done | bytes 655392 | tf_op jit(solution)/shard_map/ppermute | solution.py:539
  77.2 13.6 %collective-permute-done.5 = bf16[4,64,1280]{2,1,0:T(8,128)(2,1)} collective-permute-done((bf16[4,64,1280]{2,1,0:T(8,128)(2,1)S(1)}, bf16[4,64,1280]{2,1,0:T(8,128)(2,1)}, u32[]{:S(2)}, u32[]{:S(2)}) %collective-permute-start.5) | collective-permute-done | bytes 655392 | tf_op jit(solution)/shard_map/ppermute | solution.py:539
  100.9 6.5 %join_own.2 = (bf16[1280,1280]{1,0:T(8,128)(2,1)}, bf16[1280,768]{1,0:T(8,128)(2,1)S(1)}, bf16[1280,768]{1,0:T(8,128)(2,1)S(1)}) custom-call(s32[2]{0:T(128)S(1)} %pad_add_fusion.where_ref, bf16[320,1280]{1,0:T(8,128)(2,1)S(1)} %bitcast.213, bf16[320,768]{1,0:T(8,128)(2,1)S(1)} %bitcast.218, bf16[320,768]{1,0:T(8,128)(2,1)S(1)} %bitcast.217, ...), custom_call_target="tpu_custom_call" | custom-call | bytes 1351680 | tf_op jit(solution)/shard_map/join_own/pallas_call | solution.py:418
  107.5 6.0 %convolution_convert_fusion.2 = bf16[2048,1280]{1,0:T(8,128)(2,1)} fusion(bf16[2048,768]{1,0:T(8,128)(2,1)S(1)} %copy-done.24, bf16[1280,768]{1,0:T(8,128)(2,1)S(1)} %get-tuple-element.100.key_ref), kind=kOutput, calls=%fused_computation.6 | convolution fusion | flops 4029153280 | bytes 10354688 | tf_op jit(solution)/shard_map/dot_general | solution.py:22
  117.4 5.8 %collective-permute-done.8 = bf16[16,80,128]{2,0,1:T(8,128)(2,1)S(1)} collective-permute-done((bf16[16,80,128]{2,0,1:T(8,128)(2,1)S(1)}, bf16[16,80,128]{2,0,1:T(8,128)(2,1)S(1)}, u32[]{:S(2)}, u32[]{:S(2)}) %collective-permute-start.8) | collective-permute-done | bytes 327712 | tf_op jit(solution)/shard_map/ppermute | solution.py:539
  123.9 7.3 %lse.1.refs_0_ = f32[4,8,256]{2,1,0:T(8,128)S(1)} custom-call(bf16[4,4,64,1280]{3,2,1,0:T(8,128)(2,1)S(1)} %bitcast.205, bf16[4,512,1280]{2,1,0:T(8,128)(2,1)} %bitcast.219, s32[4,1,256]{2,1,0:T(1,128)S(1)} %broadcast_in_dim_reshape.10.lat_seg_ref, s32[4,512,1]{2,1,0:T(8,128)S(1)} %copy-done.1), custom_call_target="tpu_custom_call" | custom-call | flops 268435456 | bytes 984576 | tf_op jit(solution)/shard_map/lse/pallas_call | solution.py:246
  139.8 8.8 %convolution_convert_fusion.1 = bf16[2048,1280]{1,0:T(8,128)(2,1)} fusion(bf16[2048,768]{1,0:T(8,128)(2,1)} %byte_norm.1, bf16[1280,768]{1,0:T(8,128)(2,1)S(1)} %copy-done.7), kind=kOutput, calls=%fused_computation.5 | convolution fusion | flops 4029153280 | bytes 10354688 | tf_op jit(solution)/shard_map/dot_general | solution.py:22
  148.6 9.4 %attend.1 = (bf16[4,4,64,1280]{3,2,1,0:T(8,128)(2,1)S(1)}, f32[4,8,256]{2,1,0:T(8,128)S(1)}) custom-call(bf16[4,4,64,1280]{3,2,1,0:T(8,128)(2,1)} %bitcast.206, bf16[4,512,1280]{2,1,0:T(8,128)(2,1)} %bitcast.220, bf16[4,512,1280]{2,1,0:T(8,128)(2,1)} %bitcast.225, s32[4,1,256]{2,1,0:T(1,128)S(1)} %broadcast_in_dim_reshape.10.lat_seg_ref, ...), custom_call_target="tpu_custom_call" | custom-call | flops 536870912 | bytes 1656320 | tf_op jit(solution)/shard_map/attend/pallas_call | solution.py:246
  161.1 11.8 %collective-permute-done.13 = bf16[4,64,1280]{2,1,0:T(8,128)(2,1)} collective-permute-done((bf16[4,64,1280]{2,1,0:T(8,128)(2,1)S(1)}, bf16[4,64,1280]{2,1,0:T(8,128)(2,1)}, u32[]{:S(2)}, u32[]{:S(2)}) %collective-permute-start.13) | collective-permute-done | bytes 655392 | tf_op jit(solution)/shard_map/ppermute | solution.py:539
  172.8 13.5 %all-gather.7.cloned.1.call-done = bf16[12,15,80,128]{3,2,1,0:T(8,128)(2,1)} async-done(((bf16[3,15,80,128]{3,2,1,0:T(8,128)(2,1)}), bf16[12,15,80,128]{3,2,1,0:T(8,128)(2,1)}) %all-gather.7.cloned.1.call-update) | async-done | bytes 3686416 | tf_op jit(solution)/shard_map/all_gather | solution.py:579
  199.5 7.7 %join_own.3 = (bf16[1280,1280]{1,0:T(8,128)(2,1)S(1)}, bf16[1280,1280]{1,0:T(8,128)(2,1)}, bf16[1280,1280]{1,0:T(8,128)(2,1)}) custom-call(s32[2]{0:T(128)S(1)} %pad_add_fusion.where_ref, bf16[320,1280]{1,0:T(8,128)(2,1)S(1)} %copy-done.11, bf16[320,1280]{1,0:T(8,128)(2,1)S(1)} %bitcast.214, bf16[320,1280]{1,0:T(8,128)(2,1)S(1)} %copy-done.9, ...), custom_call_target="tpu_custom_call" | custom-call | bytes 1843200 | tf_op jit(solution)/shard_map/join_own/pallas_call | solution.py:418
  217.0 13.7 %collective-permute-done.16 = bf16[4,64,1280]{2,1,0:T(8,128)(2,1)S(1)} collective-permute-done((bf16[4,64,1280]{2,1,0:T(8,128)(2,1)S(1)}, bf16[4,64,1280]{2,1,0:T(8,128)(2,1)S(1)}, u32[]{:S(2)}, u32[]{:S(2)}) %collective-permute-start.16) | collective-permute-done | bytes 655392 | tf_op jit(solution)/shard_map/ppermute | solution.py:539
  232.8 12.6 %feed.1 = (f32[256,1280]{1,0:T(8,128)}, bf16[256,1280]{1,0:T(8,128)(2,1)}, bf16[256,1280]{1,0:T(8,128)(2,1)}, bf16[256,1280]{1,0:T(8,128)(2,1)}, f32[256,1280]{1...) custom-call(f32[256,1280]{1,0:T(8,128)} %bitcast.222, ...), custom_call_target="tpu_custom_call" | custom-call | flops 419430400 | bytes 1640960 | tf_op jit(solution)/shard_map/feed/pallas_call | solution.py:264
  252.9 8.8 %grads.1 = (bf16[4,4,15,80,128]{4,3,2,1,0:T(8,128)(2,1)}, bf16[4,4,15,80,128]{4,3,2,1,0:T(8,128)(2,1)}) custom-call(s32[1]{0:T(128)} %bitcast.14.core_ref, bf16[256,1280]{1,0:T(8,128)(2,1)} %get-tuple-element.119.refs_0_, bf16[256,1280]{1,0:T(8,128)(2,1)} %get-tuple-element.120.refs_1_, bf16[256,1280]{1,0:T(8,128)(2,1)} %bitcast.236, ...), custom_call_target="tpu_custom_call" | custom-call | flops 314572800 | bytes 491520 | tf_op jit(solution)/shard_map/grads/pallas_call | solution.py:479
  267.9 8.2 %collective-permute-done.22.b_ref = bf16[4,4,15,80,128]{4,3,2,1,0:T(8,128)(2,1)} collective-permute-done((bf16[4,4,15,80,128]{4,3,2,1,0:T(8,128)(2,1)}, bf16[4,4,15,80,128]{4,3,2,1,0:T(8,128)(2,1)}, u32[]{:S(2)}, u32[]{:S(2)}) %collective-permute-start.22) | collective-permute-done | bytes 4915232 | tf_op jit(solution)/shard_map/ppermute | solution.py:536
  276.1 6.6 %add_packed.2 = bf16[4,4,15,80,128]{4,3,2,1,0:T(8,128)(2,1)} custom-call(bf16[4,4,15,80,128]{4,3,2,1,0:T(8,128)(2,1)} %get-tuple-element.128.a_ref, bf16[4,4,15,80,128]{4,3,2,1,0:T(8,128)(2,1)} %collective-permute-done.22.b_ref), custom_call_target="tpu_custom_call" | custom-call | bytes 1228800 | tf_op jit(solution)/shard_map/add_packed/pallas_call | solution.py:461
  294.6 8.8 %collective-permute-done.23.refs_3_ = bf16[4,64,1280]{2,1,0:T(8,128)(2,1)} collective-permute-done((bf16[4,64,1280]{2,1,0:T(8,128)(2,1)S(1)}, bf16[4,64,1280]{2,1,0:T(8,128)(2,1)}, u32[]{:S(2)}, u32[]{:S(2)}) %collective-permute-start.23) | collective-permute-done | bytes 655392 | tf_op jit(solution)/shard_map/ppermute | solution.py:539
  303.3 16.9 %attend_back.1 = (bf16[4,4,64,1280]{3,2,1,0:T(8,128)(2,1)}, bf16[4,512,1280]{2,1,0:T(8,128)(2,1)}, bf16[4,512,1280]{2,1,0:T(8,128)(2,1)}) custom-call(bf16[4,4,64,1280]{3,2,1,0:T(8,128)(2,1)} %bitcast.207, bf16[4,512,1280]{2,1,0:T(8,128)(2,1)} %bitcast.221, bf16[4,512,1280]{2,1,0:T(8,128)(2,1)} %bitcast.226, ...), custom_call_target="tpu_custom_call" | custom-call | flops 1342177280 | bytes 1975808 | tf_op jit(solution)/shard_map/attend_back/pallas_call | solution.py:246
  326.9 4.3 convolution_convert_fusion.4.refs_2_
  331.2 5.2 %collective-permute-done.28 = bf16[4,7,80,128]{3,2,1,0:T(8,128)(2,1)S(1)} collective-permute-done((bf16[4,7,80,128]{3,2,1,0:T(8,128)(2,1)S(1)}, bf16[4,7,80,128]{3,2,1,0:T(8,128)(2,1)S(1)}, u32[]{:S(2)}, u32[]{:S(2)}) %collective-permute-start.28) | collective-permute-done | bytes 573472 | tf_op jit(solution)/shard_map/ppermute | solution.py:536
  336.6 4.9 collective-permute-done.26
  351.2 5.0 %convolution_convert_fusion.refs_0_ = bf16[1280,1280]{1,0:T(8,128)(2,1)} fusion(bf16[1024,1280]{1,0:T(8,128)(2,1)S(1)} %bitcast.251, bf16[1024,1280]{1,0:T(8,128)(2,1)S(1)} %bitcast.249), kind=kOutput, calls=%fused_computation.4 | convolution fusion | flops 3357081600 | bytes 8519680 | tf_op jit(solution)/shard_map/dot_general | solution.py:22
  356.2 5.8 %split.1 = (bf16[4,4,11,80,128]{4,3,2,1,0:T(8,128)(2,1)}, bf16[4,4,11,80,128]{4,3,2,1,0:T(8,128)(2,1)}) custom-call(s32[1]{0:T(128)} %bitcast.14.core_ref, bf16[1280,1280]{1,0:T(8,128)(2,1)} %convolution_convert_fusion.refs_0_, bf16[1280,768]{1,0:T(8,128)(2,1)S(1)} %convolution_convert_fusion.3.refs_1_, bf16[1280,768]{1,0:T(8,128)(2,1)S(1)} %convolution_convert_fusion.4.refs_2_), custom_call_target="tpu_custom_call" | custom-call | bytes 1802240 | tf_op jit(solution)/shard_map/split/pallas_call | solution.py:445
  362.0 6.1 %collective-permute-done.29 = bf16[4,64,1280]{2,1,0:T(8,128)(2,1)} collective-permute-done((bf16[4,64,1280]{2,1,0:T(8,128)(2,1)S(1)}, bf16[4,64,1280]{2,1,0:T(8,128)(2,1)}, u32[]{:S(2)}, u32[]{:S(2)}) %collective-permute-start.29) | collective-permute-done | bytes 655392 | tf_op jit(solution)/shard_map/ppermute | solution.py:539
  377.7 5.5 %add_packed.3 = bf16[4,4,11,80,128]{4,3,2,1,0:T(8,128)(2,1)} custom-call(bf16[4,4,11,80,128]{4,3,2,1,0:T(8,128)(2,1)} %get-tuple-element.147.a_ref, bf16[4,4,11,80,128]{4,3,2,1,0:T(8,128)(2,1)} %collective-permute-done.33.b_ref), custom_call_target="tpu_custom_call" | custom-call | bytes 901120 | tf_op jit(solution)/shard_map/add_packed/pallas_call | solution.py:461
  391.6 15.6 %byte_back.1 = (f32[2048,768]{1,0:T(8,128)}, f32[1,768]{1,0:T(1,128)}) custom-call(f32[2048,768]{1,0:T(8,128)} %bitcast.224, f32[1,768]{1,0:T(1,128)} %broadcast_in_dim.27.gain_ref, bf16[1280,768]{1,0:T(8,128)(2,1)} %copy-done.5, bf16[1280,768]{1,0:T(8,128)(2,1)} %copy-done.6, bf16[2048,1280]{1,0:T(8,128)(2,1)} %bitcast.238, bf16[2048,1280]{1,0:T(8,128)(2,1)} %bitcast.242), custom_call_target="tpu_custom_call" | custom-call | flops 1006632960 | bytes 2589056 | tf_op jit(solution)/shard_map/byte_back/pallas_call | solution.py:264
  429.6 14.8 %collective-permute-done.40 = bf16[12,80,128]{2,1,0:T(8,128)(2,1)S(1)} collective-permute-done((bf16[12,80,128]{2,1,0:T(8,128)(2,1)S(1)}, bf16[12,80,128]{2,1,0:T(8,128)(2,1)S(1)}, u32[]{:S(2)}, u32[]{:S(2)}) %collective-permute-start.40) | collective-permute-done | bytes 245792 | tf_op jit(solution)/shard_map/ppermute | solution.py:539
  455.3 5.3 %collective-permute-done.44 = bf16[12,80,128]{2,1,0:T(8,128)(2,1)S(1)} collective-permute-done((bf16[12,80,128]{2,1,0:T(8,128)(2,1)S(1)}, bf16[12,80,128]{2,1,0:T(8,128)(2,1)S(1)}, u32[]{:S(2)}, u32[]{:S(2)}) %collective-permute-start.44) | collective-permute-done | bytes 245792 | tf_op jit(solution)/shard_map/ppermute | solution.py:536
  473.7 6.7 %collective-permute-done.48 = bf16[15,80,128]{2,1,0:T(8,128)(2,1)S(1)} collective-permute-done((bf16[15,80,128]{2,1,0:T(8,128)(2,1)S(1)}, bf16[15,80,128]{2,1,0:T(8,128)(2,1)S(1)}, u32[]{:S(2)}, u32[]{:S(2)}) %collective-permute-start.48) | collective-permute-done | bytes 307232 | tf_op jit(solution)/shard_map/ppermute | solution.py:536
  (325 shorter events, 188.3 us)
Async XLA Ops:
  7.2 83.6 %all-gather.5.cloned.1.call-start = ((), (), s32[]{:S(2)}) async-start(), calls=%async_computation | async-start | bytes 3379200 | tf_op jit(solution)/shard_map/all_gather | solution.py:579
  11.0 27.4 %collective-permute-start.1 = (bf16[11,80,128]{2,0,1:T(8,128)(2,1)S(1)}, bf16[11,80,128]{2,0,1:T(8,128)(2,1)}, u32[]{:S(2)}, u32[]{:S(2)}) collective-permute-start(bf16[11,80,128]{2,0,1:T(8,128)(2,1)S(1)} %pad_maximum_fusion.13), channel_id=1, source_target_pairs={{0,2},{1,3},{2,0},{3,1},{4,6},{5,7},{6,4},{7,5},{8,10},{9,11},{10,... | collective-permute-start | bytes 675848 | tf_op jit(solution)/shard_map/ppermute | solution.py:539
  12.1 29.3 %collective-permute-start.2 = (bf16[11,80,128]{2,0,1:T(8,128)(2,1)S(1)}, bf16[11,80,128]{2,0,1:T(8,128)(2,1)}, u32[]{:S(2)}, u32[]{:S(2)}) collective-permute-start(bf16[11,80,128]{2,0,1:T(8,128)(2,1)S(1)} %pad_maximum_fusion.13), channel_id=1, source_target_pairs={{0,3},{1,0},{2,1},{3,2},{4,7},{5,4},{6,5},{7,6},{8,11},{9,8},{10,9... | collective-permute-start | bytes 675848 | tf_op jit(solution)/shard_map/ppermute | solution.py:539
  43.8 142.6 %all-gather.7.cloned.1.call-start = ((), (), s32[]{:S(2)}) async-start(), calls=%async_computation.1 | async-start | bytes 4608000 | tf_op jit(solution)/shard_map/all_gather | solution.py:579
  43.8 16.0 %collective-permute-start.3 = (bf16[4,64,1280]{2,1,0:T(8,128)(2,1)S(1)}, bf16[4,64,1280]{2,1,0:T(8,128)(2,1)S(1)}, u32[]{:S(2)}, u32[]{:S(2)}) collective-permute-start(bf16[4,64,1280]{2,1,0:T(8,128)(2,1)S(1)} %multiply_convert_fusion.1), channel_id=1, source_target_pairs={{0,1},{1,2},{2,3},{3,0},{4,5},{5,6},{6,7},{7,4},{8,9},{9,10},{10,1... | collective-permute-start | bytes 1966088 | tf_op jit(solution)/shard_map/ppermute | solution.py:539
  60.6 15.1 %collective-permute-start.4 = (bf16[4,64,1280]{2,1,0:T(8,128)(2,1)S(1)}, bf16[4,64,1280]{2,1,0:T(8,128)(2,1)S(1)}, u32[]{:S(2)}, u32[]{:S(2)}) collective-permute-start(bf16[4,64,1280]{2,1,0:T(8,128)(2,1)S(1)} %collective-permute-done.3), channel_id=1, source_target_pairs={{0,1},{1,2},{2,3},{3,0},{4,5},{5,6},{6,7},{7,4},{8,9},{9,10},{10,1... | collective-permute-start | bytes 1966088 | tf_op jit(solution)/shard_map/ppermute | solution.py:539
  76.5 14.3 %collective-permute-start.5 = (bf16[4,64,1280]{2,1,0:T(8,128)(2,1)S(1)}, bf16[4,64,1280]{2,1,0:T(8,128)(2,1)}, u32[]{:S(2)}, u32[]{:S(2)}) collective-permute-start(bf16[4,64,1280]{2,1,0:T(8,128)(2,1)S(1)} %collective-permute-done.4), channel_id=1, source_target_pairs={{0,1},{1,2},{2,3},{3,0},{4,5},{5,6},{6,7},{7,4},{8,9},{9,10},{10,1... | collective-permute-start | bytes 1966088 | tf_op jit(solution)/shard_map/ppermute | solution.py:539
  134.4 14.2 %collective-permute-start.10 = (f32[4,8,256]{2,1,0:T(8,128)S(1)}, f32[4,8,256]{2,1,0:T(8,128)S(1)}, u32[]{:S(2)}, u32[]{:S(2)}) collective-permute-start(f32[4,8,256]{2,1,0:T(8,128)S(1)} %lse.1.refs_0_), channel_id=1, source_target_pairs={{0,1},{1,2},{2,3},{3,0},{4,5},{5,6},{6,7},{7,4},{8,9},{9,10},{10,1... | collective-permute-start | bytes 98312 | tf_op jit(solution)/shard_map/ppermute | solution.py:539
  135.4 13.2 %collective-permute-start.11 = (f32[4,8,256]{2,1,0:T(8,128)S(1)}, f32[4,8,256]{2,1,0:T(8,128)S(1)}, u32[]{:S(2)}, u32[]{:S(2)}) collective-permute-start(f32[4,8,256]{2,1,0:T(8,128)S(1)} %lse.1.refs_0_), channel_id=1, source_target_pairs={{0,2},{1,3},{2,0},{3,1},{4,6},{5,7},{6,4},{7,5},{8,10},{9,11},{10,... | collective-permute-start | bytes 98312 | tf_op jit(solution)/shard_map/ppermute | solution.py:539
  159.6 13.2 %collective-permute-start.13 = (bf16[4,64,1280]{2,1,0:T(8,128)(2,1)S(1)}, bf16[4,64,1280]{2,1,0:T(8,128)(2,1)}, u32[]{:S(2)}, u32[]{:S(2)}) collective-permute-start(bf16[4,64,1280]{2,1,0:T(8,128)(2,1)S(1)} %slice_bitcast_fusion.1), channel_id=1, source_target_pairs={{0,1},{1,2},{2,3},{3,0},{4,5},{5,6},{6,7},{7,4},{8,9},{9,10},{10,1... | collective-permute-start | bytes 1966088 | tf_op jit(solution)/shard_map/ppermute | solution.py:539
  196.2 16.4 %collective-permute-start.14 = (bf16[4,64,1280]{2,1,0:T(8,128)(2,1)S(1)}, bf16[4,64,1280]{2,1,0:T(8,128)(2,1)S(1)}, u32[]{:S(2)}, u32[]{:S(2)}) collective-permute-start(bf16[4,64,1280]{2,1,0:T(8,128)(2,1)S(1)} %fusion.10), channel_id=1, source_target_pairs={{0,1},{1,2},{2,3},{3,0},{4,5},{5,6},{6,7},{7,4},{8,9},{9,10},{10,1... | collective-permute-start | bytes 1966088 | tf_op jit(solution)/shard_map/ppermute | solution.py:539
  213.9 16.8 %collective-permute-start.16 = (bf16[4,64,1280]{2,1,0:T(8,128)(2,1)S(1)}, bf16[4,64,1280]{2,1,0:T(8,128)(2,1)S(1)}, u32[]{:S(2)}, u32[]{:S(2)}) collective-permute-start(bf16[4,64,1280]{2,1,0:T(8,128)(2,1)S(1)} %fusion.9), channel_id=1, source_target_pairs={{0,1},{1,2},{2,3},{3,0},{4,5},{5,6},{6,7},{7,4},{8,9},{9,10},{10,1... | collective-permute-start | bytes 1966088 | tf_op jit(solution)/shard_map/ppermute | solution.py:539
  245.4 22.0 %collective-permute-start.17 = (bf16[4,64,1280]{2,1,0:T(8,128)(2,1)}, bf16[4,64,1280]{2,1,0:T(8,128)(2,1)S(1)}, u32[]{:S(2)}, u32[]{:S(2)}) collective-permute-start(bf16[4,64,1280]{2,1,0:T(8,128)(2,1)} %bitcast.215), channel_id=1, source_target_pairs={{0,1},{1,2},{2,3},{3,0},{4,5},{5,6},{6,7},{7,4},{8,9},{9,10},{10,1... | collective-permute-start | bytes 1966088 | tf_op jit(solution)/shard_map/ppermute | solution.py:539
  246.7 15.6 %collective-permute-start.18 = (f32[4,8,64]{2,1,0:T(8,128)S(1)}, f32[4,8,64]{2,1,0:T(8,128)S(1)}, u32[]{:S(2)}, u32[]{:S(2)}) collective-permute-start(f32[4,8,64]{2,1,0:T(8,128)S(1)} %bitcast.268), channel_id=1, source_target_pairs={{0,1},{1,2},{2,3},{3,0},{4,5},{5,6},{6,7},{7,4},{8,9},{9,10},{10,1... | collective-permute-start | bytes 24584 | tf_op jit(solution)/shard_map/ppermute | solution.py:539
  248.0 16.3 %collective-permute-start.19 = (f32[4,8,64]{2,1,0:T(8,128)S(1)}, f32[4,8,64]{2,1,0:T(8,128)S(1)}, u32[]{:S(2)}, u32[]{:S(2)}) collective-permute-start(f32[4,8,64]{2,1,0:T(8,128)S(1)} %bitcast.269), channel_id=1, source_target_pairs={{0,2},{1,3},{2,0},{3,1},{4,6},{5,7},{6,4},{7,5},{8,10},{9,11},{10,... | collective-permute-start | bytes 24584 | tf_op jit(solution)/shard_map/ppermute | solution.py:539
  251.6 15.7 %collective-permute-start.20 = (f32[4,8,64]{2,1,0:T(8,128)S(1)}, f32[4,8,64]{2,1,0:T(8,128)S(1)}, u32[]{:S(2)}, u32[]{:S(2)}) collective-permute-start(f32[4,8,64]{2,1,0:T(8,128)S(1)} %bitcast.270), channel_id=1, source_target_pairs={{0,3},{1,0},{2,1},{3,2},{4,7},{5,4},{6,5},{7,6},{8,11},{9,8},{10,9... | collective-permute-start | bytes 24584 | tf_op jit(solution)/shard_map/ppermute | solution.py:539
  267.9 16.3 %collective-permute-start.21 = (bf16[4,64,1280]{2,1,0:T(8,128)(2,1)S(1)}, bf16[4,64,1280]{2,1,0:T(8,128)(2,1)S(1)}, u32[]{:S(2)}, u32[]{:S(2)}) collective-permute-start(bf16[4,64,1280]{2,1,0:T(8,128)(2,1)S(1)} %collective-permute-done.17.refs_1_), channel_id=1, source_target_pairs={{0,1},{1,2},{2,3},{3,0},{4,5},{5,6},{6,7},{7,4},{8,9},{9,10},{10,1... | collective-permute-start | bytes 1966088 | tf_op jit(solution)/shard_map/ppermute | solution.py:539
  286.0 17.3 %collective-permute-start.23 = (bf16[4,64,1280]{2,1,0:T(8,128)(2,1)S(1)}, bf16[4,64,1280]{2,1,0:T(8,128)(2,1)}, u32[]{:S(2)}, u32[]{:S(2)}) collective-permute-start(bf16[4,64,1280]{2,1,0:T(8,128)(2,1)S(1)} %collective-permute-done.21.refs_2_), channel_id=1, source_target_pairs={{0,1},{1,2},{2,3},{3,0},{4,5},{5,6},{6,7},{7,4},{8,9},{9,10},{10,1... | collective-permute-start | bytes 1966088 | tf_op jit(solution)/shard_map/ppermute | solution.py:539
  288.6 33.0 %collective-permute-start.27 = (bf16[2,4,7,80,128]{4,3,2,1,0:T(8,128)(2,1)}, bf16[2,4,7,80,128]{4,3,2,1,0:T(8,128)(2,1)}, u32[]{:S(2)}, u32[]{:S(2)}) collective-permute-start(bf16[2,4,7,80,128]{4,3,2,1,0:T(8,128)(2,1)} %dynamic-slice_bitcast_fusion.1), channel_id=1, source_target_pairs={{0,16},{4,20},{8,24},{12,28},{16,0},{20,4},{24,8},{28,12},{1,17},{... | collective-permute-start | bytes 3440648 | tf_op jit(solution)/shard_map/ppermute | solution.py:536
  294.3 30.3 %collective-permute-start.25 = (bf16[2,4,8,80,128]{4,3,2,1,0:T(8,128)(2,1)}, bf16[2,4,8,80,128]{4,3,2,1,0:T(8,128)(2,1)}, u32[]{:S(2)}, u32[]{:S(2)}) collective-permute-start(bf16[2,4,8,80,128]{4,3,2,1,0:T(8,128)(2,1)} %dynamic-slice_bitcast_fusion), channel_id=1, source_target_pairs={{0,8},{4,12},{8,0},{12,4},{16,24},{20,28},{24,16},{28,20},{1,9},{5... | collective-permute-start | bytes 3932168 | tf_op jit(solution)/shard_map/ppermute | solution.py:536
  321.5 20.2 %collective-permute-start.24 = (bf16[4,64,1280]{2,1,0:T(8,128)(2,1)S(1)}, bf16[4,64,1280]{2,1,0:T(8,128)(2,1)S(1)}, u32[]{:S(2)}, u32[]{:S(2)}) collective-permute-start(bf16[4,64,1280]{2,1,0:T(8,128)(2,1)S(1)} %slice_bitcast_fusion), channel_id=1, source_target_pairs={{0,1},{1,2},{2,3},{3,0},{4,5},{5,6},{6,7},{7,4},{8,9},{9,10},{10,1... | collective-permute-start | bytes 1966088 | tf_op jit(solution)/shard_map/ppermute | solution.py:539
  326.7 14.8 %collective-permute-start.26 = (bf16[4,8,80,128]{3,2,1,0:T(8,128)(2,1)S(1)}, bf16[4,8,80,128]{3,2,1,0:T(8,128)(2,1)S(1)}, u32[]{:S(2)}, u32[]{:S(2)}) collective-permute-start(bf16[4,8,80,128]{3,2,1,0:T(8,128)(2,1)S(1)} %dynamic-slice_bitcast_fusion.4), channel_id=1, source_target_pairs={{0,16},{4,20},{8,24},{12,28},{16,0},{20,4},{24,8},{28,12},{1,17},{... | collective-permute-start | bytes 1966088 | tf_op jit(solution)/shard_map/ppermute | solution.py:536
  346.4 15.6 %collective-permute-start.30 = (bf16[15,80,128]{2,1,0:T(8,128)(2,1)S(1)}, bf16[15,80,128]{2,1,0:T(8,128)(2,1)S(1)}, u32[]{:S(2)}, u32[]{:S(2)}) collective-permute-start(bf16[15,80,128]{2,1,0:T(8,128)(2,1)S(1)} %dynamic-slice_bitcast_fusion.8), channel_id=1, source_target_pairs={{0,1},{1,2},{2,3},{3,0},{4,5},{5,6},{6,7},{7,4},{8,9},{9,10},{10,1... | collective-permute-start | bytes 921608 | tf_op jit(solution)/shard_map/ppermute | solution.py:539
  346.9 21.2 %collective-permute-start.29 = (bf16[4,64,1280]{2,1,0:T(8,128)(2,1)S(1)}, bf16[4,64,1280]{2,1,0:T(8,128)(2,1)}, u32[]{:S(2)}, u32[]{:S(2)}) collective-permute-start(bf16[4,64,1280]{2,1,0:T(8,128)(2,1)S(1)} %fusion.6), channel_id=1, source_target_pairs={{0,1},{1,2},{2,3},{3,0},{4,5},{5,6},{6,7},{7,4},{8,9},{9,10},{10,1... | collective-permute-start | bytes 1966088 | tf_op jit(solution)/shard_map/ppermute | solution.py:539
  372.5 37.6 %collective-permute-start.32 = (bf16[15,80,128]{2,1,0:T(8,128)(2,1)}, bf16[15,80,128]{2,1,0:T(8,128)(2,1)S(1)}, u32[]{:S(2)}, u32[]{:S(2)}) collective-permute-start(bf16[15,80,128]{2,1,0:T(8,128)(2,1)} %fusion.16), channel_id=1, source_target_pairs={{0,1},{1,2},{2,3},{3,0},{4,5},{5,6},{6,7},{7,4},{8,9},{9,10},{10,1... | collective-permute-start | bytes 921608 | tf_op jit(solution)/shard_map/ppermute | solution.py:539
  386.6 21.3 %collective-permute-start.35 = (bf16[2,4,5,80,128]{4,3,2,1,0:T(8,128)(2,1)S(1)}, bf16[2,4,5,80,128]{4,3,2,1,0:T(8,128)(2,1)}, u32[]{:S(2)}, u32[]{:S(2)}) collective-permute-start(bf16[2,4,5,80,128]{4,3,2,1,0:T(8,128)(2,1)S(1)} %dynamic-slice_bitcast_fusion.3), channel_id=1, source_target_pairs={{0,16},{4,20},{8,24},{12,28},{16,0},{20,4},{24,8},{28,12},{1,17},{... | collective-permute-start | bytes 2457608 | tf_op jit(solution)/shard_map/ppermute | solution.py:536
  386.8 23.0 %collective-permute-start.34 = (bf16[2,4,6,80,128]{4,3,2,1,0:T(8,128)(2,1)S(1)}, bf16[2,4,6,80,128]{4,3,2,1,0:T(8,128)(2,1)S(1)}, u32[]{:S(2)}, u32[]{:S(2)}) collective-permute-start(bf16[2,4,6,80,128]{4,3,2,1,0:T(8,128)(2,1)S(1)} %dynamic-slice_bitcast_fusion.2), channel_id=1, source_target_pairs={{0,8},{4,12},{8,0},{12,4},{16,24},{20,28},{24,16},{28,20},{1,9},{5... | collective-permute-start | bytes 2949128 | tf_op jit(solution)/shard_map/ppermute | solution.py:536
  390.5 19.5 %collective-permute-start.31 = (bf16[4,64,1280]{2,1,0:T(8,128)(2,1)}, bf16[4,64,1280]{2,1,0:T(8,128)(2,1)}, u32[]{:S(2)}, u32[]{:S(2)}) collective-permute-start(bf16[4,64,1280]{2,1,0:T(8,128)(2,1)} %fusion.5), channel_id=1, source_target_pairs={{0,1},{1,2},{2,3},{3,0},{4,5},{5,6},{6,7},{7,4},{8,9},{9,10},{10,1... | collective-permute-start | bytes 1966088 | tf_op jit(solution)/shard_map/ppermute | solution.py:539
  423.8 20.6 %collective-permute-start.40 = (bf16[12,80,128]{2,1,0:T(8,128)(2,1)S(1)}, bf16[12,80,128]{2,1,0:T(8,128)(2,1)S(1)}, u32[]{:S(2)}, u32[]{:S(2)}) collective-permute-start(bf16[12,80,128]{2,1,0:T(8,128)(2,1)S(1)} %get-tuple-element.185), channel_id=1, source_target_pairs={{0,2},{1,3},{2,0},{3,1},{4,6},{5,7},{6,4},{7,5},{8,10},{9,11},{10,... | collective-permute-start | bytes 737288 | tf_op jit(solution)/shard_map/ppermute | solution.py:539
  428.1 20.6 %collective-permute-start.41 = (bf16[12,80,128]{2,1,0:T(8,128)(2,1)S(1)}, bf16[12,80,128]{2,1,0:T(8,128)(2,1)S(1)}, u32[]{:S(2)}, u32[]{:S(2)}) collective-permute-start(bf16[12,80,128]{2,1,0:T(8,128)(2,1)S(1)} %get-tuple-element.186), channel_id=1, source_target_pairs={{0,3},{1,0},{2,1},{3,2},{4,7},{5,4},{6,5},{7,6},{8,11},{9,8},{10,9... | collective-permute-start | bytes 737288 | tf_op jit(solution)/shard_map/ppermute | solution.py:539
  461.6 23.2 %collective-permute-start.45 = (bf16[4,1,12,80,128]{4,3,2,1,0:T(8,128)(2,1)S(1)}, bf16[4,1,12,80,128]{4,3,2,1,0:T(8,128)(2,1)S(1)}, u32[]{:S(2)}, u32[]{:S(2)}) collective-permute-start(bf16[4,1,12,80,128]{4,3,2,1,0:T(8,128)(2,1)S(1)} %bitcast.210), channel_id=1, source_target_pairs={{0,4},{4,0},{8,12},{12,8},{16,20},{20,16},{24,28},{28,24},{1,5},{5... | collective-permute-start | bytes 2949128 | tf_op jit(solution)/shard_map/ppermute | solution.py:536
  465.7 14.6 %collective-permute-start.48 = (bf16[15,80,128]{2,1,0:T(8,128)(2,1)S(1)}, bf16[15,80,128]{2,1,0:T(8,128)(2,1)S(1)}, u32[]{:S(2)}, u32[]{:S(2)}) collective-permute-start(bf16[15,80,128]{2,1,0:T(8,128)(2,1)S(1)} %fusion.14), channel_id=1, source_target_pairs={{0,24},{4,28},{8,16},{12,20},{16,8},{20,12},{24,0},{28,4},{1,25},{... | collective-permute-start | bytes 921608 | tf_op jit(solution)/shard_map/ppermute | solution.py:536
  (72 other events, 681.6 us)
Sparse Core Ops, SparseCore 0:
  43.9 40.2 all-gather.4
  134.6 51.7 all-gather.6

commit v5 on v4

--- a/solution.py
+++ b/solution.py
@@ -105,7 +105,6 @@
     grad_hidden_ref,
     grad_attn_ref,
     grad_att_ref,
-    delta_ref,
     sums_ref,
     hidden_ref,
 ):
@@ -127,13 +126,22 @@
     sums_ref[2:3, :] = jnp.sum(grad_hidden_ref[...], axis=0, keepdims=True)
     sums_ref[3:4, :] = jnp.sum(cotangent_ref[...], axis=0, keepdims=True)
     grad_attn_ref[...] = grad_hidden_ref[...].astype(BF16)
-    grad_att_ref[...] = dot(grad_attn_ref[...], out_ref[...], NT).astype(BF16)
+    width = attended_ref.shape[1]
+    grad_att_ref[:, :width] = dot(grad_attn_ref[...], out_ref[...], NT).astype(BF16)
+    lane = lax.broadcasted_iota(jnp.int32, (attended_ref.shape[0], LANES), 1)
+    packed = jnp.zeros(lane.shape, F32)
+    heads = width // HEAD_DIM
     for head, (base, low, high) in enumerate(windows(attended_ref.shape[1])):
         product = attended_ref[:, base : base + 2 * LANES].astype(F32) * grad_att_ref[
             :, base : base + 2 * LANES
         ].astype(F32)
         product = jnp.where(own_columns(product.shape, low, high), product, 0.0)
-        delta_ref[:, head : head + 1] = jnp.sum(product, 1, keepdims=True)
+        rest = jnp.sum(product, 1, keepdims=True)
+        for part in range(3):
+            rounded = rest.astype(BF16).astype(F32)
+            packed = jnp.where(lane == part * heads + head, rounded, packed)
+            rest = rest - rounded
+    grad_att_ref[:, width:] = packed.astype(BF16)
     result_ref[...] = hidden_ref[...] + dot(activated_ref[...], down_ref[...]) + b_down_ref[...]
 
 
@@ -204,10 +212,13 @@
     lat_seg_ref,
     byte_seg_ref,
     lse_ref,
-    delta_ref,
     *refs,
 ):
     grad_refs, (grad_query_ref, grad_key_ref, grad_value_ref) = refs[:-3], refs[-3:]
+    width = query_ref.shape[3]
+    heads = width // HEAD_DIM
+    delta = jnp.concatenate([ref[0, :, width:] for ref in grad_refs]).astype(F32).T
+    delta = delta[:heads] + (delta[heads : 2 * heads] + delta[2 * heads : 3 * heads])
     allowed = byte_seg_ref[0] == lat_seg_ref[0]
     query_tiles, key_tiles, value_tiles = (
         Tiles(grad_query_ref),
@@ -225,7 +236,7 @@
         scores = jnp.where(allowed, dot(key, query, NT), NEG)
         probs = jnp.exp(scores - lse_ref[0, head : head + 1, :])
         grad_probs = dot(value, grad, NT)
-        grad_scores = (probs * (grad_probs - delta_ref[0, head : head + 1, :])).astype(BF16)
+        grad_scores = (probs * (grad_probs - delta[head : head + 1, :])).astype(BF16)
         value_tiles.add(base, dot(probs.astype(BF16), grad))
         key_tiles.add(base, dot(grad_scores, query))
         query_tiles.add(base, jnp.where(mine, dot(grad_scores, key, TN), 0.0))
@@ -299,7 +310,7 @@
                 for chip in range(chips):
                     out_refs[m][chip * part : (chip + 1) * part, at : at + LANES] = ref[
                         chip, 0, number
-                    ]
+                    ].astype(out_refs[m].dtype)
 
     @pl.when(core_ref[0] == 0)
     def _():
@@ -352,8 +363,13 @@
         copy((sent_ref, kept_ref))
 
 
-def add_kernel(a_ref, b_ref, out_ref):
-    out_ref[...] = (a_ref[...].astype(F32) + b_ref[...].astype(F32)).astype(out_ref.dtype)
+def add_kernel(a_ref, b_ref, *out_refs):
+    first = 0
+    for out_ref in out_refs:
+        group = slice(first, first + out_ref.shape[2])
+        total = a_ref[:, :, group].astype(F32) + b_ref[:, :, group].astype(F32)
+        out_ref[...] = total.astype(out_ref.dtype)
+        first += out_ref.shape[2]
 
 
 def split_kernel(widths, core_ref, *refs):
@@ -387,7 +403,7 @@
     return pl.BlockSpec((lines, width), lambda z: (z, 0))
 
 
-def join(core, mine, other, widths):
+def join(core, mine, other, widths, kinds):
     chips, blocks, _, part, _ = mine.shape
     lines = chips * part
     return pl.pallas_call(
@@ -399,7 +415,10 @@
             packed_spec(mine.shape),
         ],
         out_specs=[matrix_spec(lines, width) for width in widths],
-        out_shape=[jax.ShapeDtypeStruct((blocks * lines, width), mine.dtype) for width in widths],
+        out_shape=[
+            jax.ShapeDtypeStruct((blocks * lines, width), kind)
+            for width, kind in zip(widths, kinds)
+        ],
         name="join",
         cost_estimate=pl.CostEstimate(
             flops=0, bytes_accessed=mine.size, transcendentals=0
@@ -458,12 +477,14 @@
 
 
 def add_packed(a, b):
+    middle = (a.shape[2] + 1) // 2
+    shapes = [a.shape[:2] + (count,) + a.shape[3:] for count in (middle, a.shape[2] - middle)]
     return pl.pallas_call(
         add_kernel,
         grid=(a.shape[1],),
         in_specs=[packed_spec(a.shape)] * 2,
-        out_specs=packed_spec(a.shape),
-        out_shape=jax.ShapeDtypeStruct(a.shape, a.dtype),
+        out_specs=[packed_spec(shape) for shape in shapes],
+        out_shape=[jax.ShapeDtypeStruct(shape, a.dtype) for shape in shapes],
         name="add_packed",
         cost_estimate=pl.CostEstimate(flops=0, bytes_accessed=a.size // 2, transcendentals=0),
     )(a, b)
@@ -578,10 +599,10 @@
         chips, _ = self.cut(lines)
         return lax.all_gather(x, "dp", axis=0, axis_index_groups=self.chip_groups(chips))
 
-    def both_cores(self, own, mine):
+    def both_cores(self, own, mine, other):
         where = jnp.stack([self.core, self.mp_index])
         widths = [shard.shape[1] for shard in own]
-        return join_own(where, own, mine, self.swap(mine, 1), widths, self.mp)
+        return join_own(where, own, mine, other, widths, self.mp)
 
     def split_core(self, pairs, lines):
         chips, _ = self.cut(lines)
@@ -594,13 +615,12 @@
             total, "dp", scatter_dimension=0, axis_index_groups=self.chip_groups(chips)
         )
 
-    def link_pieces(self, total, lines):
+    def link_pieces(self, groups, lines):
         chips, _ = self.cut(lines)
         bits = [1 << b for b in range(chips.bit_length() - 1)]
-        middle = (total.shape[2] + 1) // 2
         return [
             (piece.reshape((2,) * len(bits) + piece.shape[1:]), order, sorted(bits, reverse=True))
-            for order, piece in ((bits, total[:, :, :middle]), (bits[::-1], total[:, :, middle:]))
+            for order, piece in zip((bits, bits[::-1]), groups)
         ]
 
     def link_step(self, pieces, *earlier):
@@ -631,7 +651,7 @@
             for r in range(self.mp)
         ]
 
-    def sum_blocks(self, total, lines, small=None):
+    def sum_blocks(self, total, lines):
         _, rest = self.cut(lines)
         for bit in rest:
             total = add(total, self.swap(total, bit))
@@ -639,13 +659,9 @@
             lax.dynamic_index_in_dim(total, (self.mp_index + step) % self.mp, 0, False)
             for step in range(self.mp)
         ]
-        if small is not None:
-            panel = small.astype(BF16)
-            panel = jnp.pad(panel, (0, total[0, 0].size - panel.size)).reshape(1, -1, LANES)
-            blocks = [jnp.concatenate([block, panel]) for block in blocks]
         return add(blocks[0], *[self.shift(blocks[step], step) for step in range(1, self.mp)])
 
-    def finish_sum(self, total, lines, widths, small=0):
+    def share(self, total, lines, small=False):
         chips, rest = self.cut(lines)
         slices = [total] + [self.swap(total, 2 * k) for k in range(1, chips)]
         if small:
@@ -654,13 +670,7 @@
                 panel = add(panel, self.swap(panel, bit))
             slices = [jnp.concatenate([piece[:-1], panel[None]]) for piece in slices]
         chip = self.dp_index // 2 % chips
-        mine = pick(jnp.stack(slices), chip ^ jnp.arange(chips), 0)[:, None]
-        other = self.swap(mine, 1)
-        out = join(self.core[None], mine, other, widths)
-        if not small:
-            return out
-        panel = mine[0, 0, -1].astype(F32) + other[0, 0, -1].astype(F32)
-        return out, panel.reshape(-1)[:small]
+        return pick(jnp.stack(slices), chip ^ jnp.arange(chips), 0)[:, None]
 
     def turned(self, x, axis):
         blocks = x.reshape(x.shape[:axis] + (self.mp, -1) + x.shape[axis + 1 :])
@@ -729,7 +739,7 @@
     lat_blocks = net.ring_gather(lat_norm)
     feed_blocks = [feed_slice, net.shift(after(feed_slice, lat_blocks[-1]), 1)]
     head_slices = after(head_slices, lat_blocks[-1])
-    query_t, key_t, value_t = net.both_cores(head_own, head_slices)
+    query_t, key_t, value_t = net.both_cores(head_own, head_slices, net.swap(head_slices, 1))
 
     real_seg = jnp.where(byte_pad == 1, byte_seg, -1)
     real_seg = lax.dynamic_slice_in_dim(real_seg, mp_index * byte_len, byte_len, 1)
@@ -743,9 +753,6 @@
     lat_all = jnp.stack(lat_blocks)
     lat_flat = after(lat_all.reshape(rows * lat_len, lat_width), keys)
     queries = (dot(lat_flat, query_t, NT) * score_scale).astype(BF16).reshape(lat_all.shape)
-    queries, feed_blocks[2] = lax.optimization_barrier((queries, feed_blocks[2]))
-    for _ in range(3, mp):
-        feed_blocks.append(net.shift(feed_blocks[-1], 1))
     (lse_part,) = row_call(
         lse_kernel,
         "lse",
@@ -753,13 +760,16 @@
         [shape((rows, heads, lat_len), F32)],
         unit,
     )
-    lse_part, feed_blocks[-1] = lax.optimization_barrier((lse_part, feed_blocks[-1]))
+    lse_part, feed_blocks[2] = lax.optimization_barrier((lse_part, feed_blocks[2]))
+    for _ in range(3, mp):
+        feed_blocks.append(net.shift(feed_blocks[-1], 1))
     lse_parts = [lse_part] + [net.shift(lse_part, step) for step in range(1, mp)]
+    values = dot(after(byte_norm, lse_part), value_t, NT).astype(BF16)
+    values = values.reshape(rows, byte_len, lat_width)
+    values, feed_blocks[-1] = lax.optimization_barrier((values, feed_blocks[-1]))
     feed_slices = net.gather_chips(jnp.stack([block[:-1] for block in feed_blocks[1:]]), lines)
     b_up_all = from_three_parts(jnp.stack([block[-1] for block in feed_blocks]), b_up.shape[0])
     b_up_all = net.turned(b_up_all, 0)
-    values = dot(after(byte_norm, lse_part), value_t, NT).astype(BF16)
-    values = values.reshape(rows, byte_len, lat_width)
     lat_shape = shape(lat_all.shape, BF16)
     parts, lse = row_call(
         functools.partial(attend_kernel, own_lat),
@@ -771,10 +781,12 @@
     attended = parts[1]
     for step in range(2, mp + 1):
         moved = net.shift(attended, 1)
-        if step == 2:
+        if step == mp - 1:
             feed_slices = after(feed_slices, moved)
-            out_w, up_t, down_w = net.both_cores(feed_own, feed_slices)
-        if step == mp - 1:
+            out_w, up_t, down_w = net.both_cores(
+                feed_own, feed_slices, net.swap(feed_slices, 1)
+            )
+        if step == mp:
             moved, out_w = lax.optimization_barrier((moved, out_w))
         attended = add(moved, parts[step % mp])
     attended = attended.reshape(own_lines, lat_width)
@@ -789,7 +801,6 @@
         grad_hidden,
         grad_attn,
         grad_att,
-        delta,
         feed_vectors,
     ) = block_call(
         feed_kernel,
@@ -800,27 +811,23 @@
         + [(w, False) for w in (out_w, up_t, down_w)]
         + [(attended, True)],
         [(wide, True), (whole, True), (whole, True), (whole, True), (wide, True), (whole, True)]
-        + [(whole, True), (shape((own_lines, heads), F32), True)]
+        + [(shape((own_lines, lat_width + LANES), BF16), True)]
         + [(shape((4, lat_width), F32), False)],
         8 * own_lines * lat_width * lat_width,
         [pltpu.VMEM((own_lines, lat_width), F32)],
     )
 
-    grads = [grad_att.reshape(rows, own_lat, lat_width)]
+    grads = [grad_att.reshape(rows, own_lat, lat_width + LANES)]
     block = net.shift(grads[0], 1)
     feed_kept, feed_sent = net.split_core(
         [(activated, cotangent.astype(BF16)), (grad_pre, mid_norm), (attended, grad_attn)], lines
     )
-    delta = delta.reshape(rows, own_lat, heads).transpose(0, 2, 1)
-    delta = jnp.concatenate([delta] + [net.shift(delta, step) for step in range(1, mp)], 2)
-    block, feed_kept, feed_sent, delta = lax.optimization_barrier(
-        (block, feed_kept, feed_sent, delta)
-    )
+    block, feed_kept, feed_sent = lax.optimization_barrier((block, feed_kept, feed_sent))
     grads.append(block)
     feed_sums = add_packed(feed_kept, net.swap(feed_sent, 1))
     if mp > 2:
         block = net.shift(grads[-1], 1)
-        block, feed_sums = lax.optimization_barrier((block, feed_sums))
+        block, *feed_sums = lax.optimization_barrier((block, *feed_sums))
         grads.append(block)
     for _ in range(3, mp):
         grads.append(net.shift(grads[-1], 1))
@@ -831,7 +838,7 @@
     back, grad_keys, grad_values = row_call(
         attend_back_kernel,
         "attend_back",
-        [queries, keys, values, lat_row, byte_col, lse, delta] + grads,
+        [queries, keys, values, lat_row, byte_col, lse] + grads,
         [lat_shape] + [shape((rows, byte_len, lat_width), BF16)] * 2,
         5 * unit,
     )
@@ -839,27 +846,24 @@
     grad_values = grad_values.reshape(-1, lat_width)
     total = back[1]
     moved = net.shift(total, 1)
-    products = [dot(grad_values, byte_norm, TN).astype(BF16)]
+    products = [dot(grad, byte_norm, TN).astype(BF16) for grad in (grad_keys, grad_values)]
     while feed_sums[0][1]:
         feed_sums = net.link_step(feed_sums)
-    moved, products[0], feed_half = lax.optimization_barrier(
-        (moved, products[0], net.arrays(feed_sums))
+    moved, products, feed_half = lax.optimization_barrier(
+        (moved, products, net.arrays(feed_sums))
     )
     feed_parts = net.blocks_back(jnp.concatenate(feed_half, 1), lines)
     feed_total = feed_parts[1]
     total = add(moved, back[2 % mp])
-    grad_keys, back_flat = lax.optimization_barrier(
-        (grad_keys, back.reshape(-1, lat_width), moved)
-    )[:2]
-    products.insert(0, dot(grad_keys, byte_norm, TN).astype(BF16))
+    back_flat = after(back.reshape(-1, lat_width), total, feed_total)
     products.insert(0, dot(back_flat, lat_flat, TN).astype(BF16))
     kept, sent = split(net.core[None], products, net.cut(lines)[0], lines)
-    if mp > 2:
-        moved, feed_moved = net.shift(total, 1), net.shift(feed_total, 1)
-        moved, feed_moved, sent = lax.optimization_barrier((moved, feed_moved, sent))
-        total = add(moved, back[3 % mp])
-        feed_total = add(feed_moved, feed_parts[2])
-    head_sums = net.link_pieces(add_packed(kept, net.swap(sent, 1)), lines)
+    head_sums = add_packed(kept, net.swap(sent, 1))
+    added = head_sums[0]
+    feed_moved, added = lax.optimization_barrier((net.shift(feed_total, 1), added))
+    feed_total = add(feed_moved, feed_parts[2 % mp])
+    total = after(total, added)
+    head_sums = net.link_pieces(head_sums, lines)
     if head_sums[0][1]:
         head_sums = net.link_step(head_sums)
     grad_bytes, grad_byte_gain = block_call(
@@ -867,34 +871,39 @@
         "byte_back",
         byte_len,
         [(byte_in, True), (byte_gain[None], False), (key_t, False), (value_t, False)]
-        + [(after(grad_keys, sent), True), (grad_values, True)],
+        + [(after(grad_keys, added), True), (grad_values, True)],
         [(shape(byte_in.shape, F32), True), (shape((1, byte_width), F32), False)],
         4 * rows * byte_len * lat_width * byte_width,
     )
-    if mp > 3:
-        moved, feed_moved = net.shift(total, 1), net.shift(feed_total, 1)
-        grad_bytes, moved, feed_moved, done = lax.optimization_barrier(
-            (grad_bytes, moved, feed_moved, net.arrays(head_sums))
-        )
-        head_sums = net.with_arrays(head_sums, done)
-        total = add(moved, back[4 % mp])
-        feed_total = add(feed_moved, feed_parts[3])
-    for step in range(5, mp + 1):
+    for step in range(3, mp + 1):
+        if step == 4:
+            total = after(total, grad_bytes)
         total = add(net.shift(total, 1), back[step % mp])
-        feed_total = add(net.shift(feed_total, 1), feed_parts[step - 1])
+    grad_bytes, done = lax.optimization_barrier((grad_bytes, net.arrays(head_sums)))
+    head_sums = net.with_arrays(head_sums, done)
     while head_sums[0][1]:
         head_sums = net.link_step(head_sums)
-    feed_total = add(net.shift(feed_total, 1), feed_parts[0])
-    feed_total, done = lax.optimization_barrier((feed_total, net.arrays(head_sums)))
-    head_sums = net.with_arrays(head_sums, done)
-    feed_grads = net.finish_sum(feed_total, lines, feed_widths)
+    for step in range(3, mp + 1):
+        if step == mp:
+            feed_total = after(feed_total, *net.arrays(head_sums))
+        feed_total = add(net.shift(feed_total, 1), feed_parts[step % mp])
+    feed_mine = net.share(feed_total, lines)
     grad_lat_norm = score_scale * dot(total.reshape(own_lines, lat_width), query_t)
     grad_lat_back, grad_latent_gain = norm_back(grad_lat_norm, lat_hat, lat_inv, latent_gain)
     grad_latents = grad_hidden + grad_lat_back
     small = jnp.concatenate([grad_byte_gain[0], grad_latent_gain, feed_vectors.reshape(-1)])
     head_sums = jnp.concatenate(net.arrays(head_sums), 1)
-    head_total = net.sum_blocks(head_sums, lines, small)
-    head_grads, sums = net.finish_sum(head_total, lines, head_widths, small.size)
+    head_total = net.sum_blocks(head_sums, lines)
+    panel = small.astype(BF16)
+    panel = jnp.pad(panel, (0, head_total[0].size - panel.size)).reshape(1, -1, LANES)
+    panel = add(panel, *[net.shift(panel, step) for step in range(1, mp)])
+    head_total, panel, feed_mine = lax.optimization_barrier((head_total, panel, feed_mine))
+    head_mine = net.share(jnp.concatenate([head_total, panel]), lines, True)
+    feed_other, head_other = net.swap(feed_mine, 1), net.swap(head_mine, 1)
+    feed_grads = join(net.core[None], feed_mine, feed_other, feed_widths, [F32, BF16, F32])
+    head_grads = join(net.core[None], head_mine, head_other, head_widths, [BF16] * 3)
+    sums = head_mine[0, 0, -1].astype(F32) + head_other[0, 0, -1].astype(F32)
+    sums = sums.reshape(-1)[: small.size]
     sums = [sums[:byte_width]] + list(sums[byte_width:].reshape(5, lat_width))
     own_units = b_up.shape[0]
     return (
@@ -907,11 +916,11 @@
         head_grads[0].astype(F32).T * score_scale,
         head_grads[1].astype(F32).T,
         head_grads[2].astype(F32).T,
-        feed_grads[2].astype(F32),
+        feed_grads[2],
         sums[4],
         feed_grads[1].astype(F32).T,
         lax.dynamic_slice_in_dim(sums[3], mp_index * own_units, own_units, 0),
-        feed_grads[0].astype(F32),
+        feed_grads[0],
         sums[5],
     )
 

time: 511 us -> 495 us (0.969)
  waiting for transfers between devices: 202 us -> 178 us
  starting transfers between devices: 59.8 us -> 74.7 us
    ppermute x20, waiting for transfers between devices: 42.9 us -> 24.6 us  [swap(): return lax.ppermute(x, 'dp', [(i, i ^ bit) for i in range(self.dp)])]
    ppermute x20, starting transfers between devices: 22.9 us -> 33.2 us  [swap(): return lax.ppermute(x, 'dp', [(i, i ^ bit) for i in range(self.dp)])]
    all_gather x2, waiting for transfers between devices: 13.5 us -> 5.99 us  [gather_chips(): lax.all_gather(x, 'dp', axis=0, axis_index_groups=self.chip_groups(chips))]
    slice x8 -> x3, local copies, waits for them, and re-layouts: 7.04 us -> 0.05 us  [share(): slices = [jnp.concatenate([piece[:-1], panel[None]]) for piece in slices]]
    convert_element_type x19 -> x20, other arithmetic: 15.6 us -> 11.4 us  [add(): return total.astype(first.dtype)]
    unnamed x102 -> x104, local copies, waits for them, and re-layouts: 11.6 us -> 9.52 us
  transfers between devices with their start and end apart: 52 -> 52, of which waited for: 33 -> 26; matrix products, arithmetic and copies ran while one was open for 15% -> 14% of each run, Pallas kernels for 19% -> 19%
where the time goes in v5:
time: 495 us; the launch traced here: 486 us
  waiting for transfers between devices  178 us (36%)
  Pallas kernels  112 us (23%)
  starting transfers between devices  74.7 us (15%)
  local copies, waits for them, and re-layouts  40.3 us (8%)
  matrix products  34.5 us (7%)
  other arithmetic  31.2 us (6%)
  between operations  15.6 us (3%)
    ppermute x30, waiting for transfers between devices, shift(): return lax.ppermute(x, 'mp', ring(self.mp, step))  148 us
    ppermute x30, starting transfers between devices, shift(): return lax.ppermute(x, 'mp', ring(self.mp, step))  41.5 us
    pallas_call x3, Pallas kernels, row_call(): pl.pallas_call(kernel, grid=(outs[-1].shape[0],), in_specs=[spec(a.shape)...  34.7 us
    dot_general x7, matrix products, dot(): return lax.dot_general(a, b, dims, preferred_element_type=F32)  34.5 us
    pallas_call x3, Pallas kernels, block_call(): pl.pallas_call(kernel, grid=(args[0][0].shape[0] // lines,), in_specs=[sp...  33.9 us
    ppermute x20, starting transfers between devices, swap(): return lax.ppermute(x, 'dp', [(i, i ^ bit) for i in range(self.dp)])  33.2 us
    ppermute x20, waiting for transfers between devices, swap(): return lax.ppermute(x, 'dp', [(i, i ^ bit) for i in range(self.dp)])  24.6 us
    pallas_call x2, Pallas kernels, join_own(): pl.pallas_call(functools.partial(join_own_kernel, widths), grid_spec=pltp...  14 us
  transfers between devices with their start and end apart: 52, of which 26 were waited for; matrix products, arithmetic and copies ran while one was open for 14% of the time, Pallas kernels for 19%

profile of v5, /device:TPU:9, one launch (start us, length us, event | category | flops | bytes accessed | tf_op | source)
XLA Modules:
  0.0 486.3 jit_solution(7006462448363511055)
XLA Ops:
  15.7 5.7 %byte_norm.1 = bf16[2048,768]{1,0:T(8,128)(2,1)} custom-call(f32[2048,768]{1,0:T(8,128)} %bitcast.226, f32[1,768]{1,0:T(1,128)} %broadcast_in_dim.27.gain_ref), custom_call_target="tpu_custom_call" | custom-call | flops 1966080 | bytes 786816 | tf_op jit(solution)/shard_map/byte_norm/pallas_call | solution.py:275
  22.4 16.1 %collective-permute-done.1 = bf16[11,80,128]{2,0,1:T(8,128)(2,1)} collective-permute-done((bf16[11,80,128]{2,0,1:T(8,128)(2,1)S(1)}, bf16[11,80,128]{2,0,1:T(8,128)(2,1)}, u32[]{:S(2)}, u32[]{:S(2)}) %collective-permute-start.1) | collective-permute-done | bytes 225312 | tf_op jit(solution)/shard_map/ppermute | solution.py:560
  43.9 15.9 %collective-permute-done.3 = bf16[4,64,1280]{2,1,0:T(8,128)(2,1)S(1)} collective-permute-done((bf16[4,64,1280]{2,1,0:T(8,128)(2,1)S(1)}, bf16[4,64,1280]{2,1,0:T(8,128)(2,1)S(1)}, u32[]{:S(2)}, u32[]{:S(2)}) %collective-permute-start.3) | collective-permute-done | bytes 655392 | tf_op jit(solution)/shard_map/ppermute | solution.py:560
  60.9 14.8 %collective-permute-done.4 = bf16[4,64,1280]{2,1,0:T(8,128)(2,1)S(1)} collective-permute-done((bf16[4,64,1280]{2,1,0:T(8,128)(2,1)S(1)}, bf16[4,64,1280]{2,1,0:T(8,128)(2,1)S(1)}, u32[]{:S(2)}, u32[]{:S(2)}) %collective-permute-start.4) | collective-permute-done | bytes 655392 | tf_op jit(solution)/shard_map/ppermute | solution.py:560
  77.2 13.6 %collective-permute-done.5 = bf16[4,64,1280]{2,1,0:T(8,128)(2,1)} collective-permute-done((bf16[4,64,1280]{2,1,0:T(8,128)(2,1)S(1)}, bf16[4,64,1280]{2,1,0:T(8,128)(2,1)}, u32[]{:S(2)}, u32[]{:S(2)}) %collective-permute-start.5) | collective-permute-done | bytes 655392 | tf_op jit(solution)/shard_map/ppermute | solution.py:560
  102.4 6.3 %join_own.2 = (bf16[1280,1280]{1,0:T(8,128)(2,1)}, bf16[1280,768]{1,0:T(8,128)(2,1)S(1)}, bf16[1280,768]{1,0:T(8,128)(2,1)S(1)}) custom-call(s32[2]{0:T(128)S(1)} %pad_add_fusion.where_ref, bf16[320,1280]{1,0:T(8,128)(2,1)S(1)} %bitcast.216, bf16[320,768]{1,0:T(8,128)(2,1)S(1)} %bitcast.221, bf16[320,768]{1,0:T(8,128)(2,1)S(1)} %bitcast.220, ...), custom_call_target="tpu_custom_call" | custom-call | bytes 1351680 | tf_op jit(solution)/shard_map/join_own/pallas_call | solution.py:437
  108.8 6.0 %convolution_convert_fusion.2 = bf16[2048,1280]{1,0:T(8,128)(2,1)} fusion(bf16[2048,768]{1,0:T(8,128)(2,1)S(1)} %copy-done.17, bf16[1280,768]{1,0:T(8,128)(2,1)S(1)} %get-tuple-element.103.key_ref), kind=kOutput, calls=%fused_computation.6 | convolution fusion | flops 4029153280 | bytes 10354688 | tf_op jit(solution)/shard_map/dot_general | solution.py:22
  118.7 8.2 %lse.1.refs_0_ = f32[4,8,256]{2,1,0:T(8,128)S(1)} custom-call(bf16[4,4,64,1280]{3,2,1,0:T(8,128)(2,1)S(1)} %bitcast.208, bf16[4,512,1280]{2,1,0:T(8,128)(2,1)} %bitcast.222, s32[4,1,256]{2,1,0:T(1,128)S(1)} %broadcast_in_dim_reshape.10.lat_seg_ref, s32[4,512,1]{2,1,0:T(8,128)S(1)} %copy-done.1), custom_call_target="tpu_custom_call" | custom-call | flops 268435456 | bytes 984576 | tf_op jit(solution)/shard_map/lse/pallas_call | solution.py:257
  130.7 6.0 %convolution_convert_fusion.1 = bf16[2048,1280]{1,0:T(8,128)(2,1)} fusion(bf16[2048,768]{1,0:T(8,128)(2,1)S(1)} %copy-done.17, bf16[1280,768]{1,0:T(8,128)(2,1)S(1)} %get-tuple-element.109.value_ref), kind=kOutput, calls=%fused_computation.5 | convolution fusion | flops 4029153280 | bytes 10354688 | tf_op jit(solution)/shard_map/dot_general | solution.py:22
  146.2 9.7 %attend.1 = (bf16[4,4,64,1280]{3,2,1,0:T(8,128)(2,1)S(1)}, f32[4,8,256]{2,1,0:T(8,128)S(1)}) custom-call(bf16[4,4,64,1280]{3,2,1,0:T(8,128)(2,1)} %bitcast.209, bf16[4,512,1280]{2,1,0:T(8,128)(2,1)} %bitcast.223, bf16[4,512,1280]{2,1,0:T(8,128)(2,1)} %bitcast.228, s32[4,1,256]{2,1,0:T(1,128)S(1)} %broadcast_in_dim_reshape.10.lat_seg_ref, ...), custom_call_target="tpu_custom_call" | custom-call | flops 536870912 | bytes 1656320 | tf_op jit(solution)/shard_map/attend/pallas_call | solution.py:257
  156.0 13.1 %collective-permute-done.13 = bf16[4,64,1280]{2,1,0:T(8,128)(2,1)S(1)} collective-permute-done((bf16[4,64,1280]{2,1,0:T(8,128)(2,1)S(1)}, bf16[4,64,1280]{2,1,0:T(8,128)(2,1)S(1)}, u32[]{:S(2)}, u32[]{:S(2)}) %collective-permute-start.13) | collective-permute-done | bytes 655392 | tf_op jit(solution)/shard_map/ppermute | solution.py:560
  170.3 13.6 %collective-permute-done.14 = bf16[4,64,1280]{2,1,0:T(8,128)(2,1)} collective-permute-done((bf16[4,64,1280]{2,1,0:T(8,128)(2,1)S(1)}, bf16[4,64,1280]{2,1,0:T(8,128)(2,1)}, u32[]{:S(2)}, u32[]{:S(2)}) %collective-permute-start.14) | collective-permute-done | bytes 655392 | tf_op jit(solution)/shard_map/ppermute | solution.py:560
  183.8 6.0 %all-gather.7.cloned.1.call-done = bf16[12,15,80,128]{3,2,1,0:T(8,128)(2,1)} async-done(((bf16[3,15,80,128]{3,2,1,0:T(8,128)(2,1)}), bf16[12,15,80,128]{3,2,1,0:T(8,128)(2,1)}) %all-gather.7.cloned.1.call-update) | async-done | bytes 3686416 | tf_op jit(solution)/shard_map/all_gather | solution.py:600
  206.8 7.7 %join_own.3 = (bf16[1280,1280]{1,0:T(8,128)(2,1)S(1)}, bf16[1280,1280]{1,0:T(8,128)(2,1)}, bf16[1280,1280]{1,0:T(8,128)(2,1)}) custom-call(s32[2]{0:T(128)S(1)} %pad_add_fusion.where_ref, bf16[320,1280]{1,0:T(8,128)(2,1)S(1)} %copy-done.10, bf16[320,1280]{1,0:T(8,128)(2,1)S(1)} %bitcast.217, bf16[320,1280]{1,0:T(8,128)(2,1)S(1)} %copy-done.8, ...), custom_call_target="tpu_custom_call" | custom-call | bytes 1843200 | tf_op jit(solution)/shard_map/join_own/pallas_call | solution.py:437
  219.0 12.6 %feed.1 = (f32[256,1280]{1,0:T(8,128)}, bf16[256,1280]{1,0:T(8,128)(2,1)}, bf16[256,1280]{1,0:T(8,128)(2,1)}, bf16[256,1280]{1,0:T(8,128)(2,1)}, f32[256,1280]{1...) custom-call(f32[256,1280]{1,0:T(8,128)} %bitcast.225, ...), custom_call_target="tpu_custom_call" | custom-call | flops 419430400 | bytes 1640960 | tf_op jit(solution)/shard_map/feed/pallas_call | solution.py:275
  233.8 8.9 %grads.1 = (bf16[4,4,15,80,128]{4,3,2,1,0:T(8,128)(2,1)}, bf16[4,4,15,80,128]{4,3,2,1,0:T(8,128)(2,1)}) custom-call(s32[1]{0:T(128)} %bitcast.14.core_ref, bf16[256,1280]{1,0:T(8,128)(2,1)} %get-tuple-element.122.refs_0_, bf16[256,1280]{1,0:T(8,128)(2,1)} %get-tuple-element.123.refs_1_, bf16[256,1280]{1,0:T(8,128)(2,1)} %bitcast.231, ...), custom_call_target="tpu_custom_call" | custom-call | flops 314572800 | bytes 491520 | tf_op jit(solution)/shard_map/grads/pallas_call | solution.py:500
  242.7 7.4 %collective-permute-done.17.refs_1_ = bf16[4,64,1408]{2,1,0:T(8,128)(2,1)S(1)} collective-permute-done((bf16[4,64,1408]{2,1,0:T(8,128)(2,1)}, bf16[4,64,1408]{2,1,0:T(8,128)(2,1)S(1)}, u32[]{:S(2)}, u32[]{:S(2)}) %collective-permute-start.17) | collective-permute-done | bytes 720928 | tf_op jit(solution)/shard_map/ppermute | solution.py:560
  251.6 8.0 %collective-permute-done.19.b_ref = bf16[4,4,15,80,128]{4,3,2,1,0:T(8,128)(2,1)} collective-permute-done((bf16[4,4,15,80,128]{4,3,2,1,0:T(8,128)(2,1)}, bf16[4,4,15,80,128]{4,3,2,1,0:T(8,128)(2,1)}, u32[]{:S(2)}, u32[]{:S(2)}) %collective-permute-start.19) | collective-permute-done | bytes 4915232 | tf_op jit(solution)/shard_map/ppermute | solution.py:557
  259.6 6.7 %add_packed.2 = (bf16[4,4,8,80,128]{4,3,2,1,0:T(8,128)(2,1)}, bf16[4,4,7,80,128]{4,3,2,1,0:T(8,128)(2,1)}) custom-call(bf16[4,4,15,80,128]{4,3,2,1,0:T(8,128)(2,1)} %get-tuple-element.129.a_ref, bf16[4,4,15,80,128]{4,3,2,1,0:T(8,128)(2,1)} %collective-permute-done.19.b_ref), custom_call_target="tpu_custom_call" | custom-call | bytes 1228800 | tf_op jit(solution)/shard_map/add_packed/pallas_call | solution.py:482
  271.2 9.9 %collective-permute-start.20 = (bf16[4,64,1408]{2,1,0:T(8,128)(2,1)S(1)}, bf16[4,64,1408]{2,1,0:T(8,128)(2,1)S(1)}, u32[]{:S(2)}, u32[]{:S(2)}) collective-permute-start(bf16[4,64,1408]{2,1,0:T(8,128)(2,1)S(1)} %collective-permute-done.18.refs_2_), channel_id=1, source_target_pairs={{0,1},{1,2},{2,3},{3,0},{4,5},{5,6},{6,7},{7,4},{8,9},{9,10},{10,1... | collective-permute-start | bytes 2162696 | tf_op jit(solution)/shard_map/ppermute | solution.py:560
  286.6 13.4 %collective-permute-done.20.refs_3_ = bf16[4,64,1408]{2,1,0:T(8,128)(2,1)S(1)} collective-permute-done((bf16[4,64,1408]{2,1,0:T(8,128)(2,1)S(1)}, bf16[4,64,1408]{2,1,0:T(8,128)(2,1)S(1)}, u32[]{:S(2)}, u32[]{:S(2)}) %collective-permute-start.20) | collective-permute-done | bytes 720928 | tf_op jit(solution)/shard_map/ppermute | solution.py:560
  299.9 16.9 %attend_back.1 = (bf16[4,4,64,1280]{3,2,1,0:T(8,128)(2,1)}, bf16[4,512,1280]{2,1,0:T(8,128)(2,1)}, bf16[4,512,1280]{2,1,0:T(8,128)(2,1)}) custom-call(bf16[4,4,64,1280]{3,2,1,0:T(8,128)(2,1)} %bitcast.210, bf16[4,512,1280]{2,1,0:T(8,128)(2,1)} %bitcast.224, bf16[4,512,1280]{2,1,0:T(8,128)(2,1)} %bitcast.229, ...), custom_call_target="tpu_custom_call" | custom-call | flops 1342177280 | bytes 2004480 | tf_op jit(solution)/shard_map/attend_back/pallas_call | solution.py:257
  318.2 6.9 %convolution_convert_fusion.3.refs_2_ = bf16[1280,768]{1,0:T(8,128)(2,1)S(1)} fusion(bf16[2048,1280]{1,0:T(8,128)(2,1)} %bitcast.237, bf16[2048,768]{1,0:T(8,128)(2,1)S(1)} %copy-done.18), kind=kOutput, calls=%fused_computation.8 | convolution fusion | flops 4027514880 | bytes 10354688 | tf_op jit(solution)/shard_map/dot_general | solution.py:22
  332.9 5.8 %collective-permute-done.25 = bf16[4,7,80,128]{3,2,1,0:T(8,128)(2,1)S(1)} collective-permute-done((bf16[4,7,80,128]{3,2,1,0:T(8,128)(2,1)S(1)}, bf16[4,7,80,128]{3,2,1,0:T(8,128)(2,1)S(1)}, u32[]{:S(2)}, u32[]{:S(2)}) %collective-permute-start.25) | collective-permute-done | bytes 573472 | tf_op jit(solution)/shard_map/ppermute | solution.py:557
  344.9 5.2 %convolution_convert_fusion.refs_0_ = bf16[1280,1280]{1,0:T(8,128)(2,1)} fusion(bf16[1024,1280]{1,0:T(8,128)(2,1)S(1)} %bitcast.248, bf16[1024,1280]{1,0:T(8,128)(2,1)S(1)} %bitcast.244), kind=kOutput, calls=%fused_computation.4 | convolution fusion | flops 3357081600 | bytes 8519680 | tf_op jit(solution)/shard_map/dot_general | solution.py:22
  350.2 5.8 %split.1 = (bf16[4,4,11,80,128]{4,3,2,1,0:T(8,128)(2,1)}, bf16[4,4,11,80,128]{4,3,2,1,0:T(8,128)(2,1)}) custom-call(s32[1]{0:T(128)} %bitcast.14.core_ref, bf16[1280,1280]{1,0:T(8,128)(2,1)} %convolution_convert_fusion.refs_0_, bf16[1280,768]{1,0:T(8,128)(2,1)S(1)} %convolution_convert_fusion.4.refs_1_, bf16[1280,768]{1,0:T(8,128)(2,1)S(1)} %convolution_convert_fusion.3.refs_2_), custom_call_target="tpu_custom_call" | custom-call | bytes 1802240 | tf_op jit(solution)/shard_map/split/pallas_call | solution.py:464
  364.8 5.5 %add_packed.3 = (bf16[4,4,6,80,128]{4,3,2,1,0:T(8,128)(2,1)}, bf16[4,4,5,80,128]{4,3,2,1,0:T(8,128)(2,1)}) custom-call(bf16[4,4,11,80,128]{4,3,2,1,0:T(8,128)(2,1)} %get-tuple-element.145.a_ref, bf16[4,4,11,80,128]{4,3,2,1,0:T(8,128)(2,1)} %collective-permute-done.27.b_ref), custom_call_target="tpu_custom_call" | custom-call | bytes 901120 | tf_op jit(solution)/shard_map/add_packed/pallas_call | solution.py:482
  380.4 15.6 %byte_back.1 = (f32[2048,768]{1,0:T(8,128)}, f32[1,768]{1,0:T(1,128)}) custom-call(f32[2048,768]{1,0:T(8,128)} %bitcast.227, f32[1,768]{1,0:T(1,128)} %broadcast_in_dim.27.gain_ref, bf16[1280,768]{1,0:T(8,128)(2,1)} %copy-done.5, bf16[1280,768]{1,0:T(8,128)(2,1)} %copy-done.6, bf16[2048,1280]{1,0:T(8,128)(2,1)} %bitcast.233, bf16[2048,1280]{1,0:T(8,128)(2,1)} %bitcast.238), custom_call_target="tpu_custom_call" | custom-call | flops 1006632960 | bytes 2589056 | tf_op jit(solution)/shard_map/byte_back/pallas_call | solution.py:275
  403.1 10.8 %collective-permute-done.31 = bf16[4,64,1280]{2,1,0:T(8,128)(2,1)S(1)} collective-permute-done((bf16[4,64,1280]{2,1,0:T(8,128)(2,1)S(1)}, bf16[4,64,1280]{2,1,0:T(8,128)(2,1)S(1)}, u32[]{:S(2)}, u32[]{:S(2)}) %collective-permute-start.31) | collective-permute-done | bytes 655392 | tf_op jit(solution)/shard_map/ppermute | solution.py:560
  427.5 7.5 %collective-permute-done.39 = bf16[1,80,128]{2,1,0:T(8,128)(2,1)S(1)} collective-permute-done((bf16[1,80,128]{2,1,0:T(8,128)(2,1)S(1)}, bf16[1,80,128]{2,1,0:T(8,128)(2,1)S(1)}, u32[]{:S(2)}, u32[]{:S(2)}) %collective-permute-start.39) | collective-permute-done | bytes 20512 | tf_op jit(solution)/shard_map/ppermute | solution.py:560
  437.4 5.2 %collective-permute-done.35 = bf16[11,80,128]{2,1,0:T(8,128)(2,1)S(1)} collective-permute-done((bf16[11,80,128]{2,1,0:T(8,128)(2,1)S(1)}, bf16[11,80,128]{2,1,0:T(8,128)(2,1)S(1)}, u32[]{:S(2)}, u32[]{:S(2)}) %collective-permute-start.35) | collective-permute-done | bytes 225312 | tf_op jit(solution)/shard_map/ppermute | solution.py:560
  461.3 5.3 %collective-permute-start.48 = (bf16[4,1,12,80,128]{4,3,2,1,0:T(8,128)(2,1)S(1)}, bf16[4,1,12,80,128]{4,3,2,1,0:T(8,128)(2,1)S(1)}, u32[]{:S(2)}, u32[]{:S(2)}) collective-permute-start(bf16[4,1,12,80,128]{4,3,2,1,0:T(8,128)(2,1)S(1)} %bitcast.213), channel_id=1, source_target_pairs={{0,4},{4,0},{8,12},{12,8},{16,20},{20,16},{24,28},{28,24},{1,5},{5... | collective-permute-start | bytes 2949128 | tf_op jit(solution)/shard_map/ppermute | solution.py:557
  (318 shorter events, 170.7 us)
Async XLA Ops:
  7.2 83.6 %all-gather.5.cloned.1.call-start = ((), (), s32[]{:S(2)}) async-start(), calls=%async_computation | async-start | bytes 3379200 | tf_op jit(solution)/shard_map/all_gather | solution.py:600
  9.7 12.7 %collective-permute-start = (bf16[11,80,128]{2,0,1:T(8,128)(2,1)S(1)}, bf16[11,80,128]{2,0,1:T(8,128)(2,1)S(1)}, u32[]{:S(2)}, u32[]{:S(2)}) collective-permute-start(bf16[11,80,128]{2,0,1:T(8,128)(2,1)S(1)} %pad_maximum_fusion.9), channel_id=1, source_target_pairs={{0,1},{1,2},{2,3},{3,0},{4,5},{5,6},{6,7},{7,4},{8,9},{9,10},{10,1... | collective-permute-start | bytes 675848 | tf_op jit(solution)/shard_map/ppermute | solution.py:560
  11.0 27.4 %collective-permute-start.1 = (bf16[11,80,128]{2,0,1:T(8,128)(2,1)S(1)}, bf16[11,80,128]{2,0,1:T(8,128)(2,1)}, u32[]{:S(2)}, u32[]{:S(2)}) collective-permute-start(bf16[11,80,128]{2,0,1:T(8,128)(2,1)S(1)} %pad_maximum_fusion.9), channel_id=1, source_target_pairs={{0,2},{1,3},{2,0},{3,1},{4,6},{5,7},{6,4},{7,5},{8,10},{9,11},{10,... | collective-permute-start | bytes 675848 | tf_op jit(solution)/shard_map/ppermute | solution.py:560
  12.1 29.3 %collective-permute-start.2 = (bf16[11,80,128]{2,0,1:T(8,128)(2,1)S(1)}, bf16[11,80,128]{2,0,1:T(8,128)(2,1)}, u32[]{:S(2)}, u32[]{:S(2)}) collective-permute-start(bf16[11,80,128]{2,0,1:T(8,128)(2,1)S(1)} %pad_maximum_fusion.9), channel_id=1, source_target_pairs={{0,3},{1,0},{2,1},{3,2},{4,7},{5,4},{6,5},{7,6},{8,11},{9,8},{10,9... | collective-permute-start | bytes 675848 | tf_op jit(solution)/shard_map/ppermute | solution.py:560
  43.8 146.1 %all-gather.7.cloned.1.call-start = ((), (), s32[]{:S(2)}) async-start(), calls=%async_computation.1 | async-start | bytes 4608000 | tf_op jit(solution)/shard_map/all_gather | solution.py:600
  43.8 16.0 %collective-permute-start.3 = (bf16[4,64,1280]{2,1,0:T(8,128)(2,1)S(1)}, bf16[4,64,1280]{2,1,0:T(8,128)(2,1)S(1)}, u32[]{:S(2)}, u32[]{:S(2)}) collective-permute-start(bf16[4,64,1280]{2,1,0:T(8,128)(2,1)S(1)} %multiply_convert_fusion.1), channel_id=1, source_target_pairs={{0,1},{1,2},{2,3},{3,0},{4,5},{5,6},{6,7},{7,4},{8,9},{9,10},{10,1... | collective-permute-start | bytes 1966088 | tf_op jit(solution)/shard_map/ppermute | solution.py:560
  60.6 15.1 %collective-permute-start.4 = (bf16[4,64,1280]{2,1,0:T(8,128)(2,1)S(1)}, bf16[4,64,1280]{2,1,0:T(8,128)(2,1)S(1)}, u32[]{:S(2)}, u32[]{:S(2)}) collective-permute-start(bf16[4,64,1280]{2,1,0:T(8,128)(2,1)S(1)} %collective-permute-done.3), channel_id=1, source_target_pairs={{0,1},{1,2},{2,3},{3,0},{4,5},{5,6},{6,7},{7,4},{8,9},{9,10},{10,1... | collective-permute-start | bytes 1966088 | tf_op jit(solution)/shard_map/ppermute | solution.py:560
  76.5 14.3 %collective-permute-start.5 = (bf16[4,64,1280]{2,1,0:T(8,128)(2,1)S(1)}, bf16[4,64,1280]{2,1,0:T(8,128)(2,1)}, u32[]{:S(2)}, u32[]{:S(2)}) collective-permute-start(bf16[4,64,1280]{2,1,0:T(8,128)(2,1)S(1)} %collective-permute-done.4), channel_id=1, source_target_pairs={{0,1},{1,2},{2,3},{3,0},{4,5},{5,6},{6,7},{7,4},{8,9},{9,10},{10,1... | collective-permute-start | bytes 1966088 | tf_op jit(solution)/shard_map/ppermute | solution.py:560
  155.9 13.1 %collective-permute-start.13 = (bf16[4,64,1280]{2,1,0:T(8,128)(2,1)S(1)}, bf16[4,64,1280]{2,1,0:T(8,128)(2,1)S(1)}, u32[]{:S(2)}, u32[]{:S(2)}) collective-permute-start(bf16[4,64,1280]{2,1,0:T(8,128)(2,1)S(1)} %slice_bitcast_fusion.1), channel_id=1, source_target_pairs={{0,1},{1,2},{2,3},{3,0},{4,5},{5,6},{6,7},{7,4},{8,9},{9,10},{10,1... | collective-permute-start | bytes 1966088 | tf_op jit(solution)/shard_map/ppermute | solution.py:560
  169.3 14.6 %collective-permute-start.14 = (bf16[4,64,1280]{2,1,0:T(8,128)(2,1)S(1)}, bf16[4,64,1280]{2,1,0:T(8,128)(2,1)}, u32[]{:S(2)}, u32[]{:S(2)}) collective-permute-start(bf16[4,64,1280]{2,1,0:T(8,128)(2,1)S(1)} %fusion.10), channel_id=1, source_target_pairs={{0,1},{1,2},{2,3},{3,0},{4,5},{5,6},{6,7},{7,4},{8,9},{9,10},{10,1... | collective-permute-start | bytes 1966088 | tf_op jit(solution)/shard_map/ppermute | solution.py:560
  189.8 17.0 %collective-permute-start.16 = (bf16[4,3,15,80,128]{4,3,2,1,0:T(8,128)(2,1)}, bf16[4,3,15,80,128]{4,3,2,1,0:T(8,128)(2,1)}, u32[]{:S(2)}, u32[]{:S(2)}) collective-permute-start(bf16[4,3,15,80,128]{4,3,2,1,0:T(8,128)(2,1)} %bitcast.239), channel_id=1, source_target_pairs={{0,4},{4,0},{8,12},{12,8},{16,20},{20,16},{24,28},{28,24},{1,5},{5... | collective-permute-start | bytes 11059208 | tf_op jit(solution)/shard_map/ppermute | solution.py:557
  200.0 16.7 %collective-permute-start.15 = (bf16[4,64,1280]{2,1,0:T(8,128)(2,1)}, bf16[4,64,1280]{2,1,0:T(8,128)(2,1)}, u32[]{:S(2)}, u32[]{:S(2)}) collective-permute-start(bf16[4,64,1280]{2,1,0:T(8,128)(2,1)} %fusion.9), channel_id=1, source_target_pairs={{0,1},{1,2},{2,3},{3,0},{4,5},{5,6},{6,7},{7,4},{8,9},{9,10},{10,1... | collective-permute-start | bytes 1966088 | tf_op jit(solution)/shard_map/ppermute | solution.py:560
  231.6 18.5 %collective-permute-start.17 = (bf16[4,64,1408]{2,1,0:T(8,128)(2,1)}, bf16[4,64,1408]{2,1,0:T(8,128)(2,1)S(1)}, u32[]{:S(2)}, u32[]{:S(2)}) collective-permute-start(bf16[4,64,1408]{2,1,0:T(8,128)(2,1)} %bitcast.218), channel_id=1, source_target_pairs={{0,1},{1,2},{2,3},{3,0},{4,5},{5,6},{6,7},{7,4},{8,9},{9,10},{10,1... | collective-permute-start | bytes 2162696 | tf_op jit(solution)/shard_map/ppermute | solution.py:560
  251.5 19.8 %collective-permute-start.18 = (bf16[4,64,1408]{2,1,0:T(8,128)(2,1)S(1)}, bf16[4,64,1408]{2,1,0:T(8,128)(2,1)S(1)}, u32[]{:S(2)}, u32[]{:S(2)}) collective-permute-start(bf16[4,64,1408]{2,1,0:T(8,128)(2,1)S(1)} %collective-permute-done.17.refs_1_), channel_id=1, source_target_pairs={{0,1},{1,2},{2,3},{3,0},{4,5},{5,6},{6,7},{7,4},{8,9},{9,10},{10,1... | collective-permute-start | bytes 2162696 | tf_op jit(solution)/shard_map/ppermute | solution.py:560
  271.2 28.7 %collective-permute-start.20 = (bf16[4,64,1408]{2,1,0:T(8,128)(2,1)S(1)}, bf16[4,64,1408]{2,1,0:T(8,128)(2,1)S(1)}, u32[]{:S(2)}, u32[]{:S(2)}) collective-permute-start(bf16[4,64,1408]{2,1,0:T(8,128)(2,1)S(1)} %collective-permute-done.18.refs_2_), channel_id=1, source_target_pairs={{0,1},{1,2},{2,3},{3,0},{4,5},{5,6},{6,7},{7,4},{8,9},{9,10},{10,1... | collective-permute-start | bytes 2162696 | tf_op jit(solution)/shard_map/ppermute | solution.py:560
  282.6 42.6 %collective-permute-start.24 = (bf16[2,4,7,80,128]{4,3,2,1,0:T(8,128)(2,1)S(1)}, bf16[2,4,7,80,128]{4,3,2,1,0:T(8,128)(2,1)S(1)}, u32[]{:S(2)}, u32[]{:S(2)}) collective-permute-start(bf16[2,4,7,80,128]{4,3,2,1,0:T(8,128)(2,1)S(1)} %dynamic-slice_bitcast_fusion.1), channel_id=1, source_target_pairs={{0,16},{4,20},{8,24},{12,28},{16,0},{20,4},{24,8},{28,12},{1,17},{... | collective-permute-start | bytes 3440648 | tf_op jit(solution)/shard_map/ppermute | solution.py:557
  285.3 41.5 %collective-permute-start.22 = (bf16[2,4,8,80,128]{4,3,2,1,0:T(8,128)(2,1)S(1)}, bf16[2,4,8,80,128]{4,3,2,1,0:T(8,128)(2,1)S(1)}, u32[]{:S(2)}, u32[]{:S(2)}) collective-permute-start(bf16[2,4,8,80,128]{4,3,2,1,0:T(8,128)(2,1)S(1)} %dynamic-slice_bitcast_fusion), channel_id=1, source_target_pairs={{0,8},{4,12},{8,0},{12,4},{16,24},{20,28},{24,16},{28,20},{1,9},{5... | collective-permute-start | bytes 3932168 | tf_op jit(solution)/shard_map/ppermute | solution.py:557
  318.1 24.1 %collective-permute-start.21 = (bf16[4,64,1280]{2,1,0:T(8,128)(2,1)S(1)}, bf16[4,64,1280]{2,1,0:T(8,128)(2,1)S(1)}, u32[]{:S(2)}, u32[]{:S(2)}) collective-permute-start(bf16[4,64,1280]{2,1,0:T(8,128)(2,1)S(1)} %slice_bitcast_fusion), channel_id=1, source_target_pairs={{0,1},{1,2},{2,3},{3,0},{4,5},{5,6},{6,7},{7,4},{8,9},{9,10},{10,1... | collective-permute-start | bytes 1966088 | tf_op jit(solution)/shard_map/ppermute | solution.py:560
  325.5 13.2 %collective-permute-start.25 = (bf16[4,7,80,128]{3,2,1,0:T(8,128)(2,1)S(1)}, bf16[4,7,80,128]{3,2,1,0:T(8,128)(2,1)S(1)}, u32[]{:S(2)}, u32[]{:S(2)}) collective-permute-start(bf16[4,7,80,128]{3,2,1,0:T(8,128)(2,1)S(1)} %dynamic-slice_bitcast_fusion.5), channel_id=1, source_target_pairs={{0,8},{4,12},{8,0},{12,4},{16,24},{20,28},{24,16},{28,20},{1,9},{5... | collective-permute-start | bytes 1720328 | tf_op jit(solution)/shard_map/ppermute | solution.py:557
  327.3 14.7 %collective-permute-start.23 = (bf16[4,8,80,128]{3,2,1,0:T(8,128)(2,1)S(1)}, bf16[4,8,80,128]{3,2,1,0:T(8,128)(2,1)S(1)}, u32[]{:S(2)}, u32[]{:S(2)}) collective-permute-start(bf16[4,8,80,128]{3,2,1,0:T(8,128)(2,1)S(1)} %dynamic-slice_bitcast_fusion.4), channel_id=1, source_target_pairs={{0,16},{4,20},{8,24},{12,28},{16,0},{20,4},{24,8},{28,12},{1,17},{... | collective-permute-start | bytes 1966088 | tf_op jit(solution)/shard_map/ppermute | solution.py:557
  370.4 26.4 %collective-permute-start.40 = (bf16[15,80,128]{2,1,0:T(8,128)(2,1)S(1)}, bf16[15,80,128]{2,1,0:T(8,128)(2,1)}, u32[]{:S(2)}, u32[]{:S(2)}) collective-permute-start(bf16[15,80,128]{2,1,0:T(8,128)(2,1)S(1)} %fusion.16), channel_id=1, source_target_pairs={{0,1},{1,2},{2,3},{3,0},{4,5},{5,6},{6,7},{7,4},{8,9},{9,10},{10,1... | collective-permute-start | bytes 921608 | tf_op jit(solution)/shard_map/ppermute | solution.py:560
  371.7 26.2 %collective-permute-start.30 = (bf16[4,64,1280]{2,1,0:T(8,128)(2,1)}, bf16[4,64,1280]{2,1,0:T(8,128)(2,1)}, u32[]{:S(2)}, u32[]{:S(2)}) collective-permute-start(bf16[4,64,1280]{2,1,0:T(8,128)(2,1)} %fusion.6), channel_id=1, source_target_pairs={{0,1},{1,2},{2,3},{3,0},{4,5},{5,6},{6,7},{7,4},{8,9},{9,10},{10,1... | collective-permute-start | bytes 1966088 | tf_op jit(solution)/shard_map/ppermute | solution.py:560
  377.8 21.5 %collective-permute-start.29 = (bf16[2,4,5,80,128]{4,3,2,1,0:T(8,128)(2,1)}, bf16[2,4,5,80,128]{4,3,2,1,0:T(8,128)(2,1)}, u32[]{:S(2)}, u32[]{:S(2)}) collective-permute-start(bf16[2,4,5,80,128]{4,3,2,1,0:T(8,128)(2,1)} %dynamic-slice_bitcast_fusion.3), channel_id=1, source_target_pairs={{0,16},{4,20},{8,24},{12,28},{16,0},{20,4},{24,8},{28,12},{1,17},{... | collective-permute-start | bytes 2457608 | tf_op jit(solution)/shard_map/ppermute | solution.py:557
  379.1 22.1 %collective-permute-start.28 = (bf16[2,4,6,80,128]{4,3,2,1,0:T(8,128)(2,1)S(1)}, bf16[2,4,6,80,128]{4,3,2,1,0:T(8,128)(2,1)S(1)}, u32[]{:S(2)}, u32[]{:S(2)}) collective-permute-start(bf16[2,4,6,80,128]{4,3,2,1,0:T(8,128)(2,1)S(1)} %dynamic-slice_bitcast_fusion.2), channel_id=1, source_target_pairs={{0,8},{4,12},{8,0},{12,4},{16,24},{20,28},{24,16},{28,20},{1,9},{5... | collective-permute-start | bytes 2949128 | tf_op jit(solution)/shard_map/ppermute | solution.py:557
  399.1 14.8 %collective-permute-start.31 = (bf16[4,64,1280]{2,1,0:T(8,128)(2,1)S(1)}, bf16[4,64,1280]{2,1,0:T(8,128)(2,1)S(1)}, u32[]{:S(2)}, u32[]{:S(2)}) collective-permute-start(bf16[4,64,1280]{2,1,0:T(8,128)(2,1)S(1)} %fusion.5), channel_id=1, source_target_pairs={{0,1},{1,2},{2,3},{3,0},{4,5},{5,6},{6,7},{7,4},{8,9},{9,10},{10,1... | collective-permute-start | bytes 1966088 | tf_op jit(solution)/shard_map/ppermute | solution.py:560
  401.5 12.6 %collective-permute-start.33 = (bf16[4,5,80,128]{3,2,1,0:T(8,128)(2,1)S(1)}, bf16[4,5,80,128]{3,2,1,0:T(8,128)(2,1)S(1)}, u32[]{:S(2)}, u32[]{:S(2)}) collective-permute-start(bf16[4,5,80,128]{3,2,1,0:T(8,128)(2,1)S(1)} %dynamic-slice_bitcast_fusion.7), channel_id=1, source_target_pairs={{0,8},{4,12},{8,0},{12,4},{16,24},{20,28},{24,16},{28,20},{1,9},{5... | collective-permute-start | bytes 1228808 | tf_op jit(solution)/shard_map/ppermute | solution.py:557
  422.7 13.5 %collective-permute-start.34 = (bf16[11,80,128]{2,1,0:T(8,128)(2,1)S(1)}, bf16[11,80,128]{2,1,0:T(8,128)(2,1)S(1)}, u32[]{:S(2)}, u32[]{:S(2)}) collective-permute-start(bf16[11,80,128]{2,1,0:T(8,128)(2,1)S(1)} %get-tuple-element.174), channel_id=1, source_target_pairs={{0,1},{1,2},{2,3},{3,0},{4,5},{5,6},{6,7},{7,4},{8,9},{9,10},{10,1... | collective-permute-start | bytes 675848 | tf_op jit(solution)/shard_map/ppermute | solution.py:560
  424.3 18.4 %collective-permute-start.35 = (bf16[11,80,128]{2,1,0:T(8,128)(2,1)S(1)}, bf16[11,80,128]{2,1,0:T(8,128)(2,1)S(1)}, u32[]{:S(2)}, u32[]{:S(2)}) collective-permute-start(bf16[11,80,128]{2,1,0:T(8,128)(2,1)S(1)} %get-tuple-element.175), channel_id=1, source_target_pairs={{0,2},{1,3},{2,0},{3,1},{4,6},{5,7},{6,4},{7,5},{8,10},{9,11},{10,... | collective-permute-start | bytes 675848 | tf_op jit(solution)/shard_map/ppermute | solution.py:560
  426.2 21.1 %collective-permute-start.36 = (bf16[11,80,128]{2,1,0:T(8,128)(2,1)S(1)}, bf16[11,80,128]{2,1,0:T(8,128)(2,1)S(1)}, u32[]{:S(2)}, u32[]{:S(2)}) collective-permute-start(bf16[11,80,128]{2,1,0:T(8,128)(2,1)S(1)} %get-tuple-element.176), channel_id=1, source_target_pairs={{0,3},{1,0},{2,1},{3,2},{4,7},{5,4},{6,5},{7,6},{8,11},{9,8},{10,9... | collective-permute-start | bytes 675848 | tf_op jit(solution)/shard_map/ppermute | solution.py:560
  426.2 21.1 %collective-permute-start.42 = (bf16[15,80,128]{2,1,0:T(8,128)(2,1)S(1)}, bf16[15,80,128]{2,1,0:T(8,128)(2,1)S(1)}, u32[]{:S(2)}, u32[]{:S(2)}) collective-permute-start(bf16[15,80,128]{2,1,0:T(8,128)(2,1)S(1)} %fusion.14), channel_id=1, source_target_pairs={{0,8},{4,12},{8,0},{12,4},{16,24},{20,28},{24,16},{28,20},{1,9},{5... | collective-permute-start | bytes 921608 | tf_op jit(solution)/shard_map/ppermute | solution.py:557
  435.0 12.4 %collective-permute-start.43 = (bf16[15,80,128]{2,1,0:T(8,128)(2,1)S(1)}, bf16[15,80,128]{2,1,0:T(8,128)(2,1)S(1)}, u32[]{:S(2)}, u32[]{:S(2)}) collective-permute-start(bf16[15,80,128]{2,1,0:T(8,128)(2,1)S(1)} %fusion.14), channel_id=1, source_target_pairs={{0,16},{4,20},{8,24},{12,28},{16,0},{20,4},{24,8},{28,12},{1,17},{... | collective-permute-start | bytes 921608 | tf_op jit(solution)/shard_map/ppermute | solution.py:557
  451.1 19.1 %collective-permute-start.49 = (bf16[4,1,15,80,128]{4,3,2,1,0:T(8,128)(2,1)S(1)}, bf16[4,1,15,80,128]{4,3,2,1,0:T(8,128)(2,1)S(1)}, u32[]{:S(2)}, u32[]{:S(2)}) collective-permute-start(bf16[4,1,15,80,128]{4,3,2,1,0:T(8,128)(2,1)S(1)} %bitcast.211), channel_id=1, source_target_pairs={{0,4},{4,0},{8,12},{12,8},{16,20},{20,16},{24,28},{28,24},{1,5},{5... | collective-permute-start | bytes 3686408 | tf_op jit(solution)/shard_map/ppermute | solution.py:557
  (73 other events, 715.5 us)
Sparse Core Ops, SparseCore 0:
  43.9 40.2 all-gather.4
  139.5 50.2 all-gather.6

commit v6 on v5

--- a/solution.py
+++ b/solution.py
@@ -715,8 +715,7 @@
 
     head_own = [w_query.T, w_key.T, w_value.T]
     feed_own = [w_out, w_up.T, w_down]
-    head_slice = net.slice_of(head_own)
-    head_blocks = [net.shift(head_slice, step) for step in range(1, mp)]
+    head_blocks = net.ring_gather(net.slice_of(head_own))[1:]
     latents = latents.reshape(own_lines, lat_width)
     cotangent = cotangent.reshape(own_lines, lat_width)
     byte_in = byte_in.reshape(rows * byte_len, byte_width)
@@ -732,8 +731,9 @@
     )
     feed_slice = net.slice_of(feed_own)
     feed_slice = jnp.concatenate([feed_slice, three_parts(b_up, feed_slice.shape[1:])[None]])
-    head_blocks, byte_norm, lat_norm, feed_slice = lax.optimization_barrier(
-        (head_blocks, byte_norm, lat_norm, feed_slice)
+    flat = [v[None] for v in (mlp_gain, b_out, b_down)]
+    head_blocks[-1], byte_norm, lat_norm, feed_slice, flat = lax.optimization_barrier(
+        (head_blocks[-1], byte_norm, lat_norm, feed_slice, flat)
     )
     head_slices = net.gather_chips(jnp.stack(head_blocks), lines)
     lat_blocks = net.ring_gather(lat_norm)
@@ -769,7 +769,7 @@
     values, feed_blocks[-1] = lax.optimization_barrier((values, feed_blocks[-1]))
     feed_slices = net.gather_chips(jnp.stack([block[:-1] for block in feed_blocks[1:]]), lines)
     b_up_all = from_three_parts(jnp.stack([block[-1] for block in feed_blocks]), b_up.shape[0])
-    b_up_all = net.turned(b_up_all, 0)
+    b_up_all = net.turned(b_up_all, 0)[None]
     lat_shape = shape(lat_all.shape, BF16)
     parts, lse = row_call(
         functools.partial(attend_kernel, own_lat),
@@ -781,6 +781,8 @@
     attended = parts[1]
     for step in range(2, mp + 1):
         moved = net.shift(attended, 1)
+        if step == 2:
+            moved, b_up_all = lax.optimization_barrier((moved, b_up_all))
         if step == mp - 1:
             feed_slices = after(feed_slices, moved)
             out_w, up_t, down_w = net.both_cores(
@@ -807,7 +809,7 @@
         "feed",
         own_lines,
         [(latents, True), (cotangent, True)]
-        + [(v[None], False) for v in (mlp_gain, b_out, b_up_all, b_down)]
+        + [(v, False) for v in (flat[0], flat[1], b_up_all, flat[2])]
         + [(w, False) for w in (out_w, up_t, down_w)]
         + [(attended, True)],
         [(wide, True), (whole, True), (whole, True), (whole, True), (wide, True), (whole, True)]
@@ -827,7 +829,7 @@
     feed_sums = add_packed(feed_kept, net.swap(feed_sent, 1))
     if mp > 2:
         block = net.shift(grads[-1], 1)
-        block, *feed_sums = lax.optimization_barrier((block, *feed_sums))
+        block = after(block, feed_sums[0])
         grads.append(block)
     for _ in range(3, mp):
         grads.append(net.shift(grads[-1], 1))

time: 495 us -> 490 us (0.990)
    all_gather x2, waiting for transfers between devices: 5.99 us -> 0.01 us  [gather_chips(): lax.all_gather(x, 'dp', axis=0, axis_index_groups=self.chip_groups(chips))]
where the time goes in v6:
time: 490 us; the launch traced here: 480 us
  waiting for transfers between devices  174 us (36%)
  Pallas kernels  112 us (23%)
  starting transfers between devices  72.3 us (15%)
  local copies, waits for them, and re-layouts  42.5 us (9%)
  matrix products  34.5 us (7%)
  other arithmetic  29.8 us (6%)
  between operations  15.6 us (3%)
    ppermute x30, waiting for transfers between devices, shift(): return lax.ppermute(x, 'mp', ring(self.mp, step))  145 us
    ppermute x30, starting transfers between devices, shift(): return lax.ppermute(x, 'mp', ring(self.mp, step))  41.8 us
    pallas_call x3, Pallas kernels, row_call(): pl.pallas_call(kernel, grid=(outs[-1].shape[0],), in_specs=[spec(a.shape)...  34.7 us
    dot_general x7, matrix products, dot(): return lax.dot_general(a, b, dims, preferred_element_type=F32)  34.5 us
    pallas_call x3, Pallas kernels, block_call(): pl.pallas_call(kernel, grid=(args[0][0].shape[0] // lines,), in_specs=[sp...  33.9 us
    ppermute x20, starting transfers between devices, swap(): return lax.ppermute(x, 'dp', [(i, i ^ bit) for i in range(self.dp)])  30.4 us
    ppermute x20, waiting for transfers between devices, swap(): return lax.ppermute(x, 'dp', [(i, i ^ bit) for i in range(self.dp)])  29.4 us
    pallas_call x2, Pallas kernels, join_own(): pl.pallas_call(functools.partial(join_own_kernel, widths), grid_spec=pltp...  14 us
  transfers between devices with their start and end apart: 52, of which 26 were waited for; matrix products, arithmetic and copies ran while one was open for 14% of the time, Pallas kernels for 19%

profile of v6, /device:TPU:9, one launch (start us, length us, event | category | flops | bytes accessed | tf_op | source)
XLA Modules:
  0.0 480.5 jit_solution(12616676837826112187)
XLA Ops:
  11.5 6.8 %collective-permute-done = bf16[11,80,128]{2,0,1:T(8,128)(2,1)S(1)} collective-permute-done((bf16[11,80,128]{2,0,1:T(8,128)(2,1)S(1)}, bf16[11,80,128]{2,0,1:T(8,128)(2,1)S(1)}, u32[]{:S(2)}, u32[]{:S(2)}) %collective-permute-start) | collective-permute-done | bytes 225312 | tf_op jit(solution)/shard_map/ppermute | solution.py:560
  20.3 7.1 %collective-permute-done.1 = bf16[11,80,128]{2,0,1:T(8,128)(2,1)S(1)} collective-permute-done((bf16[11,80,128]{2,0,1:T(8,128)(2,1)S(1)}, bf16[11,80,128]{2,0,1:T(8,128)(2,1)S(1)}, u32[]{:S(2)}, u32[]{:S(2)}) %collective-permute-start.1) | collective-permute-done | bytes 225312 | tf_op jit(solution)/shard_map/ppermute | solution.py:560
  32.7 5.7 %byte_norm.1 = bf16[2048,768]{1,0:T(8,128)(2,1)} custom-call(f32[2048,768]{1,0:T(8,128)} %bitcast.226, f32[1,768]{1,0:T(1,128)} %broadcast_in_dim.25.gain_ref), custom_call_target="tpu_custom_call" | custom-call | flops 1966080 | bytes 786816 | tf_op jit(solution)/shard_map/byte_norm/pallas_call | solution.py:275
  42.1 14.5 %collective-permute-done.3 = bf16[4,64,1280]{2,1,0:T(8,128)(2,1)S(1)} collective-permute-done((bf16[4,64,1280]{2,1,0:T(8,128)(2,1)S(1)}, bf16[4,64,1280]{2,1,0:T(8,128)(2,1)S(1)}, u32[]{:S(2)}, u32[]{:S(2)}) %collective-permute-start.3) | collective-permute-done | bytes 655392 | tf_op jit(solution)/shard_map/ppermute | solution.py:560
  57.7 13.9 %collective-permute-done.4 = bf16[4,64,1280]{2,1,0:T(8,128)(2,1)S(1)} collective-permute-done((bf16[4,64,1280]{2,1,0:T(8,128)(2,1)S(1)}, bf16[4,64,1280]{2,1,0:T(8,128)(2,1)S(1)}, u32[]{:S(2)}, u32[]{:S(2)}) %collective-permute-start.4) | collective-permute-done | bytes 655392 | tf_op jit(solution)/shard_map/ppermute | solution.py:560
  72.4 14.1 %collective-permute-done.5 = bf16[4,64,1280]{2,1,0:T(8,128)(2,1)} collective-permute-done((bf16[4,64,1280]{2,1,0:T(8,128)(2,1)S(1)}, bf16[4,64,1280]{2,1,0:T(8,128)(2,1)}, u32[]{:S(2)}, u32[]{:S(2)}) %collective-permute-start.5) | collective-permute-done | bytes 655392 | tf_op jit(solution)/shard_map/ppermute | solution.py:560
  99.1 6.3 %join_own.2 = (bf16[1280,1280]{1,0:T(8,128)(2,1)}, bf16[1280,768]{1,0:T(8,128)(2,1)S(1)}, bf16[1280,768]{1,0:T(8,128)(2,1)S(1)}) custom-call(s32[2]{0:T(128)S(1)} %pad_add_fusion.where_ref, bf16[320,1280]{1,0:T(8,128)(2,1)S(1)} %bitcast.216, bf16[320,768]{1,0:T(8,128)(2,1)S(1)} %bitcast.221, bf16[320,768]{1,0:T(8,128)(2,1)S(1)} %bitcast.220, ...), custom_call_target="tpu_custom_call" | custom-call | bytes 1351680 | tf_op jit(solution)/shard_map/join_own/pallas_call | solution.py:437
  105.7 6.0 %convolution_convert_fusion.2 = bf16[2048,1280]{1,0:T(8,128)(2,1)} fusion(bf16[2048,768]{1,0:T(8,128)(2,1)S(1)} %copy-done.18, bf16[1280,768]{1,0:T(8,128)(2,1)S(1)} %get-tuple-element.103.key_ref), kind=kOutput, calls=%fused_computation.6 | convolution fusion | flops 4029153280 | bytes 10354688 | tf_op jit(solution)/shard_map/dot_general | solution.py:22
  116.9 8.2 %lse.1.refs_0_ = f32[4,8,256]{2,1,0:T(8,128)S(1)} custom-call(bf16[4,4,64,1280]{3,2,1,0:T(8,128)(2,1)S(1)} %bitcast.208, bf16[4,512,1280]{2,1,0:T(8,128)(2,1)} %bitcast.222, s32[4,1,256]{2,1,0:T(1,128)S(1)} %broadcast_in_dim_reshape.10.lat_seg_ref, s32[4,512,1]{2,1,0:T(8,128)S(1)} %copy-done.1), custom_call_target="tpu_custom_call" | custom-call | flops 268435456 | bytes 984576 | tf_op jit(solution)/shard_map/lse/pallas_call | solution.py:257
  129.5 6.0 %convolution_convert_fusion.1 = bf16[2048,1280]{1,0:T(8,128)(2,1)} fusion(bf16[2048,768]{1,0:T(8,128)(2,1)S(1)} %copy-done.18, bf16[1280,768]{1,0:T(8,128)(2,1)S(1)} %get-tuple-element.109.value_ref), kind=kOutput, calls=%fused_computation.5 | convolution fusion | flops 4029153280 | bytes 10354688 | tf_op jit(solution)/shard_map/dot_general | solution.py:22
  144.9 9.6 %attend.1 = (bf16[4,4,64,1280]{3,2,1,0:T(8,128)(2,1)S(1)}, f32[4,8,256]{2,1,0:T(8,128)S(1)}) custom-call(bf16[4,4,64,1280]{3,2,1,0:T(8,128)(2,1)} %bitcast.209, bf16[4,512,1280]{2,1,0:T(8,128)(2,1)} %bitcast.223, bf16[4,512,1280]{2,1,0:T(8,128)(2,1)} %bitcast.228, s32[4,1,256]{2,1,0:T(1,128)S(1)} %broadcast_in_dim_reshape.10.lat_seg_ref, ...), custom_call_target="tpu_custom_call" | custom-call | flops 536870912 | bytes 1656320 | tf_op jit(solution)/shard_map/attend/pallas_call | solution.py:257
  160.0 11.6 %collective-permute-done.13 = bf16[4,64,1280]{2,1,0:T(8,128)(2,1)} collective-permute-done((bf16[4,64,1280]{2,1,0:T(8,128)(2,1)}, bf16[4,64,1280]{2,1,0:T(8,128)(2,1)}, u32[]{:S(2)}, u32[]{:S(2)}) %collective-permute-start.13) | collective-permute-done | bytes 655392 | tf_op jit(solution)/shard_map/ppermute | solution.py:560
  174.0 14.9 %collective-permute-done.14 = bf16[4,64,1280]{2,1,0:T(8,128)(2,1)} collective-permute-done((bf16[4,64,1280]{2,1,0:T(8,128)(2,1)S(1)}, bf16[4,64,1280]{2,1,0:T(8,128)(2,1)}, u32[]{:S(2)}, u32[]{:S(2)}) %collective-permute-start.14) | collective-permute-done | bytes 655392 | tf_op jit(solution)/shard_map/ppermute | solution.py:560
  200.6 7.7 %join_own.3 = (bf16[1280,1280]{1,0:T(8,128)(2,1)S(1)}, bf16[1280,1280]{1,0:T(8,128)(2,1)}, bf16[1280,1280]{1,0:T(8,128)(2,1)}) custom-call(s32[2]{0:T(128)S(1)} %pad_add_fusion.where_ref, bf16[320,1280]{1,0:T(8,128)(2,1)S(1)} %copy-done.10, bf16[320,1280]{1,0:T(8,128)(2,1)S(1)} %bitcast.217, bf16[320,1280]{1,0:T(8,128)(2,1)S(1)} %copy-done.8, ...), custom_call_target="tpu_custom_call" | custom-call | bytes 1843200 | tf_op jit(solution)/shard_map/join_own/pallas_call | solution.py:437
  214.5 12.6 %feed.1 = (f32[256,1280]{1,0:T(8,128)}, bf16[256,1280]{1,0:T(8,128)(2,1)}, bf16[256,1280]{1,0:T(8,128)(2,1)}, bf16[256,1280]{1,0:T(8,128)(2,1)}, f32[256,1280]{1...) custom-call(f32[256,1280]{1,0:T(8,128)} %bitcast.225, ...), custom_call_target="tpu_custom_call" | custom-call | flops 419430400 | bytes 1640960 | tf_op jit(solution)/shard_map/feed/pallas_call | solution.py:275
  228.1 8.8 %grads.1 = (bf16[4,4,15,80,128]{4,3,2,1,0:T(8,128)(2,1)}, bf16[4,4,15,80,128]{4,3,2,1,0:T(8,128)(2,1)}) custom-call(s32[1]{0:T(128)} %bitcast.19.core_ref, bf16[256,1280]{1,0:T(8,128)(2,1)} %get-tuple-element.126.refs_0_, bf16[256,1280]{1,0:T(8,128)(2,1)} %get-tuple-element.127.refs_1_, bf16[256,1280]{1,0:T(8,128)(2,1)} %bitcast.231, ...), custom_call_target="tpu_custom_call" | custom-call | flops 314572800 | bytes 491520 | tf_op jit(solution)/shard_map/grads/pallas_call | solution.py:500
  236.9 9.2 %collective-permute-done.17.refs_1_ = bf16[4,64,1408]{2,1,0:T(8,128)(2,1)S(1)} collective-permute-done((bf16[4,64,1408]{2,1,0:T(8,128)(2,1)}, bf16[4,64,1408]{2,1,0:T(8,128)(2,1)S(1)}, u32[]{:S(2)}, u32[]{:S(2)}) %collective-permute-start.17) | collective-permute-done | bytes 720928 | tf_op jit(solution)/shard_map/ppermute | solution.py:560
  247.5 8.2 %collective-permute-done.19.b_ref = bf16[4,4,15,80,128]{4,3,2,1,0:T(8,128)(2,1)} collective-permute-done((bf16[4,4,15,80,128]{4,3,2,1,0:T(8,128)(2,1)}, bf16[4,4,15,80,128]{4,3,2,1,0:T(8,128)(2,1)}, u32[]{:S(2)}, u32[]{:S(2)}) %collective-permute-start.19) | collective-permute-done | bytes 4915232 | tf_op jit(solution)/shard_map/ppermute | solution.py:557
  255.7 6.7 %add_packed.2 = (bf16[4,4,8,80,128]{4,3,2,1,0:T(8,128)(2,1)}, bf16[4,4,7,80,128]{4,3,2,1,0:T(8,128)(2,1)}) custom-call(bf16[4,4,15,80,128]{4,3,2,1,0:T(8,128)(2,1)} %get-tuple-element.133.a_ref, bf16[4,4,15,80,128]{4,3,2,1,0:T(8,128)(2,1)} %collective-permute-done.19.b_ref), custom_call_target="tpu_custom_call" | custom-call | bytes 1228800 | tf_op jit(solution)/shard_map/add_packed/pallas_call | solution.py:482
  262.3 4.9 %collective-permute-done.18.refs_2_ = bf16[4,64,1408]{2,1,0:T(8,128)(2,1)S(1)} collective-permute-done((bf16[4,64,1408]{2,1,0:T(8,128)(2,1)S(1)}, bf16[4,64,1408]{2,1,0:T(8,128)(2,1)S(1)}, u32[]{:S(2)}, u32[]{:S(2)}) %collective-permute-start.18) | collective-permute-done | bytes 720928 | tf_op jit(solution)/shard_map/ppermute | solution.py:560
  267.3 9.9 %collective-permute-start.20 = (bf16[4,64,1408]{2,1,0:T(8,128)(2,1)S(1)}, bf16[4,64,1408]{2,1,0:T(8,128)(2,1)S(1)}, u32[]{:S(2)}, u32[]{:S(2)}) collective-permute-start(bf16[4,64,1408]{2,1,0:T(8,128)(2,1)S(1)} %collective-permute-done.18.refs_2_), channel_id=1, source_target_pairs={{0,1},{1,2},{2,3},{3,0},{4,5},{5,6},{6,7},{7,4},{8,9},{9,10},{10,1... | collective-permute-start | bytes 2162696 | tf_op jit(solution)/shard_map/ppermute | solution.py:560
  281.5 14.4 %collective-permute-done.20.refs_3_ = bf16[4,64,1408]{2,1,0:T(8,128)(2,1)S(1)} collective-permute-done((bf16[4,64,1408]{2,1,0:T(8,128)(2,1)S(1)}, bf16[4,64,1408]{2,1,0:T(8,128)(2,1)S(1)}, u32[]{:S(2)}, u32[]{:S(2)}) %collective-permute-start.20) | collective-permute-done | bytes 720928 | tf_op jit(solution)/shard_map/ppermute | solution.py:560
  296.0 16.9 %attend_back.1 = (bf16[4,4,64,1280]{3,2,1,0:T(8,128)(2,1)}, bf16[4,512,1280]{2,1,0:T(8,128)(2,1)}, bf16[4,512,1280]{2,1,0:T(8,128)(2,1)}) custom-call(bf16[4,4,64,1280]{3,2,1,0:T(8,128)(2,1)} %bitcast.210, bf16[4,512,1280]{2,1,0:T(8,128)(2,1)} %bitcast.224, bf16[4,512,1280]{2,1,0:T(8,128)(2,1)} %bitcast.229, ...), custom_call_target="tpu_custom_call" | custom-call | flops 1342177280 | bytes 2004480 | tf_op jit(solution)/shard_map/attend_back/pallas_call | solution.py:257
  314.2 6.9 %convolution_convert_fusion.3.refs_2_ = bf16[1280,768]{1,0:T(8,128)(2,1)S(1)} fusion(bf16[2048,1280]{1,0:T(8,128)(2,1)} %bitcast.237, bf16[2048,768]{1,0:T(8,128)(2,1)S(1)} %copy-done.19), kind=kOutput, calls=%fused_computation.8 | convolution fusion | flops 4027514880 | bytes 10354688 | tf_op jit(solution)/shard_map/dot_general | solution.py:22
  327.9 6.8 %collective-permute-done.25 = bf16[4,7,80,128]{3,2,1,0:T(8,128)(2,1)S(1)} collective-permute-done((bf16[4,7,80,128]{3,2,1,0:T(8,128)(2,1)S(1)}, bf16[4,7,80,128]{3,2,1,0:T(8,128)(2,1)S(1)}, u32[]{:S(2)}, u32[]{:S(2)}) %collective-permute-start.25) | collective-permute-done | bytes 573472 | tf_op jit(solution)/shard_map/ppermute | solution.py:557
  341.2 5.2 %convolution_convert_fusion.refs_0_ = bf16[1280,1280]{1,0:T(8,128)(2,1)} fusion(bf16[1024,1280]{1,0:T(8,128)(2,1)S(1)} %bitcast.248, bf16[1024,1280]{1,0:T(8,128)(2,1)S(1)} %bitcast.244), kind=kOutput, calls=%fused_computation.4 | convolution fusion | flops 3357081600 | bytes 8519680 | tf_op jit(solution)/shard_map/dot_general | solution.py:22
  346.4 5.8 %split.1 = (bf16[4,4,11,80,128]{4,3,2,1,0:T(8,128)(2,1)}, bf16[4,4,11,80,128]{4,3,2,1,0:T(8,128)(2,1)}) custom-call(s32[1]{0:T(128)} %bitcast.19.core_ref, bf16[1280,1280]{1,0:T(8,128)(2,1)} %convolution_convert_fusion.refs_0_, bf16[1280,768]{1,0:T(8,128)(2,1)S(1)} %convolution_convert_fusion.4.refs_1_, bf16[1280,768]{1,0:T(8,128)(2,1)S(1)} %convolution_convert_fusion.3.refs_2_), custom_call_target="tpu_custom_call" | custom-call | bytes 1802240 | tf_op jit(solution)/shard_map/split/pallas_call | solution.py:464
  360.8 5.5 %add_packed.3 = (bf16[4,4,6,80,128]{4,3,2,1,0:T(8,128)(2,1)}, bf16[4,4,5,80,128]{4,3,2,1,0:T(8,128)(2,1)}) custom-call(bf16[4,4,11,80,128]{4,3,2,1,0:T(8,128)(2,1)} %get-tuple-element.147.a_ref, bf16[4,4,11,80,128]{4,3,2,1,0:T(8,128)(2,1)} %collective-permute-done.27.b_ref), custom_call_target="tpu_custom_call" | custom-call | bytes 901120 | tf_op jit(solution)/shard_map/add_packed/pallas_call | solution.py:482
  375.3 15.6 %byte_back.1 = (f32[2048,768]{1,0:T(8,128)}, f32[1,768]{1,0:T(1,128)}) custom-call(f32[2048,768]{1,0:T(8,128)} %bitcast.227, f32[1,768]{1,0:T(1,128)} %broadcast_in_dim.25.gain_ref, bf16[1280,768]{1,0:T(8,128)(2,1)} %copy-done.5, bf16[1280,768]{1,0:T(8,128)(2,1)} %copy-done.6, bf16[2048,1280]{1,0:T(8,128)(2,1)} %bitcast.233, bf16[2048,1280]{1,0:T(8,128)(2,1)} %bitcast.238), custom_call_target="tpu_custom_call" | custom-call | flops 1006632960 | bytes 2589056 | tf_op jit(solution)/shard_map/byte_back/pallas_call | solution.py:275
  398.1 10.8 %collective-permute-done.31 = bf16[4,64,1280]{2,1,0:T(8,128)(2,1)S(1)} collective-permute-done((bf16[4,64,1280]{2,1,0:T(8,128)(2,1)S(1)}, bf16[4,64,1280]{2,1,0:T(8,128)(2,1)S(1)}, u32[]{:S(2)}, u32[]{:S(2)}) %collective-permute-start.31) | collective-permute-done | bytes 655392 | tf_op jit(solution)/shard_map/ppermute | solution.py:560
  421.7 8.0 %collective-permute-done.39 = bf16[1,80,128]{2,1,0:T(8,128)(2,1)S(1)} collective-permute-done((bf16[1,80,128]{2,1,0:T(8,128)(2,1)S(1)}, bf16[1,80,128]{2,1,0:T(8,128)(2,1)S(1)}, u32[]{:S(2)}, u32[]{:S(2)}) %collective-permute-start.39) | collective-permute-done | bytes 20512 | tf_op jit(solution)/shard_map/ppermute | solution.py:560
  431.1 6.7 %collective-permute-done.35 = bf16[11,80,128]{2,1,0:T(8,128)(2,1)S(1)} collective-permute-done((bf16[11,80,128]{2,1,0:T(8,128)(2,1)S(1)}, bf16[11,80,128]{2,1,0:T(8,128)(2,1)S(1)}, u32[]{:S(2)}, u32[]{:S(2)}) %collective-permute-start.35) | collective-permute-done | bytes 225312 | tf_op jit(solution)/shard_map/ppermute | solution.py:560
  (318 shorter events, 169.6 us)
Async XLA Ops:
  7.2 79.4 %all-gather.5.cloned.1.call-start = ((), (), s32[]{:S(2)}) async-start(), calls=%async_computation | async-start | bytes 3379200 | tf_op jit(solution)/shard_map/all_gather | solution.py:600
  27.4 11.9 %collective-permute-start.2 = (bf16[11,80,128]{2,0,1:T(8,128)(2,1)S(1)}, bf16[11,80,128]{2,0,1:T(8,128)(2,1)S(1)}, u32[]{:S(2)}, u32[]{:S(2)}) collective-permute-start(bf16[11,80,128]{2,0,1:T(8,128)(2,1)S(1)} %collective-permute-done.1), channel_id=1, source_target_pairs={{0,1},{1,2},{2,3},{3,0},{4,5},{5,6},{6,7},{7,4},{8,9},{9,10},{10,1... | collective-permute-start | bytes 675848 | tf_op jit(solution)/shard_map/ppermute | solution.py:560
  40.6 148.2 %all-gather.7.cloned.1.call-start = ((), (), s32[]{:S(2)}) async-start(), calls=%async_computation.1 | async-start | bytes 4608000 | tf_op jit(solution)/shard_map/all_gather | solution.py:600
  40.7 15.9 %collective-permute-start.3 = (bf16[4,64,1280]{2,1,0:T(8,128)(2,1)S(1)}, bf16[4,64,1280]{2,1,0:T(8,128)(2,1)S(1)}, u32[]{:S(2)}, u32[]{:S(2)}) collective-permute-start(bf16[4,64,1280]{2,1,0:T(8,128)(2,1)S(1)} %multiply_convert_fusion.1), channel_id=1, source_target_pairs={{0,1},{1,2},{2,3},{3,0},{4,5},{5,6},{6,7},{7,4},{8,9},{9,10},{10,1... | collective-permute-start | bytes 1966088 | tf_op jit(solution)/shard_map/ppermute | solution.py:560
  56.6 15.0 %collective-permute-start.4 = (bf16[4,64,1280]{2,1,0:T(8,128)(2,1)S(1)}, bf16[4,64,1280]{2,1,0:T(8,128)(2,1)S(1)}, u32[]{:S(2)}, u32[]{:S(2)}) collective-permute-start(bf16[4,64,1280]{2,1,0:T(8,128)(2,1)S(1)} %collective-permute-done.3), channel_id=1, source_target_pairs={{0,1},{1,2},{2,3},{3,0},{4,5},{5,6},{6,7},{7,4},{8,9},{9,10},{10,1... | collective-permute-start | bytes 1966088 | tf_op jit(solution)/shard_map/ppermute | solution.py:560
  72.4 14.1 %collective-permute-start.5 = (bf16[4,64,1280]{2,1,0:T(8,128)(2,1)S(1)}, bf16[4,64,1280]{2,1,0:T(8,128)(2,1)}, u32[]{:S(2)}, u32[]{:S(2)}) collective-permute-start(bf16[4,64,1280]{2,1,0:T(8,128)(2,1)S(1)} %collective-permute-done.4), channel_id=1, source_target_pairs={{0,1},{1,2},{2,3},{3,0},{4,5},{5,6},{6,7},{7,4},{8,9},{9,10},{10,1... | collective-permute-start | bytes 1966088 | tf_op jit(solution)/shard_map/ppermute | solution.py:560
  111.7 13.4 %collective-permute-start.8 = (bf16[16,80,128]{2,0,1:T(8,128)(2,1)S(1)}, bf16[16,80,128]{2,0,1:T(8,128)(2,1)S(1)}, u32[]{:S(2)}, u32[]{:S(2)}) collective-permute-start(bf16[16,80,128]{2,0,1:T(8,128)(2,1)S(1)} %collective-permute-done.7), channel_id=1, source_target_pairs={{0,1},{1,2},{2,3},{3,0},{4,5},{5,6},{6,7},{7,4},{8,9},{9,10},{10,1... | collective-permute-start | bytes 983048 | tf_op jit(solution)/shard_map/ppermute | solution.py:560
  156.9 14.7 %collective-permute-start.13 = (bf16[4,64,1280]{2,1,0:T(8,128)(2,1)}, bf16[4,64,1280]{2,1,0:T(8,128)(2,1)}, u32[]{:S(2)}, u32[]{:S(2)}) collective-permute-start(bf16[4,64,1280]{2,1,0:T(8,128)(2,1)} %slice_bitcast_fusion.1), channel_id=1, source_target_pairs={{0,1},{1,2},{2,3},{3,0},{4,5},{5,6},{6,7},{7,4},{8,9},{9,10},{10,1... | collective-permute-start | bytes 1966088 | tf_op jit(solution)/shard_map/ppermute | solution.py:560
  173.0 15.8 %collective-permute-start.14 = (bf16[4,64,1280]{2,1,0:T(8,128)(2,1)S(1)}, bf16[4,64,1280]{2,1,0:T(8,128)(2,1)}, u32[]{:S(2)}, u32[]{:S(2)}) collective-permute-start(bf16[4,64,1280]{2,1,0:T(8,128)(2,1)S(1)} %fusion.10), channel_id=1, source_target_pairs={{0,1},{1,2},{2,3},{3,0},{4,5},{5,6},{6,7},{7,4},{8,9},{9,10},{10,1... | collective-permute-start | bytes 1966088 | tf_op jit(solution)/shard_map/ppermute | solution.py:560
  194.0 18.4 %collective-permute-start.15 = (bf16[4,64,1280]{2,1,0:T(8,128)(2,1)S(1)}, bf16[4,64,1280]{2,1,0:T(8,128)(2,1)S(1)}, u32[]{:S(2)}, u32[]{:S(2)}) collective-permute-start(bf16[4,64,1280]{2,1,0:T(8,128)(2,1)S(1)} %fusion.9), channel_id=1, source_target_pairs={{0,1},{1,2},{2,3},{3,0},{4,5},{5,6},{6,7},{7,4},{8,9},{9,10},{10,1... | collective-permute-start | bytes 1966088 | tf_op jit(solution)/shard_map/ppermute | solution.py:560
  227.1 19.1 %collective-permute-start.17 = (bf16[4,64,1408]{2,1,0:T(8,128)(2,1)}, bf16[4,64,1408]{2,1,0:T(8,128)(2,1)S(1)}, u32[]{:S(2)}, u32[]{:S(2)}) collective-permute-start(bf16[4,64,1408]{2,1,0:T(8,128)(2,1)} %bitcast.218), channel_id=1, source_target_pairs={{0,1},{1,2},{2,3},{3,0},{4,5},{5,6},{6,7},{7,4},{8,9},{9,10},{10,1... | collective-permute-start | bytes 2162696 | tf_op jit(solution)/shard_map/ppermute | solution.py:560
  247.5 19.8 %collective-permute-start.18 = (bf16[4,64,1408]{2,1,0:T(8,128)(2,1)S(1)}, bf16[4,64,1408]{2,1,0:T(8,128)(2,1)S(1)}, u32[]{:S(2)}, u32[]{:S(2)}) collective-permute-start(bf16[4,64,1408]{2,1,0:T(8,128)(2,1)S(1)} %collective-permute-done.17.refs_1_), channel_id=1, source_target_pairs={{0,1},{1,2},{2,3},{3,0},{4,5},{5,6},{6,7},{7,4},{8,9},{9,10},{10,1... | collective-permute-start | bytes 2162696 | tf_op jit(solution)/shard_map/ppermute | solution.py:560
  267.3 28.7 %collective-permute-start.20 = (bf16[4,64,1408]{2,1,0:T(8,128)(2,1)S(1)}, bf16[4,64,1408]{2,1,0:T(8,128)(2,1)S(1)}, u32[]{:S(2)}, u32[]{:S(2)}) collective-permute-start(bf16[4,64,1408]{2,1,0:T(8,128)(2,1)S(1)} %collective-permute-done.18.refs_2_), channel_id=1, source_target_pairs={{0,1},{1,2},{2,3},{3,0},{4,5},{5,6},{6,7},{7,4},{8,9},{9,10},{10,1... | collective-permute-start | bytes 2162696 | tf_op jit(solution)/shard_map/ppermute | solution.py:560
  278.6 42.6 %collective-permute-start.24 = (bf16[2,4,7,80,128]{4,3,2,1,0:T(8,128)(2,1)S(1)}, bf16[2,4,7,80,128]{4,3,2,1,0:T(8,128)(2,1)S(1)}, u32[]{:S(2)}, u32[]{:S(2)}) collective-permute-start(bf16[2,4,7,80,128]{4,3,2,1,0:T(8,128)(2,1)S(1)} %dynamic-slice_bitcast_fusion.1), channel_id=1, source_target_pairs={{0,16},{4,20},{8,24},{12,28},{16,0},{20,4},{24,8},{28,12},{1,17},{... | collective-permute-start | bytes 3440648 | tf_op jit(solution)/shard_map/ppermute | solution.py:557
  280.3 41.5 %collective-permute-start.22 = (bf16[2,4,8,80,128]{4,3,2,1,0:T(8,128)(2,1)S(1)}, bf16[2,4,8,80,128]{4,3,2,1,0:T(8,128)(2,1)S(1)}, u32[]{:S(2)}, u32[]{:S(2)}) collective-permute-start(bf16[2,4,8,80,128]{4,3,2,1,0:T(8,128)(2,1)S(1)} %dynamic-slice_bitcast_fusion), channel_id=1, source_target_pairs={{0,8},{4,12},{8,0},{12,4},{16,24},{20,28},{24,16},{28,20},{1,9},{5... | collective-permute-start | bytes 3932168 | tf_op jit(solution)/shard_map/ppermute | solution.py:557
  314.1 24.3 %collective-permute-start.21 = (bf16[4,64,1280]{2,1,0:T(8,128)(2,1)S(1)}, bf16[4,64,1280]{2,1,0:T(8,128)(2,1)S(1)}, u32[]{:S(2)}, u32[]{:S(2)}) collective-permute-start(bf16[4,64,1280]{2,1,0:T(8,128)(2,1)S(1)} %slice_bitcast_fusion), channel_id=1, source_target_pairs={{0,1},{1,2},{2,3},{3,0},{4,5},{5,6},{6,7},{7,4},{8,9},{9,10},{10,1... | collective-permute-start | bytes 1966088 | tf_op jit(solution)/shard_map/ppermute | solution.py:560
  321.6 13.2 %collective-permute-start.25 = (bf16[4,7,80,128]{3,2,1,0:T(8,128)(2,1)S(1)}, bf16[4,7,80,128]{3,2,1,0:T(8,128)(2,1)S(1)}, u32[]{:S(2)}, u32[]{:S(2)}) collective-permute-start(bf16[4,7,80,128]{3,2,1,0:T(8,128)(2,1)S(1)} %dynamic-slice_bitcast_fusion.5), channel_id=1, source_target_pairs={{0,8},{4,12},{8,0},{12,4},{16,24},{20,28},{24,16},{28,20},{1,9},{5... | collective-permute-start | bytes 1720328 | tf_op jit(solution)/shard_map/ppermute | solution.py:557
  323.3 14.9 %collective-permute-start.23 = (bf16[4,8,80,128]{3,2,1,0:T(8,128)(2,1)S(1)}, bf16[4,8,80,128]{3,2,1,0:T(8,128)(2,1)S(1)}, u32[]{:S(2)}, u32[]{:S(2)}) collective-permute-start(bf16[4,8,80,128]{3,2,1,0:T(8,128)(2,1)S(1)} %dynamic-slice_bitcast_fusion.4), channel_id=1, source_target_pairs={{0,16},{4,20},{8,24},{12,28},{16,0},{20,4},{24,8},{28,12},{1,17},{... | collective-permute-start | bytes 1966088 | tf_op jit(solution)/shard_map/ppermute | solution.py:557
  366.5 25.3 %collective-permute-start.40 = (bf16[15,80,128]{2,1,0:T(8,128)(2,1)S(1)}, bf16[15,80,128]{2,1,0:T(8,128)(2,1)}, u32[]{:S(2)}, u32[]{:S(2)}) collective-permute-start(bf16[15,80,128]{2,1,0:T(8,128)(2,1)S(1)} %fusion.16), channel_id=1, source_target_pairs={{0,1},{1,2},{2,3},{3,0},{4,5},{5,6},{6,7},{7,4},{8,9},{9,10},{10,1... | collective-permute-start | bytes 921608 | tf_op jit(solution)/shard_map/ppermute | solution.py:560
  367.9 24.9 %collective-permute-start.30 = (bf16[4,64,1280]{2,1,0:T(8,128)(2,1)}, bf16[4,64,1280]{2,1,0:T(8,128)(2,1)}, u32[]{:S(2)}, u32[]{:S(2)}) collective-permute-start(bf16[4,64,1280]{2,1,0:T(8,128)(2,1)} %fusion.6), channel_id=1, source_target_pairs={{0,1},{1,2},{2,3},{3,0},{4,5},{5,6},{6,7},{7,4},{8,9},{9,10},{10,1... | collective-permute-start | bytes 1966088 | tf_op jit(solution)/shard_map/ppermute | solution.py:560
  373.8 20.6 %collective-permute-start.29 = (bf16[2,4,5,80,128]{4,3,2,1,0:T(8,128)(2,1)}, bf16[2,4,5,80,128]{4,3,2,1,0:T(8,128)(2,1)}, u32[]{:S(2)}, u32[]{:S(2)}) collective-permute-start(bf16[2,4,5,80,128]{4,3,2,1,0:T(8,128)(2,1)} %dynamic-slice_bitcast_fusion.3), channel_id=1, source_target_pairs={{0,16},{4,20},{8,24},{12,28},{16,0},{20,4},{24,8},{28,12},{1,17},{... | collective-permute-start | bytes 2457608 | tf_op jit(solution)/shard_map/ppermute | solution.py:557
  374.1 22.1 %collective-permute-start.28 = (bf16[2,4,6,80,128]{4,3,2,1,0:T(8,128)(2,1)S(1)}, bf16[2,4,6,80,128]{4,3,2,1,0:T(8,128)(2,1)S(1)}, u32[]{:S(2)}, u32[]{:S(2)}) collective-permute-start(bf16[2,4,6,80,128]{4,3,2,1,0:T(8,128)(2,1)S(1)} %dynamic-slice_bitcast_fusion.2), channel_id=1, source_target_pairs={{0,8},{4,12},{8,0},{12,4},{16,24},{20,28},{24,16},{28,20},{1,9},{5... | collective-permute-start | bytes 2949128 | tf_op jit(solution)/shard_map/ppermute | solution.py:557
  394.1 14.8 %collective-permute-start.31 = (bf16[4,64,1280]{2,1,0:T(8,128)(2,1)S(1)}, bf16[4,64,1280]{2,1,0:T(8,128)(2,1)S(1)}, u32[]{:S(2)}, u32[]{:S(2)}) collective-permute-start(bf16[4,64,1280]{2,1,0:T(8,128)(2,1)S(1)} %fusion.5), channel_id=1, source_target_pairs={{0,1},{1,2},{2,3},{3,0},{4,5},{5,6},{6,7},{7,4},{8,9},{9,10},{10,1... | collective-permute-start | bytes 1966088 | tf_op jit(solution)/shard_map/ppermute | solution.py:560
  396.5 12.6 %collective-permute-start.33 = (bf16[4,5,80,128]{3,2,1,0:T(8,128)(2,1)S(1)}, bf16[4,5,80,128]{3,2,1,0:T(8,128)(2,1)S(1)}, u32[]{:S(2)}, u32[]{:S(2)}) collective-permute-start(bf16[4,5,80,128]{3,2,1,0:T(8,128)(2,1)S(1)} %dynamic-slice_bitcast_fusion.7), channel_id=1, source_target_pairs={{0,8},{4,12},{8,0},{12,4},{16,24},{20,28},{24,16},{28,20},{1,9},{5... | collective-permute-start | bytes 1228808 | tf_op jit(solution)/shard_map/ppermute | solution.py:557
  417.9 11.8 %collective-permute-start.39 = (bf16[1,80,128]{2,1,0:T(8,128)(2,1)S(1)}, bf16[1,80,128]{2,1,0:T(8,128)(2,1)S(1)}, u32[]{:S(2)}, u32[]{:S(2)}) collective-permute-start(bf16[1,80,128]{2,1,0:T(8,128)(2,1)S(1)} %fusion.43), channel_id=1, source_target_pairs={{0,3},{1,0},{2,1},{3,2},{4,7},{5,4},{6,5},{7,6},{8,11},{9,8},{10,9... | collective-permute-start | bytes 61448 | tf_op jit(solution)/shard_map/ppermute | solution.py:560
  418.0 11.9 %collective-permute-start.34 = (bf16[11,80,128]{2,1,0:T(8,128)(2,1)S(1)}, bf16[11,80,128]{2,1,0:T(8,128)(2,1)S(1)}, u32[]{:S(2)}, u32[]{:S(2)}) collective-permute-start(bf16[11,80,128]{2,1,0:T(8,128)(2,1)S(1)} %get-tuple-element.176), channel_id=1, source_target_pairs={{0,1},{1,2},{2,3},{3,0},{4,5},{5,6},{6,7},{7,4},{8,9},{9,10},{10,1... | collective-permute-start | bytes 675848 | tf_op jit(solution)/shard_map/ppermute | solution.py:560
  419.5 18.3 %collective-permute-start.35 = (bf16[11,80,128]{2,1,0:T(8,128)(2,1)S(1)}, bf16[11,80,128]{2,1,0:T(8,128)(2,1)S(1)}, u32[]{:S(2)}, u32[]{:S(2)}) collective-permute-start(bf16[11,80,128]{2,1,0:T(8,128)(2,1)S(1)} %get-tuple-element.177), channel_id=1, source_target_pairs={{0,2},{1,3},{2,0},{3,1},{4,6},{5,7},{6,4},{7,5},{8,10},{9,11},{10,... | collective-permute-start | bytes 675848 | tf_op jit(solution)/shard_map/ppermute | solution.py:560
  421.4 21.1 %collective-permute-start.36 = (bf16[11,80,128]{2,1,0:T(8,128)(2,1)S(1)}, bf16[11,80,128]{2,1,0:T(8,128)(2,1)S(1)}, u32[]{:S(2)}, u32[]{:S(2)}) collective-permute-start(bf16[11,80,128]{2,1,0:T(8,128)(2,1)S(1)} %get-tuple-element.178), channel_id=1, source_target_pairs={{0,3},{1,0},{2,1},{3,2},{4,7},{5,4},{6,5},{7,6},{8,11},{9,8},{10,9... | collective-permute-start | bytes 675848 | tf_op jit(solution)/shard_map/ppermute | solution.py:560
  421.5 21.1 %collective-permute-start.42 = (bf16[15,80,128]{2,1,0:T(8,128)(2,1)S(1)}, bf16[15,80,128]{2,1,0:T(8,128)(2,1)S(1)}, u32[]{:S(2)}, u32[]{:S(2)}) collective-permute-start(bf16[15,80,128]{2,1,0:T(8,128)(2,1)S(1)} %fusion.14), channel_id=1, source_target_pairs={{0,8},{4,12},{8,0},{12,4},{16,24},{20,28},{24,16},{28,20},{1,9},{5... | collective-permute-start | bytes 921608 | tf_op jit(solution)/shard_map/ppermute | solution.py:557
  429.7 12.9 %collective-permute-start.43 = (bf16[15,80,128]{2,1,0:T(8,128)(2,1)S(1)}, bf16[15,80,128]{2,1,0:T(8,128)(2,1)S(1)}, u32[]{:S(2)}, u32[]{:S(2)}) collective-permute-start(bf16[15,80,128]{2,1,0:T(8,128)(2,1)S(1)} %fusion.14), channel_id=1, source_target_pairs={{0,16},{4,20},{8,24},{12,28},{16,0},{20,4},{24,8},{28,12},{1,17},{... | collective-permute-start | bytes 921608 | tf_op jit(solution)/shard_map/ppermute | solution.py:557
  429.9 12.7 %collective-permute-start.44 = (bf16[15,80,128]{2,1,0:T(8,128)(2,1)S(1)}, bf16[15,80,128]{2,1,0:T(8,128)(2,1)S(1)}, u32[]{:S(2)}, u32[]{:S(2)}) collective-permute-start(bf16[15,80,128]{2,1,0:T(8,128)(2,1)S(1)} %fusion.14), channel_id=1, source_target_pairs={{0,24},{4,28},{8,16},{12,20},{16,8},{20,12},{24,0},{28,4},{1,25},{... | collective-permute-start | bytes 921608 | tf_op jit(solution)/shard_map/ppermute | solution.py:557
  446.4 18.1 %collective-permute-start.49 = (bf16[4,1,15,80,128]{4,3,2,1,0:T(8,128)(2,1)S(1)}, bf16[4,1,15,80,128]{4,3,2,1,0:T(8,128)(2,1)S(1)}, u32[]{:S(2)}, u32[]{:S(2)}) collective-permute-start(bf16[4,1,15,80,128]{4,3,2,1,0:T(8,128)(2,1)S(1)} %bitcast.211), channel_id=1, source_target_pairs={{0,4},{4,0},{8,12},{12,8},{16,20},{20,16},{24,28},{28,24},{1,5},{5... | collective-permute-start | bytes 3686408 | tf_op jit(solution)/shard_map/ppermute | solution.py:557
  (73 other events, 789.7 us)
Sparse Core Ops, SparseCore 0:
  40.8 45.7 all-gather.4
  138.3 49.3 all-gather.6

commit v7 on v6

--- a/solution.py
+++ b/solution.py
@@ -261,7 +261,7 @@
         out_specs=[spec(o.shape) for o in outs],
         out_shape=outs,
         name=name,
-        cost_estimate=pl.CostEstimate(flops=flops // 8, bytes_accessed=moved // 8, transcendentals=0),
+        cost_estimate=pl.CostEstimate(flops=flops, bytes_accessed=moved, transcendentals=0),
         compiler_params=pltpu.CompilerParams(vmem_limit_bytes=48 * 1024 * 1024),
     )(*args)
 
@@ -280,7 +280,7 @@
         out_shape=[o for o, _ in outs],
         scratch_shapes=list(scratch),
         name=name,
-        cost_estimate=pl.CostEstimate(flops=flops // 8, bytes_accessed=moved // 8, transcendentals=0),
+        cost_estimate=pl.CostEstimate(flops=flops, bytes_accessed=moved, transcendentals=0),
         compiler_params=pltpu.CompilerParams(vmem_limit_bytes=56 * 1024 * 1024),
     )(*[a for a, _ in args])
 

time: 490 us -> 484 us (0.988)
  local copies, waits for them, and re-layouts: 42.5 us -> 36.4 us
    unnamed x104 -> x100, local copies, waits for them, and re-layouts: 12.8 us -> 9.62 us
  transfers between devices with their start and end apart: 52 -> 52, of which waited for: 26 -> 27; matrix products, arithmetic and copies ran while one was open for 14% -> 13% of each run, Pallas kernels for 19% -> 20%
where the time goes in v7:
time: 484 us; the launch traced here: 475 us
  waiting for transfers between devices  175 us (36%)
  Pallas kernels  112 us (23%)
  starting transfers between devices  73.1 us (15%)
  local copies, waits for them, and re-layouts  36.4 us (8%)
  matrix products  34.4 us (7%)
  other arithmetic  28.8 us (6%)
  between operations  15.6 us (3%)
    ppermute x30, waiting for transfers between devices, shift(): return lax.ppermute(x, 'mp', ring(self.mp, step))  142 us
    ppermute x30, starting transfers between devices, shift(): return lax.ppermute(x, 'mp', ring(self.mp, step))  43 us
    pallas_call x3, Pallas kernels, row_call(): pl.pallas_call(kernel, grid=(outs[-1].shape[0],), in_specs=[spec(a.shape)...  34.8 us
    dot_general x7, matrix products, dot(): return lax.dot_general(a, b, dims, preferred_element_type=F32)  34.4 us
    pallas_call x3, Pallas kernels, block_call(): pl.pallas_call(kernel, grid=(args[0][0].shape[0] // lines,), in_specs=[sp...  33.9 us
    ppermute x20, waiting for transfers between devices, swap(): return lax.ppermute(x, 'dp', [(i, i ^ bit) for i in range(self.dp)])  30.1 us
    ppermute x20, starting transfers between devices, swap(): return lax.ppermute(x, 'dp', [(i, i ^ bit) for i in range(self.dp)])  30 us
    pallas_call x2, Pallas kernels, join_own(): pl.pallas_call(functools.partial(join_own_kernel, widths), grid_spec=pltp...  14 us
  transfers between devices with their start and end apart: 52, of which 27 were waited for; matrix products, arithmetic and copies ran while one was open for 13% of the time, Pallas kernels for 20%

profile of v7, /device:TPU:9, one launch (start us, length us, event | category | flops | bytes accessed | tf_op | source)
XLA Modules:
  0.0 475.4 jit_solution(7993237393861842343)
XLA Ops:
  11.5 6.7 %collective-permute-done = bf16[11,80,128]{2,0,1:T(8,128)(2,1)S(1)} collective-permute-done((bf16[11,80,128]{2,0,1:T(8,128)(2,1)S(1)}, bf16[11,80,128]{2,0,1:T(8,128)(2,1)S(1)}, u32[]{:S(2)}, u32[]{:S(2)}) %collective-permute-start) | collective-permute-done | bytes 225312 | tf_op jit(solution)/shard_map/ppermute | solution.py:560
  20.3 7.2 %collective-permute-done.1 = bf16[11,80,128]{2,0,1:T(8,128)(2,1)} collective-permute-done((bf16[11,80,128]{2,0,1:T(8,128)(2,1)S(1)}, bf16[11,80,128]{2,0,1:T(8,128)(2,1)}, u32[]{:S(2)}, u32[]{:S(2)}) %collective-permute-start.1) | collective-permute-done | bytes 225312 | tf_op jit(solution)/shard_map/ppermute | solution.py:560
  30.0 5.7 %byte_norm.1 = bf16[2048,768]{1,0:T(8,128)(2,1)} custom-call(f32[2048,768]{1,0:T(8,128)} %bitcast.223, f32[1,768]{1,0:T(1,128)} %broadcast_in_dim.25.gain_ref), custom_call_target="tpu_custom_call" | custom-call | flops 15728640 | bytes 6294528 | tf_op jit(solution)/shard_map/byte_norm/pallas_call | solution.py:275
  40.3 13.8 %collective-permute-done.3 = bf16[4,64,1280]{2,1,0:T(8,128)(2,1)S(1)} collective-permute-done((bf16[4,64,1280]{2,1,0:T(8,128)(2,1)S(1)}, bf16[4,64,1280]{2,1,0:T(8,128)(2,1)S(1)}, u32[]{:S(2)}, u32[]{:S(2)}) %collective-permute-start.3) | collective-permute-done | bytes 655392 | tf_op jit(solution)/shard_map/ppermute | solution.py:560
  56.0 12.3 %collective-permute-done.4 = bf16[4,64,1280]{2,1,0:T(8,128)(2,1)S(1)} collective-permute-done((bf16[4,64,1280]{2,1,0:T(8,128)(2,1)S(1)}, bf16[4,64,1280]{2,1,0:T(8,128)(2,1)S(1)}, u32[]{:S(2)}, u32[]{:S(2)}) %collective-permute-start.4) | collective-permute-done | bytes 655392 | tf_op jit(solution)/shard_map/ppermute | solution.py:560
  69.3 12.3 %collective-permute-done.5 = bf16[4,64,1280]{2,1,0:T(8,128)(2,1)} collective-permute-done((bf16[4,64,1280]{2,1,0:T(8,128)(2,1)S(1)}, bf16[4,64,1280]{2,1,0:T(8,128)(2,1)}, u32[]{:S(2)}, u32[]{:S(2)}) %collective-permute-start.5) | collective-permute-done | bytes 655392 | tf_op jit(solution)/shard_map/ppermute | solution.py:560
  92.0 6.3 %join_own.2 = (bf16[1280,1280]{1,0:T(8,128)(2,1)}, bf16[1280,768]{1,0:T(8,128)(2,1)S(1)}, bf16[1280,768]{1,0:T(8,128)(2,1)S(1)}) custom-call(s32[2]{0:T(128)S(1)} %pad_add_fusion.where_ref, bf16[320,1280]{1,0:T(8,128)(2,1)S(1)} %bitcast.216, bf16[320,768]{1,0:T(8,128)(2,1)S(1)} %bitcast.219, bf16[320,768]{1,0:T(8,128)(2,1)S(1)} %bitcast.218, ...), custom_call_target="tpu_custom_call" | custom-call | bytes 1351680 | tf_op jit(solution)/shard_map/join_own/pallas_call | solution.py:437
  100.6 6.0 %convolution_convert_fusion.2 = bf16[2048,1280]{1,0:T(8,128)(2,1)} fusion(bf16[2048,768]{1,0:T(8,128)(2,1)S(1)} %copy-done.16, bf16[1280,768]{1,0:T(8,128)(2,1)S(1)} %get-tuple-element.103.key_ref), kind=kOutput, calls=%fused_computation.6 | convolution fusion | flops 4029153280 | bytes 10354688 | tf_op jit(solution)/shard_map/dot_general | solution.py:22
  110.4 8.2 %lse.1.refs_0_ = f32[4,8,256]{2,1,0:T(8,128)S(1)} custom-call(bf16[4,4,64,1280]{3,2,1,0:T(8,128)(2,1)S(1)} %bitcast.213, bf16[4,512,1280]{2,1,0:T(8,128)(2,1)} %bitcast.228, s32[4,1,256]{2,1,0:T(1,128)S(1)} %broadcast_in_dim_reshape.10.lat_seg_ref, s32[4,512,1]{2,1,0:T(8,128)S(1)} %copy.61.byte_seg_ref), custom_call_target="tpu_custom_call" | custom-call | flops 2147483648 | bytes 7876608 | tf_op jit(solution)/shard_map/lse/pallas_call | solution.py:257
  121.9 5.9 %convolution_convert_fusion.1 = bf16[2048,1280]{1,0:T(8,128)(2,1)} fusion(bf16[2048,768]{1,0:T(8,128)(2,1)S(1)} %copy-done.16, bf16[1280,768]{1,0:T(8,128)(2,1)S(1)} %get-tuple-element.109.value_ref), kind=kOutput, calls=%fused_computation.5 | convolution fusion | flops 4029153280 | bytes 10354688 | tf_op jit(solution)/shard_map/dot_general | solution.py:22
  140.2 9.7 %attend.1 = (bf16[4,4,64,1280]{3,2,1,0:T(8,128)(2,1)S(1)}, f32[4,8,256]{2,1,0:T(8,128)S(1)}) custom-call(bf16[4,4,64,1280]{3,2,1,0:T(8,128)(2,1)} %bitcast.214, bf16[4,512,1280]{2,1,0:T(8,128)(2,1)} %bitcast.229, bf16[4,512,1280]{2,1,0:T(8,128)(2,1)} %bitcast.266, s32[4,1,256]{2,1,0:T(1,128)S(1)} %broadcast_in_dim_reshape.10.lat_seg_ref, ...), custom_call_target="tpu_custom_call" | custom-call | flops 4294967296 | bytes 13250560 | tf_op jit(solution)/shard_map/attend/pallas_call | solution.py:257
  155.4 11.2 %collective-permute-done.13 = bf16[4,64,1280]{2,1,0:T(8,128)(2,1)} collective-permute-done((bf16[4,64,1280]{2,1,0:T(8,128)(2,1)}, bf16[4,64,1280]{2,1,0:T(8,128)(2,1)}, u32[]{:S(2)}, u32[]{:S(2)}) %collective-permute-start.13) | collective-permute-done | bytes 655392 | tf_op jit(solution)/shard_map/ppermute | solution.py:560
  169.4 14.1 %collective-permute-done.14 = bf16[4,64,1280]{2,1,0:T(8,128)(2,1)} collective-permute-done((bf16[4,64,1280]{2,1,0:T(8,128)(2,1)S(1)}, bf16[4,64,1280]{2,1,0:T(8,128)(2,1)}, u32[]{:S(2)}, u32[]{:S(2)}) %collective-permute-start.14) | collective-permute-done | bytes 655392 | tf_op jit(solution)/shard_map/ppermute | solution.py:560
  195.2 7.7 %join_own.3 = (bf16[1280,1280]{1,0:T(8,128)(2,1)S(1)}, bf16[1280,1280]{1,0:T(8,128)(2,1)}, bf16[1280,1280]{1,0:T(8,128)(2,1)}) custom-call(s32[2]{0:T(128)S(1)} %pad_add_fusion.where_ref, bf16[320,1280]{1,0:T(8,128)(2,1)S(1)} %copy-done.6, bf16[320,1280]{1,0:T(8,128)(2,1)S(1)} %bitcast.217, bf16[320,1280]{1,0:T(8,128)(2,1)S(1)} %copy-done.4, ...), custom_call_target="tpu_custom_call" | custom-call | bytes 1843200 | tf_op jit(solution)/shard_map/join_own/pallas_call | solution.py:437
  209.1 12.6 %feed.1 = (f32[256,1280]{1,0:T(8,128)}, bf16[256,1280]{1,0:T(8,128)(2,1)}, bf16[256,1280]{1,0:T(8,128)(2,1)}, bf16[256,1280]{1,0:T(8,128)(2,1)}, f32[256,1280]{1...) custom-call(f32[256,1280]{1,0:T(8,128)} %bitcast.222, ...), custom_call_target="tpu_custom_call" | custom-call | flops 3355443200 | bytes 13127680 | tf_op jit(solution)/shard_map/feed/pallas_call | solution.py:275
  222.7 8.9 %grads.1 = (bf16[4,4,15,80,128]{4,3,2,1,0:T(8,128)(2,1)}, bf16[4,4,15,80,128]{4,3,2,1,0:T(8,128)(2,1)}) custom-call(s32[1]{0:T(128)} %bitcast.19.core_ref, bf16[256,1280]{1,0:T(8,128)(2,1)} %get-tuple-element.126.refs_0_, bf16[256,1280]{1,0:T(8,128)(2,1)} %get-tuple-element.127.refs_1_, bf16[256,1280]{1,0:T(8,128)(2,1)} %bitcast.226, ...), custom_call_target="tpu_custom_call" | custom-call | flops 314572800 | bytes 491520 | tf_op jit(solution)/shard_map/grads/pallas_call | solution.py:500
  231.6 9.1 %collective-permute-done.17.refs_1_ = bf16[4,64,1408]{2,1,0:T(8,128)(2,1)S(1)} collective-permute-done((bf16[4,64,1408]{2,1,0:T(8,128)(2,1)}, bf16[4,64,1408]{2,1,0:T(8,128)(2,1)S(1)}, u32[]{:S(2)}, u32[]{:S(2)}) %collective-permute-start.17) | collective-permute-done | bytes 720928 | tf_op jit(solution)/shard_map/ppermute | solution.py:560
  242.1 8.2 %collective-permute-done.19.b_ref = bf16[4,4,15,80,128]{4,3,2,1,0:T(8,128)(2,1)} collective-permute-done((bf16[4,4,15,80,128]{4,3,2,1,0:T(8,128)(2,1)}, bf16[4,4,15,80,128]{4,3,2,1,0:T(8,128)(2,1)}, u32[]{:S(2)}, u32[]{:S(2)}) %collective-permute-start.19) | collective-permute-done | bytes 4915232 | tf_op jit(solution)/shard_map/ppermute | solution.py:557
  250.2 6.7 %add_packed.2 = (bf16[4,4,8,80,128]{4,3,2,1,0:T(8,128)(2,1)}, bf16[4,4,7,80,128]{4,3,2,1,0:T(8,128)(2,1)}) custom-call(bf16[4,4,15,80,128]{4,3,2,1,0:T(8,128)(2,1)} %get-tuple-element.133.a_ref, bf16[4,4,15,80,128]{4,3,2,1,0:T(8,128)(2,1)} %collective-permute-done.19.b_ref), custom_call_target="tpu_custom_call" | custom-call | bytes 1228800 | tf_op jit(solution)/shard_map/add_packed/pallas_call | solution.py:482
  256.9 4.9 %collective-permute-done.18.refs_2_ = bf16[4,64,1408]{2,1,0:T(8,128)(2,1)S(1)} collective-permute-done((bf16[4,64,1408]{2,1,0:T(8,128)(2,1)S(1)}, bf16[4,64,1408]{2,1,0:T(8,128)(2,1)S(1)}, u32[]{:S(2)}, u32[]{:S(2)}) %collective-permute-start.18) | collective-permute-done | bytes 720928 | tf_op jit(solution)/shard_map/ppermute | solution.py:560
  261.8 9.9 %collective-permute-start.20 = (bf16[4,64,1408]{2,1,0:T(8,128)(2,1)S(1)}, bf16[4,64,1408]{2,1,0:T(8,128)(2,1)S(1)}, u32[]{:S(2)}, u32[]{:S(2)}) collective-permute-start(bf16[4,64,1408]{2,1,0:T(8,128)(2,1)S(1)} %collective-permute-done.18.refs_2_), channel_id=1, source_target_pairs={{0,1},{1,2},{2,3},{3,0},{4,5},{5,6},{6,7},{7,4},{8,9},{9,10},{10,1... | collective-permute-start | bytes 2162696 | tf_op jit(solution)/shard_map/ppermute | solution.py:560
  276.6 14.0 %collective-permute-done.20.refs_3_ = bf16[4,64,1408]{2,1,0:T(8,128)(2,1)S(1)} collective-permute-done((bf16[4,64,1408]{2,1,0:T(8,128)(2,1)S(1)}, bf16[4,64,1408]{2,1,0:T(8,128)(2,1)S(1)}, u32[]{:S(2)}, u32[]{:S(2)}) %collective-permute-start.20) | collective-permute-done | bytes 720928 | tf_op jit(solution)/shard_map/ppermute | solution.py:560
  290.5 16.9 %attend_back.1 = (bf16[4,4,64,1280]{3,2,1,0:T(8,128)(2,1)}, bf16[4,512,1280]{2,1,0:T(8,128)(2,1)}, bf16[4,512,1280]{2,1,0:T(8,128)(2,1)}) custom-call(bf16[4,4,64,1280]{3,2,1,0:T(8,128)(2,1)} %bitcast.215, bf16[4,512,1280]{2,1,0:T(8,128)(2,1)} %bitcast.230, bf16[4,512,1280]{2,1,0:T(8,128)(2,1)} %bitcast.267, ...), custom_call_target="tpu_custom_call" | custom-call | flops 10737418240 | bytes 16035840 | tf_op jit(solution)/shard_map/attend_back/pallas_call | solution.py:257
  308.8 6.9 %convolution_convert_fusion.3.refs_2_ = bf16[1280,768]{1,0:T(8,128)(2,1)S(1)} fusion(bf16[2048,1280]{1,0:T(8,128)(2,1)} %bitcast.272, bf16[2048,768]{1,0:T(8,128)(2,1)S(1)} %copy-done.17), kind=kOutput, calls=%fused_computation.8 | convolution fusion | flops 4027514880 | bytes 10354688 | tf_op jit(solution)/shard_map/dot_general | solution.py:22
  322.9 6.4 %collective-permute-done.25 = bf16[4,7,80,128]{3,2,1,0:T(8,128)(2,1)S(1)} collective-permute-done((bf16[4,7,80,128]{3,2,1,0:T(8,128)(2,1)S(1)}, bf16[4,7,80,128]{3,2,1,0:T(8,128)(2,1)S(1)}, u32[]{:S(2)}, u32[]{:S(2)}) %collective-permute-start.25) | collective-permute-done | bytes 573472 | tf_op jit(solution)/shard_map/ppermute | solution.py:557
  335.8 5.2 %convolution_convert_fusion.refs_0_ = bf16[1280,1280]{1,0:T(8,128)(2,1)} fusion(bf16[1024,1280]{1,0:T(8,128)(2,1)S(1)} %bitcast.240, bf16[1024,1280]{1,0:T(8,128)(2,1)S(1)} %bitcast.236), kind=kOutput, calls=%fused_computation.4 | convolution fusion | flops 3357081600 | bytes 8519680 | tf_op jit(solution)/shard_map/dot_general | solution.py:22
  341.0 5.8 %split.1 = (bf16[4,4,11,80,128]{4,3,2,1,0:T(8,128)(2,1)}, bf16[4,4,11,80,128]{4,3,2,1,0:T(8,128)(2,1)}) custom-call(s32[1]{0:T(128)} %bitcast.19.core_ref, bf16[1280,1280]{1,0:T(8,128)(2,1)} %convolution_convert_fusion.refs_0_, bf16[1280,768]{1,0:T(8,128)(2,1)S(1)} %convolution_convert_fusion.4.refs_1_, bf16[1280,768]{1,0:T(8,128)(2,1)S(1)} %convolution_convert_fusion.3.refs_2_), custom_call_target="tpu_custom_call" | custom-call | bytes 1802240 | tf_op jit(solution)/shard_map/split/pallas_call | solution.py:464
  355.3 5.5 %add_packed.3 = (bf16[4,4,6,80,128]{4,3,2,1,0:T(8,128)(2,1)}, bf16[4,4,5,80,128]{4,3,2,1,0:T(8,128)(2,1)}) custom-call(bf16[4,4,11,80,128]{4,3,2,1,0:T(8,128)(2,1)} %get-tuple-element.147.a_ref, bf16[4,4,11,80,128]{4,3,2,1,0:T(8,128)(2,1)} %collective-permute-done.27.b_ref), custom_call_target="tpu_custom_call" | custom-call | bytes 901120 | tf_op jit(solution)/shard_map/add_packed/pallas_call | solution.py:482
  370.3 15.6 %byte_back.1 = (f32[2048,768]{1,0:T(8,128)}, f32[1,768]{1,0:T(1,128)}) custom-call(f32[2048,768]{1,0:T(8,128)} %bitcast.224, f32[1,768]{1,0:T(1,128)} %broadcast_in_dim.25.gain_ref, bf16[1280,768]{1,0:T(8,128)(2,1)} %copy-done.9, bf16[1280,768]{1,0:T(8,128)(2,1)} %copy-done.10, bf16[2048,1280]{1,0:T(8,128)(2,1)} %bitcast.268, bf16[2048,1280]{1,0:T(8,128)(2,1)} %bitcast.273), custom_call_target="tpu_custom_call" | custom-call | flops 8053063680 | bytes 20712448 | tf_op jit(solution)/shard_map/byte_back/pallas_call | solution.py:275
  392.5 11.3 %collective-permute-done.31 = bf16[4,64,1280]{2,1,0:T(8,128)(2,1)S(1)} collective-permute-done((bf16[4,64,1280]{2,1,0:T(8,128)(2,1)S(1)}, bf16[4,64,1280]{2,1,0:T(8,128)(2,1)S(1)}, u32[]{:S(2)}, u32[]{:S(2)}) %collective-permute-start.31) | collective-permute-done | bytes 655392 | tf_op jit(solution)/shard_map/ppermute | solution.py:560
  416.7 7.6 %collective-permute-done.39 = bf16[1,80,128]{2,1,0:T(8,128)(2,1)S(1)} collective-permute-done((bf16[1,80,128]{2,1,0:T(8,128)(2,1)S(1)}, bf16[1,80,128]{2,1,0:T(8,128)(2,1)S(1)}, u32[]{:S(2)}, u32[]{:S(2)}) %collective-permute-start.39) | collective-permute-done | bytes 20512 | tf_op jit(solution)/shard_map/ppermute | solution.py:560
  426.0 6.3 %collective-permute-done.35 = bf16[11,80,128]{2,1,0:T(8,128)(2,1)S(1)} collective-permute-done((bf16[11,80,128]{2,1,0:T(8,128)(2,1)S(1)}, bf16[11,80,128]{2,1,0:T(8,128)(2,1)S(1)}, u32[]{:S(2)}, u32[]{:S(2)}) %collective-permute-start.35) | collective-permute-done | bytes 225312 | tf_op jit(solution)/shard_map/ppermute | solution.py:560
  (314 shorter events, 170.7 us)
Async XLA Ops:
  7.2 77.6 %all-gather.5.cloned.1.call-start = ((), (), s32[]{:S(2)}) async-start(), calls=%async_computation | async-start | bytes 3379200 | tf_op jit(solution)/shard_map/all_gather | solution.py:600
  38.9 144.6 %all-gather.7.cloned.1.call-start = ((), (), s32[]{:S(2)}) async-start(), calls=%async_computation.1 | async-start | bytes 4608000 | tf_op jit(solution)/shard_map/all_gather | solution.py:600
  39.0 15.1 %collective-permute-start.3 = (bf16[4,64,1280]{2,1,0:T(8,128)(2,1)S(1)}, bf16[4,64,1280]{2,1,0:T(8,128)(2,1)S(1)}, u32[]{:S(2)}, u32[]{:S(2)}) collective-permute-start(bf16[4,64,1280]{2,1,0:T(8,128)(2,1)S(1)} %multiply_convert_fusion.1), channel_id=1, source_target_pairs={{0,1},{1,2},{2,3},{3,0},{4,5},{5,6},{6,7},{7,4},{8,9},{9,10},{10,1... | collective-permute-start | bytes 1966088 | tf_op jit(solution)/shard_map/ppermute | solution.py:560
  54.1 14.2 %collective-permute-start.4 = (bf16[4,64,1280]{2,1,0:T(8,128)(2,1)S(1)}, bf16[4,64,1280]{2,1,0:T(8,128)(2,1)S(1)}, u32[]{:S(2)}, u32[]{:S(2)}) collective-permute-start(bf16[4,64,1280]{2,1,0:T(8,128)(2,1)S(1)} %collective-permute-done.3), channel_id=1, source_target_pairs={{0,1},{1,2},{2,3},{3,0},{4,5},{5,6},{6,7},{7,4},{8,9},{9,10},{10,1... | collective-permute-start | bytes 1966088 | tf_op jit(solution)/shard_map/ppermute | solution.py:560
  68.3 13.3 %collective-permute-start.5 = (bf16[4,64,1280]{2,1,0:T(8,128)(2,1)S(1)}, bf16[4,64,1280]{2,1,0:T(8,128)(2,1)}, u32[]{:S(2)}, u32[]{:S(2)}) collective-permute-start(bf16[4,64,1280]{2,1,0:T(8,128)(2,1)S(1)} %collective-permute-done.4), channel_id=1, source_target_pairs={{0,1},{1,2},{2,3},{3,0},{4,5},{5,6},{6,7},{7,4},{8,9},{9,10},{10,1... | collective-permute-start | bytes 1966088 | tf_op jit(solution)/shard_map/ppermute | solution.py:560
  106.5 12.1 %collective-permute-start.8 = (bf16[16,80,128]{2,0,1:T(8,128)(2,1)S(1)}, bf16[16,80,128]{2,0,1:T(8,128)(2,1)S(1)}, u32[]{:S(2)}, u32[]{:S(2)}) collective-permute-start(bf16[16,80,128]{2,0,1:T(8,128)(2,1)S(1)} %collective-permute-done.7), channel_id=1, source_target_pairs={{0,1},{1,2},{2,3},{3,0},{4,5},{5,6},{6,7},{7,4},{8,9},{9,10},{10,1... | collective-permute-start | bytes 983048 | tf_op jit(solution)/shard_map/ppermute | solution.py:560
  152.3 14.3 %collective-permute-start.13 = (bf16[4,64,1280]{2,1,0:T(8,128)(2,1)}, bf16[4,64,1280]{2,1,0:T(8,128)(2,1)}, u32[]{:S(2)}, u32[]{:S(2)}) collective-permute-start(bf16[4,64,1280]{2,1,0:T(8,128)(2,1)} %slice_bitcast_fusion.1), channel_id=1, source_target_pairs={{0,1},{1,2},{2,3},{3,0},{4,5},{5,6},{6,7},{7,4},{8,9},{9,10},{10,1... | collective-permute-start | bytes 1966088 | tf_op jit(solution)/shard_map/ppermute | solution.py:560
  168.1 15.4 %collective-permute-start.14 = (bf16[4,64,1280]{2,1,0:T(8,128)(2,1)S(1)}, bf16[4,64,1280]{2,1,0:T(8,128)(2,1)}, u32[]{:S(2)}, u32[]{:S(2)}) collective-permute-start(bf16[4,64,1280]{2,1,0:T(8,128)(2,1)S(1)} %fusion.10), channel_id=1, source_target_pairs={{0,1},{1,2},{2,3},{3,0},{4,5},{5,6},{6,7},{7,4},{8,9},{9,10},{10,1... | collective-permute-start | bytes 1966088 | tf_op jit(solution)/shard_map/ppermute | solution.py:560
  188.6 18.4 %collective-permute-start.15 = (bf16[4,64,1280]{2,1,0:T(8,128)(2,1)S(1)}, bf16[4,64,1280]{2,1,0:T(8,128)(2,1)S(1)}, u32[]{:S(2)}, u32[]{:S(2)}) collective-permute-start(bf16[4,64,1280]{2,1,0:T(8,128)(2,1)S(1)} %fusion.9), channel_id=1, source_target_pairs={{0,1},{1,2},{2,3},{3,0},{4,5},{5,6},{6,7},{7,4},{8,9},{9,10},{10,1... | collective-permute-start | bytes 1966088 | tf_op jit(solution)/shard_map/ppermute | solution.py:560
  221.7 19.0 %collective-permute-start.17 = (bf16[4,64,1408]{2,1,0:T(8,128)(2,1)}, bf16[4,64,1408]{2,1,0:T(8,128)(2,1)S(1)}, u32[]{:S(2)}, u32[]{:S(2)}) collective-permute-start(bf16[4,64,1408]{2,1,0:T(8,128)(2,1)} %bitcast.220), channel_id=1, source_target_pairs={{0,1},{1,2},{2,3},{3,0},{4,5},{5,6},{6,7},{7,4},{8,9},{9,10},{10,1... | collective-permute-start | bytes 2162696 | tf_op jit(solution)/shard_map/ppermute | solution.py:560
  242.1 19.8 %collective-permute-start.18 = (bf16[4,64,1408]{2,1,0:T(8,128)(2,1)S(1)}, bf16[4,64,1408]{2,1,0:T(8,128)(2,1)S(1)}, u32[]{:S(2)}, u32[]{:S(2)}) collective-permute-start(bf16[4,64,1408]{2,1,0:T(8,128)(2,1)S(1)} %collective-permute-done.17.refs_1_), channel_id=1, source_target_pairs={{0,1},{1,2},{2,3},{3,0},{4,5},{5,6},{6,7},{7,4},{8,9},{9,10},{10,1... | collective-permute-start | bytes 2162696 | tf_op jit(solution)/shard_map/ppermute | solution.py:560
  261.8 28.7 %collective-permute-start.20 = (bf16[4,64,1408]{2,1,0:T(8,128)(2,1)S(1)}, bf16[4,64,1408]{2,1,0:T(8,128)(2,1)S(1)}, u32[]{:S(2)}, u32[]{:S(2)}) collective-permute-start(bf16[4,64,1408]{2,1,0:T(8,128)(2,1)S(1)} %collective-permute-done.18.refs_2_), channel_id=1, source_target_pairs={{0,1},{1,2},{2,3},{3,0},{4,5},{5,6},{6,7},{7,4},{8,9},{9,10},{10,1... | collective-permute-start | bytes 2162696 | tf_op jit(solution)/shard_map/ppermute | solution.py:560
  273.2 42.6 %collective-permute-start.24 = (bf16[2,4,7,80,128]{4,3,2,1,0:T(8,128)(2,1)S(1)}, bf16[2,4,7,80,128]{4,3,2,1,0:T(8,128)(2,1)S(1)}, u32[]{:S(2)}, u32[]{:S(2)}) collective-permute-start(bf16[2,4,7,80,128]{4,3,2,1,0:T(8,128)(2,1)S(1)} %dynamic-slice_bitcast_fusion.1), channel_id=1, source_target_pairs={{0,16},{4,20},{8,24},{12,28},{16,0},{20,4},{24,8},{28,12},{1,17},{... | collective-permute-start | bytes 3440648 | tf_op jit(solution)/shard_map/ppermute | solution.py:557
  275.3 41.5 %collective-permute-start.22 = (bf16[2,4,8,80,128]{4,3,2,1,0:T(8,128)(2,1)S(1)}, bf16[2,4,8,80,128]{4,3,2,1,0:T(8,128)(2,1)S(1)}, u32[]{:S(2)}, u32[]{:S(2)}) collective-permute-start(bf16[2,4,8,80,128]{4,3,2,1,0:T(8,128)(2,1)S(1)} %dynamic-slice_bitcast_fusion), channel_id=1, source_target_pairs={{0,8},{4,12},{8,0},{12,4},{16,24},{20,28},{24,16},{28,20},{1,9},{5... | collective-permute-start | bytes 3932168 | tf_op jit(solution)/shard_map/ppermute | solution.py:557
  308.7 24.3 %collective-permute-start.21 = (bf16[4,64,1280]{2,1,0:T(8,128)(2,1)S(1)}, bf16[4,64,1280]{2,1,0:T(8,128)(2,1)S(1)}, u32[]{:S(2)}, u32[]{:S(2)}) collective-permute-start(bf16[4,64,1280]{2,1,0:T(8,128)(2,1)S(1)} %slice_bitcast_fusion), channel_id=1, source_target_pairs={{0,1},{1,2},{2,3},{3,0},{4,5},{5,6},{6,7},{7,4},{8,9},{9,10},{10,1... | collective-permute-start | bytes 1966088 | tf_op jit(solution)/shard_map/ppermute | solution.py:560
  316.1 13.2 %collective-permute-start.25 = (bf16[4,7,80,128]{3,2,1,0:T(8,128)(2,1)S(1)}, bf16[4,7,80,128]{3,2,1,0:T(8,128)(2,1)S(1)}, u32[]{:S(2)}, u32[]{:S(2)}) collective-permute-start(bf16[4,7,80,128]{3,2,1,0:T(8,128)(2,1)S(1)} %dynamic-slice_bitcast_fusion.5), channel_id=1, source_target_pairs={{0,8},{4,12},{8,0},{12,4},{16,24},{20,28},{24,16},{28,20},{1,9},{5... | collective-permute-start | bytes 1720328 | tf_op jit(solution)/shard_map/ppermute | solution.py:557
  317.9 14.9 %collective-permute-start.23 = (bf16[4,8,80,128]{3,2,1,0:T(8,128)(2,1)S(1)}, bf16[4,8,80,128]{3,2,1,0:T(8,128)(2,1)S(1)}, u32[]{:S(2)}, u32[]{:S(2)}) collective-permute-start(bf16[4,8,80,128]{3,2,1,0:T(8,128)(2,1)S(1)} %dynamic-slice_bitcast_fusion.4), channel_id=1, source_target_pairs={{0,16},{4,20},{8,24},{12,28},{16,0},{20,4},{24,8},{28,12},{1,17},{... | collective-permute-start | bytes 1966088 | tf_op jit(solution)/shard_map/ppermute | solution.py:557
  361.0 25.7 %collective-permute-start.40 = (bf16[15,80,128]{2,1,0:T(8,128)(2,1)S(1)}, bf16[15,80,128]{2,1,0:T(8,128)(2,1)}, u32[]{:S(2)}, u32[]{:S(2)}) collective-permute-start(bf16[15,80,128]{2,1,0:T(8,128)(2,1)S(1)} %fusion.16), channel_id=1, source_target_pairs={{0,1},{1,2},{2,3},{3,0},{4,5},{5,6},{6,7},{7,4},{8,9},{9,10},{10,1... | collective-permute-start | bytes 921608 | tf_op jit(solution)/shard_map/ppermute | solution.py:560
  364.5 25.0 %collective-permute-start.29 = (bf16[2,4,5,80,128]{4,3,2,1,0:T(8,128)(2,1)}, bf16[2,4,5,80,128]{4,3,2,1,0:T(8,128)(2,1)}, u32[]{:S(2)}, u32[]{:S(2)}) collective-permute-start(bf16[2,4,5,80,128]{4,3,2,1,0:T(8,128)(2,1)} %dynamic-slice_bitcast_fusion.3), channel_id=1, source_target_pairs={{0,16},{4,20},{8,24},{12,28},{16,0},{20,4},{24,8},{28,12},{1,17},{... | collective-permute-start | bytes 2457608 | tf_op jit(solution)/shard_map/ppermute | solution.py:557
  365.2 25.7 %collective-permute-start.28 = (bf16[2,4,6,80,128]{4,3,2,1,0:T(8,128)(2,1)S(1)}, bf16[2,4,6,80,128]{4,3,2,1,0:T(8,128)(2,1)S(1)}, u32[]{:S(2)}, u32[]{:S(2)}) collective-permute-start(bf16[2,4,6,80,128]{4,3,2,1,0:T(8,128)(2,1)S(1)} %dynamic-slice_bitcast_fusion.2), channel_id=1, source_target_pairs={{0,8},{4,12},{8,0},{12,4},{16,24},{20,28},{24,16},{28,20},{1,9},{5... | collective-permute-start | bytes 2949128 | tf_op jit(solution)/shard_map/ppermute | solution.py:557
  366.5 21.3 %collective-permute-start.30 = (bf16[4,64,1280]{2,1,0:T(8,128)(2,1)}, bf16[4,64,1280]{2,1,0:T(8,128)(2,1)}, u32[]{:S(2)}, u32[]{:S(2)}) collective-permute-start(bf16[4,64,1280]{2,1,0:T(8,128)(2,1)} %fusion.6), channel_id=1, source_target_pairs={{0,1},{1,2},{2,3},{3,0},{4,5},{5,6},{6,7},{7,4},{8,9},{9,10},{10,1... | collective-permute-start | bytes 1966088 | tf_op jit(solution)/shard_map/ppermute | solution.py:560
  389.1 14.8 %collective-permute-start.31 = (bf16[4,64,1280]{2,1,0:T(8,128)(2,1)S(1)}, bf16[4,64,1280]{2,1,0:T(8,128)(2,1)S(1)}, u32[]{:S(2)}, u32[]{:S(2)}) collective-permute-start(bf16[4,64,1280]{2,1,0:T(8,128)(2,1)S(1)} %fusion.5), channel_id=1, source_target_pairs={{0,1},{1,2},{2,3},{3,0},{4,5},{5,6},{6,7},{7,4},{8,9},{9,10},{10,1... | collective-permute-start | bytes 1966088 | tf_op jit(solution)/shard_map/ppermute | solution.py:560
  391.3 12.8 %collective-permute-start.33 = (bf16[4,5,80,128]{3,2,1,0:T(8,128)(2,1)S(1)}, bf16[4,5,80,128]{3,2,1,0:T(8,128)(2,1)S(1)}, u32[]{:S(2)}, u32[]{:S(2)}) collective-permute-start(bf16[4,5,80,128]{3,2,1,0:T(8,128)(2,1)S(1)} %dynamic-slice_bitcast_fusion.7), channel_id=1, source_target_pairs={{0,8},{4,12},{8,0},{12,4},{16,24},{20,28},{24,16},{28,20},{1,9},{5... | collective-permute-start | bytes 1228808 | tf_op jit(solution)/shard_map/ppermute | solution.py:557
  391.7 12.6 %collective-permute-start.32 = (bf16[4,6,80,128]{3,2,1,0:T(8,128)(2,1)S(1)}, bf16[4,6,80,128]{3,2,1,0:T(8,128)(2,1)S(1)}, u32[]{:S(2)}, u32[]{:S(2)}) collective-permute-start(bf16[4,6,80,128]{3,2,1,0:T(8,128)(2,1)S(1)} %dynamic-slice_bitcast_fusion.6), channel_id=1, source_target_pairs={{0,16},{4,20},{8,24},{12,28},{16,0},{20,4},{24,8},{28,12},{1,17},{... | collective-permute-start | bytes 1474568 | tf_op jit(solution)/shard_map/ppermute | solution.py:557
  412.5 11.8 %collective-permute-start.39 = (bf16[1,80,128]{2,1,0:T(8,128)(2,1)S(1)}, bf16[1,80,128]{2,1,0:T(8,128)(2,1)S(1)}, u32[]{:S(2)}, u32[]{:S(2)}) collective-permute-start(bf16[1,80,128]{2,1,0:T(8,128)(2,1)S(1)} %fusion.43), channel_id=1, source_target_pairs={{0,3},{1,0},{2,1},{3,2},{4,7},{5,4},{6,5},{7,6},{8,11},{9,8},{10,9... | collective-permute-start | bytes 61448 | tf_op jit(solution)/shard_map/ppermute | solution.py:560
  412.5 12.3 %collective-permute-start.34 = (bf16[11,80,128]{2,1,0:T(8,128)(2,1)S(1)}, bf16[11,80,128]{2,1,0:T(8,128)(2,1)S(1)}, u32[]{:S(2)}, u32[]{:S(2)}) collective-permute-start(bf16[11,80,128]{2,1,0:T(8,128)(2,1)S(1)} %get-tuple-element.176), channel_id=1, source_target_pairs={{0,1},{1,2},{2,3},{3,0},{4,5},{5,6},{6,7},{7,4},{8,9},{9,10},{10,1... | collective-permute-start | bytes 675848 | tf_op jit(solution)/shard_map/ppermute | solution.py:560
  414.1 18.3 %collective-permute-start.35 = (bf16[11,80,128]{2,1,0:T(8,128)(2,1)S(1)}, bf16[11,80,128]{2,1,0:T(8,128)(2,1)S(1)}, u32[]{:S(2)}, u32[]{:S(2)}) collective-permute-start(bf16[11,80,128]{2,1,0:T(8,128)(2,1)S(1)} %get-tuple-element.177), channel_id=1, source_target_pairs={{0,2},{1,3},{2,0},{3,1},{4,6},{5,7},{6,4},{7,5},{8,10},{9,11},{10,... | collective-permute-start | bytes 675848 | tf_op jit(solution)/shard_map/ppermute | solution.py:560
  415.9 21.1 %collective-permute-start.36 = (bf16[11,80,128]{2,1,0:T(8,128)(2,1)S(1)}, bf16[11,80,128]{2,1,0:T(8,128)(2,1)S(1)}, u32[]{:S(2)}, u32[]{:S(2)}) collective-permute-start(bf16[11,80,128]{2,1,0:T(8,128)(2,1)S(1)} %get-tuple-element.178), channel_id=1, source_target_pairs={{0,3},{1,0},{2,1},{3,2},{4,7},{5,4},{6,5},{7,6},{8,11},{9,8},{10,9... | collective-permute-start | bytes 675848 | tf_op jit(solution)/shard_map/ppermute | solution.py:560
  416.0 21.1 %collective-permute-start.42 = (bf16[15,80,128]{2,1,0:T(8,128)(2,1)S(1)}, bf16[15,80,128]{2,1,0:T(8,128)(2,1)S(1)}, u32[]{:S(2)}, u32[]{:S(2)}) collective-permute-start(bf16[15,80,128]{2,1,0:T(8,128)(2,1)S(1)} %fusion.14), channel_id=1, source_target_pairs={{0,8},{4,12},{8,0},{12,4},{16,24},{20,28},{24,16},{28,20},{1,9},{5... | collective-permute-start | bytes 921608 | tf_op jit(solution)/shard_map/ppermute | solution.py:557
  424.3 12.9 %collective-permute-start.43 = (bf16[15,80,128]{2,1,0:T(8,128)(2,1)S(1)}, bf16[15,80,128]{2,1,0:T(8,128)(2,1)S(1)}, u32[]{:S(2)}, u32[]{:S(2)}) collective-permute-start(bf16[15,80,128]{2,1,0:T(8,128)(2,1)S(1)} %fusion.14), channel_id=1, source_target_pairs={{0,16},{4,20},{8,24},{12,28},{16,0},{20,4},{24,8},{28,12},{1,17},{... | collective-permute-start | bytes 921608 | tf_op jit(solution)/shard_map/ppermute | solution.py:557
  424.9 12.3 %collective-permute-start.44 = (bf16[15,80,128]{2,1,0:T(8,128)(2,1)S(1)}, bf16[15,80,128]{2,1,0:T(8,128)(2,1)S(1)}, u32[]{:S(2)}, u32[]{:S(2)}) collective-permute-start(bf16[15,80,128]{2,1,0:T(8,128)(2,1)S(1)} %fusion.14), channel_id=1, source_target_pairs={{0,24},{4,28},{8,16},{12,20},{16,8},{20,12},{24,0},{28,4},{1,25},{... | collective-permute-start | bytes 921608 | tf_op jit(solution)/shard_map/ppermute | solution.py:557
  440.9 18.5 %collective-permute-start.49 = (bf16[4,1,15,80,128]{4,3,2,1,0:T(8,128)(2,1)S(1)}, bf16[4,1,15,80,128]{4,3,2,1,0:T(8,128)(2,1)S(1)}, u32[]{:S(2)}, u32[]{:S(2)}) collective-permute-start(bf16[4,1,15,80,128]{4,3,2,1,0:T(8,128)(2,1)S(1)} %bitcast.208), channel_id=1, source_target_pairs={{0,4},{4,0},{8,12},{12,8},{16,20},{20,16},{24,28},{28,24},{1,5},{5... | collective-permute-start | bytes 3686408 | tf_op jit(solution)/shard_map/ppermute | solution.py:557
  (71 other events, 746.4 us)
Sparse Core Ops, SparseCore 0:
  39.1 45.7 all-gather.4
  131.4 51.0 all-gather.6

commit v8 on v7

--- a/solution.py
+++ b/solution.py
@@ -261,7 +261,7 @@
         out_specs=[spec(o.shape) for o in outs],
         out_shape=outs,
         name=name,
-        cost_estimate=pl.CostEstimate(flops=flops, bytes_accessed=moved, transcendentals=0),
+        cost_estimate=pl.CostEstimate(flops=2 * flops, bytes_accessed=2 * moved, transcendentals=0),
         compiler_params=pltpu.CompilerParams(vmem_limit_bytes=48 * 1024 * 1024),
     )(*args)
 
@@ -280,7 +280,7 @@
         out_shape=[o for o, _ in outs],
         scratch_shapes=list(scratch),
         name=name,
-        cost_estimate=pl.CostEstimate(flops=flops, bytes_accessed=moved, transcendentals=0),
+        cost_estimate=pl.CostEstimate(flops=2 * flops, bytes_accessed=2 * moved, transcendentals=0),
         compiler_params=pltpu.CompilerParams(vmem_limit_bytes=56 * 1024 * 1024),
     )(*[a for a, _ in args])
 

time: 484 us -> 481 us (level)
  transfers between devices with their start and end apart: 52 -> 52, of which waited for: 27 -> 28; matrix products, arithmetic and copies ran while one was open for 13% -> 14% of each run, Pallas kernels for 20% -> 20%
where the time goes in v8:
time: 481 us; the launch traced here: 472 us
  waiting for transfers between devices  175 us (36%)
  Pallas kernels  112 us (23%)
  starting transfers between devices  72.9 us (15%)
  local copies, waits for them, and re-layouts  35 us (7%)
  matrix products  34.7 us (7%)
  other arithmetic  26.4 us (5%)
  between operations  15.6 us (3%)
    ppermute x30, waiting for transfers between devices, shift(): return lax.ppermute(x, 'mp', ring(self.mp, step))  142 us
    ppermute x30, starting transfers between devices, shift(): return lax.ppermute(x, 'mp', ring(self.mp, step))  42.8 us
    pallas_call x3, Pallas kernels, row_call(): pl.pallas_call(kernel, grid=(outs[-1].shape[0],), in_specs=[spec(a.shape)...  34.9 us
    dot_general x7, matrix products, dot(): return lax.dot_general(a, b, dims, preferred_element_type=F32)  34.7 us
    pallas_call x3, Pallas kernels, block_call(): pl.pallas_call(kernel, grid=(args[0][0].shape[0] // lines,), in_specs=[sp...  33.9 us
    ppermute x20, waiting for transfers between devices, swap(): return lax.ppermute(x, 'dp', [(i, i ^ bit) for i in range(self.dp)])  30.6 us
    ppermute x20, starting transfers between devices, swap(): return lax.ppermute(x, 'dp', [(i, i ^ bit) for i in range(self.dp)])  30 us
    pallas_call x2, Pallas kernels, join_own(): pl.pallas_call(functools.partial(join_own_kernel, widths), grid_spec=pltp...  13.9 us
  transfers between devices with their start and end apart: 52, of which 28 were waited for; matrix products, arithmetic and copies ran while one was open for 14% of the time, Pallas kernels for 20%

profile of v8, /device:TPU:9, one launch (start us, length us, event | category | flops | bytes accessed | tf_op | source)
XLA Modules:
  0.0 471.7 jit_solution(12166636937055298636)
XLA Ops:
  11.5 6.7 %collective-permute-done = bf16[11,80,128]{2,0,1:T(8,128)(2,1)S(1)} collective-permute-done((bf16[11,80,128]{2,0,1:T(8,128)(2,1)S(1)}, bf16[11,80,128]{2,0,1:T(8,128)(2,1)S(1)}, u32[]{:S(2)}, u32[]{:S(2)}) %collective-permute-start) | collective-permute-done | bytes 225312 | tf_op jit(solution)/shard_map/ppermute | solution.py:560
  20.3 7.1 %collective-permute-done.1 = bf16[11,80,128]{2,0,1:T(8,128)(2,1)S(1)} collective-permute-done((bf16[11,80,128]{2,0,1:T(8,128)(2,1)S(1)}, bf16[11,80,128]{2,0,1:T(8,128)(2,1)S(1)}, u32[]{:S(2)}, u32[]{:S(2)}) %collective-permute-start.1) | collective-permute-done | bytes 225312 | tf_op jit(solution)/shard_map/ppermute | solution.py:560
  29.9 5.7 %byte_norm.1 = bf16[2048,768]{1,0:T(8,128)(2,1)} custom-call(f32[2048,768]{1,0:T(8,128)} %bitcast.223, f32[1,768]{1,0:T(1,128)} %broadcast_in_dim.25.gain_ref), custom_call_target="tpu_custom_call" | custom-call | flops 31457280 | bytes 12589056 | tf_op jit(solution)/shard_map/byte_norm/pallas_call | solution.py:275
  39.3 14.0 %collective-permute-done.3 = bf16[4,64,1280]{2,1,0:T(8,128)(2,1)S(1)} collective-permute-done((bf16[4,64,1280]{2,1,0:T(8,128)(2,1)S(1)}, bf16[4,64,1280]{2,1,0:T(8,128)(2,1)S(1)}, u32[]{:S(2)}, u32[]{:S(2)}) %collective-permute-start.3) | collective-permute-done | bytes 655392 | tf_op jit(solution)/shard_map/ppermute | solution.py:560
  54.9 12.8 %collective-permute-done.4 = bf16[4,64,1280]{2,1,0:T(8,128)(2,1)S(1)} collective-permute-done((bf16[4,64,1280]{2,1,0:T(8,128)(2,1)S(1)}, bf16[4,64,1280]{2,1,0:T(8,128)(2,1)S(1)}, u32[]{:S(2)}, u32[]{:S(2)}) %collective-permute-start.4) | collective-permute-done | bytes 655392 | tf_op jit(solution)/shard_map/ppermute | solution.py:560
  68.2 13.1 %collective-permute-done.5 = bf16[4,64,1280]{2,1,0:T(8,128)(2,1)} collective-permute-done((bf16[4,64,1280]{2,1,0:T(8,128)(2,1)S(1)}, bf16[4,64,1280]{2,1,0:T(8,128)(2,1)}, u32[]{:S(2)}, u32[]{:S(2)}) %collective-permute-start.5) | collective-permute-done | bytes 655392 | tf_op jit(solution)/shard_map/ppermute | solution.py:560
  91.5 6.3 %join_own.2 = (bf16[1280,1280]{1,0:T(8,128)(2,1)}, bf16[1280,768]{1,0:T(8,128)(2,1)S(1)}, bf16[1280,768]{1,0:T(8,128)(2,1)S(1)}) custom-call(s32[2]{0:T(128)S(1)} %pad_add_fusion.where_ref, bf16[320,1280]{1,0:T(8,128)(2,1)S(1)} %bitcast.213, bf16[320,768]{1,0:T(8,128)(2,1)S(1)} %bitcast.216, bf16[320,768]{1,0:T(8,128)(2,1)S(1)} %bitcast.215, ...), custom_call_target="tpu_custom_call" | custom-call | bytes 1351680 | tf_op jit(solution)/shard_map/join_own/pallas_call | solution.py:437
  100.1 6.0 %convolution_convert_fusion.2 = bf16[2048,1280]{1,0:T(8,128)(2,1)} fusion(bf16[2048,768]{1,0:T(8,128)(2,1)S(1)} %copy-done.17, bf16[1280,768]{1,0:T(8,128)(2,1)S(1)} %get-tuple-element.103.key_ref), kind=kOutput, calls=%fused_computation.6 | convolution fusion | flops 4029153280 | bytes 10354688 | tf_op jit(solution)/shard_map/dot_general | solution.py:22
  109.9 8.2 %lse.1.refs_0_ = f32[4,8,256]{2,1,0:T(8,128)S(1)} custom-call(bf16[4,4,64,1280]{3,2,1,0:T(8,128)(2,1)S(1)} %bitcast.219, bf16[4,512,1280]{2,1,0:T(8,128)(2,1)} %bitcast.263, s32[4,1,256]{2,1,0:T(1,128)S(1)} %broadcast_in_dim_reshape.10.lat_seg_ref, s32[4,512,1]{2,1,0:T(8,128)S(1)} %copy.61.byte_seg_ref), custom_call_target="tpu_custom_call" | custom-call | flops 4294967296 | bytes 15753216 | tf_op jit(solution)/shard_map/lse/pallas_call | solution.py:257
  121.4 6.0 %convolution_convert_fusion.1 = bf16[2048,1280]{1,0:T(8,128)(2,1)} fusion(bf16[2048,768]{1,0:T(8,128)(2,1)S(1)} %copy-done.17, bf16[1280,768]{1,0:T(8,128)(2,1)S(1)} %get-tuple-element.109.value_ref), kind=kOutput, calls=%fused_computation.5 | convolution fusion | flops 4029153280 | bytes 10354688 | tf_op jit(solution)/shard_map/dot_general | solution.py:22
  139.6 9.8 %attend.1 = (bf16[4,4,64,1280]{3,2,1,0:T(8,128)(2,1)S(1)}, f32[4,8,256]{2,1,0:T(8,128)S(1)}) custom-call(bf16[4,4,64,1280]{3,2,1,0:T(8,128)(2,1)} %bitcast.220, bf16[4,512,1280]{2,1,0:T(8,128)(2,1)} %bitcast.264, bf16[4,512,1280]{2,1,0:T(8,128)(2,1)} %bitcast.266, s32[4,1,256]{2,1,0:T(1,128)S(1)} %broadcast_in_dim_reshape.10.lat_seg_ref, ...), custom_call_target="tpu_custom_call" | custom-call | flops 8589934592 | bytes 26501120 | tf_op jit(solution)/shard_map/attend/pallas_call | solution.py:257
  153.3 10.5 %collective-permute-done.13 = bf16[4,64,1280]{2,1,0:T(8,128)(2,1)} collective-permute-done((bf16[4,64,1280]{2,1,0:T(8,128)(2,1)}, bf16[4,64,1280]{2,1,0:T(8,128)(2,1)}, u32[]{:S(2)}, u32[]{:S(2)}) %collective-permute-start.13) | collective-permute-done | bytes 655392 | tf_op jit(solution)/shard_map/ppermute | solution.py:560
  167.0 14.2 %collective-permute-done.14 = bf16[4,64,1280]{2,1,0:T(8,128)(2,1)} collective-permute-done((bf16[4,64,1280]{2,1,0:T(8,128)(2,1)S(1)}, bf16[4,64,1280]{2,1,0:T(8,128)(2,1)}, u32[]{:S(2)}, u32[]{:S(2)}) %collective-permute-start.14) | collective-permute-done | bytes 655392 | tf_op jit(solution)/shard_map/ppermute | solution.py:560
  193.0 7.6 %join_own.3 = (bf16[1280,1280]{1,0:T(8,128)(2,1)S(1)}, bf16[1280,1280]{1,0:T(8,128)(2,1)}, bf16[1280,1280]{1,0:T(8,128)(2,1)}) custom-call(s32[2]{0:T(128)S(1)} %pad_add_fusion.where_ref, bf16[320,1280]{1,0:T(8,128)(2,1)S(1)} %copy-done.6, bf16[320,1280]{1,0:T(8,128)(2,1)S(1)} %bitcast.214, bf16[320,1280]{1,0:T(8,128)(2,1)S(1)} %copy-done.4, ...), custom_call_target="tpu_custom_call" | custom-call | bytes 1843200 | tf_op jit(solution)/shard_map/join_own/pallas_call | solution.py:437
  205.3 12.6 %feed.1 = (f32[256,1280]{1,0:T(8,128)}, bf16[256,1280]{1,0:T(8,128)(2,1)}, bf16[256,1280]{1,0:T(8,128)(2,1)}, bf16[256,1280]{1,0:T(8,128)(2,1)}, f32[256,1280]{1...) custom-call(f32[256,1280]{1,0:T(8,128)} %bitcast.222, ...), custom_call_target="tpu_custom_call" | custom-call | flops 6710886400 | bytes 26255360 | tf_op jit(solution)/shard_map/feed/pallas_call | solution.py:275
  218.9 8.9 %grads.1 = (bf16[4,4,15,80,128]{4,3,2,1,0:T(8,128)(2,1)}, bf16[4,4,15,80,128]{4,3,2,1,0:T(8,128)(2,1)}) custom-call(s32[1]{0:T(128)} %bitcast.19.core_ref, bf16[256,1280]{1,0:T(8,128)(2,1)} %get-tuple-element.126.refs_0_, bf16[256,1280]{1,0:T(8,128)(2,1)} %get-tuple-element.127.refs_1_, bf16[256,1280]{1,0:T(8,128)(2,1)} %bitcast.236, ...), custom_call_target="tpu_custom_call" | custom-call | flops 314572800 | bytes 491520 | tf_op jit(solution)/shard_map/grads/pallas_call | solution.py:500
  227.9 8.9 %collective-permute-done.17.refs_1_ = bf16[4,64,1408]{2,1,0:T(8,128)(2,1)S(1)} collective-permute-done((bf16[4,64,1408]{2,1,0:T(8,128)(2,1)}, bf16[4,64,1408]{2,1,0:T(8,128)(2,1)S(1)}, u32[]{:S(2)}, u32[]{:S(2)}) %collective-permute-start.17) | collective-permute-done | bytes 720928 | tf_op jit(solution)/shard_map/ppermute | solution.py:560
  238.3 8.2 %collective-permute-done.19.b_ref = bf16[4,4,15,80,128]{4,3,2,1,0:T(8,128)(2,1)} collective-permute-done((bf16[4,4,15,80,128]{4,3,2,1,0:T(8,128)(2,1)}, bf16[4,4,15,80,128]{4,3,2,1,0:T(8,128)(2,1)}, u32[]{:S(2)}, u32[]{:S(2)}) %collective-permute-start.19) | collective-permute-done | bytes 4915232 | tf_op jit(solution)/shard_map/ppermute | solution.py:557
  246.5 6.6 %add_packed.2 = (bf16[4,4,8,80,128]{4,3,2,1,0:T(8,128)(2,1)}, bf16[4,4,7,80,128]{4,3,2,1,0:T(8,128)(2,1)}) custom-call(bf16[4,4,15,80,128]{4,3,2,1,0:T(8,128)(2,1)} %get-tuple-element.133.a_ref, bf16[4,4,15,80,128]{4,3,2,1,0:T(8,128)(2,1)} %collective-permute-done.19.b_ref), custom_call_target="tpu_custom_call" | custom-call | bytes 1228800 | tf_op jit(solution)/shard_map/add_packed/pallas_call | solution.py:482
  253.1 5.0 %collective-permute-done.18.refs_2_ = bf16[4,64,1408]{2,1,0:T(8,128)(2,1)S(1)} collective-permute-done((bf16[4,64,1408]{2,1,0:T(8,128)(2,1)S(1)}, bf16[4,64,1408]{2,1,0:T(8,128)(2,1)S(1)}, u32[]{:S(2)}, u32[]{:S(2)}) %collective-permute-start.18) | collective-permute-done | bytes 720928 | tf_op jit(solution)/shard_map/ppermute | solution.py:560
  258.1 9.9 %collective-permute-start.20 = (bf16[4,64,1408]{2,1,0:T(8,128)(2,1)S(1)}, bf16[4,64,1408]{2,1,0:T(8,128)(2,1)S(1)}, u32[]{:S(2)}, u32[]{:S(2)}) collective-permute-start(bf16[4,64,1408]{2,1,0:T(8,128)(2,1)S(1)} %collective-permute-done.18.refs_2_), channel_id=1, source_target_pairs={{0,1},{1,2},{2,3},{3,0},{4,5},{5,6},{6,7},{7,4},{8,9},{9,10},{10,1... | collective-permute-start | bytes 2162696 | tf_op jit(solution)/shard_map/ppermute | solution.py:560
  272.7 14.0 %collective-permute-done.20.refs_3_ = bf16[4,64,1408]{2,1,0:T(8,128)(2,1)S(1)} collective-permute-done((bf16[4,64,1408]{2,1,0:T(8,128)(2,1)S(1)}, bf16[4,64,1408]{2,1,0:T(8,128)(2,1)S(1)}, u32[]{:S(2)}, u32[]{:S(2)}) %collective-permute-start.20) | collective-permute-done | bytes 720928 | tf_op jit(solution)/shard_map/ppermute | solution.py:560
  286.8 16.9 %attend_back.1 = (bf16[4,4,64,1280]{3,2,1,0:T(8,128)(2,1)}, bf16[4,512,1280]{2,1,0:T(8,128)(2,1)}, bf16[4,512,1280]{2,1,0:T(8,128)(2,1)}) custom-call(bf16[4,4,64,1280]{3,2,1,0:T(8,128)(2,1)} %bitcast.221, bf16[4,512,1280]{2,1,0:T(8,128)(2,1)} %bitcast.265, bf16[4,512,1280]{2,1,0:T(8,128)(2,1)} %bitcast.267, ...), custom_call_target="tpu_custom_call" | custom-call | flops 21474836480 | bytes 32071680 | tf_op jit(solution)/shard_map/attend_back/pallas_call | solution.py:257
  305.1 7.0 %convolution_convert_fusion.3.refs_2_ = bf16[1280,768]{1,0:T(8,128)(2,1)S(1)} fusion(bf16[2048,1280]{1,0:T(8,128)(2,1)} %bitcast.272, bf16[2048,768]{1,0:T(8,128)(2,1)S(1)} %copy-done.18), kind=kOutput, calls=%fused_computation.8 | convolution fusion | flops 4027514880 | bytes 10354688 | tf_op jit(solution)/shard_map/dot_general | solution.py:22
  319.2 6.4 %collective-permute-done.25 = bf16[4,7,80,128]{3,2,1,0:T(8,128)(2,1)S(1)} collective-permute-done((bf16[4,7,80,128]{3,2,1,0:T(8,128)(2,1)S(1)}, bf16[4,7,80,128]{3,2,1,0:T(8,128)(2,1)S(1)}, u32[]{:S(2)}, u32[]{:S(2)}) %collective-permute-start.25) | collective-permute-done | bytes 573472 | tf_op jit(solution)/shard_map/ppermute | solution.py:557
  332.1 5.3 %convolution_convert_fusion.refs_0_ = bf16[1280,1280]{1,0:T(8,128)(2,1)} fusion(bf16[1024,1280]{1,0:T(8,128)(2,1)S(1)} %bitcast.234, bf16[1024,1280]{1,0:T(8,128)(2,1)S(1)} %bitcast.230), kind=kOutput, calls=%fused_computation.4 | convolution fusion | flops 3357081600 | bytes 8519680 | tf_op jit(solution)/shard_map/dot_general | solution.py:22
  337.4 5.8 %split.1 = (bf16[4,4,11,80,128]{4,3,2,1,0:T(8,128)(2,1)}, bf16[4,4,11,80,128]{4,3,2,1,0:T(8,128)(2,1)}) custom-call(s32[1]{0:T(128)} %bitcast.19.core_ref, bf16[1280,1280]{1,0:T(8,128)(2,1)} %convolution_convert_fusion.refs_0_, bf16[1280,768]{1,0:T(8,128)(2,1)S(1)} %convolution_convert_fusion.4.refs_1_, bf16[1280,768]{1,0:T(8,128)(2,1)S(1)} %convolution_convert_fusion.3.refs_2_), custom_call_target="tpu_custom_call" | custom-call | bytes 1802240 | tf_op jit(solution)/shard_map/split/pallas_call | solution.py:464
  351.7 5.5 %add_packed.3 = (bf16[4,4,6,80,128]{4,3,2,1,0:T(8,128)(2,1)}, bf16[4,4,5,80,128]{4,3,2,1,0:T(8,128)(2,1)}) custom-call(bf16[4,4,11,80,128]{4,3,2,1,0:T(8,128)(2,1)} %get-tuple-element.147.a_ref, bf16[4,4,11,80,128]{4,3,2,1,0:T(8,128)(2,1)} %collective-permute-done.27.b_ref), custom_call_target="tpu_custom_call" | custom-call | bytes 901120 | tf_op jit(solution)/shard_map/add_packed/pallas_call | solution.py:482
  366.6 15.6 %byte_back.1 = (f32[2048,768]{1,0:T(8,128)}, f32[1,768]{1,0:T(1,128)}) custom-call(f32[2048,768]{1,0:T(8,128)} %bitcast.224, f32[1,768]{1,0:T(1,128)} %broadcast_in_dim.25.gain_ref, bf16[1280,768]{1,0:T(8,128)(2,1)} %copy-done.10, bf16[1280,768]{1,0:T(8,128)(2,1)} %copy-done.11, bf16[2048,1280]{1,0:T(8,128)(2,1)} %bitcast.268, bf16[2048,1280]{1,0:T(8,128)(2,1)} %bitcast.273), custom_call_target="tpu_custom_call" | custom-call | flops 16106127360 | bytes 41424896 | tf_op jit(solution)/shard_map/byte_back/pallas_call | solution.py:275
  388.9 11.2 %collective-permute-done.31 = bf16[4,64,1280]{2,1,0:T(8,128)(2,1)S(1)} collective-permute-done((bf16[4,64,1280]{2,1,0:T(8,128)(2,1)S(1)}, bf16[4,64,1280]{2,1,0:T(8,128)(2,1)S(1)}, u32[]{:S(2)}, u32[]{:S(2)}) %collective-permute-start.31) | collective-permute-done | bytes 655392 | tf_op jit(solution)/shard_map/ppermute | solution.py:560
  413.0 7.7 %collective-permute-done.39 = bf16[1,80,128]{2,1,0:T(8,128)(2,1)S(1)} collective-permute-done((bf16[1,80,128]{2,1,0:T(8,128)(2,1)S(1)}, bf16[1,80,128]{2,1,0:T(8,128)(2,1)S(1)}, u32[]{:S(2)}, u32[]{:S(2)}) %collective-permute-start.39) | collective-permute-done | bytes 20512 | tf_op jit(solution)/shard_map/ppermute | solution.py:560
  422.3 6.4 %collective-permute-done.35 = bf16[11,80,128]{2,1,0:T(8,128)(2,1)S(1)} collective-permute-done((bf16[11,80,128]{2,1,0:T(8,128)(2,1)S(1)}, bf16[11,80,128]{2,1,0:T(8,128)(2,1)S(1)}, u32[]{:S(2)}, u32[]{:S(2)}) %collective-permute-start.35) | collective-permute-done | bytes 225312 | tf_op jit(solution)/shard_map/ppermute | solution.py:560
  (312 shorter events, 166.2 us)
Async XLA Ops:
  7.2 76.6 %all-gather.5.cloned.1.call-start = ((), (), s32[]{:S(2)}) async-start(), calls=%async_computation | async-start | bytes 3379200 | tf_op jit(solution)/shard_map/all_gather | solution.py:600
  37.9 143.6 %all-gather.7.cloned.1.call-start = ((), (), s32[]{:S(2)}) async-start(), calls=%async_computation.1 | async-start | bytes 4608000 | tf_op jit(solution)/shard_map/all_gather | solution.py:600
  37.9 15.4 %collective-permute-start.3 = (bf16[4,64,1280]{2,1,0:T(8,128)(2,1)S(1)}, bf16[4,64,1280]{2,1,0:T(8,128)(2,1)S(1)}, u32[]{:S(2)}, u32[]{:S(2)}) collective-permute-start(bf16[4,64,1280]{2,1,0:T(8,128)(2,1)S(1)} %multiply_convert_fusion.1), channel_id=1, source_target_pairs={{0,1},{1,2},{2,3},{3,0},{4,5},{5,6},{6,7},{7,4},{8,9},{9,10},{10,1... | collective-permute-start | bytes 1966088 | tf_op jit(solution)/shard_map/ppermute | solution.py:560
  53.3 14.4 %collective-permute-start.4 = (bf16[4,64,1280]{2,1,0:T(8,128)(2,1)S(1)}, bf16[4,64,1280]{2,1,0:T(8,128)(2,1)S(1)}, u32[]{:S(2)}, u32[]{:S(2)}) collective-permute-start(bf16[4,64,1280]{2,1,0:T(8,128)(2,1)S(1)} %collective-permute-done.3), channel_id=1, source_target_pairs={{0,1},{1,2},{2,3},{3,0},{4,5},{5,6},{6,7},{7,4},{8,9},{9,10},{10,1... | collective-permute-start | bytes 1966088 | tf_op jit(solution)/shard_map/ppermute | solution.py:560
  67.7 13.6 %collective-permute-start.5 = (bf16[4,64,1280]{2,1,0:T(8,128)(2,1)S(1)}, bf16[4,64,1280]{2,1,0:T(8,128)(2,1)}, u32[]{:S(2)}, u32[]{:S(2)}) collective-permute-start(bf16[4,64,1280]{2,1,0:T(8,128)(2,1)S(1)} %collective-permute-done.4), channel_id=1, source_target_pairs={{0,1},{1,2},{2,3},{3,0},{4,5},{5,6},{6,7},{7,4},{8,9},{9,10},{10,1... | collective-permute-start | bytes 1966088 | tf_op jit(solution)/shard_map/ppermute | solution.py:560
  100.0 18.1 %collective-permute-start.8 = (bf16[16,80,128]{2,0,1:T(8,128)(2,1)S(1)}, bf16[16,80,128]{2,0,1:T(8,128)(2,1)S(1)}, u32[]{:S(2)}, u32[]{:S(2)}) collective-permute-start(bf16[16,80,128]{2,0,1:T(8,128)(2,1)S(1)} %collective-permute-done.7), channel_id=1, source_target_pairs={{0,1},{1,2},{2,3},{3,0},{4,5},{5,6},{6,7},{7,4},{8,9},{9,10},{10,1... | collective-permute-start | bytes 983048 | tf_op jit(solution)/shard_map/ppermute | solution.py:560
  150.2 13.6 %collective-permute-start.13 = (bf16[4,64,1280]{2,1,0:T(8,128)(2,1)}, bf16[4,64,1280]{2,1,0:T(8,128)(2,1)}, u32[]{:S(2)}, u32[]{:S(2)}) collective-permute-start(bf16[4,64,1280]{2,1,0:T(8,128)(2,1)} %slice_bitcast_fusion.1), channel_id=1, source_target_pairs={{0,1},{1,2},{2,3},{3,0},{4,5},{5,6},{6,7},{7,4},{8,9},{9,10},{10,1... | collective-permute-start | bytes 1966088 | tf_op jit(solution)/shard_map/ppermute | solution.py:560
  165.0 16.2 %collective-permute-start.14 = (bf16[4,64,1280]{2,1,0:T(8,128)(2,1)S(1)}, bf16[4,64,1280]{2,1,0:T(8,128)(2,1)}, u32[]{:S(2)}, u32[]{:S(2)}) collective-permute-start(bf16[4,64,1280]{2,1,0:T(8,128)(2,1)S(1)} %fusion.10), channel_id=1, source_target_pairs={{0,1},{1,2},{2,3},{3,0},{4,5},{5,6},{6,7},{7,4},{8,9},{9,10},{10,1... | collective-permute-start | bytes 1966088 | tf_op jit(solution)/shard_map/ppermute | solution.py:560
  186.0 18.3 %collective-permute-start.15 = (bf16[4,64,1280]{2,1,0:T(8,128)(2,1)S(1)}, bf16[4,64,1280]{2,1,0:T(8,128)(2,1)S(1)}, u32[]{:S(2)}, u32[]{:S(2)}) collective-permute-start(bf16[4,64,1280]{2,1,0:T(8,128)(2,1)S(1)} %fusion.9), channel_id=1, source_target_pairs={{0,1},{1,2},{2,3},{3,0},{4,5},{5,6},{6,7},{7,4},{8,9},{9,10},{10,1... | collective-permute-start | bytes 1966088 | tf_op jit(solution)/shard_map/ppermute | solution.py:560
  218.0 18.8 %collective-permute-start.17 = (bf16[4,64,1408]{2,1,0:T(8,128)(2,1)}, bf16[4,64,1408]{2,1,0:T(8,128)(2,1)S(1)}, u32[]{:S(2)}, u32[]{:S(2)}) collective-permute-start(bf16[4,64,1408]{2,1,0:T(8,128)(2,1)} %bitcast.217), channel_id=1, source_target_pairs={{0,1},{1,2},{2,3},{3,0},{4,5},{5,6},{6,7},{7,4},{8,9},{9,10},{10,1... | collective-permute-start | bytes 2162696 | tf_op jit(solution)/shard_map/ppermute | solution.py:560
  238.3 19.8 %collective-permute-start.18 = (bf16[4,64,1408]{2,1,0:T(8,128)(2,1)S(1)}, bf16[4,64,1408]{2,1,0:T(8,128)(2,1)S(1)}, u32[]{:S(2)}, u32[]{:S(2)}) collective-permute-start(bf16[4,64,1408]{2,1,0:T(8,128)(2,1)S(1)} %collective-permute-done.17.refs_1_), channel_id=1, source_target_pairs={{0,1},{1,2},{2,3},{3,0},{4,5},{5,6},{6,7},{7,4},{8,9},{9,10},{10,1... | collective-permute-start | bytes 2162696 | tf_op jit(solution)/shard_map/ppermute | solution.py:560
  258.1 28.7 %collective-permute-start.20 = (bf16[4,64,1408]{2,1,0:T(8,128)(2,1)S(1)}, bf16[4,64,1408]{2,1,0:T(8,128)(2,1)S(1)}, u32[]{:S(2)}, u32[]{:S(2)}) collective-permute-start(bf16[4,64,1408]{2,1,0:T(8,128)(2,1)S(1)} %collective-permute-done.18.refs_2_), channel_id=1, source_target_pairs={{0,1},{1,2},{2,3},{3,0},{4,5},{5,6},{6,7},{7,4},{8,9},{9,10},{10,1... | collective-permute-start | bytes 2162696 | tf_op jit(solution)/shard_map/ppermute | solution.py:560
  269.4 42.7 %collective-permute-start.24 = (bf16[2,4,7,80,128]{4,3,2,1,0:T(8,128)(2,1)S(1)}, bf16[2,4,7,80,128]{4,3,2,1,0:T(8,128)(2,1)S(1)}, u32[]{:S(2)}, u32[]{:S(2)}) collective-permute-start(bf16[2,4,7,80,128]{4,3,2,1,0:T(8,128)(2,1)S(1)} %dynamic-slice_bitcast_fusion.1), channel_id=1, source_target_pairs={{0,16},{4,20},{8,24},{12,28},{16,0},{20,4},{24,8},{28,12},{1,17},{... | collective-permute-start | bytes 3440648 | tf_op jit(solution)/shard_map/ppermute | solution.py:557
  271.5 41.6 %collective-permute-start.22 = (bf16[2,4,8,80,128]{4,3,2,1,0:T(8,128)(2,1)S(1)}, bf16[2,4,8,80,128]{4,3,2,1,0:T(8,128)(2,1)S(1)}, u32[]{:S(2)}, u32[]{:S(2)}) collective-permute-start(bf16[2,4,8,80,128]{4,3,2,1,0:T(8,128)(2,1)S(1)} %dynamic-slice_bitcast_fusion), channel_id=1, source_target_pairs={{0,8},{4,12},{8,0},{12,4},{16,24},{20,28},{24,16},{28,20},{1,9},{5... | collective-permute-start | bytes 3932168 | tf_op jit(solution)/shard_map/ppermute | solution.py:557
  305.0 24.4 %collective-permute-start.21 = (bf16[4,64,1280]{2,1,0:T(8,128)(2,1)S(1)}, bf16[4,64,1280]{2,1,0:T(8,128)(2,1)S(1)}, u32[]{:S(2)}, u32[]{:S(2)}) collective-permute-start(bf16[4,64,1280]{2,1,0:T(8,128)(2,1)S(1)} %slice_bitcast_fusion), channel_id=1, source_target_pairs={{0,1},{1,2},{2,3},{3,0},{4,5},{5,6},{6,7},{7,4},{8,9},{9,10},{10,1... | collective-permute-start | bytes 1966088 | tf_op jit(solution)/shard_map/ppermute | solution.py:560
  312.5 13.2 %collective-permute-start.25 = (bf16[4,7,80,128]{3,2,1,0:T(8,128)(2,1)S(1)}, bf16[4,7,80,128]{3,2,1,0:T(8,128)(2,1)S(1)}, u32[]{:S(2)}, u32[]{:S(2)}) collective-permute-start(bf16[4,7,80,128]{3,2,1,0:T(8,128)(2,1)S(1)} %dynamic-slice_bitcast_fusion.5), channel_id=1, source_target_pairs={{0,8},{4,12},{8,0},{12,4},{16,24},{20,28},{24,16},{28,20},{1,9},{5... | collective-permute-start | bytes 1720328 | tf_op jit(solution)/shard_map/ppermute | solution.py:557
  314.2 14.9 %collective-permute-start.23 = (bf16[4,8,80,128]{3,2,1,0:T(8,128)(2,1)S(1)}, bf16[4,8,80,128]{3,2,1,0:T(8,128)(2,1)S(1)}, u32[]{:S(2)}, u32[]{:S(2)}) collective-permute-start(bf16[4,8,80,128]{3,2,1,0:T(8,128)(2,1)S(1)} %dynamic-slice_bitcast_fusion.4), channel_id=1, source_target_pairs={{0,16},{4,20},{8,24},{12,28},{16,0},{20,4},{24,8},{28,12},{1,17},{... | collective-permute-start | bytes 1966088 | tf_op jit(solution)/shard_map/ppermute | solution.py:557
  357.4 25.7 %collective-permute-start.40 = (bf16[15,80,128]{2,1,0:T(8,128)(2,1)S(1)}, bf16[15,80,128]{2,1,0:T(8,128)(2,1)}, u32[]{:S(2)}, u32[]{:S(2)}) collective-permute-start(bf16[15,80,128]{2,1,0:T(8,128)(2,1)S(1)} %fusion.16), channel_id=1, source_target_pairs={{0,1},{1,2},{2,3},{3,0},{4,5},{5,6},{6,7},{7,4},{8,9},{9,10},{10,1... | collective-permute-start | bytes 921608 | tf_op jit(solution)/shard_map/ppermute | solution.py:560
  360.9 25.0 %collective-permute-start.29 = (bf16[2,4,5,80,128]{4,3,2,1,0:T(8,128)(2,1)}, bf16[2,4,5,80,128]{4,3,2,1,0:T(8,128)(2,1)}, u32[]{:S(2)}, u32[]{:S(2)}) collective-permute-start(bf16[2,4,5,80,128]{4,3,2,1,0:T(8,128)(2,1)} %dynamic-slice_bitcast_fusion.3), channel_id=1, source_target_pairs={{0,16},{4,20},{8,24},{12,28},{16,0},{20,4},{24,8},{28,12},{1,17},{... | collective-permute-start | bytes 2457608 | tf_op jit(solution)/shard_map/ppermute | solution.py:557
  361.5 25.7 %collective-permute-start.28 = (bf16[2,4,6,80,128]{4,3,2,1,0:T(8,128)(2,1)S(1)}, bf16[2,4,6,80,128]{4,3,2,1,0:T(8,128)(2,1)S(1)}, u32[]{:S(2)}, u32[]{:S(2)}) collective-permute-start(bf16[2,4,6,80,128]{4,3,2,1,0:T(8,128)(2,1)S(1)} %dynamic-slice_bitcast_fusion.2), channel_id=1, source_target_pairs={{0,8},{4,12},{8,0},{12,4},{16,24},{20,28},{24,16},{28,20},{1,9},{5... | collective-permute-start | bytes 2949128 | tf_op jit(solution)/shard_map/ppermute | solution.py:557
  362.8 21.3 %collective-permute-start.30 = (bf16[4,64,1280]{2,1,0:T(8,128)(2,1)}, bf16[4,64,1280]{2,1,0:T(8,128)(2,1)}, u32[]{:S(2)}, u32[]{:S(2)}) collective-permute-start(bf16[4,64,1280]{2,1,0:T(8,128)(2,1)} %fusion.6), channel_id=1, source_target_pairs={{0,1},{1,2},{2,3},{3,0},{4,5},{5,6},{6,7},{7,4},{8,9},{9,10},{10,1... | collective-permute-start | bytes 1966088 | tf_op jit(solution)/shard_map/ppermute | solution.py:560
  385.4 14.8 %collective-permute-start.31 = (bf16[4,64,1280]{2,1,0:T(8,128)(2,1)S(1)}, bf16[4,64,1280]{2,1,0:T(8,128)(2,1)S(1)}, u32[]{:S(2)}, u32[]{:S(2)}) collective-permute-start(bf16[4,64,1280]{2,1,0:T(8,128)(2,1)S(1)} %fusion.5), channel_id=1, source_target_pairs={{0,1},{1,2},{2,3},{3,0},{4,5},{5,6},{6,7},{7,4},{8,9},{9,10},{10,1... | collective-permute-start | bytes 1966088 | tf_op jit(solution)/shard_map/ppermute | solution.py:560
  387.6 12.8 %collective-permute-start.33 = (bf16[4,5,80,128]{3,2,1,0:T(8,128)(2,1)S(1)}, bf16[4,5,80,128]{3,2,1,0:T(8,128)(2,1)S(1)}, u32[]{:S(2)}, u32[]{:S(2)}) collective-permute-start(bf16[4,5,80,128]{3,2,1,0:T(8,128)(2,1)S(1)} %dynamic-slice_bitcast_fusion.7), channel_id=1, source_target_pairs={{0,8},{4,12},{8,0},{12,4},{16,24},{20,28},{24,16},{28,20},{1,9},{5... | collective-permute-start | bytes 1228808 | tf_op jit(solution)/shard_map/ppermute | solution.py:557
  388.0 12.6 %collective-permute-start.32 = (bf16[4,6,80,128]{3,2,1,0:T(8,128)(2,1)S(1)}, bf16[4,6,80,128]{3,2,1,0:T(8,128)(2,1)S(1)}, u32[]{:S(2)}, u32[]{:S(2)}) collective-permute-start(bf16[4,6,80,128]{3,2,1,0:T(8,128)(2,1)S(1)} %dynamic-slice_bitcast_fusion.6), channel_id=1, source_target_pairs={{0,16},{4,20},{8,24},{12,28},{16,0},{20,4},{24,8},{28,12},{1,17},{... | collective-permute-start | bytes 1474568 | tf_op jit(solution)/shard_map/ppermute | solution.py:557
  408.8 11.8 %collective-permute-start.39 = (bf16[1,80,128]{2,1,0:T(8,128)(2,1)S(1)}, bf16[1,80,128]{2,1,0:T(8,128)(2,1)S(1)}, u32[]{:S(2)}, u32[]{:S(2)}) collective-permute-start(bf16[1,80,128]{2,1,0:T(8,128)(2,1)S(1)} %fusion.43), channel_id=1, source_target_pairs={{0,3},{1,0},{2,1},{3,2},{4,7},{5,4},{6,5},{7,6},{8,11},{9,8},{10,9... | collective-permute-start | bytes 61448 | tf_op jit(solution)/shard_map/ppermute | solution.py:560
  408.9 12.3 %collective-permute-start.34 = (bf16[11,80,128]{2,1,0:T(8,128)(2,1)S(1)}, bf16[11,80,128]{2,1,0:T(8,128)(2,1)S(1)}, u32[]{:S(2)}, u32[]{:S(2)}) collective-permute-start(bf16[11,80,128]{2,1,0:T(8,128)(2,1)S(1)} %get-tuple-element.176), channel_id=1, source_target_pairs={{0,1},{1,2},{2,3},{3,0},{4,5},{5,6},{6,7},{7,4},{8,9},{9,10},{10,1... | collective-permute-start | bytes 675848 | tf_op jit(solution)/shard_map/ppermute | solution.py:560
  410.4 18.3 %collective-permute-start.35 = (bf16[11,80,128]{2,1,0:T(8,128)(2,1)S(1)}, bf16[11,80,128]{2,1,0:T(8,128)(2,1)S(1)}, u32[]{:S(2)}, u32[]{:S(2)}) collective-permute-start(bf16[11,80,128]{2,1,0:T(8,128)(2,1)S(1)} %get-tuple-element.177), channel_id=1, source_target_pairs={{0,2},{1,3},{2,0},{3,1},{4,6},{5,7},{6,4},{7,5},{8,10},{9,11},{10,... | collective-permute-start | bytes 675848 | tf_op jit(solution)/shard_map/ppermute | solution.py:560
  412.3 21.1 %collective-permute-start.36 = (bf16[11,80,128]{2,1,0:T(8,128)(2,1)S(1)}, bf16[11,80,128]{2,1,0:T(8,128)(2,1)S(1)}, u32[]{:S(2)}, u32[]{:S(2)}) collective-permute-start(bf16[11,80,128]{2,1,0:T(8,128)(2,1)S(1)} %get-tuple-element.178), channel_id=1, source_target_pairs={{0,3},{1,0},{2,1},{3,2},{4,7},{5,4},{6,5},{7,6},{8,11},{9,8},{10,9... | collective-permute-start | bytes 675848 | tf_op jit(solution)/shard_map/ppermute | solution.py:560
  412.4 21.1 %collective-permute-start.42 = (bf16[15,80,128]{2,1,0:T(8,128)(2,1)S(1)}, bf16[15,80,128]{2,1,0:T(8,128)(2,1)S(1)}, u32[]{:S(2)}, u32[]{:S(2)}) collective-permute-start(bf16[15,80,128]{2,1,0:T(8,128)(2,1)S(1)} %fusion.14), channel_id=1, source_target_pairs={{0,8},{4,12},{8,0},{12,4},{16,24},{20,28},{24,16},{28,20},{1,9},{5... | collective-permute-start | bytes 921608 | tf_op jit(solution)/shard_map/ppermute | solution.py:557
  420.6 12.9 %collective-permute-start.43 = (bf16[15,80,128]{2,1,0:T(8,128)(2,1)S(1)}, bf16[15,80,128]{2,1,0:T(8,128)(2,1)S(1)}, u32[]{:S(2)}, u32[]{:S(2)}) collective-permute-start(bf16[15,80,128]{2,1,0:T(8,128)(2,1)S(1)} %fusion.14), channel_id=1, source_target_pairs={{0,16},{4,20},{8,24},{12,28},{16,0},{20,4},{24,8},{28,12},{1,17},{... | collective-permute-start | bytes 921608 | tf_op jit(solution)/shard_map/ppermute | solution.py:557
  421.2 12.3 %collective-permute-start.44 = (bf16[15,80,128]{2,1,0:T(8,128)(2,1)S(1)}, bf16[15,80,128]{2,1,0:T(8,128)(2,1)S(1)}, u32[]{:S(2)}, u32[]{:S(2)}) collective-permute-start(bf16[15,80,128]{2,1,0:T(8,128)(2,1)S(1)} %fusion.14), channel_id=1, source_target_pairs={{0,24},{4,28},{8,16},{12,20},{16,8},{20,12},{24,0},{28,4},{1,25},{... | collective-permute-start | bytes 921608 | tf_op jit(solution)/shard_map/ppermute | solution.py:557
  437.3 18.4 %collective-permute-start.49 = (bf16[4,1,15,80,128]{4,3,2,1,0:T(8,128)(2,1)S(1)}, bf16[4,1,15,80,128]{4,3,2,1,0:T(8,128)(2,1)S(1)}, u32[]{:S(2)}, u32[]{:S(2)}) collective-permute-start(bf16[4,1,15,80,128]{4,3,2,1,0:T(8,128)(2,1)S(1)} %bitcast.208), channel_id=1, source_target_pairs={{0,4},{4,0},{8,12},{12,8},{16,20},{20,16},{24,28},{28,24},{1,5},{5... | collective-permute-start | bytes 3686408 | tf_op jit(solution)/shard_map/ppermute | solution.py:557
  (70 other events, 706.1 us)
Sparse Core Ops, SparseCore 0:
  38.0 45.7 all-gather.4
  130.4 51.0 all-gather.6
